TPU v7x, 32 devices: a whole 2x2x4 slice. The times are simulated.
32 devices in a mesh: dp: 16 (over z, y, x), rep: 2 (over core).
Axes of the slice: x: 2, y: 2, z: 4, core: 2. Of those that a mesh axis runs over, the one named last changes fastest.
Arguments:
- tokens_in: bfloat16 [8192, 576], P(('dp', 'rep')), may hold values from -12 to 12
- positions: int32 [8192], P(('dp', 'rep')), may hold values from 0 to 127, as said below
- params: bfloat16 [3540096], P('dp'), may hold values from -0.5 to 1.5, as said below
- cotangent: bfloat16 [8192, 576], P(('dp', 'rep')), may hold values from -6 to 6
Outputs:
- output: bfloat16 [8192, 576], P(('dp', 'rep'))
- grad_input: float32 [8192, 576], P(('dp', 'rep'))
- grad_params: float32 [3540096], P('dp')
- grad_gain_mid: float32 [576], replicated
Inputs may be any that keep to these rules, and one draw needn't show every extreme that they name: `positions`: positions count up by one from 0 and restart at 0 where a document begins, several times in most sequences; in sequence 0 they run 0 to 127. `params`: the norm gains lie in 0.5 to 1.5.
All inputs are finite; a program needn't handle non-finite values.
Results may differ from a plain program's by a relative error of at most 0.012.
Values may be sent and summed in bfloat16 or wider, within the bound.
No kernel may reach another device: no remote copies, remote signals or barrier semaphores. Data moves between devices by JAX's collectives and lax.ppermute only.
A program may use at most 128 MiB of HBM per device.

v0:
```python
import jax
import jax.numpy as jnp
from jax import lax
from jax.experimental import pallas as pl
from jax.experimental.pallas import tpu as pltpu
from jax.sharding import PartitionSpec as P

HEADS = 9
KV_HEADS = 3
HEAD = 64
FF = 1536
SEQ_LEN = 128
PLANES = 4
CANON = 16

EPS = 1e-05
ROPE_BASE = 100000.0

F32, BF16 = jnp.float32, jnp.bfloat16
ROWS, HALF = 1728, 880
NARROW, WIDE = 384, 144
VMEM_LIMIT = 52 * 1024 * 1024


class Layout:
    def __init__(self, count, total, width):
        self.count = count
        self.width = width
        self.gains = 2 * width
        self.shard = total // count
        self.chunk = (total - self.gains) // count
        self.step = self.gains // count
        self.rows = self.chunk // 128
        half = -(-(self.rows + 10) // 2)
        self.half = -(-half // 16) * 16
        self.first = -(-(self.half // 2) // 16) * 16
        self.extra = 2 * self.half - self.rows
        self.bits = count.bit_length() - 1
        rest = self.bits - 2
        self.x_bits = -(-rest // 2)
        self.y_bits = rest - self.x_bits
        self.in_plane = 1 << rest


def pack_wide(flat, width):
    panels = width // 128
    return flat.reshape(-1, panels, 128).transpose(1, 0, 2).reshape(-1, 128)


def unpack_wide(rows, width):
    panels = width // 128
    return rows.reshape(panels, -1, 128).transpose(1, 0, 2).reshape(-1)


def pack_narrow(flat):
    rows = flat.reshape(-1, 576)
    count = rows.shape[0]
    panels = rows[:, :512].reshape(count, 4, 128).transpose(1, 0, 2).reshape(-1, 128)
    tail = rows[:, 512:]
    return jnp.concatenate([panels, jnp.concatenate([tail[: count // 2], tail[count // 2 :]], 1)], 0)


def unpack_narrow(packed):
    count = packed.shape[0] * 2 // 9
    panels = packed[: 4 * count].reshape(4, count, 128).transpose(1, 0, 2).reshape(count, 512)
    half = packed[4 * count :]
    tail = jnp.concatenate([half[:, :64], half[:, 64:]], 0)
    return jnp.concatenate([panels, tail], 1).reshape(-1)


def head_narrow(flat):
    rows = flat.reshape(2, 576)
    tail = jnp.pad(rows[:, 512:], ((0, 0), (64, 0)))
    return jnp.concatenate([rows[:, :512].reshape(8, 128), tail], 0)


def unhead_narrow(rows):
    return jnp.concatenate([rows[:8].reshape(2, 512), rows[8:10, 64:]], 1).reshape(-1)


def head_wide(flat):
    return jnp.pad(flat.reshape(9, 128), ((0, 1), (0, 0)))


def unhead_wide(rows):
    return rows[:9].reshape(-1)


def is_wide(index, count):
    return (index >= count // 4) & (index < 3 * count // 4)


def pack_payload(window, index, lay):
    head, chunk = window[: lay.gains], window[lay.gains :]
    body = jnp.where(is_wide(index, lay.count), pack_wide(chunk, FF), pack_narrow(chunk))
    top = jnp.where(is_wide(index - 1, lay.count), head_wide(head), head_narrow(head))
    return jnp.concatenate([body, jnp.pad(top, ((0, lay.extra - 10), (0, 0)))], 0)


def unpack_payload(rows, index, lay):
    body, top = rows[: lay.rows], rows[lay.rows : lay.rows + 10]
    chunk = jnp.where(is_wide(index, lay.count), unpack_wide(body, FF), unpack_narrow(body))
    head = jnp.where(is_wide(index - 1, lay.count), unhead_wide(top), unhead_narrow(top))
    return jnp.concatenate([head, chunk])


def swap(value, mask, count):
    return lax.ppermute(value, "dp", [(i, i ^ mask) for i in range(count)])


def swap_rep(value):
    return lax.ppermute(value, "rep", [(0, 1), (1, 0)])


def gather_axis(value, shift, size, count):
    return jnp.stack([value] + [swap(value, d << shift, count) for d in range(1, size)], 0)


def gather(half, lay):
    n = lay.count
    x_size, y_size = 1 << lay.x_bits, 1 << lay.y_bits
    planes = [half] + [swap(half, s << (lay.bits - 2), n) for s in range(1, PLANES)]
    own, twin = [], []
    for plane in planes:
        first, second = plane[: lay.first], plane[lay.first :]
        first = gather_axis(gather_axis(first, 0, x_size, n), lay.x_bits, y_size, n)
        second = gather_axis(gather_axis(second, lay.x_bits, y_size, n), 0, x_size, n)
        second = second.transpose(1, 0, 2, 3)
        whole = jnp.concatenate([first, second], 2).reshape(lay.in_plane, lay.half, 128)
        own.append(whole)
        twin.append(swap_rep(whole))
    return own, twin


def add_axis(value, shift, size, count):
    total = value[0].astype(jnp.float32)
    for d in range(1, size):
        total = total + swap(value[d], d << shift, count).astype(jnp.float32)
    return total.astype(value.dtype)


def reduce_plane(value, lay):
    n = lay.count
    x_size, y_size = 1 << lay.x_bits, 1 << lay.y_bits
    grid = value.reshape(y_size, x_size, lay.half, 128)
    first, second = grid[:, :, : lay.first], grid[:, :, lay.first :]
    first = add_axis(add_axis(first, lay.x_bits, y_size, n), 0, x_size, n)
    second = add_axis(add_axis(second.transpose(1, 0, 2, 3), 0, x_size, n), lay.x_bits, y_size, n)
    return jnp.concatenate([first, second], 0)


def sum_everywhere(value, lay):
    value = value + swap_rep(value)
    for bit in range(lay.bits):
        value = value + swap(value, 1 << bit, lay.count)
    return value


def rope_tables(places):
    expon = jnp.arange(HEAD // 2).astype(jnp.float32) * (2.0 / HEAD)
    inverse = jnp.power(ROPE_BASE, -expon)
    angle = places.astype(jnp.float32)[..., None] * inverse
    return (jnp.cos(angle), jnp.sin(angle))


def dot(left, right):
    return jnp.dot(left, right, preferred_element_type=F32)


def dot_nt(left, right):
    return lax.dot_general(left, right, (((1,), (1,)), ((), ())), preferred_element_type=F32)


def dot_tn(left, right):
    return dot(left.astype(F32).T.astype(BF16), right)


def row_of_head(head, which):
    parts = [head[4 * which + j : 4 * which + j + 1] for j in range(4)]
    return jnp.concatenate(parts + [head[8 + which : 9 + which, 64:]], 1)


def head_of_rows(rows):
    parts = [row[:, 128 * j : 128 * j + 128] for row in rows for j in range(4)]
    zeros = jnp.zeros((1, 64), F32)
    parts = parts + [jnp.concatenate([zeros, row[:, 512:]], 1) for row in rows]
    return jnp.concatenate(parts + [jnp.zeros((6, 128), F32)], 0)


def load_narrow(ref, index):
    parts = [ref[index, NARROW * j : NARROW * (j + 1), :] for j in range(4)]
    half = ref[index, 4 * NARROW : ROWS, :]
    tail = jnp.concatenate([half[:, :64], half[:, 64:]], 0)
    return jnp.concatenate(parts + [tail], 1)


def store_narrow(ref, index, value):
    for j in range(4):
        ref[index, NARROW * j : NARROW * (j + 1), :] = value[:, 128 * j : 128 * (j + 1)].astype(BF16)
    tail = value[:, 512:]
    tail = jnp.concatenate([tail[: NARROW // 2], tail[NARROW // 2 :]], 1)
    ref[index, 4 * NARROW : ROWS, :] = tail.astype(BF16)


def narrow_tiles():
    tiles = [(NARROW * (j + 1) - 16, j, 4 + j) for j in range(4)]
    return tiles + [(ROWS - 16, 8, 9)]


def add_tail(ref, index, wide):
    head = ref[index + 1, ROWS : ROWS + 16, :].astype(F32)
    row = lax.broadcasted_iota(jnp.int32, (16, 128), 0)
    if wide:
        for k in range(9):
            at = WIDE * (4 + k) - 16
            tile = ref[index, at : at + 16, :].astype(F32)
            tile = tile + jnp.where(row == 15, head[k : k + 1], 0.0)
            ref[index, at : at + 16, :] = tile.astype(BF16)
    else:
        for at, upper, lower in narrow_tiles():
            tile = ref[index, at : at + 16, :].astype(F32)
            tile = tile + jnp.where(row == 14, head[upper : upper + 1], 0.0)
            tile = tile + jnp.where(row == 15, head[lower : lower + 1], 0.0)
            ref[index, at : at + 16, :] = tile.astype(BF16)


def tail_of(ref, index, wide):
    if wide:
        parts = []
        for k in range(9):
            at = WIDE * (4 + k) - 16
            parts.append(ref[index, at : at + 16, :].astype(F32)[15:16])
        return jnp.concatenate(parts + [jnp.zeros((7, 128), F32)], 0)
    tiles = [ref[index, at : at + 16, :].astype(F32) for at, _, _ in narrow_tiles()]
    parts = [tile[14:15] for tile in tiles[:4]] + [tile[15:16] for tile in tiles[:4]]
    parts = parts + [tiles[4][14:15], tiles[4][15:16]]
    return jnp.concatenate(parts + [jnp.zeros((6, 128), F32)], 0)


def spread(value, first, second, out):
    for m in range(3):
        part = value[:, 192 * m : 192 * (m + 1)].astype(F32)
        first[pl.ds(m, 192, stride=3), :] = part[:, :128]
        second[pl.ds(m, 192, stride=3), :] = jnp.concatenate([part[:, 128:], part[:, 128:]], 1)
    out[:, :128] = first[...].astype(BF16)
    out[:, 128:] = second[:, :64].astype(BF16)


def unspread(value, first, second):
    first[...] = value[:, :128]
    second[...] = jnp.concatenate([value[:, 128:], value[:, 128:]], 1)
    parts = []
    for m in range(3):
        parts.append(first[pl.ds(m, 192, stride=3), :])
        parts.append(second[pl.ds(m, 192, stride=3), :][:, :64])
    return jnp.concatenate(parts, 1)


def turn(vector, cosine, sine):
    swapped = jnp.concatenate([vector[:, 32:], vector[:, :32]], 1)
    return vector * cosine + swapped * sine


def piece_copies(idx, refs, dst, plane_base, sems, outward):
    plane, place, core = idx[0], idx[1], idx[2]
    copies = []
    for s, (own, twin) in enumerate(refs):
        for d in range(4):
            chunk = jnp.bitwise_xor(place, d)
            if plane_base is None:
                chunk = chunk + 4 * jnp.bitwise_xor(plane, s)
            else:
                chunk = chunk + plane_base + 4 * s
            for which, ref in enumerate((own, twin)):
                at = jnp.bitwise_xor(core, which) * HALF
                inner = dst.at[chunk, pl.ds(pl.multiple_of(at, 16), HALF), :]
                outer = ref.at[d]
                pair = (inner, outer) if outward else (outer, inner)
                copies.append(pltpu.make_async_copy(pair[0], pair[1], sems.at[len(copies)]))
    return copies


def first_kernel(
    idx, own0, own1, own2, own3, twin0, twin1, twin2, twin3, tok, cot, cos, sin,
    y_out, dr_out, att_out, p_out, q_out, k_out, v_out, wq, wk, wv, wo, gain_out, dg_out,
    keep1, keep2, keep3, send1, send2, send3,
    w, g, att, n2_ref, n2t_ref, y_acc, dn_acc, first, second, sems, out_sems,
):
    loads = piece_copies(
        idx, [(own0, twin0), (own1, twin1), (own2, twin2), (own3, twin3)], w, None, sems, False
    )
    for copy in loads:
        copy.start()
    tokens = tok.shape[0]
    x = tok[...].astype(F32)
    normed = x * lax.rsqrt(jnp.mean(x * x, -1, keepdims=True) + EPS)
    for copy in loads:
        copy.wait()
    for c in (0, 1, 2, 3, 12, 13, 14):
        add_tail(w, c, False)

    def fix(i, carry):
        add_tail(w, i + 4, True)
        return carry

    lax.fori_loop(0, 8, fix, 0)
    gains = w[0, ROWS : ROWS + 16, :].astype(F32)
    gain_in, gain_mid = row_of_head(gains, 0), row_of_head(gains, 1)
    gain_out[...] = gain_in
    n1 = (normed * gain_in).astype(BF16)
    wq[:NARROW, :] = load_narrow(w, 0)
    mixed_chunk = load_narrow(w, 1)
    wq[NARROW:, :] = mixed_chunk[:192]
    spread(mixed_chunk[192:], first, second, wk)
    mixed_chunk = load_narrow(w, 2)
    spread(mixed_chunk[:192], first, second, wv)
    wo[:192, :] = mixed_chunk[192:]
    wo[192:, :] = load_narrow(w, 3)

    query, keys, values = dot(n1, wq[...]), dot(n1, wk[...]), dot(n1, wv[...])
    row = lax.broadcasted_iota(jnp.int32, (3 * SEQ_LEN, SEQ_LEN), 0)
    causal = jnp.bitwise_and(row, SEQ_LEN - 1) >= lax.broadcasted_iota(
        jnp.int32, (3 * SEQ_LEN, SEQ_LEN), 1
    )
    for b in range(tokens // SEQ_LEN):
        part = slice(SEQ_LEN * b, SEQ_LEN * (b + 1))
        cosine, sine = cos[part, :], sin[part, :]
        for kv in range(KV_HEADS):
            at = KV_HEADS * b + kv
            heads = [
                turn(query[part, HEAD * h : HEAD * (h + 1)], cosine, sine)
                for h in range(3 * kv, 3 * kv + 3)
            ]
            q3 = jnp.concatenate(heads, 0).astype(BF16)
            k1 = turn(keys[part, HEAD * kv : HEAD * (kv + 1)], cosine, sine).astype(BF16)
            v1 = values[part, HEAD * kv : HEAD * (kv + 1)].astype(BF16)
            q_out[at], k_out[at], v_out[at] = q3, k1, v1
            score = jnp.where(causal, dot_nt(q3, k1) * HEAD**-0.5, -1e30)
            expon = jnp.exp(score - jnp.max(score, -1, keepdims=True))
            probs = expon / jnp.sum(expon, -1, keepdims=True)
            p_out[at] = probs
            mix = dot(probs.astype(BF16), v1)
            for r in range(3):
                h = 3 * kv + r
                att[part, HEAD * h : HEAD * (h + 1)] = mix[SEQ_LEN * r : SEQ_LEN * (r + 1)]
    attended = att[...].astype(BF16)
    att_out[...] = attended
    mixed = x + dot(attended, wo[...])
    inverse = lax.rsqrt(jnp.mean(mixed * mixed, -1, keepdims=True) + EPS)
    normed_mid = mixed * inverse
    n2 = normed_mid * gain_mid
    n2_ref[...] = n2.astype(BF16)
    n2t_ref[...] = n2.astype(BF16).astype(F32).T.astype(BF16)
    y_acc[...] = mixed
    dn_acc[...] = jnp.zeros_like(dn_acc)

    def block(k, carry):
        def wide(base, p):
            at = pl.multiple_of((3 * k + p) * WIDE, 16)
            return jnp.concatenate([w[base + d, pl.ds(at, WIDE), :] for d in range(4)], 0)

        w_gate = jnp.concatenate([wide(4, p) for p in range(3)], 1)
        w_up = jnp.concatenate([wide(8, p) for p in range(3)], 1)
        w_down = load_narrow(w, 12 + k)
        c = cot[...]
        gate, up = dot(n2_ref[...], w_gate), dot(n2_ref[...], w_up)
        sigma = 1.0 / (1.0 + jnp.exp(-gate))
        silu = gate * sigma
        hidden = (silu * up).astype(BF16)
        y_acc[...] += dot(hidden, w_down)
        store_narrow(g, 8 + k, dot_tn(hidden, c))
        d_hidden = dot_nt(c, w_down)
        d_gate = (d_hidden * up * sigma * (1.0 + gate * (1.0 - sigma))).astype(BF16)
        d_up = (d_hidden * silu).astype(BF16)
        dn_acc[...] += dot_nt(d_gate, w_gate) + dot_nt(d_up, w_up)
        for base, d_out in ((0, d_gate), (4, d_up)):
            grad = dot(n2t_ref[...], d_out).astype(BF16)
            for p in range(3):
                at = pl.multiple_of((3 * k + p) * WIDE, 16)
                for d in range(4):
                    g[base + d, pl.ds(at, WIDE), :] = grad[
                        WIDE * d : WIDE * (d + 1), 128 * p : 128 * (p + 1)
                    ]
        return carry

    lax.fori_loop(0, 4, block, 0)
    zeros = jnp.zeros((HALF * 2 - ROWS, 128), BF16)
    g[0, ROWS:, :] = zeros
    for c in range(1, 12):
        g[c, ROWS:, :] = zeros
        g[c, ROWS : ROWS + 16, :] = tail_of(g, c - 1, c - 1 < 8).astype(BF16)
    stores = piece_copies(
        idx, [(keep1, send1), (keep2, send2), (keep3, send3)], g, 0, out_sems, True
    )
    for copy in stores:
        copy.start()
    y_out[...] = y_acc[...].astype(BF16)
    d_norm = dn_acc[...]
    d_gain = jnp.sum(d_norm * normed_mid, 0, keepdims=True)
    dg_out[...] = d_gain
    scaled = d_norm * gain_mid
    dr_out[...] = cot[...].astype(F32) + inverse * (
        scaled - normed_mid * jnp.mean(scaled * normed_mid, -1, keepdims=True)
    )
    for copy in stores:
        copy.wait()


def second_kernel(
    idx, tok, cos, sin, dr, att, p_in, q_in, k_in, v_in, wq, wk, wv, wo, gain, dg,
    dx_out, keep, send,
    g, dq_ref, dk_ref, dv_ref, first, second, out_sems,
):
    tokens = tok.shape[0]
    d_mixed = dr[...]
    branch = d_mixed.astype(BF16)
    dw_out = dot_tn(att[...], branch)
    d_att = dot_nt(branch, wo[...])
    for b in range(tokens // SEQ_LEN):
        part = slice(SEQ_LEN * b, SEQ_LEN * (b + 1))
        cosine, sine = cos[part, :], -sin[part, :]
        for kv in range(KV_HEADS):
            at = KV_HEADS * b + kv
            heads = [d_att[part, HEAD * h : HEAD * (h + 1)] for h in range(3 * kv, 3 * kv + 3)]
            d3 = jnp.concatenate(heads, 0).astype(BF16)
            probs, q3, k1, v1 = p_in[at], q_in[at], k_in[at], v_in[at]
            d_probs = dot_nt(d3, v1)
            dv_ref[part, HEAD * kv : HEAD * (kv + 1)] = dot_tn(probs.astype(BF16), d3)
            inner = jnp.sum(d_probs * probs, -1, keepdims=True)
            d_score = (probs * (d_probs - inner)).astype(BF16)
            dq3 = dot(d_score, k1) * HEAD**-0.5
            for r in range(3):
                h = 3 * kv + r
                dq_ref[part, HEAD * h : HEAD * (h + 1)] = turn(
                    dq3[SEQ_LEN * r : SEQ_LEN * (r + 1)], cosine, sine
                )
            dk_ref[part, HEAD * kv : HEAD * (kv + 1)] = turn(
                dot_tn(d_score, q3) * HEAD**-0.5, cosine, sine
            )
    dq, dk, dv = dq_ref[...].astype(BF16), dk_ref[...].astype(BF16), dv_ref[...].astype(BF16)
    x = tok[...].astype(F32)
    inverse = lax.rsqrt(jnp.mean(x * x, -1, keepdims=True) + EPS)
    normed = x * inverse
    n1t = (normed * gain[...]).astype(BF16).astype(F32).T.astype(BF16)
    dw_query = dot(n1t, dq)
    store_narrow(g, 0, dw_query[:NARROW])
    dw = unspread(dot(n1t, dk), first, second)
    store_narrow(g, 1, jnp.concatenate([dw_query[NARROW:], dw], 0))
    dw = unspread(dot(n1t, dv), first, second)
    store_narrow(g, 2, jnp.concatenate([dw, dw_out[:192]], 0))
    store_narrow(g, 3, dw_out[192:])
    d_norm = dot_nt(dq, wq[...]) + dot_nt(dk, wk[...]) + dot_nt(dv, wv[...])
    d_gain = jnp.sum(d_norm * normed, 0, keepdims=True)
    for c in range(4):
        g[c, ROWS:, :] = jnp.zeros((HALF * 2 - ROWS, 128), BF16)
        if c:
            g[c, ROWS : ROWS + 16, :] = tail_of(g, c - 1, False).astype(BF16)
    g[0, ROWS : ROWS + 16, :] = head_of_rows([d_gain, dg[...]]).astype(BF16)
    g[0, ROWS + 16 : ROWS + 32, :] = tail_of(g, 3, False).astype(BF16)
    stores = piece_copies(idx, [(keep, send)], g, 0, out_sems, True)
    for copy in stores:
        copy.start()
    scaled = d_norm * gain[...]
    dx_out[...] = d_mixed + inverse * (
        scaled - normed * jnp.mean(scaled * normed, -1, keepdims=True)
    )
    for copy in stores:
        copy.wait()


def run_layer(idx, own, twin, tokens, cotangent, positions):
    length, width = tokens.shape
    groups = length // SEQ_LEN * KV_HEADS
    cosine, sine = rope_tables(positions)
    cosine = jnp.concatenate([cosine, cosine], 1)
    sine = jnp.concatenate([-sine, sine], 1)
    kv_width = KV_HEADS * HEAD
    smem = pl.BlockSpec(memory_space=pltpu.SMEM)
    vmem = pl.BlockSpec(memory_space=pltpu.VMEM)
    anywhere = pl.BlockSpec(memory_space=pl.ANY)

    def sds(shape, dtype):
        return jax.ShapeDtypeStruct(shape, dtype)

    piece = sds((4, HALF, 128), BF16)
    weights = [sds((width, width), BF16), sds((width, kv_width), BF16)]
    weights = weights + [weights[1], weights[0]]
    saved = [
        sds((groups, 3 * SEQ_LEN, SEQ_LEN), F32),
        sds((groups, 3 * SEQ_LEN, HEAD), BF16),
        sds((groups, SEQ_LEN, HEAD), BF16),
        sds((groups, SEQ_LEN, HEAD), BF16),
    ]
    outs = [sds((length, width), BF16), sds((length, width), F32), sds((length, width), BF16)]
    outs = outs + saved + weights + [sds((1, width), F32)] * 2
    results = pl.pallas_call(
        first_kernel,
        name="forward_and_ff_backward",
        in_specs=[smem] + [anywhere] * 8 + [vmem] * 4,
        out_specs=[vmem] * len(outs) + [anywhere] * 6,
        out_shape=outs + [piece] * 6,
        scratch_shapes=[
            pltpu.VMEM((CANON, 2 * HALF, 128), BF16),
            pltpu.VMEM((12, 2 * HALF, 128), BF16),
            pltpu.VMEM((length, width), F32),
            pltpu.VMEM((length, width), BF16),
            pltpu.VMEM((width, length), BF16),
            pltpu.VMEM((length, width), F32),
            pltpu.VMEM((length, width), F32),
            pltpu.VMEM((width, 128), F32),
            pltpu.VMEM((width, 128), F32),
            pltpu.SemaphoreType.DMA((32,)),
            pltpu.SemaphoreType.DMA((24,)),
        ],
        compiler_params=pltpu.CompilerParams(vmem_limit_bytes=VMEM_LIMIT),
        cost_estimate=pl.CostEstimate(
            flops=20 * length * width * FF, bytes_accessed=16_000_000, transcendentals=600_000
        ),
    )(idx, *own, *twin, tokens, cotangent, cosine, sine)
    output, d_mixed, attended, probs, q3, k1, v1, wq, wk, wv, wo, gain, d_gain = results[:13]
    keeps, sends = list(results[13:16]), list(results[16:19])
    d_input, keep, send = pl.pallas_call(
        second_kernel,
        name="attention_backward",
        in_specs=[smem] + [vmem] * 15,
        out_specs=[vmem] + [anywhere] * 2,
        out_shape=[sds((length, width), F32), piece, piece],
        scratch_shapes=[
            pltpu.VMEM((4, 2 * HALF, 128), BF16),
            pltpu.VMEM((length, width), F32),
            pltpu.VMEM((length, kv_width), F32),
            pltpu.VMEM((length, kv_width), F32),
            pltpu.VMEM((width, 128), F32),
            pltpu.VMEM((width, 128), F32),
            pltpu.SemaphoreType.DMA((8,)),
        ],
        compiler_params=pltpu.CompilerParams(vmem_limit_bytes=VMEM_LIMIT),
        cost_estimate=pl.CostEstimate(
            flops=10 * length * width * width, bytes_accessed=10_000_000, transcendentals=0
        ),
    )(idx, tokens, cosine, sine, d_mixed, attended, probs, q3, k1, v1, wq, wk, wv, wo, gain, d_gain)
    return output, d_input, d_gain[0], [keep] + keeps, [send] + sends


def flat_of(payloads, lay):
    n = lay.count
    heads = payloads[:, lay.rows : lay.rows + 10]
    flats = [unhead_narrow(heads[0])]
    for i in range(n):
        wide = n // 4 <= i < 3 * n // 4
        body = payloads[i, : lay.rows]
        flat = unpack_wide(body, FF) if wide else unpack_narrow(body)
        if i + 1 < n:
            tail = unhead_wide(heads[i + 1]) if wide else unhead_narrow(heads[i + 1])
            flat = jnp.concatenate([flat[: -lay.gains], flat[-lay.gains :] + tail])
        flats.append(flat)
    return jnp.concatenate(flats)


def payloads_of(flat, lay):
    windows = [
        flat[i * lay.chunk : (i + 1) * lay.chunk + lay.gains] for i in range(lay.count)
    ]
    return jnp.stack([pack_payload(window, i, lay) for i, window in enumerate(windows)], 0)


def canonical(own, twin, lay, canon, index, core):
    own, twin = jnp.stack(own, 0), jnp.stack(twin, 0)
    both = jnp.where(core == 0, jnp.stack([own, twin], 2), jnp.stack([twin, own], 2))
    both = both.reshape(lay.count, 2 * lay.half, 128)
    both = jnp.take(both, jnp.arange(lay.count, dtype=jnp.int32) ^ index, axis=0)
    flat = flat_of(both, lay)
    zeros = jnp.zeros((canon.gains,), flat.dtype)
    rows = []
    for i in range(CANON):
        window = flat[i * canon.chunk : (i + 1) * canon.chunk + canon.gains]
        if i:
            window = jnp.concatenate([zeros, window[canon.gains :]])
        rows.append(pack_payload(window, i, canon))
    rows = jnp.stack(rows, 0).reshape(PLANES, 4, 2, canon.half, 128)
    return [list(rows[:, :, c]) for c in range(2)]


def from_canonical(keeps, sends, lay, canon, place, core):
    rows = jnp.stack([jnp.stack(keeps, 0), jnp.stack(sends, 0)], 2)
    rows = rows.reshape(CANON, 2 * canon.half, 128)
    flats = [unhead_narrow(rows[0, canon.rows : canon.rows + 10])]
    for i in range(CANON):
        body = rows[i, : canon.rows]
        flats.append(unpack_wide(body, FF) if 4 <= i < 12 else unpack_narrow(body))
    rows = payloads_of(jnp.concatenate(flats), lay)
    rows = rows.reshape(PLANES, lay.in_plane, 2, lay.half, 128)
    rows = jnp.take(rows, jnp.arange(lay.in_plane, dtype=jnp.int32) ^ place, axis=1)
    return list(jnp.take(rows, core, axis=2)), list(jnp.take(rows, 1 - core, axis=2))


def on_device(lay, canon, tokens_in, positions, params, cotangent):
    index = lax.axis_index("dp")
    core = lax.axis_index("rep")
    n, half, in_plane = lay.count, lay.half, lay.in_plane
    plane, place = index // in_plane, index % in_plane
    same = n == CANON
    window = jnp.zeros((lay.gains + lay.chunk,), params.dtype)
    window = lax.dynamic_update_slice(window, params, (index * lay.step,))
    payload = pack_payload(window, index, lay)
    mine = lax.dynamic_slice_in_dim(payload, core * half, half, 0)
    own, twin = gather(mine, lay)

    if same:
        idx = jnp.stack([plane, place, core]).astype(jnp.int32)
    else:
        own, twin = canonical(own, twin, lay, canon, index, core)
        idx = jnp.zeros((3,), jnp.int32)
    output, d_input, d_gain, keeps, sends = run_layer(
        idx, own, twin, tokens_in, cotangent, positions
    )
    if not same:
        keeps, sends = from_canonical(keeps, sends, lay, canon, place, core)
    planes = []
    for keep, send in zip(keeps, sends):
        pair = keep.astype(F32) + swap_rep(send).astype(F32)
        planes.append(reduce_plane(pair.astype(BF16), lay))
    if same:
        at = ROWS - HALF
        late = jnp.where(core == 1, planes[0][at + 16 : at + 32], jnp.zeros((16, 128), BF16))
        planes[1] = jnp.concatenate([planes[1][:at], planes[1][at : at + 16] + late, planes[1][at + 16 :]])
    planes = jnp.stack(planes, 0)
    total = jnp.take(planes, plane, axis=0).astype(F32)
    for s in range(1, PLANES):
        part = swap(jnp.take(planes, plane ^ s, axis=0), s << (lay.bits - 2), n)
        total = total + part.astype(F32)
    other = swap_rep(total)
    whole = jnp.where(core == 0, jnp.stack([total, other], 0), jnp.stack([other, total], 0))
    window = unpack_payload(whole.reshape(2 * half, 128), index, lay)
    grad_params = lax.dynamic_slice(window, (index * lay.step,), (lay.shard,))
    return output, d_input, grad_params, sum_everywhere(d_gain, lay)


def solution(mesh):
    def run(tokens_in, positions, params, cotangent):
        total, width = params.shape[0], tokens_in.shape[1]
        lay = Layout(mesh.shape["dp"], total, width)
        canon = Layout(CANON, total, width)
        rows = P(("dp", "rep"), None)
        return jax.shard_map(
            lambda *args: on_device(lay, canon, *args),
            mesh=mesh,
            in_specs=(rows, P(("dp", "rep")), P("dp"), rows),
            out_specs=(rows, rows, P("dp"), P()),
            check_vma=False,
        )(tokens_in, positions, params, cotangent)

    return run
```

profile of v0, /device:TPU:0, one launch (start us, length us, event | category | flops | bytes accessed | tf_op | source)
XLA Modules:
  0.0 191.3 jit_solution(4143204666282559147)
XLA Ops:
  0.7 7.1 %dynamic_update_slice.3 = bf16[222336]{0:T(1024)(128)(2,1)S(1)} dynamic-update-slice(bf16[222336]{0:T(1024)(128)(2,1)S(1)} %broadcast_in_dim.17, bf16[221256]{0:T(1024)(128)(2,1)} %param.8, s32[]{:T(128)S(6)} %select_n.79) | dynamic-update-slice | bytes 885028 | tf_op jit(solution)/shard_map/dynamic_update_slice | solution.py:604
  9.6 5.1 %collective-permute-start.14 = (bf16[880,128]{1,0:T(8,128)(2,1)S(1)}, bf16[880,128]{1,0:T(8,128)(2,1)S(1)}, u32[]{:S(2)}, u32[]{:S(2)}) collective-permute-start(bf16[880,128]{1,0:T(8,128)(2,1)S(1)} %fusion.19), channel_id=1, source_target_pairs={{0,24},{2,26},{4,28},{6,30},{8,16},{10,18},{12,20},{14,22},{16,8},... | collective-permute-start | bytes 675848 | tf_op jit(solution)/shard_map/ppermute | solution.py:108
  15.3 1.7 collective-permute-start.2
  20.2 1.7 collective-permute-start.3
  24.4 9.4 %collective-permute-done.9 = bf16[880,128]{1,0:T(8,128)(2,1)S(1)} collective-permute-done((bf16[880,128]{1,0:T(8,128)(2,1)S(1)}, bf16[880,128]{1,0:T(8,128)(2,1)S(1)}, u32[]{:S(2)}, u32[]{:S(2)}) %collective-permute-start.9) | collective-permute-done | bytes 225312 | tf_op jit(solution)/shard_map/ppermute | solution.py:108
  37.0 1.6 collective-permute-done.17
  40.1 3.6 %collective-permute-done.12 = bf16[432,128]{1,0:T(8,128)(2,1)S(1)} collective-permute-done((bf16[432,128]{1,0:T(8,128)(2,1)S(1)}, bf16[432,128]{1,0:T(8,128)(2,1)S(1)}, u32[]{:S(2)}, u32[]{:S(2)}) %collective-permute-start.12) | collective-permute-done | bytes 110624 | tf_op jit(solution)/shard_map/ppermute | solution.py:108
  43.7 1.8 collective-permute-start.7
  45.5 3.0 %collective-permute-done.7 = bf16[432,128]{1,0:T(8,128)(2,1)S(1)} collective-permute-done((bf16[432,128]{1,0:T(8,128)(2,1)S(1)}, bf16[432,128]{1,0:T(8,128)(2,1)S(1)}, u32[]{:S(2)}, u32[]{:S(2)}) %collective-permute-start.7) | collective-permute-done | bytes 110624 | tf_op jit(solution)/shard_map/ppermute | solution.py:108
  50.6 1.6 collective-permute-start.13
  52.2 2.3 %collective-permute-done.5 = bf16[448,128]{1,0:T(8,128)(2,1)S(1)} collective-permute-done((bf16[448,128]{1,0:T(8,128)(2,1)S(1)}, bf16[448,128]{1,0:T(8,128)(2,1)S(1)}, u32[]{:S(2)}, u32[]{:S(2)}) %collective-permute-start.5) | collective-permute-done | bytes 114720 | tf_op jit(solution)/shard_map/ppermute | solution.py:108
  54.5 1.8 collective-permute-start.16
  61.5 2.4 %collective-permute-done.11 = bf16[2,448,128]{2,1,0:T(8,128)(2,1)S(1)} collective-permute-done((bf16[2,448,128]{2,1,0:T(8,128)(2,1)S(1)}, bf16[2,448,128]{2,1,0:T(8,128)(2,1)S(1)}, u32[]{:S(2)}, u32[]{:S(2)}) %collective-permute-start.11) | collective-permute-done | bytes 229408 | tf_op jit(solution)/shard_map/ppermute | solution.py:108
  64.1 2.3 %collective-permute-done.6 = bf16[2,448,128]{2,1,0:T(8,128)(2,1)S(1)} collective-permute-done((bf16[2,448,128]{2,1,0:T(8,128)(2,1)S(1)}, bf16[2,448,128]{2,1,0:T(8,128)(2,1)S(1)}, u32[]{:S(2)}, u32[]{:S(2)}) %collective-permute-start.6) | collective-permute-done | bytes 229408 | tf_op jit(solution)/shard_map/ppermute | solution.py:108
  70.2 21.2 %forward_and_ff_backward.1 = (bf16[256,576]{1,0:T(8,128)(2,1)S(1)}, f32[256,576]{1,0:T(8,128)}, bf16[256,576]{1,0:T(8,128)(2,1)S(1)}, f32[6,384,128]{2,1,0:T(8,1...) custom-call(s32[3]{0:T(128)S(1)} %pad_add_fusion.idx, ...), custom_call_target="tpu_custom_call" | custom-call | flops 4529848320 | bytes 16000000 | tf_op jit(solution)/shard_map/forward_and_ff_backward/pallas_call | solution.py:496
  91.5 9.2 %attention_backward.1 = (f32[256,576]{1,0:T(8,128)}, bf16[4,880,128]{2,1,0:T(8,128)(2,1)}, bf16[4,880,128]{2,1,0:T(8,128)(2,1)}) custom-call(s32[3]{0:T(128)S(1)} %pad_add_fusion.idx, bf16[256,576]{1,0:T(8,128)(2,1)S(1)} %copy-done, f32[256,64]{1,0:T(8,128)S(1)} %get-tuple-element.122.cos, f32[256,64]{1,0:T(8,128)S(1)} %get-tuple-element.123.sin, ...), custom_call_target="tpu_custom_call" | custom-call | flops 849346560 | bytes 10000000 | tf_op jit(solution)/shard_map/attention_backward/pallas_call | solution.py:522
  101.7 1.7 collective-permute-done.23
  109.9 1.6 collective-permute-start.26
  114.2 4.1 %collective-permute-done.26 = bf16[2,432,128]{2,1,0:T(8,128)(2,1)S(1)} collective-permute-done((bf16[2,432,128]{2,1,0:T(8,128)(2,1)S(1)}, bf16[2,432,128]{2,1,0:T(8,128)(2,1)S(1)}, u32[]{:S(2)}, u32[]{:S(2)}) %collective-permute-start.26) | collective-permute-done | bytes 221216 | tf_op jit(solution)/shard_map/ppermute | solution.py:108
  119.9 3.2 %collective-permute-done.31 = bf16[2,432,128]{2,1,0:T(8,128)(2,1)S(1)} collective-permute-done((bf16[2,432,128]{2,1,0:T(8,128)(2,1)S(1)}, bf16[2,432,128]{2,1,0:T(8,128)(2,1)S(1)}, u32[]{:S(2)}, u32[]{:S(2)}) %collective-permute-start.31) | collective-permute-done | bytes 221216 | tf_op jit(solution)/shard_map/ppermute | solution.py:108
  124.3 2.6 %collective-permute-done.36 = bf16[2,432,128]{2,1,0:T(8,128)(2,1)S(1)} collective-permute-done((bf16[2,432,128]{2,1,0:T(8,128)(2,1)S(1)}, bf16[2,432,128]{2,1,0:T(8,128)(2,1)S(1)}, u32[]{:S(2)}, u32[]{:S(2)}) %collective-permute-start.36) | collective-permute-done | bytes 221216 | tf_op jit(solution)/shard_map/ppermute | solution.py:108
  128.5 5.0 %collective-permute-done.41 = bf16[2,432,128]{2,1,0:T(8,128)(2,1)S(1)} collective-permute-done((bf16[2,432,128]{2,1,0:T(8,128)(2,1)S(1)}, bf16[2,432,128]{2,1,0:T(8,128)(2,1)S(1)}, u32[]{:S(2)}, u32[]{:S(2)}) %collective-permute-start.41) | collective-permute-done | bytes 221216 | tf_op jit(solution)/shard_map/ppermute | solution.py:108
  138.1 1.6 collective-permute-start.25
  144.4 2.3 %collective-permute-done.35 = bf16[448,128]{1,0:T(8,128)(2,1)S(1)} collective-permute-done((bf16[448,128]{1,0:T(8,128)(2,1)S(1)}, bf16[448,128]{1,0:T(8,128)(2,1)S(1)}, u32[]{:S(2)}, u32[]{:S(2)}) %collective-permute-start.35) | collective-permute-done | bytes 114720 | tf_op jit(solution)/shard_map/ppermute | solution.py:108
  148.4 3.2 %collective-permute-start.44 = (bf16[880,128]{1,0:T(8,128)(2,1)S(1)}, bf16[880,128]{1,0:T(8,128)(2,1)S(1)}, u32[]{:S(2)}, u32[]{:S(2)}) collective-permute-start(bf16[880,128]{1,0:T(8,128)(2,1)S(1)} %get-tuple-element.80), channel_id=1, source_target_pairs={{0,16},{2,18},{4,20},{6,22},{8,24},{10,26},{12,28},{14,30},{16,0},... | collective-permute-start | bytes 675848 | tf_op jit(solution)/shard_map/ppermute | solution.py:108
  152.7 4.8 %collective-permute-done.43 = bf16[880,128]{1,0:T(8,128)(2,1)S(1)} collective-permute-done((bf16[880,128]{1,0:T(8,128)(2,1)S(1)}, bf16[880,128]{1,0:T(8,128)(2,1)S(1)}, u32[]{:S(2)}, u32[]{:S(2)}) %collective-permute-start.43) | collective-permute-done | bytes 225312 | tf_op jit(solution)/shard_map/ppermute | solution.py:108
  157.6 8.0 %collective-permute-done.44 = bf16[880,128]{1,0:T(8,128)(2,1)S(1)} collective-permute-done((bf16[880,128]{1,0:T(8,128)(2,1)S(1)}, bf16[880,128]{1,0:T(8,128)(2,1)S(1)}, u32[]{:S(2)}, u32[]{:S(2)}) %collective-permute-start.44) | collective-permute-done | bytes 225312 | tf_op jit(solution)/shard_map/ppermute | solution.py:108
  168.8 2.4 %collective-permute-done.48 = f32[576]{0:T(1024)S(1)} collective-permute-done((f32[576]{0:T(1024)S(1)}, f32[576]{0:T(1024)S(1)}, u32[]{:S(2)}, u32[]{:S(2)}) %collective-permute-start.48) | collective-permute-done | bytes 2336 | tf_op jit(solution)/shard_map/ppermute | solution.py:108
  172.1 2.7 %collective-permute-done.49 = f32[576]{0:T(1024)S(1)} collective-permute-done((f32[576]{0:T(1024)S(1)}, f32[576]{0:T(1024)S(1)}, u32[]{:S(2)}, u32[]{:S(2)}) %collective-permute-start.49) | collective-permute-done | bytes 2336 | tf_op jit(solution)/shard_map/ppermute | solution.py:108
  174.8 3.0 %collective-permute-start.50 = (f32[576]{0:T(1024)S(1)}, f32[576]{0:T(1024)S(1)}, u32[]{:S(2)}, u32[]{:S(2)}) collective-permute-start(f32[576]{0:T(1024)S(1)} %add.138), channel_id=1, source_target_pairs={{0,8},{2,10},{4,12},{6,14},{8,0},{10,2},{12,4},{14,6},{16,24},{18,... | collective-permute-start | bytes 6920 | tf_op jit(solution)/shard_map/ppermute | solution.py:108
  177.8 1.6 collective-permute-done.50
  179.3 3.0 %collective-permute-start.51 = (f32[576]{0:T(1024)S(1)}, f32[576]{0:T(1024)S(1)}, u32[]{:S(2)}, u32[]{:S(2)}) collective-permute-start(f32[576]{0:T(1024)S(1)} %add.139), channel_id=1, source_target_pairs={{0,16},{2,18},{4,20},{6,22},{8,24},{10,26},{12,28},{14,30},{16,0},... | collective-permute-start | bytes 6920 | tf_op jit(solution)/shard_map/ppermute | solution.py:108
  (217 shorter events, 63.4 us)
Async XLA Ops:
  9.6 14.0 %collective-permute-start.14 = (bf16[880,128]{1,0:T(8,128)(2,1)S(1)}, bf16[880,128]{1,0:T(8,128)(2,1)S(1)}, u32[]{:S(2)}, u32[]{:S(2)}) collective-permute-start(bf16[880,128]{1,0:T(8,128)(2,1)S(1)} %fusion.19), channel_id=1, source_target_pairs={{0,24},{2,26},{4,28},{6,30},{8,16},{10,18},{12,20},{14,22},{16,8},... | collective-permute-start | bytes 675848 | tf_op jit(solution)/shard_map/ppermute | solution.py:108
  14.7 19.1 %collective-permute-start.9 = (bf16[880,128]{1,0:T(8,128)(2,1)S(1)}, bf16[880,128]{1,0:T(8,128)(2,1)S(1)}, u32[]{:S(2)}, u32[]{:S(2)}) collective-permute-start(bf16[880,128]{1,0:T(8,128)(2,1)S(1)} %fusion.19), channel_id=1, source_target_pairs={{0,16},{2,18},{4,20},{6,22},{8,24},{10,26},{12,28},{14,30},{16,0},... | collective-permute-start | bytes 675848 | tf_op jit(solution)/shard_map/ppermute | solution.py:108
  14.7 20.7 %collective-permute-start.4 = (bf16[880,128]{1,0:T(8,128)(2,1)S(1)}, bf16[880,128]{1,0:T(8,128)(2,1)S(1)}, u32[]{:S(2)}, u32[]{:S(2)}) collective-permute-start(bf16[880,128]{1,0:T(8,128)(2,1)S(1)} %fusion.19), channel_id=1, source_target_pairs={{0,8},{2,10},{4,12},{6,14},{8,0},{10,2},{12,4},{14,6},{16,24},{18,... | collective-permute-start | bytes 675848 | tf_op jit(solution)/shard_map/ppermute | solution.py:108
  20.2 36.1 %collective-permute-start.3 = (bf16[2,432,128]{2,1,0:T(8,128)(2,1)S(1)}, bf16[2,432,128]{2,1,0:T(8,128)(2,1)S(1)}, u32[]{:S(2)}, u32[]{:S(2)}) collective-permute-start(bf16[2,432,128]{2,1,0:T(8,128)(2,1)S(1)} %get-tuple-element.116), channel_id=1, source_target_pairs={{0,2},{2,0},{4,6},{6,4},{8,10},{10,8},{12,14},{14,12},{16,18},{18,... | collective-permute-start | bytes 663560 | tf_op jit(solution)/shard_map/ppermute | solution.py:108
  22.7 35.2 %collective-permute-start.1 = (bf16[2,448,128]{2,1,0:T(8,128)(2,1)S(1)}, bf16[2,448,128]{2,1,0:T(8,128)(2,1)S(1)}, u32[]{:S(2)}, u32[]{:S(2)}) collective-permute-start(bf16[2,448,128]{2,1,0:T(8,128)(2,1)S(1)} %get-tuple-element.92), channel_id=1, source_target_pairs={{0,4},{2,6},{4,0},{6,2},{8,12},{10,14},{12,8},{14,10},{16,20},{18,... | collective-permute-start | bytes 688136 | tf_op jit(solution)/shard_map/ppermute | solution.py:108
  23.5 26.4 %collective-permute-start.15 = (bf16[448,128]{1,0:T(8,128)(2,1)S(1)}, bf16[448,128]{1,0:T(8,128)(2,1)S(1)}, u32[]{:S(2)}, u32[]{:S(2)}) collective-permute-start(bf16[448,128]{1,0:T(8,128)(2,1)S(1)} %get-tuple-element.94), channel_id=1, source_target_pairs={{0,2},{2,0},{4,6},{6,4},{8,10},{10,8},{12,14},{14,12},{16,18},{18,... | collective-permute-start | bytes 344072 | tf_op jit(solution)/shard_map/ppermute | solution.py:108
  35.4 15.2 %collective-permute-start.10 = (bf16[448,128]{1,0:T(8,128)(2,1)S(1)}, bf16[448,128]{1,0:T(8,128)(2,1)S(1)}, u32[]{:S(2)}, u32[]{:S(2)}) collective-permute-start(bf16[448,128]{1,0:T(8,128)(2,1)S(1)} %get-tuple-element.98), channel_id=1, source_target_pairs={{0,2},{2,0},{4,6},{6,4},{8,10},{10,8},{12,14},{14,12},{16,18},{18,... | collective-permute-start | bytes 344072 | tf_op jit(solution)/shard_map/ppermute | solution.py:108
  50.0 9.0 %collective-permute-start.18 = (bf16[2,432,128]{2,1,0:T(8,128)(2,1)S(1)}, bf16[2,432,128]{2,1,0:T(8,128)(2,1)S(1)}, u32[]{:S(2)}, u32[]{:S(2)}) collective-permute-start(bf16[2,432,128]{2,1,0:T(8,128)(2,1)S(1)} %get-tuple-element.110), channel_id=1, source_target_pairs={{0,2},{2,0},{4,6},{6,4},{8,10},{10,8},{12,14},{14,12},{16,18},{18,... | collective-permute-start | bytes 663560 | tf_op jit(solution)/shard_map/ppermute | solution.py:108
  50.6 10.7 %collective-permute-start.13 = (bf16[2,432,128]{2,1,0:T(8,128)(2,1)S(1)}, bf16[2,432,128]{2,1,0:T(8,128)(2,1)S(1)}, u32[]{:S(2)}, u32[]{:S(2)}) collective-permute-start(bf16[2,432,128]{2,1,0:T(8,128)(2,1)S(1)} %get-tuple-element.112), channel_id=1, source_target_pairs={{0,2},{2,0},{4,6},{6,4},{8,10},{10,8},{12,14},{14,12},{16,18},{18,... | collective-permute-start | bytes 663560 | tf_op jit(solution)/shard_map/ppermute | solution.py:108
  54.5 6.3 %collective-permute-start.16 = (bf16[2,448,128]{2,1,0:T(8,128)(2,1)S(1)}, bf16[2,448,128]{2,1,0:T(8,128)(2,1)S(1)}, u32[]{:S(2)}, u32[]{:S(2)}) collective-permute-start(bf16[2,448,128]{2,1,0:T(8,128)(2,1)S(1)} %get-tuple-element.86), channel_id=1, source_target_pairs={{0,4},{2,6},{4,0},{6,2},{8,12},{10,14},{12,8},{14,10},{16,20},{18,... | collective-permute-start | bytes 688136 | tf_op jit(solution)/shard_map/ppermute | solution.py:108
  56.3 7.8 %collective-permute-start.8 = (bf16[2,432,128]{2,1,0:T(8,128)(2,1)S(1)}, bf16[2,432,128]{2,1,0:T(8,128)(2,1)S(1)}, u32[]{:S(2)}, u32[]{:S(2)}) collective-permute-start(bf16[2,432,128]{2,1,0:T(8,128)(2,1)S(1)} %get-tuple-element.114), channel_id=1, source_target_pairs={{0,2},{2,0},{4,6},{6,4},{8,10},{10,8},{12,14},{14,12},{16,18},{18,... | collective-permute-start | bytes 663560 | tf_op jit(solution)/shard_map/ppermute | solution.py:108
  59.0 7.4 %collective-permute-start.6 = (bf16[2,448,128]{2,1,0:T(8,128)(2,1)S(1)}, bf16[2,448,128]{2,1,0:T(8,128)(2,1)S(1)}, u32[]{:S(2)}, u32[]{:S(2)}) collective-permute-start(bf16[2,448,128]{2,1,0:T(8,128)(2,1)S(1)} %get-tuple-element.90), channel_id=1, source_target_pairs={{0,4},{2,6},{4,0},{6,2},{8,12},{10,14},{12,8},{14,10},{16,20},{18,... | collective-permute-start | bytes 688136 | tf_op jit(solution)/shard_map/ppermute | solution.py:108
  60.8 9.2 %collective-permute-start.19 = (bf16[4,880,128]{2,1,0:T(8,128)(2,1)S(1)}, bf16[4,880,128]{2,1,0:T(8,128)(2,1)}, u32[]{:S(2)}, u32[]{:S(2)}) collective-permute-start(bf16[4,880,128]{2,1,0:T(8,128)(2,1)S(1)} %bitcast.262), channel_id=1, source_target_pairs={{0,1},{1,0},{2,3},{3,2},{4,5},{5,4},{6,7},{7,6},{8,9},{9,8},{10,11... | collective-permute-start | bytes 2703368 | tf_op jit(solution)/shard_map/ppermute | solution.py:112
  61.3 8.7 %collective-permute-start.22 = (bf16[4,880,128]{2,1,0:T(8,128)(2,1)S(1)}, bf16[4,880,128]{2,1,0:T(8,128)(2,1)}, u32[]{:S(2)}, u32[]{:S(2)}) collective-permute-start(bf16[4,880,128]{2,1,0:T(8,128)(2,1)S(1)} %bitcast.264), channel_id=1, source_target_pairs={{0,1},{1,0},{2,3},{3,2},{4,5},{5,4},{6,7},{7,6},{8,9},{9,8},{10,11... | collective-permute-start | bytes 2703368 | tf_op jit(solution)/shard_map/ppermute | solution.py:112
  109.0 25.7 %collective-permute-start.24 = (bf16[2,448,128]{2,1,0:T(8,128)(2,1)S(1)}, bf16[2,448,128]{2,1,0:T(8,128)(2,1)S(1)}, u32[]{:S(2)}, u32[]{:S(2)}) collective-permute-start(bf16[2,448,128]{2,1,0:T(8,128)(2,1)S(1)} %slice_bitcast_fusion.7), channel_id=1, source_target_pairs={{0,4},{2,6},{4,0},{6,2},{8,12},{10,14},{12,8},{14,10},{16,20},{18,... | collective-permute-start | bytes 688136 | tf_op jit(solution)/shard_map/ppermute | solution.py:108
  109.9 8.4 %collective-permute-start.26 = (bf16[2,432,128]{2,1,0:T(8,128)(2,1)S(1)}, bf16[2,432,128]{2,1,0:T(8,128)(2,1)S(1)}, u32[]{:S(2)}, u32[]{:S(2)}) collective-permute-start(bf16[2,432,128]{2,1,0:T(8,128)(2,1)S(1)} %slice_bitcast_fusion.15), channel_id=1, source_target_pairs={{0,2},{2,0},{4,6},{6,4},{8,10},{10,8},{12,14},{14,12},{16,18},{18,... | collective-permute-start | bytes 663560 | tf_op jit(solution)/shard_map/ppermute | solution.py:108
  111.5 11.5 %collective-permute-start.31 = (bf16[2,432,128]{2,1,0:T(8,128)(2,1)S(1)}, bf16[2,432,128]{2,1,0:T(8,128)(2,1)S(1)}, u32[]{:S(2)}, u32[]{:S(2)}) collective-permute-start(bf16[2,432,128]{2,1,0:T(8,128)(2,1)S(1)} %slice_bitcast_fusion.13), channel_id=1, source_target_pairs={{0,2},{2,0},{4,6},{6,4},{8,10},{10,8},{12,14},{14,12},{16,18},{18,... | collective-permute-start | bytes 663560 | tf_op jit(solution)/shard_map/ppermute | solution.py:108
  112.1 23.6 %collective-permute-start.29 = (bf16[2,448,128]{2,1,0:T(8,128)(2,1)S(1)}, bf16[2,448,128]{2,1,0:T(8,128)(2,1)S(1)}, u32[]{:S(2)}, u32[]{:S(2)}) collective-permute-start(bf16[2,448,128]{2,1,0:T(8,128)(2,1)S(1)} %slice_bitcast_fusion.5), channel_id=1, source_target_pairs={{0,4},{2,6},{4,0},{6,2},{8,12},{10,14},{12,8},{14,10},{16,20},{18,... | collective-permute-start | bytes 688136 | tf_op jit(solution)/shard_map/ppermute | solution.py:108
  113.3 23.8 %collective-permute-start.34 = (bf16[2,448,128]{2,1,0:T(8,128)(2,1)S(1)}, bf16[2,448,128]{2,1,0:T(8,128)(2,1)S(1)}, u32[]{:S(2)}, u32[]{:S(2)}) collective-permute-start(bf16[2,448,128]{2,1,0:T(8,128)(2,1)S(1)} %slice_bitcast_fusion.3), channel_id=1, source_target_pairs={{0,4},{2,6},{4,0},{6,2},{8,12},{10,14},{12,8},{14,10},{16,20},{18,... | collective-permute-start | bytes 688136 | tf_op jit(solution)/shard_map/ppermute | solution.py:108
  118.3 8.6 %collective-permute-start.36 = (bf16[2,432,128]{2,1,0:T(8,128)(2,1)S(1)}, bf16[2,432,128]{2,1,0:T(8,128)(2,1)S(1)}, u32[]{:S(2)}, u32[]{:S(2)}) collective-permute-start(bf16[2,432,128]{2,1,0:T(8,128)(2,1)S(1)} %slice_bitcast_fusion.11), channel_id=1, source_target_pairs={{0,2},{2,0},{4,6},{6,4},{8,10},{10,8},{12,14},{14,12},{16,18},{18,... | collective-permute-start | bytes 663560 | tf_op jit(solution)/shard_map/ppermute | solution.py:108
  123.0 15.1 %collective-permute-start.39 = (bf16[2,448,128]{2,1,0:T(8,128)(2,1)S(1)}, bf16[2,448,128]{2,1,0:T(8,128)(2,1)S(1)}, u32[]{:S(2)}, u32[]{:S(2)}) collective-permute-start(bf16[2,448,128]{2,1,0:T(8,128)(2,1)S(1)} %slice_bitcast_fusion.1), channel_id=1, source_target_pairs={{0,4},{2,6},{4,0},{6,2},{8,12},{10,14},{12,8},{14,10},{16,20},{18,... | collective-permute-start | bytes 688136 | tf_op jit(solution)/shard_map/ppermute | solution.py:108
  126.9 6.6 %collective-permute-start.41 = (bf16[2,432,128]{2,1,0:T(8,128)(2,1)S(1)}, bf16[2,432,128]{2,1,0:T(8,128)(2,1)S(1)}, u32[]{:S(2)}, u32[]{:S(2)}) collective-permute-start(bf16[2,432,128]{2,1,0:T(8,128)(2,1)S(1)} %slice_bitcast_fusion.9), channel_id=1, source_target_pairs={{0,2},{2,0},{4,6},{6,4},{8,10},{10,8},{12,14},{14,12},{16,18},{18,... | collective-permute-start | bytes 663560 | tf_op jit(solution)/shard_map/ppermute | solution.py:108
  133.5 6.3 %collective-permute-start.27 = (bf16[432,128]{1,0:T(8,128)(2,1)S(1)}, bf16[432,128]{1,0:T(8,128)(2,1)S(1)}, u32[]{:S(2)}, u32[]{:S(2)}) collective-permute-start(bf16[432,128]{1,0:T(8,128)(2,1)S(1)} %slice_bitcast_fusion.31), channel_id=1, source_target_pairs={{0,4},{2,6},{4,0},{6,2},{8,12},{10,14},{12,8},{14,10},{16,20},{18,... | collective-permute-start | bytes 331784 | tf_op jit(solution)/shard_map/ppermute | solution.py:108
  134.7 6.7 %collective-permute-start.32 = (bf16[432,128]{1,0:T(8,128)(2,1)S(1)}, bf16[432,128]{1,0:T(8,128)(2,1)S(1)}, u32[]{:S(2)}, u32[]{:S(2)}) collective-permute-start(bf16[432,128]{1,0:T(8,128)(2,1)S(1)} %slice_bitcast_fusion.29), channel_id=1, source_target_pairs={{0,4},{2,6},{4,0},{6,2},{8,12},{10,14},{12,8},{14,10},{16,20},{18,... | collective-permute-start | bytes 331784 | tf_op jit(solution)/shard_map/ppermute | solution.py:108
  135.8 7.3 %collective-permute-start.37 = (bf16[432,128]{1,0:T(8,128)(2,1)S(1)}, bf16[432,128]{1,0:T(8,128)(2,1)S(1)}, u32[]{:S(2)}, u32[]{:S(2)}) collective-permute-start(bf16[432,128]{1,0:T(8,128)(2,1)S(1)} %slice_bitcast_fusion.27), channel_id=1, source_target_pairs={{0,4},{2,6},{4,0},{6,2},{8,12},{10,14},{12,8},{14,10},{16,20},{18,... | collective-permute-start | bytes 331784 | tf_op jit(solution)/shard_map/ppermute | solution.py:108
  137.1 7.1 %collective-permute-start.42 = (bf16[432,128]{1,0:T(8,128)(2,1)S(1)}, bf16[432,128]{1,0:T(8,128)(2,1)S(1)}, u32[]{:S(2)}, u32[]{:S(2)}) collective-permute-start(bf16[432,128]{1,0:T(8,128)(2,1)S(1)} %slice_bitcast_fusion.25), channel_id=1, source_target_pairs={{0,4},{2,6},{4,0},{6,2},{8,12},{10,14},{12,8},{14,10},{16,20},{18,... | collective-permute-start | bytes 331784 | tf_op jit(solution)/shard_map/ppermute | solution.py:108
  138.1 6.2 %collective-permute-start.25 = (bf16[448,128]{1,0:T(8,128)(2,1)S(1)}, bf16[448,128]{1,0:T(8,128)(2,1)S(1)}, u32[]{:S(2)}, u32[]{:S(2)}) collective-permute-start(bf16[448,128]{1,0:T(8,128)(2,1)S(1)} %slice_bitcast_fusion.23), channel_id=1, source_target_pairs={{0,2},{2,0},{4,6},{6,4},{8,10},{10,8},{12,14},{14,12},{16,18},{18,... | collective-permute-start | bytes 344072 | tf_op jit(solution)/shard_map/ppermute | solution.py:108
  139.8 8.2 %collective-permute-start.30 = (bf16[448,128]{1,0:T(8,128)(2,1)S(1)}, bf16[448,128]{1,0:T(8,128)(2,1)S(1)}, u32[]{:S(2)}, u32[]{:S(2)}) collective-permute-start(bf16[448,128]{1,0:T(8,128)(2,1)S(1)} %slice_bitcast_fusion.21), channel_id=1, source_target_pairs={{0,2},{2,0},{4,6},{6,4},{8,10},{10,8},{12,14},{14,12},{16,18},{18,... | collective-permute-start | bytes 344072 | tf_op jit(solution)/shard_map/ppermute | solution.py:108
  148.3 9.3 %collective-permute-start.43 = (bf16[880,128]{1,0:T(8,128)(2,1)S(1)}, bf16[880,128]{1,0:T(8,128)(2,1)S(1)}, u32[]{:S(2)}, u32[]{:S(2)}) collective-permute-start(bf16[880,128]{1,0:T(8,128)(2,1)S(1)} %get-tuple-element.78), channel_id=1, source_target_pairs={{0,8},{2,10},{4,12},{6,14},{8,0},{10,2},{12,4},{14,6},{16,24},{18,... | collective-permute-start | bytes 675848 | tf_op jit(solution)/shard_map/ppermute | solution.py:108
  148.4 17.2 %collective-permute-start.44 = (bf16[880,128]{1,0:T(8,128)(2,1)S(1)}, bf16[880,128]{1,0:T(8,128)(2,1)S(1)}, u32[]{:S(2)}, u32[]{:S(2)}) collective-permute-start(bf16[880,128]{1,0:T(8,128)(2,1)S(1)} %get-tuple-element.80), channel_id=1, source_target_pairs={{0,16},{2,18},{4,20},{6,22},{8,24},{10,26},{12,28},{14,30},{16,0},... | collective-permute-start | bytes 675848 | tf_op jit(solution)/shard_map/ppermute | solution.py:108
  151.6 13.9 %collective-permute-start.45 = (bf16[880,128]{1,0:T(8,128)(2,1)S(1)}, bf16[880,128]{1,0:T(8,128)(2,1)S(1)}, u32[]{:S(2)}, u32[]{:S(2)}) collective-permute-start(bf16[880,128]{1,0:T(8,128)(2,1)S(1)} %get-tuple-element.79), channel_id=1, source_target_pairs={{0,24},{2,26},{4,28},{6,30},{8,16},{10,18},{12,20},{14,22},{16,8},... | collective-permute-start | bytes 675848 | tf_op jit(solution)/shard_map/ppermute | solution.py:108
  165.7 19.2 %collective-permute-start.46 = (f32[880,128]{1,0:T(8,128)S(1)}, f32[880,128]{1,0:T(8,128)S(1)}, u32[]{:S(2)}, u32[]{:S(2)}) collective-permute-start(f32[880,128]{1,0:T(8,128)S(1)} %convert_add_fusion.4), channel_id=1, source_target_pairs={{0,1},{1,0},{2,3},{3,2},{4,5},{5,4},{6,7},{7,6},{8,9},{9,8},{10,11... | collective-permute-start | bytes 1351688 | tf_op jit(solution)/shard_map/ppermute | solution.py:112
  (32 other events, 190.5 us)
where the time goes:
time: 192 us; the launch traced here: 191 us
  waiting for transfers between devices  71.8 us (37%)
  starting transfers between devices  60.9 us (32%)
  Pallas kernels  30.4 us (16%)
  local copies, waits for them, and re-layouts  18.2 us (9%)
  other arithmetic  8.52 us (4%)
    ppermute x42, waiting for transfers between devices, swap(): return lax.ppermute(value, 'dp', [(i, i ^ mask) for i in range(count)])  66.7 us
    ppermute x42, starting transfers between devices, swap(): return lax.ppermute(value, 'dp', [(i, i ^ mask) for i in range(count)])  59 us
    pallas_call x1, Pallas kernels, run_layer(): pl.pallas_call(first_kernel, name='forward_and_ff_backward', in_specs=[sm...  21.2 us
    pallas_call x1, Pallas kernels, run_layer(): pl.pallas_call(second_kernel, name='attention_backward', in_specs=[smem]...  9.17 us
    dynamic_update_slice x1, local copies, waits for them, and re-layouts, on_device(): window = lax.dynamic_update_slice(window, params, (index * lay.step,))  7.12 us
    ppermute x10, waiting for transfers between devices, swap_rep(): return lax.ppermute(value, 'rep', [(0, 1), (1, 0)])  5.11 us
    unnamed x28, local copies, waits for them, and re-layouts  4.81 us
  transfers between devices with their start and end apart: 52, of which 29 were waited for; matrix products, arithmetic and copies ran while one was open for 5% of the time, Pallas kernels for 0%

commit v1 on v0

--- a/solution.py
+++ b/solution.py
@@ -40,6 +40,7 @@
         self.x_bits = -(-rest // 2)
         self.y_bits = rest - self.x_bits
         self.in_plane = 1 << rest
+        self.flip = self.x_bits == self.y_bits
 
 
 def pack_wide(flat, width):
@@ -112,41 +113,47 @@
     return lax.ppermute(value, "rep", [(0, 1), (1, 0)])
 
 
-def gather_axis(value, shift, size, count):
-    return jnp.stack([value] + [swap(value, d << shift, count) for d in range(1, size)], 0)
+def hop(value, masks, count):
+    pairs = [(2 * i + c, 2 * (i ^ masks[c]) + c) for i in range(count) for c in range(2)]
+    return lax.ppermute(value, ("dp", "rep"), pairs)
+
+
+def hops(lay):
+    xs = [d for d in range(1, 1 << lay.x_bits)]
+    ys = [e << lay.x_bits for e in range(1, 1 << lay.y_bits)]
+    if lay.flip:
+        return list(zip(xs, ys)), list(zip(ys, xs))
+    return list(zip(xs, xs)), list(zip(ys, ys))
+
+
+def gather_hops(value, masks, count):
+    return jnp.stack([value] + [hop(value, pair, count) for pair in masks], 0)
 
 
 def gather(half, lay):
     n = lay.count
-    x_size, y_size = 1 << lay.x_bits, 1 << lay.y_bits
+    first, second = hops(lay)
     planes = [half] + [swap(half, s << (lay.bits - 2), n) for s in range(1, PLANES)]
     own, twin = [], []
     for plane in planes:
-        first, second = plane[: lay.first], plane[lay.first :]
-        first = gather_axis(gather_axis(first, 0, x_size, n), lay.x_bits, y_size, n)
-        second = gather_axis(gather_axis(second, lay.x_bits, y_size, n), 0, x_size, n)
-        second = second.transpose(1, 0, 2, 3)
-        whole = jnp.concatenate([first, second], 2).reshape(lay.in_plane, lay.half, 128)
+        whole = gather_hops(gather_hops(plane, first, n), second, n)
+        whole = whole.reshape(lay.in_plane, lay.half, 128)
         own.append(whole)
         twin.append(swap_rep(whole))
     return own, twin
 
 
-def add_axis(value, shift, size, count):
-    total = value[0].astype(jnp.float32)
-    for d in range(1, size):
-        total = total + swap(value[d], d << shift, count).astype(jnp.float32)
+def add_hops(value, masks, count):
+    total = value[0].astype(F32)
+    for d, pair in enumerate(masks):
+        total = total + hop(value[d + 1], pair, count).astype(F32)
     return total.astype(value.dtype)
 
 
 def reduce_plane(value, lay):
-    n = lay.count
-    x_size, y_size = 1 << lay.x_bits, 1 << lay.y_bits
-    grid = value.reshape(y_size, x_size, lay.half, 128)
-    first, second = grid[:, :, : lay.first], grid[:, :, lay.first :]
-    first = add_axis(add_axis(first, lay.x_bits, y_size, n), 0, x_size, n)
-    second = add_axis(add_axis(second.transpose(1, 0, 2, 3), 0, x_size, n), lay.x_bits, y_size, n)
-    return jnp.concatenate([first, second], 0)
+    first, second = hops(lay)
+    grid = value.reshape(len(second) + 1, len(first) + 1, lay.half, 128)
+    return add_hops(add_hops(grid, second, lay.count), first, lay.count)
 
 
 def sum_everywhere(value, lay):
@@ -185,6 +192,12 @@
     zeros = jnp.zeros((1, 64), F32)
     parts = parts + [jnp.concatenate([zeros, row[:, 512:]], 1) for row in rows]
     return jnp.concatenate(parts + [jnp.zeros((6, 128), F32)], 0)
+
+
+def gain_rows(gain, low):
+    parts = [gain[:, 128 * j : 128 * j + 128] for j in range(4)]
+    parts = parts + [jnp.concatenate([gain[:, 512:], gain[:, 512:]], 1)]
+    return jnp.concatenate([low[:10]] + parts + [jnp.zeros((1, 128), F32)], 0)
 
 
 def load_narrow(ref, index):
@@ -261,49 +274,63 @@
     return vector * cosine + swapped * sine
 
 
-def piece_copies(idx, refs, dst, plane_base, sems, outward):
-    plane, place, core = idx[0], idx[1], idx[2]
+def piece_copies(idx, refs, dst, relative, sems, outward):
+    plane, place, core, flip = idx[0], idx[1], idx[2], idx[3]
     copies = []
     for s, (own, twin) in enumerate(refs):
+        at_plane = jnp.bitwise_xor(plane, s) if relative else s
         for d in range(4):
-            chunk = jnp.bitwise_xor(place, d)
-            if plane_base is None:
-                chunk = chunk + 4 * jnp.bitwise_xor(plane, s)
-            else:
-                chunk = chunk + plane_base + 4 * s
+            turned = ((d & 1) << 1) | (d >> 1)
             for which, ref in enumerate((own, twin)):
-                at = jnp.bitwise_xor(core, which) * HALF
-                inner = dst.at[chunk, pl.ds(pl.multiple_of(at, 16), HALF), :]
-                outer = ref.at[d]
+                side = jnp.bitwise_xor(core, which)
+                offset = jnp.where(side * flip == 1, turned, d)
+                chunk = 4 * at_plane + jnp.bitwise_xor(place, offset)
+                rows = pl.ds(pl.multiple_of(side * HALF, 16), HALF)
+                inner, outer = dst.at[chunk, rows, :], ref.at[d]
                 pair = (inner, outer) if outward else (outer, inner)
-                copies.append(pltpu.make_async_copy(pair[0], pair[1], sems.at[len(copies)]))
+                copies.append(
+                    pltpu.make_async_copy(pair[0], pair[1], sems.at[at_plane, 2 * d + which])
+                )
     return copies
 
 
 def first_kernel(
-    idx, own0, own1, own2, own3, twin0, twin1, twin2, twin3, tok, cot, cos, sin,
+    idx, own0, own1, own2, own3, twin0, twin1, twin2, twin3, tok_hbm, cot_hbm, cos_hbm, sin_hbm,
     y_out, dr_out, att_out, p_out, q_out, k_out, v_out, wq, wk, wv, wo, gain_out, dg_out,
     keep1, keep2, keep3, send1, send2, send3,
-    w, g, att, n2_ref, n2t_ref, y_acc, dn_acc, first, second, sems, out_sems,
+    w, g, tok, cot, cos, sin, att, n2_ref, n2t_ref, y_acc, dn_acc, first, second,
+    in_sems, sems, out_sems,
 ):
+    inputs = [
+        pltpu.make_async_copy(src, dst, in_sems.at[i])
+        for i, (src, dst) in enumerate(
+            ((tok_hbm, tok), (cos_hbm, cos), (sin_hbm, sin), (cot_hbm, cot))
+        )
+    ]
+    for copy in inputs:
+        copy.start()
     loads = piece_copies(
-        idx, [(own0, twin0), (own1, twin1), (own2, twin2), (own3, twin3)], w, None, sems, False
+        idx, [(own0, twin0), (own1, twin1), (own2, twin2), (own3, twin3)], w, True, sems, False
     )
     for copy in loads:
         copy.start()
+
+    def arrived(plane):
+        for j in range(8):
+            pltpu.make_async_copy(
+                own0.at[0], w.at[4 * plane, pl.ds(0, HALF), :], sems.at[plane, j]
+            ).wait()
+
     tokens = tok.shape[0]
+    for copy in inputs:
+        copy.wait()
     x = tok[...].astype(F32)
     normed = x * lax.rsqrt(jnp.mean(x * x, -1, keepdims=True) + EPS)
-    for copy in loads:
-        copy.wait()
-    for c in (0, 1, 2, 3, 12, 13, 14):
+    arrived(0)
+    for c in range(3):
         add_tail(w, c, False)
-
-    def fix(i, carry):
-        add_tail(w, i + 4, True)
-        return carry
-
-    lax.fori_loop(0, 8, fix, 0)
+    arrived(1)
+    add_tail(w, 3, False)
     gains = w[0, ROWS : ROWS + 16, :].astype(F32)
     gain_in, gain_mid = row_of_head(gains, 0), row_of_head(gains, 1)
     gain_out[...] = gain_in
@@ -353,6 +380,16 @@
     n2t_ref[...] = n2.astype(BF16).astype(F32).T.astype(BF16)
     y_acc[...] = mixed
     dn_acc[...] = jnp.zeros_like(dn_acc)
+    arrived(2)
+    arrived(3)
+
+    def fix(i, carry):
+        add_tail(w, i + 4, True)
+        return carry
+
+    lax.fori_loop(0, 8, fix, 0)
+    for c in (12, 13, 14):
+        add_tail(w, c, False)
 
     def block(k, carry):
         def wide(base, p):
@@ -384,20 +421,19 @@
         return carry
 
     lax.fori_loop(0, 4, block, 0)
-    zeros = jnp.zeros((HALF * 2 - ROWS, 128), BF16)
-    g[0, ROWS:, :] = zeros
-    for c in range(1, 12):
-        g[c, ROWS:, :] = zeros
-        g[c, ROWS : ROWS + 16, :] = tail_of(g, c - 1, c - 1 < 8).astype(BF16)
+    d_norm = dn_acc[...]
+    d_gain = jnp.sum(d_norm * normed_mid, 0, keepdims=True)
+    dg_out[...] = d_gain
+    for c in range(12):
+        top = tail_of(g, c - 1, c - 1 < 8) if c else jnp.zeros((16, 128), F32)
+        g[c, ROWS : ROWS + 16, :] = top.astype(BF16)
+        g[c, ROWS + 16 :, :] = gain_rows(d_gain, jnp.zeros((16, 128), F32)).astype(BF16)
     stores = piece_copies(
-        idx, [(keep1, send1), (keep2, send2), (keep3, send3)], g, 0, out_sems, True
+        idx, [(keep1, send1), (keep2, send2), (keep3, send3)], g, False, out_sems, True
     )
     for copy in stores:
         copy.start()
     y_out[...] = y_acc[...].astype(BF16)
-    d_norm = dn_acc[...]
-    d_gain = jnp.sum(d_norm * normed_mid, 0, keepdims=True)
-    dg_out[...] = d_gain
     scaled = d_norm * gain_mid
     dr_out[...] = cot[...].astype(F32) + inverse * (
         scaled - normed_mid * jnp.mean(scaled * normed_mid, -1, keepdims=True)
@@ -452,12 +488,11 @@
     d_norm = dot_nt(dq, wq[...]) + dot_nt(dk, wk[...]) + dot_nt(dv, wv[...])
     d_gain = jnp.sum(d_norm * normed, 0, keepdims=True)
     for c in range(4):
-        g[c, ROWS:, :] = jnp.zeros((HALF * 2 - ROWS, 128), BF16)
-        if c:
-            g[c, ROWS : ROWS + 16, :] = tail_of(g, c - 1, False).astype(BF16)
-    g[0, ROWS : ROWS + 16, :] = head_of_rows([d_gain, dg[...]]).astype(BF16)
-    g[0, ROWS + 16 : ROWS + 32, :] = tail_of(g, 3, False).astype(BF16)
-    stores = piece_copies(idx, [(keep, send)], g, 0, out_sems, True)
+        top = tail_of(g, c - 1, False) if c else head_of_rows([d_gain, dg[...]])
+        low = jnp.zeros((16, 128), F32) if c else tail_of(g, 3, False)
+        g[c, ROWS : ROWS + 16, :] = top.astype(BF16)
+        g[c, ROWS + 16 :, :] = gain_rows(dg[...], low).astype(BF16)
+    stores = piece_copies(idx, [(keep, send)], g, False, out_sems, True)
     for copy in stores:
         copy.start()
     scaled = d_norm * gain[...]
@@ -466,6 +501,167 @@
     )
     for copy in stores:
         copy.wait()
+
+
+def halves_turned(low, high):
+    lane = lax.broadcasted_iota(jnp.int32, low.shape, 1)
+    return jnp.where(lane < 64, pltpu.roll(low, 64, 1), pltpu.roll(high, 64, 1))
+
+
+def pack_kernel(idx, flat, out, rolled, window, packed, mixed):
+    index, core, down, right = idx[0], idx[1], idx[2], idx[3]
+    lane = lax.broadcasted_iota(jnp.int32, (1, 128), 1)
+    rolled[0:16, :] = jnp.zeros((16, 128), F32)
+    rolled[16:1752, :] = pltpu.roll(flat[...].astype(F32), right, 1)
+    rolled[1752:1760, :] = jnp.zeros((8, 128), F32)
+    window[...] = jnp.where(
+        lane >= right, rolled[pl.ds(16 - down, 1744), :], rolled[pl.ds(15 - down, 1744), :]
+    )
+    head = [window[k : k + 1, :] for k in range(9)]
+    wide = (index >= 4) & (index < 12)
+
+    @pl.when(wide)
+    def _():
+        for j in range(12):
+            packed[WIDE * j : WIDE * (j + 1), :] = window[pl.ds(9 + j, WIDE, stride=12), :]
+
+    @pl.when(jnp.logical_not(wide))
+    def _():
+        parts = [window[pl.ds(9 + k, NARROW // 2, stride=9), :] for k in range(9)]
+        for j in range(4):
+            packed[pl.ds(NARROW * j, NARROW // 2, stride=2), :] = parts[j]
+            packed[pl.ds(NARROW * j + 1, NARROW // 2, stride=2), :] = halves_turned(
+                parts[4 + j], parts[5 + j]
+            )
+        mixed[pl.ds(0, NARROW // 2, stride=2), :] = parts[4]
+        mixed[pl.ds(1, NARROW // 2, stride=2), :] = pltpu.roll(parts[8], 64, 1)
+        packed[4 * NARROW : ROWS, :] = jnp.where(
+            lane < 64, mixed[: NARROW // 2, :], pltpu.roll(mixed[NARROW // 2 :, :], 64, 1)
+        )
+
+    last = jnp.zeros((23, 128), F32)
+    after_wide = (index >= 5) & (index < 13)
+
+    @pl.when(after_wide)
+    def _():
+        packed[ROWS:, :] = jnp.concatenate(head + [last], 0)
+
+    @pl.when(jnp.logical_not(after_wide))
+    def _():
+        rows = head[:4] + [halves_turned(head[4 + j], head[5 + j]) for j in range(4)]
+        rows.append(jnp.where(lane < 64, 0.0, pltpu.roll(head[4], 64, 1)))
+        rows.append(jnp.where(lane < 64, 0.0, head[8]))
+        packed[ROWS:, :] = jnp.concatenate(rows + [last[:22]], 0)
+
+    out[...] = packed[pl.ds(pl.multiple_of(core * HALF, 16), HALF), :].astype(BF16)
+
+
+def unpack_kernel(idx, own, twin, out, packed, window, mixed):
+    index, core, down, left = idx[0], idx[1], idx[2], idx[3]
+    lane = lax.broadcasted_iota(jnp.int32, (1, 128), 1)
+    packed[pl.ds(pl.multiple_of(core * HALF, 16), HALF), :] = own[...]
+    packed[pl.ds(pl.multiple_of((1 - core) * HALF, 16), HALF), :] = twin[...]
+    head = [packed[ROWS + k : ROWS + k + 1, :] for k in range(10)]
+    window[1737:, :] = jnp.zeros((15, 128), F32)
+    wide = (index >= 4) & (index < 12)
+
+    @pl.when(wide)
+    def _():
+        for j in range(12):
+            window[pl.ds(9 + j, WIDE, stride=12), :] = packed[WIDE * j : WIDE * (j + 1), :]
+
+    @pl.when(jnp.logical_not(wide))
+    def _():
+        half = packed[4 * NARROW : ROWS, :]
+        mixed[: NARROW // 2, :] = half
+        mixed[NARROW // 2 :, :] = pltpu.roll(half, 64, 1)
+        odd = []
+        for j in range(4):
+            window[pl.ds(9 + j, NARROW // 2, stride=9), :] = packed[
+                pl.ds(NARROW * j, NARROW // 2, stride=2), :
+            ]
+            odd.append(pltpu.roll(packed[pl.ds(NARROW * j + 1, NARROW // 2, stride=2), :], 64, 1))
+        odd.append(mixed[pl.ds(1, NARROW // 2, stride=2), :])
+        before = mixed[pl.ds(0, NARROW // 2, stride=2), :]
+        for j in range(4):
+            window[pl.ds(13 + j, NARROW // 2, stride=9), :] = jnp.where(lane < 64, before, odd[j])
+            before = odd[j]
+        window[pl.ds(17, NARROW // 2, stride=9), :] = jnp.where(
+            lane < 64, before, pltpu.roll(odd[4], 64, 1)
+        )
+
+    after_wide = (index >= 5) & (index < 13)
+
+    @pl.when(after_wide)
+    def _():
+        window[0:9, :] = jnp.concatenate(head[:9], 0)
+
+    @pl.when(jnp.logical_not(after_wide))
+    def _():
+        odd = [pltpu.roll(row, 64, 1) for row in head[4:8]]
+        before, rows = pltpu.roll(head[8], 64, 1), head[:4]
+        for j in range(4):
+            rows.append(jnp.where(lane < 64, before, odd[j]))
+            before = odd[j]
+        rows.append(jnp.where(lane < 64, before, head[9]))
+        window[0:9, :] = jnp.concatenate(rows, 0)
+
+    lanes = pltpu.roll(window[...], jnp.bitwise_and(128 - left, 127), 1)
+    window[...] = lanes
+    out[...] = jnp.where(
+        lane < 128 - left, window[pl.ds(down, 1736), :], window[pl.ds(down + 1, 1736), :]
+    )
+
+
+def chunk_index(index, core, lay):
+    start = index * lay.step
+    return jnp.stack([index, core, start // 128, start % 128]).astype(jnp.int32)
+
+
+def pack_own(params, index, core, lay):
+    if lay.count != CANON:
+        window = jnp.zeros((lay.gains + lay.chunk,), params.dtype)
+        window = lax.dynamic_update_slice(window, params, (index * lay.step,))
+        payload = pack_payload(window, index, lay)
+        return lax.dynamic_slice_in_dim(payload, core * lay.half, lay.half, 0)
+    flat = jnp.pad(params, (0, 1736 * 128 - lay.shard)).reshape(1736, 128)
+    vmem = pl.BlockSpec(memory_space=pltpu.VMEM)
+    return pl.pallas_call(
+        pack_kernel,
+        name="pack_own_chunk",
+        in_specs=[pl.BlockSpec(memory_space=pltpu.SMEM), vmem],
+        out_specs=vmem,
+        out_shape=jax.ShapeDtypeStruct((HALF, 128), BF16),
+        scratch_shapes=[
+            pltpu.VMEM((1760, 128), F32),
+            pltpu.VMEM((1744, 128), F32),
+            pltpu.VMEM((2 * HALF, 128), F32),
+            pltpu.VMEM((NARROW, 128), F32),
+        ],
+        compiler_params=pltpu.CompilerParams(vmem_limit_bytes=VMEM_LIMIT),
+    )(chunk_index(index, core, lay), flat)
+
+
+def unpack_own(own, twin, index, core, lay):
+    if lay.count != CANON:
+        rows = jnp.where(core == 0, jnp.stack([own, twin], 0), jnp.stack([twin, own], 0))
+        window = unpack_payload(rows.reshape(2 * lay.half, 128), index, lay)
+        return lax.dynamic_slice(window, (index * lay.step,), (lay.shard,))
+    vmem = pl.BlockSpec(memory_space=pltpu.VMEM)
+    rows = pl.pallas_call(
+        unpack_kernel,
+        name="unpack_own_chunk",
+        in_specs=[pl.BlockSpec(memory_space=pltpu.SMEM), vmem, vmem],
+        out_specs=vmem,
+        out_shape=jax.ShapeDtypeStruct((1736, 128), F32),
+        scratch_shapes=[
+            pltpu.VMEM((2 * HALF, 128), F32),
+            pltpu.VMEM((1752, 128), F32),
+            pltpu.VMEM((NARROW, 128), F32),
+        ],
+        compiler_params=pltpu.CompilerParams(vmem_limit_bytes=VMEM_LIMIT),
+    )(chunk_index(index, core, lay), own, twin)
+    return rows.reshape(-1)[: lay.shard]
 
 
 def run_layer(idx, own, twin, tokens, cotangent, positions):
@@ -496,12 +692,16 @@
     results = pl.pallas_call(
         first_kernel,
         name="forward_and_ff_backward",
-        in_specs=[smem] + [anywhere] * 8 + [vmem] * 4,
+        in_specs=[smem] + [anywhere] * 12,
         out_specs=[vmem] * len(outs) + [anywhere] * 6,
         out_shape=outs + [piece] * 6,
         scratch_shapes=[
             pltpu.VMEM((CANON, 2 * HALF, 128), BF16),
             pltpu.VMEM((12, 2 * HALF, 128), BF16),
+            pltpu.VMEM((length, width), BF16),
+            pltpu.VMEM((length, width), BF16),
+            pltpu.VMEM((length, HEAD), F32),
+            pltpu.VMEM((length, HEAD), F32),
             pltpu.VMEM((length, width), F32),
             pltpu.VMEM((length, width), BF16),
             pltpu.VMEM((width, length), BF16),
@@ -509,8 +709,9 @@
             pltpu.VMEM((length, width), F32),
             pltpu.VMEM((width, 128), F32),
             pltpu.VMEM((width, 128), F32),
-            pltpu.SemaphoreType.DMA((32,)),
-            pltpu.SemaphoreType.DMA((24,)),
+            pltpu.SemaphoreType.DMA((4,)),
+            pltpu.SemaphoreType.DMA((4, 8)),
+            pltpu.SemaphoreType.DMA((3, 8)),
         ],
         compiler_params=pltpu.CompilerParams(vmem_limit_bytes=VMEM_LIMIT),
         cost_estimate=pl.CostEstimate(
@@ -532,7 +733,7 @@
             pltpu.VMEM((length, kv_width), F32),
             pltpu.VMEM((width, 128), F32),
             pltpu.VMEM((width, 128), F32),
-            pltpu.SemaphoreType.DMA((8,)),
+            pltpu.SemaphoreType.DMA((1, 8)),
         ],
         compiler_params=pltpu.CompilerParams(vmem_limit_bytes=VMEM_LIMIT),
         cost_estimate=pl.CostEstimate(
@@ -600,17 +801,12 @@
     n, half, in_plane = lay.count, lay.half, lay.in_plane
     plane, place = index // in_plane, index % in_plane
     same = n == CANON
-    window = jnp.zeros((lay.gains + lay.chunk,), params.dtype)
-    window = lax.dynamic_update_slice(window, params, (index * lay.step,))
-    payload = pack_payload(window, index, lay)
-    mine = lax.dynamic_slice_in_dim(payload, core * half, half, 0)
-    own, twin = gather(mine, lay)
-
+    own, twin = gather(pack_own(params, index, core, lay), lay)
     if same:
-        idx = jnp.stack([plane, place, core]).astype(jnp.int32)
+        idx = jnp.stack([plane, place, core, 1]).astype(jnp.int32)
     else:
         own, twin = canonical(own, twin, lay, canon, index, core)
-        idx = jnp.zeros((3,), jnp.int32)
+        idx = jnp.zeros((4,), jnp.int32)
     output, d_input, d_gain, keeps, sends = run_layer(
         idx, own, twin, tokens_in, cotangent, positions
     )
@@ -622,18 +818,22 @@
         planes.append(reduce_plane(pair.astype(BF16), lay))
     if same:
         at = ROWS - HALF
-        late = jnp.where(core == 1, planes[0][at + 16 : at + 32], jnp.zeros((16, 128), BF16))
+        row = jnp.arange(16)[:, None]
+        late = jnp.where((core == 1) & (row < 10), planes[0][at + 16 : at + 32], jnp.zeros((16, 128), BF16))
         planes[1] = jnp.concatenate([planes[1][:at], planes[1][at : at + 16] + late, planes[1][at + 16 :]])
     planes = jnp.stack(planes, 0)
-    total = jnp.take(planes, plane, axis=0).astype(F32)
+    parts = [jnp.take(planes, plane, axis=0).astype(F32)]
     for s in range(1, PLANES):
         part = swap(jnp.take(planes, plane ^ s, axis=0), s << (lay.bits - 2), n)
-        total = total + part.astype(F32)
+        parts.append(part.astype(F32))
+    total = (parts[0] + parts[1]) + (parts[2] + parts[3])
     other = swap_rep(total)
-    whole = jnp.where(core == 0, jnp.stack([total, other], 0), jnp.stack([other, total], 0))
-    window = unpack_payload(whole.reshape(2 * half, 128), index, lay)
-    grad_params = lax.dynamic_slice(window, (index * lay.step,), (lay.shard,))
-    return output, d_input, grad_params, sum_everywhere(d_gain, lay)
+    if same:
+        at = ROWS + 26 - HALF
+        d_gain = jnp.where(core == 1, total[at : at + 5], other[at : at + 5]).reshape(-1)[: lay.width]
+    else:
+        d_gain = sum_everywhere(d_gain, lay)
+    return output, d_input, unpack_own(total, other, index, core, lay), d_gain
 
 
 def solution(mesh):

time: 192 us -> 150 us (0.78)
  starting transfers between devices: 60.9 us -> 43.5 us
  waiting for transfers between devices: 71.8 us -> 57.5 us
  local copies, waits for them, and re-layouts: 18.2 us -> 5.01 us
  Pallas kernels: 30.4 us -> 33.8 us
    ppermute x42 -> x6, starting transfers between devices: 59 us -> 12.4 us  [swap(): return lax.ppermute(value, 'dp', [(i, i ^ mask) for i in range(count)])]
    ppermute x42 -> x6, waiting for transfers between devices: 66.7 us -> 25.3 us  [swap(): return lax.ppermute(value, 'dp', [(i, i ^ mask) for i in range(count)])]
    ppermute x0 -> x16, waiting for transfers between devices: none -> 32.1 us  [hop(): return lax.ppermute(value, ('dp', 'rep'), pairs)]
    ppermute x0 -> x16, starting transfers between devices: none -> 26.1 us  [hop(): return lax.ppermute(value, ('dp', 'rep'), pairs)]
    dynamic_update_slice x1 -> x0, local copies, waits for them, and re-layouts: 7.12 us -> none  [on_device(): window = lax.dynamic_update_slice(window, params, (index * lay.step,))]
    ppermute x10 -> x9, waiting for transfers between devices: 5.11 us -> 0.02 us  [swap_rep(): return lax.ppermute(value, 'rep', [(0, 1), (1, 0)])]
    pallas_call x0 -> x2, Pallas kernels: none -> 3.37 us  [the longest x1 2.21 us: unpack_own(): pl.pallas_call(unpack_kernel, name='unpack_own_chunk', in_specs=[pl.Block...]
    ppermute x10 -> x9, starting transfers between devices: 1.94 us -> 5.05 us  [swap_rep(): return lax.ppermute(value, 'rep', [(0, 1), (1, 0)])]
  transfers between devices with their start and end apart: 52 -> 31, of which waited for: 29 -> 12; matrix products, arithmetic and copies ran while one was open for 5% -> 7% of each run, Pallas kernels for 0% -> 6%
where the time goes in v1:
time: 150 us; the launch traced here: 149 us
  waiting for transfers between devices  57.5 us (38%)
  starting transfers between devices  43.5 us (29%)
  Pallas kernels  33.8 us (23%)
  other arithmetic  7.66 us (5%)
  local copies, waits for them, and re-layouts  5.01 us (3%)
    ppermute x16, waiting for transfers between devices, hop(): return lax.ppermute(value, ('dp', 'rep'), pairs)  32.1 us
    ppermute x16, starting transfers between devices, hop(): return lax.ppermute(value, ('dp', 'rep'), pairs)  26.1 us
    ppermute x6, waiting for transfers between devices, swap(): return lax.ppermute(value, 'dp', [(i, i ^ mask) for i in range(count)])  25.3 us
    pallas_call x1, Pallas kernels, run_layer(): pl.pallas_call(first_kernel, name='forward_and_ff_backward', in_specs=[sm...  21.2 us
    ppermute x6, starting transfers between devices, swap(): return lax.ppermute(value, 'dp', [(i, i ^ mask) for i in range(count)])  12.4 us
    pallas_call x1, Pallas kernels, run_layer(): pl.pallas_call(second_kernel, name='attention_backward', in_specs=[smem]...  9.17 us
    ppermute x9, starting transfers between devices, swap_rep(): return lax.ppermute(value, 'rep', [(0, 1), (1, 0)])  5.05 us
    unnamed x28, local copies, waits for them, and re-layouts  3.76 us
  transfers between devices with their start and end apart: 31, of which 12 were waited for; matrix products, arithmetic and copies ran while one was open for 7% of the time, Pallas kernels for 6%

profile of v1, /device:TPU:0, one launch (start us, length us, event | category | flops | bytes accessed | tf_op | source)
XLA Modules:
  0.0 148.5 jit_solution(1757362340191918698)
XLA Ops:
  3.0 3.9 %collective-permute-start.5 = (bf16[880,128]{1,0:T(8,128)(2,1)S(1)}, bf16[880,128]{1,0:T(8,128)(2,1)S(1)}, u32[]{:S(2)}, u32[]{:S(2)}) collective-permute-start(bf16[880,128]{1,0:T(8,128)(2,1)S(1)} %pack_own_chunk.1), channel_id=1, source_target_pairs={{0,16},{2,18},{4,20},{6,22},{8,24},{10,26},{12,28},{14,30},{16,0},... | collective-permute-start | bytes 675848 | tf_op jit(solution)/shard_map/ppermute | solution.py:109
  10.1 12.7 %collective-permute-done.5 = bf16[880,128]{1,0:T(8,128)(2,1)S(1)} collective-permute-done((bf16[880,128]{1,0:T(8,128)(2,1)S(1)}, bf16[880,128]{1,0:T(8,128)(2,1)S(1)}, u32[]{:S(2)}, u32[]{:S(2)}) %collective-permute-start.5) | collective-permute-done | bytes 225312 | tf_op jit(solution)/shard_map/ppermute | solution.py:109
  22.9 2.0 %collective-permute-start.6 = (bf16[880,128]{1,0:T(8,128)(2,1)S(1)}, bf16[880,128]{1,0:T(8,128)(2,1)S(1)}, u32[]{:S(2)}, u32[]{:S(2)}) collective-permute-start(bf16[880,128]{1,0:T(8,128)(2,1)S(1)} %collective-permute-done.5), channel_id=1, source_target_pairs={{0,2},{1,5},{2,0},{3,7},{4,6},{5,1},{6,4},{7,3},{8,10},{9,13},{10,... | collective-permute-start | bytes 675848 | tf_op jit(solution)/shard_map/ppermute | solution.py:118
  25.0 2.1 %collective-permute-start.1 = (bf16[2,880,128]{2,1,0:T(8,128)(2,1)S(1)}, bf16[2,880,128]{2,1,0:T(8,128)(2,1)S(1)}, u32[]{:S(2)}, u32[]{:S(2)}) collective-permute-start(bf16[2,880,128]{2,1,0:T(8,128)(2,1)S(1)} %get-tuple-element.78), channel_id=1, source_target_pairs={{0,4},{1,3},{2,6},{3,1},{4,0},{5,7},{6,2},{7,5},{8,12},{9,11},{10,... | collective-permute-start | bytes 1351688 | tf_op jit(solution)/shard_map/ppermute | solution.py:118
  27.1 1.5 %collective-permute-start.3 = (bf16[880,128]{1,0:T(8,128)(2,1)S(1)}, bf16[880,128]{1,0:T(8,128)(2,1)S(1)}, u32[]{:S(2)}, u32[]{:S(2)}) collective-permute-start(bf16[880,128]{1,0:T(8,128)(2,1)S(1)} %collective-permute-done.2), channel_id=1, source_target_pairs={{0,2},{1,5},{2,0},{3,7},{4,6},{5,1},{6,4},{7,3},{8,10},{9,13},{10,... | collective-permute-start | bytes 675848 | tf_op jit(solution)/shard_map/ppermute | solution.py:118
  28.6 2.7 %collective-permute-done.6 = bf16[880,128]{1,0:T(8,128)(2,1)S(1)} collective-permute-done((bf16[880,128]{1,0:T(8,128)(2,1)S(1)}, bf16[880,128]{1,0:T(8,128)(2,1)S(1)}, u32[]{:S(2)}, u32[]{:S(2)}) %collective-permute-start.6) | collective-permute-done | bytes 225312 | tf_op jit(solution)/shard_map/ppermute | solution.py:118
  31.3 2.2 %collective-permute-start.7 = (bf16[2,880,128]{2,1,0:T(8,128)(2,1)S(1)}, bf16[2,880,128]{2,1,0:T(8,128)(2,1)S(1)}, u32[]{:S(2)}, u32[]{:S(2)}) collective-permute-start(bf16[2,880,128]{2,1,0:T(8,128)(2,1)S(1)} %get-tuple-element.74), channel_id=1, source_target_pairs={{0,4},{1,3},{2,6},{3,1},{4,0},{5,7},{6,2},{7,5},{8,12},{9,11},{10,... | collective-permute-start | bytes 1351688 | tf_op jit(solution)/shard_map/ppermute | solution.py:118
  33.5 2.6 %collective-permute-done.9 = bf16[880,128]{1,0:T(8,128)(2,1)S(1)} collective-permute-done((bf16[880,128]{1,0:T(8,128)(2,1)S(1)}, bf16[880,128]{1,0:T(8,128)(2,1)S(1)}, u32[]{:S(2)}, u32[]{:S(2)}) %collective-permute-start.9) | collective-permute-done | bytes 225312 | tf_op jit(solution)/shard_map/ppermute | solution.py:118
  36.1 2.2 %collective-permute-start.10 = (bf16[2,880,128]{2,1,0:T(8,128)(2,1)S(1)}, bf16[2,880,128]{2,1,0:T(8,128)(2,1)S(1)}, u32[]{:S(2)}, u32[]{:S(2)}) collective-permute-start(bf16[2,880,128]{2,1,0:T(8,128)(2,1)S(1)} %get-tuple-element.72), channel_id=1, source_target_pairs={{0,4},{1,3},{2,6},{3,1},{4,0},{5,7},{6,2},{7,5},{8,12},{9,11},{10,... | collective-permute-start | bytes 1351688 | tf_op jit(solution)/shard_map/ppermute | solution.py:118
  38.3 2.6 %collective-permute-done.3 = bf16[880,128]{1,0:T(8,128)(2,1)S(1)} collective-permute-done((bf16[880,128]{1,0:T(8,128)(2,1)S(1)}, bf16[880,128]{1,0:T(8,128)(2,1)S(1)}, u32[]{:S(2)}, u32[]{:S(2)}) %collective-permute-start.3) | collective-permute-done | bytes 225312 | tf_op jit(solution)/shard_map/ppermute | solution.py:118
  41.0 2.2 %collective-permute-start.4 = (bf16[2,880,128]{2,1,0:T(8,128)(2,1)S(1)}, bf16[2,880,128]{2,1,0:T(8,128)(2,1)S(1)}, u32[]{:S(2)}, u32[]{:S(2)}) collective-permute-start(bf16[2,880,128]{2,1,0:T(8,128)(2,1)S(1)} %get-tuple-element.76), channel_id=1, source_target_pairs={{0,4},{1,3},{2,6},{3,1},{4,0},{5,7},{6,2},{7,5},{8,12},{9,11},{10,... | collective-permute-start | bytes 1351688 | tf_op jit(solution)/shard_map/ppermute | solution.py:118
  44.0 1.6 %collective-permute-done.10 = bf16[2,880,128]{2,1,0:T(8,128)(2,1)S(1)} collective-permute-done((bf16[2,880,128]{2,1,0:T(8,128)(2,1)S(1)}, bf16[2,880,128]{2,1,0:T(8,128)(2,1)S(1)}, u32[]{:S(2)}, u32[]{:S(2)}) %collective-permute-start.10) | collective-permute-done | bytes 450592 | tf_op jit(solution)/shard_map/ppermute | solution.py:118
  45.8 1.8 %collective-permute-start.14 = (bf16[4,880,128]{2,1,0:T(8,128)(2,1)S(1)}, bf16[4,880,128]{2,1,0:T(8,128)(2,1)}, u32[]{:S(2)}, u32[]{:S(2)}) collective-permute-start(bf16[4,880,128]{2,1,0:T(8,128)(2,1)S(1)} %bitcast.86), channel_id=1, source_target_pairs={{0,1},{1,0},{2,3},{3,2},{4,5},{5,4},{6,7},{7,6},{8,9},{9,8},{10,11... | collective-permute-start | bytes 2703368 | tf_op jit(solution)/shard_map/ppermute | solution.py:113
  47.5 2.9 %collective-permute-done.4 = bf16[2,880,128]{2,1,0:T(8,128)(2,1)S(1)} collective-permute-done((bf16[2,880,128]{2,1,0:T(8,128)(2,1)S(1)}, bf16[2,880,128]{2,1,0:T(8,128)(2,1)S(1)}, u32[]{:S(2)}, u32[]{:S(2)}) %collective-permute-start.4) | collective-permute-done | bytes 450592 | tf_op jit(solution)/shard_map/ppermute | solution.py:118
  55.6 21.2 %forward_and_ff_backward.1 = (bf16[256,576]{1,0:T(8,128)(2,1)S(1)}, f32[256,576]{1,0:T(8,128)}, bf16[256,576]{1,0:T(8,128)(2,1)S(1)}, f32[6,384,128]{2,1,0:T(8,1...) custom-call(s32[4]{0:T(128)S(1)} %pad_add_fusion.idx, ...), custom_call_target="tpu_custom_call" | custom-call | flops 4529848320 | bytes 16000000 | tf_op jit(solution)/shard_map/forward_and_ff_backward/pallas_call | solution.py:692
  77.0 9.2 %attention_backward.1 = (f32[256,576]{1,0:T(8,128)}, bf16[4,880,128]{2,1,0:T(8,128)(2,1)}, bf16[4,880,128]{2,1,0:T(8,128)(2,1)}) custom-call(s32[4]{0:T(128)S(1)} %pad_add_fusion.idx, bf16[256,576]{1,0:T(8,128)(2,1)S(1)} %copy-done, f32[256,64]{1,0:T(8,128)S(1)} %get-tuple-element.84.cos_hbm.cos, f32[256,64]{1,0:T(8,128)S(1)} %get-tuple-element.85.sin_hbm.sin, ...), custom_call_target="tpu_custom_call" | custom-call | flops 849346560 | bytes 10000000 | tf_op jit(solution)/shard_map/attention_backward/pallas_call | solution.py:723
  87.5 1.6 %collective-permute-start.19 = (bf16[2,880,128]{2,1,0:T(8,128)(2,1)S(1)}, bf16[2,880,128]{2,1,0:T(8,128)(2,1)S(1)}, u32[]{:S(2)}, u32[]{:S(2)}) collective-permute-start(bf16[2,880,128]{2,1,0:T(8,128)(2,1)S(1)} %slice.118), channel_id=1, source_target_pairs={{0,4},{1,3},{2,6},{3,1},{4,0},{5,7},{6,2},{7,5},{8,12},{9,11},{10,... | collective-permute-start | bytes 1351688 | tf_op jit(solution)/shard_map/ppermute | solution.py:118
  89.1 1.5 %add_convert_fusion.3 = bf16[4,880,128]{2,1,0:T(8,128)(2,1)S(1)} fusion(bf16[4,880,128]{2,1,0:T(8,128)(2,1)} %collective-permute-done.15, bf16[4,880,128]{2,1,0:T(8,128)(2,1)S(1)} %copy-done.7), kind=kLoop, calls=%fused_computation.3 | loop fusion | flops 1802240 | bytes 2703360 | tf_op jit(solution)/shard_map/convert_element_type | solution.py:818
  90.7 1.6 %collective-permute-start.16 = (bf16[2,880,128]{2,1,0:T(8,128)(2,1)S(1)}, bf16[2,880,128]{2,1,0:T(8,128)(2,1)S(1)}, u32[]{:S(2)}, u32[]{:S(2)}) collective-permute-start(bf16[2,880,128]{2,1,0:T(8,128)(2,1)S(1)} %slice.114), channel_id=1, source_target_pairs={{0,4},{1,3},{2,6},{3,1},{4,0},{5,7},{6,2},{7,5},{8,12},{9,11},{10,... | collective-permute-start | bytes 1351688 | tf_op jit(solution)/shard_map/ppermute | solution.py:118
  96.4 1.6 %collective-permute-start.20 = (bf16[880,128]{1,0:T(8,128)(2,1)S(1)}, bf16[880,128]{1,0:T(8,128)(2,1)S(1)}, u32[]{:S(2)}, u32[]{:S(2)}) collective-permute-start(bf16[880,128]{1,0:T(8,128)(2,1)S(1)} %slice_bitcast_fusion.4), channel_id=1, source_target_pairs={{0,2},{1,5},{2,0},{3,7},{4,6},{5,1},{6,4},{7,3},{8,10},{9,13},{10,... | collective-permute-start | bytes 675848 | tf_op jit(solution)/shard_map/ppermute | solution.py:118
  98.0 4.9 %collective-permute-done.16 = bf16[2,880,128]{2,1,0:T(8,128)(2,1)S(1)} collective-permute-done((bf16[2,880,128]{2,1,0:T(8,128)(2,1)S(1)}, bf16[2,880,128]{2,1,0:T(8,128)(2,1)S(1)}, u32[]{:S(2)}, u32[]{:S(2)}) %collective-permute-start.16) | collective-permute-done | bytes 450592 | tf_op jit(solution)/shard_map/ppermute | solution.py:118
  103.0 1.9 %collective-permute-start.17 = (bf16[880,128]{1,0:T(8,128)(2,1)S(1)}, bf16[880,128]{1,0:T(8,128)(2,1)S(1)}, u32[]{:S(2)}, u32[]{:S(2)}) collective-permute-start(bf16[880,128]{1,0:T(8,128)(2,1)S(1)} %slice_bitcast_fusion.6), channel_id=1, source_target_pairs={{0,2},{1,5},{2,0},{3,7},{4,6},{5,1},{6,4},{7,3},{8,10},{9,13},{10,... | collective-permute-start | bytes 675848 | tf_op jit(solution)/shard_map/ppermute | solution.py:118
  105.0 5.5 %collective-permute-done.22 = bf16[2,880,128]{2,1,0:T(8,128)(2,1)S(1)} collective-permute-done((bf16[2,880,128]{2,1,0:T(8,128)(2,1)S(1)}, bf16[2,880,128]{2,1,0:T(8,128)(2,1)S(1)}, u32[]{:S(2)}, u32[]{:S(2)}) %collective-permute-start.22) | collective-permute-done | bytes 450592 | tf_op jit(solution)/shard_map/ppermute | solution.py:118
  110.6 1.8 %collective-permute-start.23 = (bf16[880,128]{1,0:T(8,128)(2,1)S(1)}, bf16[880,128]{1,0:T(8,128)(2,1)S(1)}, u32[]{:S(2)}, u32[]{:S(2)}) collective-permute-start(bf16[880,128]{1,0:T(8,128)(2,1)S(1)} %slice_bitcast_fusion.2), channel_id=1, source_target_pairs={{0,2},{1,5},{2,0},{3,7},{4,6},{5,1},{6,4},{7,3},{8,10},{9,13},{10,... | collective-permute-start | bytes 675848 | tf_op jit(solution)/shard_map/ppermute | solution.py:118
  112.4 5.4 %collective-permute-done.25 = bf16[2,880,128]{2,1,0:T(8,128)(2,1)S(1)} collective-permute-done((bf16[2,880,128]{2,1,0:T(8,128)(2,1)S(1)}, bf16[2,880,128]{2,1,0:T(8,128)(2,1)S(1)}, u32[]{:S(2)}, u32[]{:S(2)}) %collective-permute-start.25) | collective-permute-done | bytes 450592 | tf_op jit(solution)/shard_map/ppermute | solution.py:118
  118.0 1.8 %collective-permute-start.26 = (bf16[880,128]{1,0:T(8,128)(2,1)S(1)}, bf16[880,128]{1,0:T(8,128)(2,1)S(1)}, u32[]{:S(2)}, u32[]{:S(2)}) collective-permute-start(bf16[880,128]{1,0:T(8,128)(2,1)S(1)} %slice_bitcast_fusion), channel_id=1, source_target_pairs={{0,2},{1,5},{2,0},{3,7},{4,6},{5,1},{6,4},{7,3},{8,10},{9,13},{10,... | collective-permute-start | bytes 675848 | tf_op jit(solution)/shard_map/ppermute | solution.py:118
  120.1 3.9 %collective-permute-done.26 = bf16[880,128]{1,0:T(8,128)(2,1)S(1)} collective-permute-done((bf16[880,128]{1,0:T(8,128)(2,1)S(1)}, bf16[880,128]{1,0:T(8,128)(2,1)S(1)}, u32[]{:S(2)}, u32[]{:S(2)}) %collective-permute-start.26) | collective-permute-done | bytes 225312 | tf_op jit(solution)/shard_map/ppermute | solution.py:118
  124.3 3.3 %collective-permute-start.27 = (bf16[880,128]{1,0:T(8,128)(2,1)S(1)}, bf16[880,128]{1,0:T(8,128)(2,1)S(1)}, u32[]{:S(2)}, u32[]{:S(2)}) collective-permute-start(bf16[880,128]{1,0:T(8,128)(2,1)S(1)} %get-tuple-element.68), channel_id=1, source_target_pairs={{0,8},{2,10},{4,12},{6,14},{8,0},{10,2},{12,4},{14,6},{16,24},{18,... | collective-permute-start | bytes 675848 | tf_op jit(solution)/shard_map/ppermute | solution.py:109
  127.6 2.0 %collective-permute-start.28 = (bf16[880,128]{1,0:T(8,128)(2,1)S(1)}, bf16[880,128]{1,0:T(8,128)(2,1)S(1)}, u32[]{:S(2)}, u32[]{:S(2)}) collective-permute-start(bf16[880,128]{1,0:T(8,128)(2,1)S(1)} %get-tuple-element.70), channel_id=1, source_target_pairs={{0,16},{2,18},{4,20},{6,22},{8,24},{10,26},{12,28},{14,30},{16,0},... | collective-permute-start | bytes 675848 | tf_op jit(solution)/shard_map/ppermute | solution.py:109
  131.0 2.3 %collective-permute-done.27 = bf16[880,128]{1,0:T(8,128)(2,1)S(1)} collective-permute-done((bf16[880,128]{1,0:T(8,128)(2,1)S(1)}, bf16[880,128]{1,0:T(8,128)(2,1)S(1)}, u32[]{:S(2)}, u32[]{:S(2)}) %collective-permute-start.27) | collective-permute-done | bytes 225312 | tf_op jit(solution)/shard_map/ppermute | solution.py:109
  133.3 10.3 %collective-permute-done.28 = bf16[880,128]{1,0:T(8,128)(2,1)S(1)} collective-permute-done((bf16[880,128]{1,0:T(8,128)(2,1)S(1)}, bf16[880,128]{1,0:T(8,128)(2,1)S(1)}, u32[]{:S(2)}, u32[]{:S(2)}) %collective-permute-start.28) | collective-permute-done | bytes 225312 | tf_op jit(solution)/shard_map/ppermute | solution.py:109
  146.3 2.2 %unpack_own_chunk.1 = f32[1736,128]{1,0:T(8,128)} custom-call(s32[4]{0:T(128)S(1)} %pad_add_fusion.1.idx, f32[880,128]{1,0:T(8,128)S(1)} %add_add_fusion.own, f32[880,128]{1,0:T(8,128)S(1)} %collective-permute-done.30.twin), custom_call_target="tpu_custom_call" | custom-call | tf_op jit(solution)/shard_map/unpack_own_chunk/pallas_call | solution.py:651
  (105 shorter events, 22.6 us)
Async XLA Ops:
  3.0 19.9 %collective-permute-start.5 = (bf16[880,128]{1,0:T(8,128)(2,1)S(1)}, bf16[880,128]{1,0:T(8,128)(2,1)S(1)}, u32[]{:S(2)}, u32[]{:S(2)}) collective-permute-start(bf16[880,128]{1,0:T(8,128)(2,1)S(1)} %pack_own_chunk.1), channel_id=1, source_target_pairs={{0,16},{2,18},{4,20},{6,22},{8,24},{10,26},{12,28},{14,30},{16,0},... | collective-permute-start | bytes 675848 | tf_op jit(solution)/shard_map/ppermute | solution.py:109
  6.8 18.1 %collective-permute-start.8 = (bf16[880,128]{1,0:T(8,128)(2,1)S(1)}, bf16[880,128]{1,0:T(8,128)(2,1)S(1)}, u32[]{:S(2)}, u32[]{:S(2)}) collective-permute-start(bf16[880,128]{1,0:T(8,128)(2,1)S(1)} %pack_own_chunk.1), channel_id=1, source_target_pairs={{0,24},{2,26},{4,28},{6,30},{8,16},{10,18},{12,20},{14,22},{16,8},... | collective-permute-start | bytes 675848 | tf_op jit(solution)/shard_map/ppermute | solution.py:109
  8.2 16.7 %collective-permute-start = (bf16[880,128]{1,0:T(8,128)(2,1)S(1)}, bf16[880,128]{1,0:T(8,128)(2,1)S(1)}, u32[]{:S(2)}, u32[]{:S(2)}) collective-permute-start(bf16[880,128]{1,0:T(8,128)(2,1)S(1)} %pack_own_chunk.1), channel_id=1, source_target_pairs={{0,2},{1,5},{2,0},{3,7},{4,6},{5,1},{6,4},{7,3},{8,10},{9,13},{10,... | collective-permute-start | bytes 675848 | tf_op jit(solution)/shard_map/ppermute | solution.py:118
  9.7 17.4 %collective-permute-start.2 = (bf16[880,128]{1,0:T(8,128)(2,1)S(1)}, bf16[880,128]{1,0:T(8,128)(2,1)S(1)}, u32[]{:S(2)}, u32[]{:S(2)}) collective-permute-start(bf16[880,128]{1,0:T(8,128)(2,1)S(1)} %pack_own_chunk.1), channel_id=1, source_target_pairs={{0,8},{2,10},{4,12},{6,14},{8,0},{10,2},{12,4},{14,6},{16,24},{18,... | collective-permute-start | bytes 675848 | tf_op jit(solution)/shard_map/ppermute | solution.py:109
  22.9 8.4 %collective-permute-start.6 = (bf16[880,128]{1,0:T(8,128)(2,1)S(1)}, bf16[880,128]{1,0:T(8,128)(2,1)S(1)}, u32[]{:S(2)}, u32[]{:S(2)}) collective-permute-start(bf16[880,128]{1,0:T(8,128)(2,1)S(1)} %collective-permute-done.5), channel_id=1, source_target_pairs={{0,2},{1,5},{2,0},{3,7},{4,6},{5,1},{6,4},{7,3},{8,10},{9,13},{10,... | collective-permute-start | bytes 675848 | tf_op jit(solution)/shard_map/ppermute | solution.py:118
  24.9 11.2 %collective-permute-start.9 = (bf16[880,128]{1,0:T(8,128)(2,1)S(1)}, bf16[880,128]{1,0:T(8,128)(2,1)S(1)}, u32[]{:S(2)}, u32[]{:S(2)}) collective-permute-start(bf16[880,128]{1,0:T(8,128)(2,1)S(1)} %collective-permute-done.8), channel_id=1, source_target_pairs={{0,2},{1,5},{2,0},{3,7},{4,6},{5,1},{6,4},{7,3},{8,10},{9,13},{10,... | collective-permute-start | bytes 675848 | tf_op jit(solution)/shard_map/ppermute | solution.py:118
  25.0 18.2 %collective-permute-start.1 = (bf16[2,880,128]{2,1,0:T(8,128)(2,1)S(1)}, bf16[2,880,128]{2,1,0:T(8,128)(2,1)S(1)}, u32[]{:S(2)}, u32[]{:S(2)}) collective-permute-start(bf16[2,880,128]{2,1,0:T(8,128)(2,1)S(1)} %get-tuple-element.78), channel_id=1, source_target_pairs={{0,4},{1,3},{2,6},{3,1},{4,0},{5,7},{6,2},{7,5},{8,12},{9,11},{10,... | collective-permute-start | bytes 1351688 | tf_op jit(solution)/shard_map/ppermute | solution.py:118
  27.1 13.8 %collective-permute-start.3 = (bf16[880,128]{1,0:T(8,128)(2,1)S(1)}, bf16[880,128]{1,0:T(8,128)(2,1)S(1)}, u32[]{:S(2)}, u32[]{:S(2)}) collective-permute-start(bf16[880,128]{1,0:T(8,128)(2,1)S(1)} %collective-permute-done.2), channel_id=1, source_target_pairs={{0,2},{1,5},{2,0},{3,7},{4,6},{5,1},{6,4},{7,3},{8,10},{9,13},{10,... | collective-permute-start | bytes 675848 | tf_op jit(solution)/shard_map/ppermute | solution.py:118
  31.3 12.0 %collective-permute-start.7 = (bf16[2,880,128]{2,1,0:T(8,128)(2,1)S(1)}, bf16[2,880,128]{2,1,0:T(8,128)(2,1)S(1)}, u32[]{:S(2)}, u32[]{:S(2)}) collective-permute-start(bf16[2,880,128]{2,1,0:T(8,128)(2,1)S(1)} %get-tuple-element.74), channel_id=1, source_target_pairs={{0,4},{1,3},{2,6},{3,1},{4,0},{5,7},{6,2},{7,5},{8,12},{9,11},{10,... | collective-permute-start | bytes 1351688 | tf_op jit(solution)/shard_map/ppermute | solution.py:118
  36.1 9.5 %collective-permute-start.10 = (bf16[2,880,128]{2,1,0:T(8,128)(2,1)S(1)}, bf16[2,880,128]{2,1,0:T(8,128)(2,1)S(1)}, u32[]{:S(2)}, u32[]{:S(2)}) collective-permute-start(bf16[2,880,128]{2,1,0:T(8,128)(2,1)S(1)} %get-tuple-element.72), channel_id=1, source_target_pairs={{0,4},{1,3},{2,6},{3,1},{4,0},{5,7},{6,2},{7,5},{8,12},{9,11},{10,... | collective-permute-start | bytes 1351688 | tf_op jit(solution)/shard_map/ppermute | solution.py:118
  41.0 9.5 %collective-permute-start.4 = (bf16[2,880,128]{2,1,0:T(8,128)(2,1)S(1)}, bf16[2,880,128]{2,1,0:T(8,128)(2,1)S(1)}, u32[]{:S(2)}, u32[]{:S(2)}) collective-permute-start(bf16[2,880,128]{2,1,0:T(8,128)(2,1)S(1)} %get-tuple-element.76), channel_id=1, source_target_pairs={{0,4},{1,3},{2,6},{3,1},{4,0},{5,7},{6,2},{7,5},{8,12},{9,11},{10,... | collective-permute-start | bytes 1351688 | tf_op jit(solution)/shard_map/ppermute | solution.py:118
  43.3 12.3 %collective-permute-start.11 = (bf16[4,880,128]{2,1,0:T(8,128)(2,1)S(1)}, bf16[4,880,128]{2,1,0:T(8,128)(2,1)}, u32[]{:S(2)}, u32[]{:S(2)}) collective-permute-start(bf16[4,880,128]{2,1,0:T(8,128)(2,1)S(1)} %bitcast.82), channel_id=1, source_target_pairs={{0,1},{1,0},{2,3},{3,2},{4,5},{5,4},{6,7},{7,6},{8,9},{9,8},{10,11... | collective-permute-start | bytes 2703368 | tf_op jit(solution)/shard_map/ppermute | solution.py:113
  43.4 12.1 %collective-permute-start.13 = (bf16[4,880,128]{2,1,0:T(8,128)(2,1)S(1)}, bf16[4,880,128]{2,1,0:T(8,128)(2,1)}, u32[]{:S(2)}, u32[]{:S(2)}) collective-permute-start(bf16[4,880,128]{2,1,0:T(8,128)(2,1)S(1)} %bitcast.84), channel_id=1, source_target_pairs={{0,1},{1,0},{2,3},{3,2},{4,5},{5,4},{6,7},{7,6},{8,9},{9,8},{10,11... | collective-permute-start | bytes 2703368 | tf_op jit(solution)/shard_map/ppermute | solution.py:113
  45.8 9.8 %collective-permute-start.14 = (bf16[4,880,128]{2,1,0:T(8,128)(2,1)S(1)}, bf16[4,880,128]{2,1,0:T(8,128)(2,1)}, u32[]{:S(2)}, u32[]{:S(2)}) collective-permute-start(bf16[4,880,128]{2,1,0:T(8,128)(2,1)S(1)} %bitcast.86), channel_id=1, source_target_pairs={{0,1},{1,0},{2,3},{3,2},{4,5},{5,4},{6,7},{7,6},{8,9},{9,8},{10,11... | collective-permute-start | bytes 2703368 | tf_op jit(solution)/shard_map/ppermute | solution.py:113
  51.5 4.0 %collective-permute-start.12 = (bf16[4,880,128]{2,1,0:T(8,128)(2,1)}, bf16[4,880,128]{2,1,0:T(8,128)(2,1)}, u32[]{:S(2)}, u32[]{:S(2)}) collective-permute-start(bf16[4,880,128]{2,1,0:T(8,128)(2,1)} %bitcast.16.own1), channel_id=1, source_target_pairs={{0,1},{1,0},{2,3},{3,2},{4,5},{5,4},{6,7},{7,6},{8,9},{9,8},{10,11... | collective-permute-start | bytes 2703368 | tf_op jit(solution)/shard_map/ppermute | solution.py:113
  55.6 21.4 %copy-start = (bf16[256,576]{1,0:T(8,128)(2,1)S(1)}, bf16[256,576]{1,0:T(8,128)(2,1)}, u32[]{:S(2)}) copy-start(bf16[256,576]{1,0:T(8,128)(2,1)} %copy.14.tok_hbm.tok) | copy-start | bytes 884740
  76.8 10.3 %collective-permute-start.18 = (bf16[4,880,128]{2,1,0:T(8,128)(2,1)}, bf16[4,880,128]{2,1,0:T(8,128)(2,1)S(1)}, u32[]{:S(2)}, u32[]{:S(2)}) collective-permute-start(bf16[4,880,128]{2,1,0:T(8,128)(2,1)} %get-tuple-element.44), channel_id=1, source_target_pairs={{0,1},{1,0},{2,3},{3,2},{4,5},{5,4},{6,7},{7,6},{8,9},{9,8},{10,11... | collective-permute-start | bytes 2703368 | tf_op jit(solution)/shard_map/ppermute | solution.py:113
  86.2 2.9 %collective-permute-start.15 = (bf16[4,880,128]{2,1,0:T(8,128)(2,1)}, bf16[4,880,128]{2,1,0:T(8,128)(2,1)}, u32[]{:S(2)}, u32[]{:S(2)}) collective-permute-start(bf16[4,880,128]{2,1,0:T(8,128)(2,1)} %get-tuple-element.42), channel_id=1, source_target_pairs={{0,1},{1,0},{2,3},{3,2},{4,5},{5,4},{6,7},{7,6},{8,9},{9,8},{10,11... | collective-permute-start | bytes 2703368 | tf_op jit(solution)/shard_map/ppermute | solution.py:113
  86.7 5.6 %collective-permute-start.21 = (bf16[4,880,128]{2,1,0:T(8,128)(2,1)}, bf16[4,880,128]{2,1,0:T(8,128)(2,1)}, u32[]{:S(2)}, u32[]{:S(2)}) collective-permute-start(bf16[4,880,128]{2,1,0:T(8,128)(2,1)} %get-tuple-element.46), channel_id=1, source_target_pairs={{0,1},{1,0},{2,3},{3,2},{4,5},{5,4},{6,7},{7,6},{8,9},{9,8},{10,11... | collective-permute-start | bytes 2703368 | tf_op jit(solution)/shard_map/ppermute | solution.py:113
  86.8 8.1 %collective-permute-start.24 = (bf16[4,880,128]{2,1,0:T(8,128)(2,1)}, bf16[4,880,128]{2,1,0:T(8,128)(2,1)S(1)}, u32[]{:S(2)}, u32[]{:S(2)}) collective-permute-start(bf16[4,880,128]{2,1,0:T(8,128)(2,1)} %get-tuple-element.48), channel_id=1, source_target_pairs={{0,1},{1,0},{2,3},{3,2},{4,5},{5,4},{6,7},{7,6},{8,9},{9,8},{10,11... | collective-permute-start | bytes 2703368 | tf_op jit(solution)/shard_map/ppermute | solution.py:113
  87.5 8.8 %collective-permute-start.19 = (bf16[2,880,128]{2,1,0:T(8,128)(2,1)S(1)}, bf16[2,880,128]{2,1,0:T(8,128)(2,1)S(1)}, u32[]{:S(2)}, u32[]{:S(2)}) collective-permute-start(bf16[2,880,128]{2,1,0:T(8,128)(2,1)S(1)} %slice.118), channel_id=1, source_target_pairs={{0,4},{1,3},{2,6},{3,1},{4,0},{5,7},{6,2},{7,5},{8,12},{9,11},{10,... | collective-permute-start | bytes 1351688 | tf_op jit(solution)/shard_map/ppermute | solution.py:118
  90.7 12.2 %collective-permute-start.16 = (bf16[2,880,128]{2,1,0:T(8,128)(2,1)S(1)}, bf16[2,880,128]{2,1,0:T(8,128)(2,1)S(1)}, u32[]{:S(2)}, u32[]{:S(2)}) collective-permute-start(bf16[2,880,128]{2,1,0:T(8,128)(2,1)S(1)} %slice.114), channel_id=1, source_target_pairs={{0,4},{1,3},{2,6},{3,1},{4,0},{5,7},{6,2},{7,5},{8,12},{9,11},{10,... | collective-permute-start | bytes 1351688 | tf_op jit(solution)/shard_map/ppermute | solution.py:118
  93.8 16.6 %collective-permute-start.22 = (bf16[2,880,128]{2,1,0:T(8,128)(2,1)S(1)}, bf16[2,880,128]{2,1,0:T(8,128)(2,1)S(1)}, u32[]{:S(2)}, u32[]{:S(2)}) collective-permute-start(bf16[2,880,128]{2,1,0:T(8,128)(2,1)S(1)} %slice.126), channel_id=1, source_target_pairs={{0,4},{1,3},{2,6},{3,1},{4,0},{5,7},{6,2},{7,5},{8,12},{9,11},{10,... | collective-permute-start | bytes 1351688 | tf_op jit(solution)/shard_map/ppermute | solution.py:118
  95.1 22.7 %collective-permute-start.25 = (bf16[2,880,128]{2,1,0:T(8,128)(2,1)S(1)}, bf16[2,880,128]{2,1,0:T(8,128)(2,1)S(1)}, u32[]{:S(2)}, u32[]{:S(2)}) collective-permute-start(bf16[2,880,128]{2,1,0:T(8,128)(2,1)S(1)} %slice.130), channel_id=1, source_target_pairs={{0,4},{1,3},{2,6},{3,1},{4,0},{5,7},{6,2},{7,5},{8,12},{9,11},{10,... | collective-permute-start | bytes 1351688 | tf_op jit(solution)/shard_map/ppermute | solution.py:118
  96.4 23.3 %collective-permute-start.20 = (bf16[880,128]{1,0:T(8,128)(2,1)S(1)}, bf16[880,128]{1,0:T(8,128)(2,1)S(1)}, u32[]{:S(2)}, u32[]{:S(2)}) collective-permute-start(bf16[880,128]{1,0:T(8,128)(2,1)S(1)} %slice_bitcast_fusion.4), channel_id=1, source_target_pairs={{0,2},{1,5},{2,0},{3,7},{4,6},{5,1},{6,4},{7,3},{8,10},{9,13},{10,... | collective-permute-start | bytes 675848 | tf_op jit(solution)/shard_map/ppermute | solution.py:118
  103.0 16.8 %collective-permute-start.17 = (bf16[880,128]{1,0:T(8,128)(2,1)S(1)}, bf16[880,128]{1,0:T(8,128)(2,1)S(1)}, u32[]{:S(2)}, u32[]{:S(2)}) collective-permute-start(bf16[880,128]{1,0:T(8,128)(2,1)S(1)} %slice_bitcast_fusion.6), channel_id=1, source_target_pairs={{0,2},{1,5},{2,0},{3,7},{4,6},{5,1},{6,4},{7,3},{8,10},{9,13},{10,... | collective-permute-start | bytes 675848 | tf_op jit(solution)/shard_map/ppermute | solution.py:118
  110.6 9.4 %collective-permute-start.23 = (bf16[880,128]{1,0:T(8,128)(2,1)S(1)}, bf16[880,128]{1,0:T(8,128)(2,1)S(1)}, u32[]{:S(2)}, u32[]{:S(2)}) collective-permute-start(bf16[880,128]{1,0:T(8,128)(2,1)S(1)} %slice_bitcast_fusion.2), channel_id=1, source_target_pairs={{0,2},{1,5},{2,0},{3,7},{4,6},{5,1},{6,4},{7,3},{8,10},{9,13},{10,... | collective-permute-start | bytes 675848 | tf_op jit(solution)/shard_map/ppermute | solution.py:118
  118.0 6.0 %collective-permute-start.26 = (bf16[880,128]{1,0:T(8,128)(2,1)S(1)}, bf16[880,128]{1,0:T(8,128)(2,1)S(1)}, u32[]{:S(2)}, u32[]{:S(2)}) collective-permute-start(bf16[880,128]{1,0:T(8,128)(2,1)S(1)} %slice_bitcast_fusion), channel_id=1, source_target_pairs={{0,2},{1,5},{2,0},{3,7},{4,6},{5,1},{6,4},{7,3},{8,10},{9,13},{10,... | collective-permute-start | bytes 675848 | tf_op jit(solution)/shard_map/ppermute | solution.py:118
  124.3 9.0 %collective-permute-start.27 = (bf16[880,128]{1,0:T(8,128)(2,1)S(1)}, bf16[880,128]{1,0:T(8,128)(2,1)S(1)}, u32[]{:S(2)}, u32[]{:S(2)}) collective-permute-start(bf16[880,128]{1,0:T(8,128)(2,1)S(1)} %get-tuple-element.68), channel_id=1, source_target_pairs={{0,8},{2,10},{4,12},{6,14},{8,0},{10,2},{12,4},{14,6},{16,24},{18,... | collective-permute-start | bytes 675848 | tf_op jit(solution)/shard_map/ppermute | solution.py:109
  127.6 16.0 %collective-permute-start.28 = (bf16[880,128]{1,0:T(8,128)(2,1)S(1)}, bf16[880,128]{1,0:T(8,128)(2,1)S(1)}, u32[]{:S(2)}, u32[]{:S(2)}) collective-permute-start(bf16[880,128]{1,0:T(8,128)(2,1)S(1)} %get-tuple-element.70), channel_id=1, source_target_pairs={{0,16},{2,18},{4,20},{6,22},{8,24},{10,26},{12,28},{14,30},{16,0},... | collective-permute-start | bytes 675848 | tf_op jit(solution)/shard_map/ppermute | solution.py:109
  129.6 14.0 %collective-permute-start.29 = (bf16[880,128]{1,0:T(8,128)(2,1)S(1)}, bf16[880,128]{1,0:T(8,128)(2,1)S(1)}, u32[]{:S(2)}, u32[]{:S(2)}) collective-permute-start(bf16[880,128]{1,0:T(8,128)(2,1)S(1)} %get-tuple-element.69), channel_id=1, source_target_pairs={{0,24},{2,26},{4,28},{6,30},{8,16},{10,18},{12,20},{14,22},{16,8},... | collective-permute-start | bytes 675848 | tf_op jit(solution)/shard_map/ppermute | solution.py:109
  143.7 2.0 %collective-permute-start.30 = (f32[880,128]{1,0:T(8,128)S(1)}, f32[880,128]{1,0:T(8,128)S(1)}, u32[]{:S(2)}, u32[]{:S(2)}) collective-permute-start(f32[880,128]{1,0:T(8,128)S(1)} %add_add_fusion.own), channel_id=1, source_target_pairs={{0,1},{1,0},{2,3},{3,2},{4,5},{5,4},{6,7},{7,6},{8,9},{9,8},{10,11... | collective-permute-start | bytes 1351688 | tf_op jit(solution)/shard_map/ppermute | solution.py:113
  (11 other events, 74.0 us)

commit v2 on v1

--- a/solution.py
+++ b/solution.py
@@ -130,17 +130,31 @@
     return jnp.stack([value] + [hop(value, pair, count) for pair in masks], 0)
 
 
-def gather(half, lay):
+def plane_of(plane, batch):
+    other = jnp.bitwise_and(jnp.bitwise_xor(plane, 2), 2)
+    return [plane, jnp.bitwise_xor(plane, 1), other, other + 1][batch]
+
+
+def gather(half, plane, core, lay, beside):
     n = lay.count
     first, second = hops(lay)
-    planes = [half] + [swap(half, s << (lay.bits - 2), n) for s in range(1, PLANES)]
+    near, far = 1 << (lay.bits - 2), 2 << (lay.bits - 2)
+    pair = swap(half, near, n)
+    pair, beside = lax.optimization_barrier((pair, beside))
+    even = plane % 2 == 0
+    low, high = jnp.where(even, half, pair), jnp.where(even, pair, half)
+    if n == CANON:
+        at = ROWS - HALF
+        extra = jnp.where(core == 1, high[at : at + 16], low[at + 16 : at + 32])
+        low = jnp.concatenate([low[: at + 16], extra], 0)
+    batches = [half, pair, swap(low, far, n), swap(high, far, n)]
     own, twin = [], []
-    for plane in planes:
-        whole = gather_hops(gather_hops(plane, first, n), second, n)
+    for batch in batches:
+        whole = gather_hops(gather_hops(batch, first, n), second, n)
         whole = whole.reshape(lay.in_plane, lay.half, 128)
         own.append(whole)
         twin.append(swap_rep(whole))
-    return own, twin
+    return own, twin, beside
 
 
 def add_hops(value, masks, count):
@@ -278,7 +292,7 @@
     plane, place, core, flip = idx[0], idx[1], idx[2], idx[3]
     copies = []
     for s, (own, twin) in enumerate(refs):
-        at_plane = jnp.bitwise_xor(plane, s) if relative else s
+        at_plane = plane_of(plane, s) if relative else s
         for d in range(4):
             turned = ((d & 1) << 1) | (d >> 1)
             for which, ref in enumerate((own, twin)):
@@ -294,46 +308,52 @@
     return copies
 
 
-def first_kernel(
-    idx, own0, own1, own2, own3, twin0, twin1, twin2, twin3, tok_hbm, cot_hbm, cos_hbm, sin_hbm,
-    y_out, dr_out, att_out, p_out, q_out, k_out, v_out, wq, wk, wv, wo, gain_out, dg_out,
-    keep1, keep2, keep3, send1, send2, send3,
-    w, g, tok, cot, cos, sin, att, n2_ref, n2t_ref, y_acc, dn_acc, first, second,
-    in_sems, sems, out_sems,
+def fetch_plane(idx, refs, w, sems):
+    plane, place, core, flip = idx[0], idx[1], idx[2], idx[3]
+    for batch in range(3):
+        copies = piece_copies(idx, [refs[batch]], w, False, sems, False)
+
+        @pl.when(jnp.minimum(plane, 2) == batch)
+        def _():
+            for copy in copies:
+                copy.start()
+
+    turned = ((place & 1) << 1) | (place >> 1)
+    spot = jnp.where(flip == 1, turned, place)
+    target = w.at[4, pl.ds(ROWS, 16), :]
+    for batch, (own, twin) in enumerate(refs):
+        at = ROWS - HALF + (16 if batch == 2 else 0)
+        for side, ref in ((1, own), (0, twin)):
+            source = ref.at[spot, pl.ds(at, 16), :]
+            right = (core == side) & (jnp.where(plane < 2, 1 - plane, 2) == batch)
+
+            @pl.when(right)
+            def _():
+                pltpu.make_async_copy(source, target, sems.at[1, 0]).start()
+
+
+def attention_kernel(
+    idx, own0, own1, own2, twin0, twin1, twin2, tok_hbm, cos, sin,
+    mixed_out, att_out, p_out, q_out, k_out, v_out, wq, wk, wv, wo, gain_out, gain_mid_out,
+    w, tok, att, first, second, in_sem, sems,
 ):
-    inputs = [
-        pltpu.make_async_copy(src, dst, in_sems.at[i])
-        for i, (src, dst) in enumerate(
-            ((tok_hbm, tok), (cos_hbm, cos), (sin_hbm, sin), (cot_hbm, cot))
-        )
-    ]
-    for copy in inputs:
-        copy.start()
-    loads = piece_copies(
-        idx, [(own0, twin0), (own1, twin1), (own2, twin2), (own3, twin3)], w, True, sems, False
-    )
-    for copy in loads:
-        copy.start()
-
-    def arrived(plane):
-        for j in range(8):
-            pltpu.make_async_copy(
-                own0.at[0], w.at[4 * plane, pl.ds(0, HALF), :], sems.at[plane, j]
-            ).wait()
-
+    load = pltpu.make_async_copy(tok_hbm, tok, in_sem.at[0])
+    load.start()
+    fetch_plane(idx, [(own0, twin0), (own1, twin1), (own2, twin2)], w, sems)
     tokens = tok.shape[0]
-    for copy in inputs:
-        copy.wait()
+    load.wait()
     x = tok[...].astype(F32)
     normed = x * lax.rsqrt(jnp.mean(x * x, -1, keepdims=True) + EPS)
-    arrived(0)
-    for c in range(3):
+    for j in range(8):
+        pltpu.make_async_copy(own0.at[0], w.at[0, pl.ds(0, HALF), :], sems.at[0, j]).wait()
+    pltpu.make_async_copy(
+        own0.at[0, pl.ds(0, 16), :], w.at[4, pl.ds(ROWS, 16), :], sems.at[1, 0]
+    ).wait()
+    for c in range(4):
         add_tail(w, c, False)
-    arrived(1)
-    add_tail(w, 3, False)
     gains = w[0, ROWS : ROWS + 16, :].astype(F32)
     gain_in, gain_mid = row_of_head(gains, 0), row_of_head(gains, 1)
-    gain_out[...] = gain_in
+    gain_out[...], gain_mid_out[...] = gain_in, gain_mid
     n1 = (normed * gain_in).astype(BF16)
     wq[:NARROW, :] = load_narrow(w, 0)
     mixed_chunk = load_narrow(w, 1)
@@ -372,7 +392,32 @@
                 att[part, HEAD * h : HEAD * (h + 1)] = mix[SEQ_LEN * r : SEQ_LEN * (r + 1)]
     attended = att[...].astype(BF16)
     att_out[...] = attended
-    mixed = x + dot(attended, wo[...])
+    mixed_out[...] = x + dot(attended, wo[...])
+
+
+def first_kernel(
+    idx, own0, own1, own2, own3, twin0, twin1, twin2, twin3, mixed_in, gain_mid_in, cot_hbm,
+    y_hbm, dr_out, dg_out, keep1, keep2, keep3, send1, send2, send3,
+    w, g, cot, y_out, n2_ref, n2t_ref, y_acc, dn_acc, in_sem, sems, out_sems,
+):
+    load = pltpu.make_async_copy(cot_hbm, cot, in_sem.at[0])
+    load.start()
+    refs = [(own0, twin0), (own1, twin1), (own2, twin2), (own3, twin3)]
+    loads = piece_copies(idx, refs, w, True, sems, False)
+    for batch in range(4):
+
+        @pl.when(plane_of(idx[0], batch) > 0)
+        def _():
+            for copy in loads[8 * batch : 8 * batch + 8]:
+                copy.start()
+
+    def arrived(plane):
+        for j in range(8):
+            pltpu.make_async_copy(
+                own0.at[0], w.at[4 * plane, pl.ds(0, HALF), :], sems.at[plane, j]
+            ).wait()
+
+    mixed, gain_mid = mixed_in[...], gain_mid_in[...]
     inverse = lax.rsqrt(jnp.mean(mixed * mixed, -1, keepdims=True) + EPS)
     normed_mid = mixed * inverse
     n2 = normed_mid * gain_mid
@@ -380,6 +425,8 @@
     n2t_ref[...] = n2.astype(BF16).astype(F32).T.astype(BF16)
     y_acc[...] = mixed
     dn_acc[...] = jnp.zeros_like(dn_acc)
+    load.wait()
+    arrived(1)
     arrived(2)
     arrived(3)
 
@@ -434,18 +481,21 @@
     for copy in stores:
         copy.start()
     y_out[...] = y_acc[...].astype(BF16)
+    y_store = pltpu.make_async_copy(y_out, y_hbm, in_sem.at[0])
+    y_store.start()
     scaled = d_norm * gain_mid
     dr_out[...] = cot[...].astype(F32) + inverse * (
         scaled - normed_mid * jnp.mean(scaled * normed_mid, -1, keepdims=True)
     )
     for copy in stores:
         copy.wait()
+    y_store.wait()
 
 
 def second_kernel(
     idx, tok, cos, sin, dr, att, p_in, q_in, k_in, v_in, wq, wk, wv, wo, gain, dg,
-    dx_out, keep, send,
-    g, dq_ref, dk_ref, dv_ref, first, second, out_sems,
+    dx_hbm, keep, send,
+    g, dx_out, dq_ref, dk_ref, dv_ref, first, second, in_sem, out_sems,
 ):
     tokens = tok.shape[0]
     d_mixed = dr[...]
@@ -499,8 +549,11 @@
     dx_out[...] = d_mixed + inverse * (
         scaled - normed * jnp.mean(scaled * normed, -1, keepdims=True)
     )
+    dx_store = pltpu.make_async_copy(dx_out, dx_hbm, in_sem.at[0])
+    dx_store.start()
     for copy in stores:
         copy.wait()
+    dx_store.wait()
 
 
 def halves_turned(low, high):
@@ -664,19 +717,26 @@
     return rows.reshape(-1)[: lay.shard]
 
 
-def run_layer(idx, own, twin, tokens, cotangent, positions):
+def tables(positions):
+    cosine, sine = rope_tables(positions)
+    return jnp.concatenate([cosine, cosine], 1), jnp.concatenate([-sine, sine], 1)
+
+
+def run_layer(idx, own, twin, tokens, cotangent, cosine, sine):
     length, width = tokens.shape
     groups = length // SEQ_LEN * KV_HEADS
-    cosine, sine = rope_tables(positions)
-    cosine = jnp.concatenate([cosine, cosine], 1)
-    sine = jnp.concatenate([-sine, sine], 1)
     kv_width = KV_HEADS * HEAD
     smem = pl.BlockSpec(memory_space=pltpu.SMEM)
     vmem = pl.BlockSpec(memory_space=pltpu.VMEM)
+    hbm = pl.BlockSpec(memory_space=pltpu.HBM)
     anywhere = pl.BlockSpec(memory_space=pl.ANY)
+    params = pltpu.CompilerParams(vmem_limit_bytes=VMEM_LIMIT)
 
     def sds(shape, dtype):
         return jax.ShapeDtypeStruct(shape, dtype)
+
+    def cost(flops):
+        return pl.CostEstimate(flops=flops, bytes_accessed=8_000_000, transcendentals=600_000)
 
     piece = sds((4, HALF, 128), BF16)
     weights = [sds((width, width), BF16), sds((width, kv_width), BF16)]
@@ -687,58 +747,71 @@
         sds((groups, SEQ_LEN, HEAD), BF16),
         sds((groups, SEQ_LEN, HEAD), BF16),
     ]
-    outs = [sds((length, width), BF16), sds((length, width), F32), sds((length, width), BF16)]
-    outs = outs + saved + weights + [sds((1, width), F32)] * 2
+    rows = sds((length, width), F32)
+    low_rows = sds((length, width), BF16)
+    outs = [rows, low_rows] + saved + weights + [sds((1, width), F32)] * 2
+    results = pl.pallas_call(
+        attention_kernel,
+        name="attention_forward",
+        in_specs=[smem] + [anywhere] * 6 + [hbm] + [vmem] * 2,
+        out_specs=[vmem] * len(outs),
+        out_shape=outs,
+        scratch_shapes=[
+            pltpu.VMEM((5, 2 * HALF, 128), BF16),
+            pltpu.VMEM((length, width), BF16),
+            pltpu.VMEM((length, width), F32),
+            pltpu.VMEM((width, 128), F32),
+            pltpu.VMEM((width, 128), F32),
+            pltpu.SemaphoreType.DMA((1,)),
+            pltpu.SemaphoreType.DMA((2, 8)),
+        ],
+        compiler_params=params,
+        cost_estimate=cost(10 * length * width * width),
+    )(idx, *own[:3], *twin[:3], tokens, cosine, sine)
+    mixed, attended, probs, q3, k1, v1, wq, wk, wv, wo, gain, gain_mid = results
     results = pl.pallas_call(
         first_kernel,
-        name="forward_and_ff_backward",
-        in_specs=[smem] + [anywhere] * 12,
-        out_specs=[vmem] * len(outs) + [anywhere] * 6,
-        out_shape=outs + [piece] * 6,
+        name="feed_forward",
+        in_specs=[smem] + [anywhere] * 8 + [vmem] * 2 + [hbm],
+        out_specs=[hbm] + [vmem] * 2 + [anywhere] * 6,
+        out_shape=[low_rows, rows, sds((1, width), F32)] + [piece] * 6,
         scratch_shapes=[
             pltpu.VMEM((CANON, 2 * HALF, 128), BF16),
             pltpu.VMEM((12, 2 * HALF, 128), BF16),
             pltpu.VMEM((length, width), BF16),
             pltpu.VMEM((length, width), BF16),
-            pltpu.VMEM((length, HEAD), F32),
-            pltpu.VMEM((length, HEAD), F32),
-            pltpu.VMEM((length, width), F32),
             pltpu.VMEM((length, width), BF16),
             pltpu.VMEM((width, length), BF16),
             pltpu.VMEM((length, width), F32),
             pltpu.VMEM((length, width), F32),
-            pltpu.VMEM((width, 128), F32),
-            pltpu.VMEM((width, 128), F32),
-            pltpu.SemaphoreType.DMA((4,)),
+            pltpu.SemaphoreType.DMA((1,)),
             pltpu.SemaphoreType.DMA((4, 8)),
             pltpu.SemaphoreType.DMA((3, 8)),
         ],
-        compiler_params=pltpu.CompilerParams(vmem_limit_bytes=VMEM_LIMIT),
-        cost_estimate=pl.CostEstimate(
-            flops=20 * length * width * FF, bytes_accessed=16_000_000, transcendentals=600_000
-        ),
-    )(idx, *own, *twin, tokens, cotangent, cosine, sine)
-    output, d_mixed, attended, probs, q3, k1, v1, wq, wk, wv, wo, gain, d_gain = results[:13]
-    keeps, sends = list(results[13:16]), list(results[16:19])
+        compiler_params=params,
+        cost_estimate=cost(18 * length * width * FF),
+    )(idx, *own, *twin, mixed, gain_mid, cotangent)
+    output, d_mixed, d_gain = results[:3]
+    keeps, sends = list(results[3:6]), list(results[6:9])
     d_input, keep, send = pl.pallas_call(
         second_kernel,
         name="attention_backward",
         in_specs=[smem] + [vmem] * 15,
-        out_specs=[vmem] + [anywhere] * 2,
-        out_shape=[sds((length, width), F32), piece, piece],
+        out_specs=[hbm] + [anywhere] * 2,
+        out_shape=[rows, piece, piece],
         scratch_shapes=[
             pltpu.VMEM((4, 2 * HALF, 128), BF16),
+            pltpu.VMEM((length, width), F32),
             pltpu.VMEM((length, width), F32),
             pltpu.VMEM((length, kv_width), F32),
             pltpu.VMEM((length, kv_width), F32),
             pltpu.VMEM((width, 128), F32),
             pltpu.VMEM((width, 128), F32),
+            pltpu.SemaphoreType.DMA((1,)),
             pltpu.SemaphoreType.DMA((1, 8)),
         ],
-        compiler_params=pltpu.CompilerParams(vmem_limit_bytes=VMEM_LIMIT),
-        cost_estimate=pl.CostEstimate(
-            flops=10 * length * width * width, bytes_accessed=10_000_000, transcendentals=0
-        ),
+        compiler_params=params,
+        cost_estimate=cost(10 * length * width * width),
     )(idx, tokens, cosine, sine, d_mixed, attended, probs, q3, k1, v1, wq, wk, wv, wo, gain, d_gain)
     return output, d_input, d_gain[0], [keep] + keeps, [send] + sends
 
@@ -765,11 +838,19 @@
     return jnp.stack([pack_payload(window, i, lay) for i, window in enumerate(windows)], 0)
 
 
+def batch_order(lay, index):
+    plane, place = index // lay.in_plane, index % lay.in_plane
+    planes = jnp.stack([plane_of(plane, batch) for batch in range(PLANES)])
+    batch = jnp.argsort(planes).astype(jnp.int32)
+    spots = jnp.arange(lay.in_plane, dtype=jnp.int32) ^ place
+    return (batch[:, None] * lay.in_plane + spots[None, :]).reshape(-1)
+
+
 def canonical(own, twin, lay, canon, index, core):
     own, twin = jnp.stack(own, 0), jnp.stack(twin, 0)
     both = jnp.where(core == 0, jnp.stack([own, twin], 2), jnp.stack([twin, own], 2))
     both = both.reshape(lay.count, 2 * lay.half, 128)
-    both = jnp.take(both, jnp.arange(lay.count, dtype=jnp.int32) ^ index, axis=0)
+    both = jnp.take(both, batch_order(lay, index), axis=0)
     flat = flat_of(both, lay)
     zeros = jnp.zeros((canon.gains,), flat.dtype)
     rows = []
@@ -801,14 +882,15 @@
     n, half, in_plane = lay.count, lay.half, lay.in_plane
     plane, place = index // in_plane, index % in_plane
     same = n == CANON
-    own, twin = gather(pack_own(params, index, core, lay), lay)
+    mine = pack_own(params, index, core, lay)
+    own, twin, beside = gather(mine, plane, core, lay, tables(positions))
     if same:
         idx = jnp.stack([plane, place, core, 1]).astype(jnp.int32)
     else:
         own, twin = canonical(own, twin, lay, canon, index, core)
         idx = jnp.zeros((4,), jnp.int32)
     output, d_input, d_gain, keeps, sends = run_layer(
-        idx, own, twin, tokens_in, cotangent, positions
+        idx, own, twin, tokens_in, cotangent, *beside
     )
     if not same:
         keeps, sends = from_canonical(keeps, sends, lay, canon, place, core)

time: 150 us -> 151 us (level)
  waiting for transfers between devices: 57.5 us -> 71.2 us
  starting transfers between devices: 43.5 us -> 30.7 us
    ppermute x16, waiting for transfers between devices: 32.1 us -> 39.6 us  [hop(): return lax.ppermute(value, ('dp', 'rep'), pairs)]
    ppermute x16, starting transfers between devices: 26.1 us -> 18.7 us  [hop(): return lax.ppermute(value, ('dp', 'rep'), pairs)]
    ppermute x6, waiting for transfers between devices: 25.3 us -> 31.3 us  [swap(): return lax.ppermute(value, 'dp', [(i, i ^ mask) for i in range(count)])]
    ppermute x9, starting transfers between devices: 5.05 us -> 1.37 us  [swap_rep(): return lax.ppermute(value, 'rep', [(0, 1), (1, 0)])]
    ppermute x6, starting transfers between devices: 12.4 us -> 10.6 us  [swap(): return lax.ppermute(value, 'dp', [(i, i ^ mask) for i in range(count)])]
    pallas_call x1 -> x2, Pallas kernels: 21.2 us -> 21.3 us  [the longest x1 14.6 us: run_layer(): pl.pallas_call(first_kernel, name='feed_forward', in_specs=[smem] + [anyw...]
  transfers between devices with their start and end apart: 31 -> 31, of which waited for: 12 -> 15; matrix products, arithmetic and copies ran while one was open for 7% -> 7% of each run, Pallas kernels for 6% -> 10%
where the time goes in v2:
time: 151 us; the launch traced here: 150 us
  waiting for transfers between devices  71.2 us (47%)
  Pallas kernels  33.3 us (22%)
  starting transfers between devices  30.7 us (20%)
  other arithmetic  8.53 us (6%)
  local copies, waits for them, and re-layouts  5.54 us (4%)
    ppermute x16, waiting for transfers between devices, hop(): return lax.ppermute(value, ('dp', 'rep'), pairs)  39.6 us
    ppermute x6, waiting for transfers between devices, swap(): return lax.ppermute(value, 'dp', [(i, i ^ mask) for i in range(count)])  31.3 us
    ppermute x16, starting transfers between devices, hop(): return lax.ppermute(value, ('dp', 'rep'), pairs)  18.7 us
    pallas_call x1, Pallas kernels, run_layer(): pl.pallas_call(first_kernel, name='feed_forward', in_specs=[smem] + [anyw...  14.6 us
    ppermute x6, starting transfers between devices, swap(): return lax.ppermute(value, 'dp', [(i, i ^ mask) for i in range(count)])  10.6 us
    pallas_call x1, Pallas kernels, run_layer(): pl.pallas_call(second_kernel, name='attention_backward', in_specs=[smem]...  8.56 us
    pallas_call x1, Pallas kernels, run_layer(): pl.pallas_call(attention_kernel, name='attention_forward', in_specs=[smem...  6.78 us
    unnamed x28, local copies, waits for them, and re-layouts  4.27 us
  transfers between devices with their start and end apart: 31, of which 15 were waited for; matrix products, arithmetic and copies ran while one was open for 7% of the time, Pallas kernels for 10%

profile of v2, /device:TPU:0, one launch (start us, length us, event | category | flops | bytes accessed | tf_op | source)
XLA Modules:
  0.0 150.4 jit_solution(3789496523646484417)
XLA Ops:
  1.8 1.2 pack_own_chunk.1
  3.0 2.9 %collective-permute-start.2 = (bf16[880,128]{1,0:T(8,128)(2,1)S(1)}, bf16[880,128]{1,0:T(8,128)(2,1)S(1)}, u32[]{:S(2)}, u32[]{:S(2)}) collective-permute-start(bf16[880,128]{1,0:T(8,128)(2,1)S(1)} %pack_own_chunk.1), channel_id=1, source_target_pairs={{0,8},{2,10},{4,12},{6,14},{8,0},{10,2},{12,4},{14,6},{16,24},{18,... | collective-permute-start | bytes 675848 | tf_op jit(solution)/shard_map/ppermute | solution.py:109
  6.6 4.8 %collective-permute-done.2 = bf16[880,128]{1,0:T(8,128)(2,1)S(1)} collective-permute-done((bf16[880,128]{1,0:T(8,128)(2,1)S(1)}, bf16[880,128]{1,0:T(8,128)(2,1)S(1)}, u32[]{:S(2)}, u32[]{:S(2)}) %collective-permute-start.2) | collective-permute-done | bytes 225312 | tf_op jit(solution)/shard_map/ppermute | solution.py:109
  11.5 2.8 %collective-permute-start.5 = (bf16[880,128]{1,0:T(8,128)(2,1)S(1)}, bf16[880,128]{1,0:T(8,128)(2,1)S(1)}, u32[]{:S(2)}, u32[]{:S(2)}) collective-permute-start(bf16[880,128]{1,0:T(8,128)(2,1)S(1)} %pad_maximum_fusion.9), channel_id=1, source_target_pairs={{0,16},{2,18},{4,20},{6,22},{8,24},{10,26},{12,28},{14,30},{16,0},... | collective-permute-start | bytes 675848 | tf_op jit(solution)/shard_map/ppermute | solution.py:109
  14.3 1.6 %collective-permute-start = (bf16[880,128]{1,0:T(8,128)(2,1)S(1)}, bf16[880,128]{1,0:T(8,128)(2,1)S(1)}, u32[]{:S(2)}, u32[]{:S(2)}) collective-permute-start(bf16[880,128]{1,0:T(8,128)(2,1)S(1)} %pack_own_chunk.1), channel_id=1, source_target_pairs={{0,2},{1,5},{2,0},{3,7},{4,6},{5,1},{6,4},{7,3},{8,10},{9,13},{10,... | collective-permute-start | bytes 675848 | tf_op jit(solution)/shard_map/ppermute | solution.py:118
  16.5 13.4 %collective-permute-done.5 = bf16[880,128]{1,0:T(8,128)(2,1)S(1)} collective-permute-done((bf16[880,128]{1,0:T(8,128)(2,1)S(1)}, bf16[880,128]{1,0:T(8,128)(2,1)S(1)}, u32[]{:S(2)}, u32[]{:S(2)}) %collective-permute-start.5) | collective-permute-done | bytes 225312 | tf_op jit(solution)/shard_map/ppermute | solution.py:109
  29.9 1.6 %collective-permute-start.6 = (bf16[880,128]{1,0:T(8,128)(2,1)S(1)}, bf16[880,128]{1,0:T(8,128)(2,1)S(1)}, u32[]{:S(2)}, u32[]{:S(2)}) collective-permute-start(bf16[880,128]{1,0:T(8,128)(2,1)S(1)} %collective-permute-done.5), channel_id=1, source_target_pairs={{0,2},{1,5},{2,0},{3,7},{4,6},{5,1},{6,4},{7,3},{8,10},{9,13},{10,... | collective-permute-start | bytes 675848 | tf_op jit(solution)/shard_map/ppermute | solution.py:118
  31.5 1.6 %collective-permute-start.1 = (bf16[2,880,128]{2,1,0:T(8,128)(2,1)S(1)}, bf16[2,880,128]{2,1,0:T(8,128)(2,1)S(1)}, u32[]{:S(2)}, u32[]{:S(2)}) collective-permute-start(bf16[2,880,128]{2,1,0:T(8,128)(2,1)S(1)} %get-tuple-element.90), channel_id=1, source_target_pairs={{0,4},{1,3},{2,6},{3,1},{4,0},{5,7},{6,2},{7,5},{8,12},{9,11},{10,... | collective-permute-start | bytes 1351688 | tf_op jit(solution)/shard_map/ppermute | solution.py:118
  33.6 1.5 %collective-permute-start.9 = (bf16[880,128]{1,0:T(8,128)(2,1)S(1)}, bf16[880,128]{1,0:T(8,128)(2,1)S(1)}, u32[]{:S(2)}, u32[]{:S(2)}) collective-permute-start(bf16[880,128]{1,0:T(8,128)(2,1)S(1)} %collective-permute-done.8), channel_id=1, source_target_pairs={{0,2},{1,5},{2,0},{3,7},{4,6},{5,1},{6,4},{7,3},{8,10},{9,13},{10,... | collective-permute-start | bytes 675848 | tf_op jit(solution)/shard_map/ppermute | solution.py:118
  35.2 1.6 %collective-permute-start.4 = (bf16[2,880,128]{2,1,0:T(8,128)(2,1)S(1)}, bf16[2,880,128]{2,1,0:T(8,128)(2,1)S(1)}, u32[]{:S(2)}, u32[]{:S(2)}) collective-permute-start(bf16[2,880,128]{2,1,0:T(8,128)(2,1)S(1)} %get-tuple-element.88), channel_id=1, source_target_pairs={{0,4},{1,3},{2,6},{3,1},{4,0},{5,7},{6,2},{7,5},{8,12},{9,11},{10,... | collective-permute-start | bytes 1351688 | tf_op jit(solution)/shard_map/ppermute | solution.py:118
  36.8 1.5 %collective-permute-done.6 = bf16[880,128]{1,0:T(8,128)(2,1)S(1)} collective-permute-done((bf16[880,128]{1,0:T(8,128)(2,1)S(1)}, bf16[880,128]{1,0:T(8,128)(2,1)S(1)}, u32[]{:S(2)}, u32[]{:S(2)}) %collective-permute-start.6) | collective-permute-done | bytes 225312 | tf_op jit(solution)/shard_map/ppermute | solution.py:118
  38.4 1.6 %collective-permute-start.7 = (bf16[2,880,128]{2,1,0:T(8,128)(2,1)S(1)}, bf16[2,880,128]{2,1,0:T(8,128)(2,1)S(1)}, u32[]{:S(2)}, u32[]{:S(2)}) collective-permute-start(bf16[2,880,128]{2,1,0:T(8,128)(2,1)S(1)} %get-tuple-element.84), channel_id=1, source_target_pairs={{0,4},{1,3},{2,6},{3,1},{4,0},{5,7},{6,2},{7,5},{8,12},{9,11},{10,... | collective-permute-start | bytes 1351688 | tf_op jit(solution)/shard_map/ppermute | solution.py:118
  40.1 3.1 %collective-permute-done.9 = bf16[880,128]{1,0:T(8,128)(2,1)S(1)} collective-permute-done((bf16[880,128]{1,0:T(8,128)(2,1)S(1)}, bf16[880,128]{1,0:T(8,128)(2,1)S(1)}, u32[]{:S(2)}, u32[]{:S(2)}) %collective-permute-start.9) | collective-permute-done | bytes 225312 | tf_op jit(solution)/shard_map/ppermute | solution.py:118
  43.3 1.6 %collective-permute-start.10 = (bf16[2,880,128]{2,1,0:T(8,128)(2,1)S(1)}, bf16[2,880,128]{2,1,0:T(8,128)(2,1)S(1)}, u32[]{:S(2)}, u32[]{:S(2)}) collective-permute-start(bf16[2,880,128]{2,1,0:T(8,128)(2,1)S(1)} %get-tuple-element.82), channel_id=1, source_target_pairs={{0,4},{1,3},{2,6},{3,1},{4,0},{5,7},{6,2},{7,5},{8,12},{9,11},{10,... | collective-permute-start | bytes 1351688 | tf_op jit(solution)/shard_map/ppermute | solution.py:118
  45.1 2.1 %collective-permute-done.4 = bf16[2,880,128]{2,1,0:T(8,128)(2,1)S(1)} collective-permute-done((bf16[2,880,128]{2,1,0:T(8,128)(2,1)S(1)}, bf16[2,880,128]{2,1,0:T(8,128)(2,1)S(1)}, u32[]{:S(2)}, u32[]{:S(2)}) %collective-permute-start.4) | collective-permute-done | bytes 450592 | tf_op jit(solution)/shard_map/ppermute | solution.py:118
  47.4 4.7 %collective-permute-done.7 = bf16[2,880,128]{2,1,0:T(8,128)(2,1)S(1)} collective-permute-done((bf16[2,880,128]{2,1,0:T(8,128)(2,1)S(1)}, bf16[2,880,128]{2,1,0:T(8,128)(2,1)S(1)}, u32[]{:S(2)}, u32[]{:S(2)}) %collective-permute-start.7) | collective-permute-done | bytes 450592 | tf_op jit(solution)/shard_map/ppermute | solution.py:118
  53.1 3.8 %collective-permute-done.10 = bf16[2,880,128]{2,1,0:T(8,128)(2,1)S(1)} collective-permute-done((bf16[2,880,128]{2,1,0:T(8,128)(2,1)S(1)}, bf16[2,880,128]{2,1,0:T(8,128)(2,1)S(1)}, u32[]{:S(2)}, u32[]{:S(2)}) %collective-permute-start.10) | collective-permute-done | bytes 450592 | tf_op jit(solution)/shard_map/ppermute | solution.py:118
  58.4 6.8 %attention_forward.1 = (f32[256,576]{1,0:T(8,128)}, bf16[256,576]{1,0:T(8,128)(2,1)S(1)}, f32[6,384,128]{2,1,0:T(8,128)}, bf16[6,384,64]{2,1,0:T(8,128)(2,1)}, b...) custom-call(s32[4]{0:T(128)S(1)} %pad_add_fusion.idx, ...), custom_call_target="tpu_custom_call" | custom-call | flops 849346560 | bytes 8000000 | tf_op jit(solution)/shard_map/attention_forward/pallas_call | solution.py:753
  66.3 14.6 %feed_forward.1 = (bf16[256,576]{1,0:T(8,128)(2,1)S(1)}, f32[256,576]{1,0:T(8,128)S(1)}, f32[1,576]{1,0:T(1,128)S(1)}, bf16[4,880,128]{2,1,0:T(8,128)(2,1)}, bf1...) custom-call(s32[4]{0:T(128)S(1)} %pad_add_fusion.idx, ...), custom_call_target="tpu_custom_call" | custom-call | flops 4076863488 | bytes 8000000 | tf_op jit(solution)/shard_map/feed_forward/pallas_call | solution.py:772
  82.2 8.6 %attention_backward.1 = (f32[256,576]{1,0:T(8,128)}, bf16[4,880,128]{2,1,0:T(8,128)(2,1)}, bf16[4,880,128]{2,1,0:T(8,128)(2,1)}) custom-call(s32[4]{0:T(128)S(1)} %pad_add_fusion.idx, bf16[256,576]{1,0:T(8,128)(2,1)S(1)} %copy.14.tok_hbm.tok, f32[256,64]{1,0:T(8,128)S(1)} %get-tuple-element.33.cos, f32[256,64]{1,0:T(8,128)S(1)} %get-tuple-element.34.sin, ...), custom_call_target="tpu_custom_call" | custom-call | flops 849346560 | bytes 8000000 | tf_op jit(solution)/shard_map/attention_backward/pallas_call | solution.py:796
  91.8 1.6 %collective-permute-start.19 = (bf16[2,880,128]{2,1,0:T(8,128)(2,1)S(1)}, bf16[2,880,128]{2,1,0:T(8,128)(2,1)S(1)}, u32[]{:S(2)}, u32[]{:S(2)}) collective-permute-start(bf16[2,880,128]{2,1,0:T(8,128)(2,1)S(1)} %slice.133), channel_id=1, source_target_pairs={{0,4},{1,3},{2,6},{3,1},{4,0},{5,7},{6,2},{7,5},{8,12},{9,11},{10,... | collective-permute-start | bytes 1351688 | tf_op jit(solution)/shard_map/ppermute | solution.py:118
  93.7 1.5 add_convert_fusion.3
  95.2 1.6 %collective-permute-start.16 = (bf16[2,880,128]{2,1,0:T(8,128)(2,1)S(1)}, bf16[2,880,128]{2,1,0:T(8,128)(2,1)S(1)}, u32[]{:S(2)}, u32[]{:S(2)}) collective-permute-start(bf16[2,880,128]{2,1,0:T(8,128)(2,1)S(1)} %slice.129), channel_id=1, source_target_pairs={{0,4},{1,3},{2,6},{3,1},{4,0},{5,7},{6,2},{7,5},{8,12},{9,11},{10,... | collective-permute-start | bytes 1351688 | tf_op jit(solution)/shard_map/ppermute | solution.py:118
  96.8 1.5 add_convert_fusion.1
  101.5 5.9 %collective-permute-done.16 = bf16[2,880,128]{2,1,0:T(8,128)(2,1)S(1)} collective-permute-done((bf16[2,880,128]{2,1,0:T(8,128)(2,1)S(1)}, bf16[2,880,128]{2,1,0:T(8,128)(2,1)S(1)}, u32[]{:S(2)}, u32[]{:S(2)}) %collective-permute-start.16) | collective-permute-done | bytes 450592 | tf_op jit(solution)/shard_map/ppermute | solution.py:118
  107.9 6.8 %collective-permute-done.22 = bf16[2,880,128]{2,1,0:T(8,128)(2,1)S(1)} collective-permute-done((bf16[2,880,128]{2,1,0:T(8,128)(2,1)S(1)}, bf16[2,880,128]{2,1,0:T(8,128)(2,1)S(1)}, u32[]{:S(2)}, u32[]{:S(2)}) %collective-permute-start.22) | collective-permute-done | bytes 450592 | tf_op jit(solution)/shard_map/ppermute | solution.py:118
  115.4 6.5 %collective-permute-done.25 = bf16[2,880,128]{2,1,0:T(8,128)(2,1)S(1)} collective-permute-done((bf16[2,880,128]{2,1,0:T(8,128)(2,1)S(1)}, bf16[2,880,128]{2,1,0:T(8,128)(2,1)S(1)}, u32[]{:S(2)}, u32[]{:S(2)}) %collective-permute-start.25) | collective-permute-done | bytes 450592 | tf_op jit(solution)/shard_map/ppermute | solution.py:118
  123.0 5.1 %collective-permute-done.26 = bf16[880,128]{1,0:T(8,128)(2,1)S(1)} collective-permute-done((bf16[880,128]{1,0:T(8,128)(2,1)S(1)}, bf16[880,128]{1,0:T(8,128)(2,1)S(1)}, u32[]{:S(2)}, u32[]{:S(2)}) %collective-permute-start.26) | collective-permute-done | bytes 225312 | tf_op jit(solution)/shard_map/ppermute | solution.py:118
  128.6 3.5 %collective-permute-start.28 = (bf16[880,128]{1,0:T(8,128)(2,1)S(1)}, bf16[880,128]{1,0:T(8,128)(2,1)S(1)}, u32[]{:S(2)}, u32[]{:S(2)}) collective-permute-start(bf16[880,128]{1,0:T(8,128)(2,1)S(1)} %get-tuple-element.80), channel_id=1, source_target_pairs={{0,16},{2,18},{4,20},{6,22},{8,24},{10,26},{12,28},{14,30},{16,0},... | collective-permute-start | bytes 675848 | tf_op jit(solution)/shard_map/ppermute | solution.py:109
  132.9 5.4 %collective-permute-done.27 = bf16[880,128]{1,0:T(8,128)(2,1)S(1)} collective-permute-done((bf16[880,128]{1,0:T(8,128)(2,1)S(1)}, bf16[880,128]{1,0:T(8,128)(2,1)S(1)}, u32[]{:S(2)}, u32[]{:S(2)}) %collective-permute-start.27) | collective-permute-done | bytes 225312 | tf_op jit(solution)/shard_map/ppermute | solution.py:109
  138.2 7.2 %collective-permute-done.28 = bf16[880,128]{1,0:T(8,128)(2,1)S(1)} collective-permute-done((bf16[880,128]{1,0:T(8,128)(2,1)S(1)}, bf16[880,128]{1,0:T(8,128)(2,1)S(1)}, u32[]{:S(2)}, u32[]{:S(2)}) %collective-permute-start.28) | collective-permute-done | bytes 225312 | tf_op jit(solution)/shard_map/ppermute | solution.py:109
  148.2 2.2 %unpack_own_chunk.1 = f32[1736,128]{1,0:T(8,128)} custom-call(s32[4]{0:T(128)S(1)} %pad_add_fusion.1.idx, f32[880,128]{1,0:T(8,128)S(1)} %add_add_fusion.own, f32[880,128]{1,0:T(8,128)S(1)} %collective-permute-done.30.twin), custom_call_target="tpu_custom_call" | custom-call | tf_op jit(solution)/shard_map/unpack_own_chunk/pallas_call | solution.py:704
  (110 shorter events, 19.2 us)
Async XLA Ops:
  3.0 8.4 %collective-permute-start.2 = (bf16[880,128]{1,0:T(8,128)(2,1)S(1)}, bf16[880,128]{1,0:T(8,128)(2,1)S(1)}, u32[]{:S(2)}, u32[]{:S(2)}) collective-permute-start(bf16[880,128]{1,0:T(8,128)(2,1)S(1)} %pack_own_chunk.1), channel_id=1, source_target_pairs={{0,8},{2,10},{4,12},{6,14},{8,0},{10,2},{12,4},{14,6},{16,24},{18,... | collective-permute-start | bytes 675848 | tf_op jit(solution)/shard_map/ppermute | solution.py:109
  11.5 18.4 %collective-permute-start.5 = (bf16[880,128]{1,0:T(8,128)(2,1)S(1)}, bf16[880,128]{1,0:T(8,128)(2,1)S(1)}, u32[]{:S(2)}, u32[]{:S(2)}) collective-permute-start(bf16[880,128]{1,0:T(8,128)(2,1)S(1)} %pad_maximum_fusion.9), channel_id=1, source_target_pairs={{0,16},{2,18},{4,20},{6,22},{8,24},{10,26},{12,28},{14,30},{16,0},... | collective-permute-start | bytes 675848 | tf_op jit(solution)/shard_map/ppermute | solution.py:109
  14.3 17.2 %collective-permute-start = (bf16[880,128]{1,0:T(8,128)(2,1)S(1)}, bf16[880,128]{1,0:T(8,128)(2,1)S(1)}, u32[]{:S(2)}, u32[]{:S(2)}) collective-permute-start(bf16[880,128]{1,0:T(8,128)(2,1)S(1)} %pack_own_chunk.1), channel_id=1, source_target_pairs={{0,2},{1,5},{2,0},{3,7},{4,6},{5,1},{6,4},{7,3},{8,10},{9,13},{10,... | collective-permute-start | bytes 675848 | tf_op jit(solution)/shard_map/ppermute | solution.py:118
  15.8 17.8 %collective-permute-start.8 = (bf16[880,128]{1,0:T(8,128)(2,1)S(1)}, bf16[880,128]{1,0:T(8,128)(2,1)S(1)}, u32[]{:S(2)}, u32[]{:S(2)}) collective-permute-start(bf16[880,128]{1,0:T(8,128)(2,1)S(1)} %get-tuple-element.85), channel_id=1, source_target_pairs={{0,16},{2,18},{4,20},{6,22},{8,24},{10,26},{12,28},{14,30},{16,0},... | collective-permute-start | bytes 675848 | tf_op jit(solution)/shard_map/ppermute | solution.py:109
  16.3 18.9 %collective-permute-start.3 = (bf16[880,128]{1,0:T(8,128)(2,1)S(1)}, bf16[880,128]{1,0:T(8,128)(2,1)S(1)}, u32[]{:S(2)}, u32[]{:S(2)}) collective-permute-start(bf16[880,128]{1,0:T(8,128)(2,1)S(1)} %collective-permute-done.2), channel_id=1, source_target_pairs={{0,2},{1,5},{2,0},{3,7},{4,6},{5,1},{6,4},{7,3},{8,10},{9,13},{10,... | collective-permute-start | bytes 675848 | tf_op jit(solution)/shard_map/ppermute | solution.py:118
  29.9 8.5 %collective-permute-start.6 = (bf16[880,128]{1,0:T(8,128)(2,1)S(1)}, bf16[880,128]{1,0:T(8,128)(2,1)S(1)}, u32[]{:S(2)}, u32[]{:S(2)}) collective-permute-start(bf16[880,128]{1,0:T(8,128)(2,1)S(1)} %collective-permute-done.5), channel_id=1, source_target_pairs={{0,2},{1,5},{2,0},{3,7},{4,6},{5,1},{6,4},{7,3},{8,10},{9,13},{10,... | collective-permute-start | bytes 675848 | tf_op jit(solution)/shard_map/ppermute | solution.py:118
  31.5 13.4 %collective-permute-start.1 = (bf16[2,880,128]{2,1,0:T(8,128)(2,1)S(1)}, bf16[2,880,128]{2,1,0:T(8,128)(2,1)S(1)}, u32[]{:S(2)}, u32[]{:S(2)}) collective-permute-start(bf16[2,880,128]{2,1,0:T(8,128)(2,1)S(1)} %get-tuple-element.90), channel_id=1, source_target_pairs={{0,4},{1,3},{2,6},{3,1},{4,0},{5,7},{6,2},{7,5},{8,12},{9,11},{10,... | collective-permute-start | bytes 1351688 | tf_op jit(solution)/shard_map/ppermute | solution.py:118
  33.6 9.5 %collective-permute-start.9 = (bf16[880,128]{1,0:T(8,128)(2,1)S(1)}, bf16[880,128]{1,0:T(8,128)(2,1)S(1)}, u32[]{:S(2)}, u32[]{:S(2)}) collective-permute-start(bf16[880,128]{1,0:T(8,128)(2,1)S(1)} %collective-permute-done.8), channel_id=1, source_target_pairs={{0,2},{1,5},{2,0},{3,7},{4,6},{5,1},{6,4},{7,3},{8,10},{9,13},{10,... | collective-permute-start | bytes 675848 | tf_op jit(solution)/shard_map/ppermute | solution.py:118
  35.2 12.0 %collective-permute-start.4 = (bf16[2,880,128]{2,1,0:T(8,128)(2,1)S(1)}, bf16[2,880,128]{2,1,0:T(8,128)(2,1)S(1)}, u32[]{:S(2)}, u32[]{:S(2)}) collective-permute-start(bf16[2,880,128]{2,1,0:T(8,128)(2,1)S(1)} %get-tuple-element.88), channel_id=1, source_target_pairs={{0,4},{1,3},{2,6},{3,1},{4,0},{5,7},{6,2},{7,5},{8,12},{9,11},{10,... | collective-permute-start | bytes 1351688 | tf_op jit(solution)/shard_map/ppermute | solution.py:118
  38.4 13.6 %collective-permute-start.7 = (bf16[2,880,128]{2,1,0:T(8,128)(2,1)S(1)}, bf16[2,880,128]{2,1,0:T(8,128)(2,1)S(1)}, u32[]{:S(2)}, u32[]{:S(2)}) collective-permute-start(bf16[2,880,128]{2,1,0:T(8,128)(2,1)S(1)} %get-tuple-element.84), channel_id=1, source_target_pairs={{0,4},{1,3},{2,6},{3,1},{4,0},{5,7},{6,2},{7,5},{8,12},{9,11},{10,... | collective-permute-start | bytes 1351688 | tf_op jit(solution)/shard_map/ppermute | solution.py:118
  43.3 13.6 %collective-permute-start.10 = (bf16[2,880,128]{2,1,0:T(8,128)(2,1)S(1)}, bf16[2,880,128]{2,1,0:T(8,128)(2,1)S(1)}, u32[]{:S(2)}, u32[]{:S(2)}) collective-permute-start(bf16[2,880,128]{2,1,0:T(8,128)(2,1)S(1)} %get-tuple-element.82), channel_id=1, source_target_pairs={{0,4},{1,3},{2,6},{3,1},{4,0},{5,7},{6,2},{7,5},{8,12},{9,11},{10,... | collective-permute-start | bytes 1351688 | tf_op jit(solution)/shard_map/ppermute | solution.py:118
  45.0 13.4 %collective-permute-start.11 = (bf16[4,880,128]{2,1,0:T(8,128)(2,1)S(1)}, bf16[4,880,128]{2,1,0:T(8,128)(2,1)}, u32[]{:S(2)}, u32[]{:S(2)}) collective-permute-start(bf16[4,880,128]{2,1,0:T(8,128)(2,1)S(1)} %bitcast.81), channel_id=1, source_target_pairs={{0,1},{1,0},{2,3},{3,2},{4,5},{5,4},{6,7},{7,6},{8,9},{9,8},{10,11... | collective-permute-start | bytes 2703368 | tf_op jit(solution)/shard_map/ppermute | solution.py:113
  47.3 11.1 %collective-permute-start.12 = (bf16[4,880,128]{2,1,0:T(8,128)(2,1)S(1)}, bf16[4,880,128]{2,1,0:T(8,128)(2,1)}, u32[]{:S(2)}, u32[]{:S(2)}) collective-permute-start(bf16[4,880,128]{2,1,0:T(8,128)(2,1)S(1)} %bitcast.84), channel_id=1, source_target_pairs={{0,1},{1,0},{2,3},{3,2},{4,5},{5,4},{6,7},{7,6},{8,9},{9,8},{10,11... | collective-permute-start | bytes 2703368 | tf_op jit(solution)/shard_map/ppermute | solution.py:113
  53.1 5.4 %collective-permute-start.13 = (bf16[4,880,128]{2,1,0:T(8,128)(2,1)}, bf16[4,880,128]{2,1,0:T(8,128)(2,1)}, u32[]{:S(2)}, u32[]{:S(2)}) collective-permute-start(bf16[4,880,128]{2,1,0:T(8,128)(2,1)} %bitcast.21.own2), channel_id=1, source_target_pairs={{0,1},{1,0},{2,3},{3,2},{4,5},{5,4},{6,7},{7,6},{8,9},{9,8},{10,11... | collective-permute-start | bytes 2703368 | tf_op jit(solution)/shard_map/ppermute | solution.py:113
  57.9 7.3 %collective-permute-start.14 = (bf16[4,880,128]{2,1,0:T(8,128)(2,1)}, bf16[4,880,128]{2,1,0:T(8,128)(2,1)}, u32[]{:S(2)}, u32[]{:S(2)}) collective-permute-start(bf16[4,880,128]{2,1,0:T(8,128)(2,1)} %bitcast.26.own3), channel_id=1, source_target_pairs={{0,1},{1,0},{2,3},{3,2},{4,5},{5,4},{6,7},{7,6},{8,9},{9,8},{10,11... | collective-permute-start | bytes 2703368 | tf_op jit(solution)/shard_map/ppermute | solution.py:113
  81.7 9.7 %collective-permute-start.18 = (bf16[4,880,128]{2,1,0:T(8,128)(2,1)}, bf16[4,880,128]{2,1,0:T(8,128)(2,1)S(1)}, u32[]{:S(2)}, u32[]{:S(2)}) collective-permute-start(bf16[4,880,128]{2,1,0:T(8,128)(2,1)} %get-tuple-element.54), channel_id=1, source_target_pairs={{0,1},{1,0},{2,3},{3,2},{4,5},{5,4},{6,7},{7,6},{8,9},{9,8},{10,11... | collective-permute-start | bytes 2703368 | tf_op jit(solution)/shard_map/ppermute | solution.py:113
  90.8 2.9 %collective-permute-start.15 = (bf16[4,880,128]{2,1,0:T(8,128)(2,1)}, bf16[4,880,128]{2,1,0:T(8,128)(2,1)}, u32[]{:S(2)}, u32[]{:S(2)}) collective-permute-start(bf16[4,880,128]{2,1,0:T(8,128)(2,1)} %get-tuple-element.52), channel_id=1, source_target_pairs={{0,1},{1,0},{2,3},{3,2},{4,5},{5,4},{6,7},{7,6},{8,9},{9,8},{10,11... | collective-permute-start | bytes 2703368 | tf_op jit(solution)/shard_map/ppermute | solution.py:113
  90.9 5.9 %collective-permute-start.21 = (bf16[4,880,128]{2,1,0:T(8,128)(2,1)}, bf16[4,880,128]{2,1,0:T(8,128)(2,1)}, u32[]{:S(2)}, u32[]{:S(2)}) collective-permute-start(bf16[4,880,128]{2,1,0:T(8,128)(2,1)} %get-tuple-element.56), channel_id=1, source_target_pairs={{0,1},{1,0},{2,3},{3,2},{4,5},{5,4},{6,7},{7,6},{8,9},{9,8},{10,11... | collective-permute-start | bytes 2703368 | tf_op jit(solution)/shard_map/ppermute | solution.py:113
  91.4 8.0 %collective-permute-start.24 = (bf16[4,880,128]{2,1,0:T(8,128)(2,1)}, bf16[4,880,128]{2,1,0:T(8,128)(2,1)S(1)}, u32[]{:S(2)}, u32[]{:S(2)}) collective-permute-start(bf16[4,880,128]{2,1,0:T(8,128)(2,1)} %get-tuple-element.58), channel_id=1, source_target_pairs={{0,1},{1,0},{2,3},{3,2},{4,5},{5,4},{6,7},{7,6},{8,9},{9,8},{10,11... | collective-permute-start | bytes 2703368 | tf_op jit(solution)/shard_map/ppermute | solution.py:113
  91.8 9.0 %collective-permute-start.19 = (bf16[2,880,128]{2,1,0:T(8,128)(2,1)S(1)}, bf16[2,880,128]{2,1,0:T(8,128)(2,1)S(1)}, u32[]{:S(2)}, u32[]{:S(2)}) collective-permute-start(bf16[2,880,128]{2,1,0:T(8,128)(2,1)S(1)} %slice.133), channel_id=1, source_target_pairs={{0,4},{1,3},{2,6},{3,1},{4,0},{5,7},{6,2},{7,5},{8,12},{9,11},{10,... | collective-permute-start | bytes 1351688 | tf_op jit(solution)/shard_map/ppermute | solution.py:118
  95.2 12.2 %collective-permute-start.16 = (bf16[2,880,128]{2,1,0:T(8,128)(2,1)S(1)}, bf16[2,880,128]{2,1,0:T(8,128)(2,1)S(1)}, u32[]{:S(2)}, u32[]{:S(2)}) collective-permute-start(bf16[2,880,128]{2,1,0:T(8,128)(2,1)S(1)} %slice.129), channel_id=1, source_target_pairs={{0,4},{1,3},{2,6},{3,1},{4,0},{5,7},{6,2},{7,5},{8,12},{9,11},{10,... | collective-permute-start | bytes 1351688 | tf_op jit(solution)/shard_map/ppermute | solution.py:118
  98.3 16.4 %collective-permute-start.22 = (bf16[2,880,128]{2,1,0:T(8,128)(2,1)S(1)}, bf16[2,880,128]{2,1,0:T(8,128)(2,1)S(1)}, u32[]{:S(2)}, u32[]{:S(2)}) collective-permute-start(bf16[2,880,128]{2,1,0:T(8,128)(2,1)S(1)} %slice.141), channel_id=1, source_target_pairs={{0,4},{1,3},{2,6},{3,1},{4,0},{5,7},{6,2},{7,5},{8,12},{9,11},{10,... | collective-permute-start | bytes 1351688 | tf_op jit(solution)/shard_map/ppermute | solution.py:118
  99.6 22.3 %collective-permute-start.25 = (bf16[2,880,128]{2,1,0:T(8,128)(2,1)S(1)}, bf16[2,880,128]{2,1,0:T(8,128)(2,1)S(1)}, u32[]{:S(2)}, u32[]{:S(2)}) collective-permute-start(bf16[2,880,128]{2,1,0:T(8,128)(2,1)S(1)} %slice.145), channel_id=1, source_target_pairs={{0,4},{1,3},{2,6},{3,1},{4,0},{5,7},{6,2},{7,5},{8,12},{9,11},{10,... | collective-permute-start | bytes 1351688 | tf_op jit(solution)/shard_map/ppermute | solution.py:118
  100.9 21.8 %collective-permute-start.20 = (bf16[880,128]{1,0:T(8,128)(2,1)S(1)}, bf16[880,128]{1,0:T(8,128)(2,1)S(1)}, u32[]{:S(2)}, u32[]{:S(2)}) collective-permute-start(bf16[880,128]{1,0:T(8,128)(2,1)S(1)} %slice_bitcast_fusion.4), channel_id=1, source_target_pairs={{0,2},{1,5},{2,0},{3,7},{4,6},{5,1},{6,4},{7,3},{8,10},{9,13},{10,... | collective-permute-start | bytes 675848 | tf_op jit(solution)/shard_map/ppermute | solution.py:118
  107.6 15.2 %collective-permute-start.17 = (bf16[880,128]{1,0:T(8,128)(2,1)S(1)}, bf16[880,128]{1,0:T(8,128)(2,1)S(1)}, u32[]{:S(2)}, u32[]{:S(2)}) collective-permute-start(bf16[880,128]{1,0:T(8,128)(2,1)S(1)} %slice_bitcast_fusion.6), channel_id=1, source_target_pairs={{0,2},{1,5},{2,0},{3,7},{4,6},{5,1},{6,4},{7,3},{8,10},{9,13},{10,... | collective-permute-start | bytes 675848 | tf_op jit(solution)/shard_map/ppermute | solution.py:118
  114.9 8.1 %collective-permute-start.23 = (bf16[880,128]{1,0:T(8,128)(2,1)S(1)}, bf16[880,128]{1,0:T(8,128)(2,1)S(1)}, u32[]{:S(2)}, u32[]{:S(2)}) collective-permute-start(bf16[880,128]{1,0:T(8,128)(2,1)S(1)} %slice_bitcast_fusion.2), channel_id=1, source_target_pairs={{0,2},{1,5},{2,0},{3,7},{4,6},{5,1},{6,4},{7,3},{8,10},{9,13},{10,... | collective-permute-start | bytes 675848 | tf_op jit(solution)/shard_map/ppermute | solution.py:118
  122.1 6.0 %collective-permute-start.26 = (bf16[880,128]{1,0:T(8,128)(2,1)S(1)}, bf16[880,128]{1,0:T(8,128)(2,1)S(1)}, u32[]{:S(2)}, u32[]{:S(2)}) collective-permute-start(bf16[880,128]{1,0:T(8,128)(2,1)S(1)} %slice_bitcast_fusion), channel_id=1, source_target_pairs={{0,2},{1,5},{2,0},{3,7},{4,6},{5,1},{6,4},{7,3},{8,10},{9,13},{10,... | collective-permute-start | bytes 675848 | tf_op jit(solution)/shard_map/ppermute | solution.py:118
  128.3 17.3 %copy-start.8 = (f32[256,576]{1,0:T(8,128)S(1)}, f32[256,576]{1,0:T(8,128)}, u32[]{:S(2)}) copy-start(f32[256,576]{1,0:T(8,128)} %get-tuple-element.75) | copy-start | bytes 1769476
  128.4 9.8 %collective-permute-start.27 = (bf16[880,128]{1,0:T(8,128)(2,1)S(1)}, bf16[880,128]{1,0:T(8,128)(2,1)S(1)}, u32[]{:S(2)}, u32[]{:S(2)}) collective-permute-start(bf16[880,128]{1,0:T(8,128)(2,1)S(1)} %get-tuple-element.78), channel_id=1, source_target_pairs={{0,8},{2,10},{4,12},{6,14},{8,0},{10,2},{12,4},{14,6},{16,24},{18,... | collective-permute-start | bytes 675848 | tf_op jit(solution)/shard_map/ppermute | solution.py:109
  128.6 16.9 %collective-permute-start.28 = (bf16[880,128]{1,0:T(8,128)(2,1)S(1)}, bf16[880,128]{1,0:T(8,128)(2,1)S(1)}, u32[]{:S(2)}, u32[]{:S(2)}) collective-permute-start(bf16[880,128]{1,0:T(8,128)(2,1)S(1)} %get-tuple-element.80), channel_id=1, source_target_pairs={{0,16},{2,18},{4,20},{6,22},{8,24},{10,26},{12,28},{14,30},{16,0},... | collective-permute-start | bytes 675848 | tf_op jit(solution)/shard_map/ppermute | solution.py:109
  132.0 13.4 %collective-permute-start.29 = (bf16[880,128]{1,0:T(8,128)(2,1)S(1)}, bf16[880,128]{1,0:T(8,128)(2,1)S(1)}, u32[]{:S(2)}, u32[]{:S(2)}) collective-permute-start(bf16[880,128]{1,0:T(8,128)(2,1)S(1)} %get-tuple-element.79), channel_id=1, source_target_pairs={{0,24},{2,26},{4,28},{6,30},{8,16},{10,18},{12,20},{14,22},{16,8},... | collective-permute-start | bytes 675848 | tf_op jit(solution)/shard_map/ppermute | solution.py:109
  145.6 2.0 %collective-permute-start.30 = (f32[880,128]{1,0:T(8,128)S(1)}, f32[880,128]{1,0:T(8,128)S(1)}, u32[]{:S(2)}, u32[]{:S(2)}) collective-permute-start(f32[880,128]{1,0:T(8,128)S(1)} %add_add_fusion.own), channel_id=1, source_target_pairs={{0,1},{1,0},{2,3},{3,2},{4,5},{5,4},{6,7},{7,6},{8,9},{9,8},{10,11... | collective-permute-start | bytes 1351688 | tf_op jit(solution)/shard_map/ppermute | solution.py:113
  (11 other events, 49.0 us)

commit v3 on v1

--- a/solution.py
+++ b/solution.py
@@ -18,6 +18,7 @@
 
 F32, BF16 = jnp.float32, jnp.bfloat16
 ROWS, HALF = 1728, 880
+MAIN, REST = 768, 112
 NARROW, WIDE = 384, 144
 VMEM_LIMIT = 52 * 1024 * 1024
 
@@ -134,26 +135,56 @@
     n = lay.count
     first, second = hops(lay)
     planes = [half] + [swap(half, s << (lay.bits - 2), n) for s in range(1, PLANES)]
-    own, twin = [], []
+    blocks = []
     for plane in planes:
-        whole = gather_hops(gather_hops(plane, first, n), second, n)
-        whole = whole.reshape(lay.in_plane, lay.half, 128)
-        own.append(whole)
-        twin.append(swap_rep(whole))
-    return own, twin
-
-
-def add_hops(value, masks, count):
-    total = value[0].astype(F32)
-    for d, pair in enumerate(masks):
-        total = total + hop(value[d + 1], pair, count).astype(F32)
-    return total.astype(value.dtype)
-
-
-def reduce_plane(value, lay):
-    first, second = hops(lay)
-    grid = value.reshape(len(second) + 1, len(first) + 1, lay.half, 128)
-    return add_hops(add_hops(grid, second, lay.count), first, lay.count)
+        block = gather_hops(plane, first, n)
+        blocks.append([block] + [hop(block, masks, n) for masks in second])
+    return blocks
+
+
+def balanced_gather(half, lay, beside):
+    n = lay.count
+    (first,), (second,) = hops(lay)
+    both = tuple(a ^ b for a, b in zip(first, second))
+    across = [swap(half, s << (lay.bits - 2), n) for s in range(1, PLANES)]
+    plane = [hop(half, masks, n) for masks in (first, second, both)]
+    across, plane, beside = lax.optimization_barrier((across, plane, beside))
+    own = jnp.stack([half] + plane, 0)
+    near = [jnp.stack([value, hop(value, first, n)], 0) for value in across]
+    far = [hop(value, second, n) for value in near]
+    early = [own] + near
+    far, twins = lax.optimization_barrier((far, [swap_rep(value) for value in early]))
+    return early + far + twins + [swap_rep(value) for value in far], beside
+
+
+def pair_sum(keep, send):
+    return [
+        (mine.astype(F32) + swap_rep(other).astype(F32)).astype(BF16)
+        for mine, other in zip(keep, send)
+    ]
+
+
+def send_blocks(blocks, masks, count):
+    return [hop(block, pair, count) for block, pair in zip(blocks[1:], masks)]
+
+
+def add_blocks(block, arrived):
+    total = block.astype(F32)
+    for value in arrived:
+        total = total + value.astype(F32)
+    return total.astype(BF16)
+
+
+def split_first(planes, lay):
+    return [jnp.stack([value[j] for value in planes], 0) for j in range(len(hops(lay)[0]) + 1)]
+
+
+def reduce_planes(planes, plane, lay):
+    parts = [jnp.take(planes, plane, axis=0).astype(F32)]
+    for s in range(1, PLANES):
+        part = swap(jnp.take(planes, plane ^ s, axis=0), s << (lay.bits - 2), lay.count)
+        parts.append(part.astype(F32))
+    return (parts[0] + parts[1]) + (parts[2] + parts[3])
 
 
 def sum_everywhere(value, lay):
@@ -274,62 +305,70 @@
     return vector * cosine + swapped * sine
 
 
-def piece_copies(idx, refs, dst, relative, sems, outward):
-    plane, place, core, flip = idx[0], idx[1], idx[2], idx[3]
+def piece_copies(idx, at_plane, sides, dst, sem, outward):
+    place, core, flip = idx[1], idx[2], idx[3]
     copies = []
-    for s, (own, twin) in enumerate(refs):
-        at_plane = jnp.bitwise_xor(plane, s) if relative else s
+    for which, refs in enumerate(sides):
+        side = jnp.bitwise_xor(core, which)
         for d in range(4):
             turned = ((d & 1) << 1) | (d >> 1)
-            for which, ref in enumerate((own, twin)):
-                side = jnp.bitwise_xor(core, which)
-                offset = jnp.where(side * flip == 1, turned, d)
-                chunk = 4 * at_plane + jnp.bitwise_xor(place, offset)
-                rows = pl.ds(pl.multiple_of(side * HALF, 16), HALF)
-                inner, outer = dst.at[chunk, rows, :], ref.at[d]
+            chunk = 4 * at_plane + jnp.bitwise_xor(place, jnp.where(side * flip == 1, turned, d))
+            if len(refs) == 1:
+                parts = [(refs[0].at[d, pl.ds(at, size), :], at, size) for at, size in ((0, MAIN), (MAIN, REST))]
+            else:
+                parts = [(refs[d // 2].at[d % 2], 0, HALF)]
+            for outer, start, rows in parts:
+                at = pl.multiple_of(side * HALF + start, 16)
+                inner = dst.at[chunk, pl.ds(at, rows), :]
                 pair = (inner, outer) if outward else (outer, inner)
-                copies.append(
-                    pltpu.make_async_copy(pair[0], pair[1], sems.at[at_plane, 2 * d + which])
-                )
+                copies.append((start > 0, pltpu.make_async_copy(pair[0], pair[1], sem)))
     return copies
 
 
-def first_kernel(
-    idx, own0, own1, own2, own3, twin0, twin1, twin2, twin3, tok_hbm, cot_hbm, cos_hbm, sin_hbm,
-    y_out, dr_out, att_out, p_out, q_out, k_out, v_out, wq, wk, wv, wo, gain_out, dg_out,
-    keep1, keep2, keep3, send1, send2, send3,
-    w, g, tok, cot, cos, sin, att, n2_ref, n2t_ref, y_acc, dn_acc, first, second,
-    in_sems, sems, out_sems,
-):
-    inputs = [
-        pltpu.make_async_copy(src, dst, in_sems.at[i])
-        for i, (src, dst) in enumerate(
-            ((tok_hbm, tok), (cos_hbm, cos), (sin_hbm, sin), (cot_hbm, cot))
-        )
+def wait_plane(ref, base, sem):
+    whole = ref.at[pl.ds(base, 4)]
+    pltpu.make_async_copy(whole, whole, sem).wait()
+
+
+def slot_plane(plane, slot):
+    own = jnp.where(plane == 0, 3, plane)
+    low = jnp.where(own == 1, 2, 1)
+    return [low, 6 - own - low, own][slot]
+
+
+def first_kernel(idx, *refs):
+    pieces = list(zip(refs[:7], refs[7:14]))
+    tok_hbm, cos, sin, cot_hbm = refs[14:18]
+    refs = refs[18:]
+    results, outs = refs[:13], refs[13:19]
+    y_acc, dr_out, dg_out, att_out, p_out, q_out, k_out, v_out, wq, wk, wv, wo, gain_out = refs[19:32]
+    w, g, tok, cot_t, cot, att, n2_ref, n2t_ref, dn_acc, first, second = refs[32:43]
+    in_sem, sems, out_sems, result_sems = refs[43:]
+    saves = [
+        pltpu.make_async_copy(src, dst, result_sems.at[i])
+        for i, (src, dst) in enumerate(zip(refs[19:32], results))
     ]
-    for copy in inputs:
-        copy.start()
-    loads = piece_copies(
-        idx, [(own0, twin0), (own1, twin1), (own2, twin2), (own3, twin3)], w, True, sems, False
-    )
-    for copy in loads:
-        copy.start()
-
-    def arrived(plane):
-        for j in range(8):
-            pltpu.make_async_copy(
-                own0.at[0], w.at[4 * plane, pl.ds(0, HALF), :], sems.at[plane, j]
-            ).wait()
-
-    tokens = tok.shape[0]
-    for copy in inputs:
-        copy.wait()
-    x = tok[...].astype(F32)
+    load = pltpu.make_async_copy(tok_hbm, tok, in_sem.at[0])
+    load.start()
+    load_cot = pltpu.make_async_copy(cot_hbm, cot_t, in_sem.at[1])
+    load_cot.start()
+    for s in range(PLANES):
+        sides = [[ref] for ref in pieces[0]]
+        if s:
+            sides = list(zip(pieces[s], pieces[s + 3]))
+        at_plane = jnp.bitwise_xor(idx[0], s)
+        for _, copy in piece_copies(idx, at_plane, sides, w, sems.at[at_plane], False):
+            copy.start()
+    tokens = tok.shape[1]
+    load.wait()
+    x = tok[...].astype(F32).T
     normed = x * lax.rsqrt(jnp.mean(x * x, -1, keepdims=True) + EPS)
-    arrived(0)
+    load_cot.wait()
+    cot[...] = cot_t[...].astype(F32).T.astype(BF16)
+    wait_plane(w, 0, sems.at[0])
     for c in range(3):
         add_tail(w, c, False)
-    arrived(1)
+    wait_plane(w, 4, sems.at[1])
     add_tail(w, 3, False)
     gains = w[0, ROWS : ROWS + 16, :].astype(F32)
     gain_in, gain_mid = row_of_head(gains, 0), row_of_head(gains, 1)
@@ -372,6 +411,8 @@
                 att[part, HEAD * h : HEAD * (h + 1)] = mix[SEQ_LEN * r : SEQ_LEN * (r + 1)]
     attended = att[...].astype(BF16)
     att_out[...] = attended
+    for copy in saves[3:]:
+        copy.start()
     mixed = x + dot(attended, wo[...])
     inverse = lax.rsqrt(jnp.mean(mixed * mixed, -1, keepdims=True) + EPS)
     normed_mid = mixed * inverse
@@ -380,8 +421,8 @@
     n2t_ref[...] = n2.astype(BF16).astype(F32).T.astype(BF16)
     y_acc[...] = mixed
     dn_acc[...] = jnp.zeros_like(dn_acc)
-    arrived(2)
-    arrived(3)
+    wait_plane(w, 8, sems.at[2])
+    wait_plane(w, 12, sems.at[3])
 
     def fix(i, carry):
         add_tail(w, i + 4, True)
@@ -393,61 +434,84 @@
 
     def block(k, carry):
         def wide(base, p):
-            at = pl.multiple_of((3 * k + p) * WIDE, 16)
+            at = pl.multiple_of((6 * k + p) * WIDE, 16)
             return jnp.concatenate([w[base + d, pl.ds(at, WIDE), :] for d in range(4)], 0)
 
-        w_gate = jnp.concatenate([wide(4, p) for p in range(3)], 1)
-        w_up = jnp.concatenate([wide(8, p) for p in range(3)], 1)
-        w_down = load_narrow(w, 12 + k)
+        w_gate = jnp.concatenate([wide(4, p) for p in range(6)], 1)
+        w_up = jnp.concatenate([wide(8, p) for p in range(6)], 1)
+        w_down = jnp.concatenate([load_narrow(w, 12 + 2 * k), load_narrow(w, 13 + 2 * k)], 0)
         c = cot[...]
         gate, up = dot(n2_ref[...], w_gate), dot(n2_ref[...], w_up)
         sigma = 1.0 / (1.0 + jnp.exp(-gate))
         silu = gate * sigma
         hidden = (silu * up).astype(BF16)
         y_acc[...] += dot(hidden, w_down)
-        store_narrow(g, 8 + k, dot_tn(hidden, c))
+        d_down = dot_tn(hidden, c)
+        store_narrow(g, 8 + 2 * k, d_down[:NARROW])
+        store_narrow(g, 9 + 2 * k, d_down[NARROW:])
         d_hidden = dot_nt(c, w_down)
         d_gate = (d_hidden * up * sigma * (1.0 + gate * (1.0 - sigma))).astype(BF16)
         d_up = (d_hidden * silu).astype(BF16)
         dn_acc[...] += dot_nt(d_gate, w_gate) + dot_nt(d_up, w_up)
         for base, d_out in ((0, d_gate), (4, d_up)):
             grad = dot(n2t_ref[...], d_out).astype(BF16)
-            for p in range(3):
-                at = pl.multiple_of((3 * k + p) * WIDE, 16)
+            for p in range(6):
+                at = pl.multiple_of((6 * k + p) * WIDE, 16)
                 for d in range(4):
                     g[base + d, pl.ds(at, WIDE), :] = grad[
                         WIDE * d : WIDE * (d + 1), 128 * p : 128 * (p + 1)
                     ]
         return carry
 
-    lax.fori_loop(0, 4, block, 0)
+    lax.fori_loop(0, 2, block, 0)
+    stores = []
+    for slot in range(3):
+        sides = [[ref] for ref in outs[2 * slot : 2 * slot + 2]]
+        at_plane = slot_plane(idx[0], slot) - 1
+        stores = stores + piece_copies(idx, at_plane, sides, g, out_sems.at[slot], True)
+    for last, copy in stores:
+        if not last:
+            copy.start()
     d_norm = dn_acc[...]
     d_gain = jnp.sum(d_norm * normed_mid, 0, keepdims=True)
     dg_out[...] = d_gain
+    scaled = d_norm * gain_mid
+    d_mixed = cot[...].astype(F32) + inverse * (
+        scaled - normed_mid * jnp.mean(scaled * normed_mid, -1, keepdims=True)
+    )
+    last_rows = dot_tn(att_out[:, 512:], d_mixed.astype(BF16))
     for c in range(12):
-        top = tail_of(g, c - 1, c - 1 < 8) if c else jnp.zeros((16, 128), F32)
+        if c:
+            top = tail_of(g, c - 1, c - 1 < 8)
+        else:
+            top = head_of_rows([last_rows[62:63], last_rows[63:64]])
         g[c, ROWS : ROWS + 16, :] = top.astype(BF16)
         g[c, ROWS + 16 :, :] = gain_rows(d_gain, jnp.zeros((16, 128), F32)).astype(BF16)
-    stores = piece_copies(
-        idx, [(keep1, send1), (keep2, send2), (keep3, send3)], g, False, out_sems, True
-    )
-    for copy in stores:
+    for last, copy in stores:
+        if last:
+            copy.start()
+    dr_out[...] = d_mixed
+    for copy in saves[:3]:
         copy.start()
-    y_out[...] = y_acc[...].astype(BF16)
-    scaled = d_norm * gain_mid
-    dr_out[...] = cot[...].astype(F32) + inverse * (
-        scaled - normed_mid * jnp.mean(scaled * normed_mid, -1, keepdims=True)
-    )
-    for copy in stores:
+    for copy in saves:
         copy.wait()
-
-
-def second_kernel(
-    idx, tok, cos, sin, dr, att, p_in, q_in, k_in, v_in, wq, wk, wv, wo, gain, dg,
-    dx_out, keep, send,
-    g, dq_ref, dk_ref, dv_ref, first, second, out_sems,
-):
-    tokens = tok.shape[0]
+    for slot in range(3):
+        wait_plane(g, 4 * slot, out_sems.at[slot])
+
+
+def second_kernel(idx, *refs):
+    y_out, dx_out, keep, send = refs[16:20]
+    tok, cos, sin, y_in, dr, dg, att, p_in, q_in, k_in, v_in, wq, wk, wv, wo, gain = refs[20:36]
+    g, y_t, dx_t, dq_ref, dk_ref, dv_ref, first, second, in_sem, out_sems = refs[36:]
+    loads = [
+        pltpu.make_async_copy(src, dst, in_sem.at[i])
+        for i, (src, dst) in enumerate(zip(refs[:16], refs[20:36]))
+    ]
+    for copy in loads:
+        copy.start()
+    tokens = tok.shape[1]
+    for copy in loads:
+        copy.wait()
     d_mixed = dr[...]
     branch = d_mixed.astype(BF16)
     dw_out = dot_tn(att[...], branch)
@@ -475,9 +539,10 @@
             )
     dq, dk, dv = dq_ref[...].astype(BF16), dk_ref[...].astype(BF16), dv_ref[...].astype(BF16)
     x = tok[...].astype(F32)
-    inverse = lax.rsqrt(jnp.mean(x * x, -1, keepdims=True) + EPS)
+    inverse = lax.rsqrt(jnp.mean(x * x, 0, keepdims=True) + EPS)
     normed = x * inverse
-    n1t = (normed * gain[...]).astype(BF16).astype(F32).T.astype(BF16)
+    gain_column = jnp.broadcast_to(gain[...], (8, gain.shape[1])).T[:, :1]
+    n1t = (normed * gain_column).astype(BF16)
     dw_query = dot(n1t, dq)
     store_narrow(g, 0, dw_query[:NARROW])
     dw = unspread(dot(n1t, dk), first, second)
@@ -485,22 +550,29 @@
     dw = unspread(dot(n1t, dv), first, second)
     store_narrow(g, 2, jnp.concatenate([dw, dw_out[:192]], 0))
     store_narrow(g, 3, dw_out[192:])
-    d_norm = dot_nt(dq, wq[...]) + dot_nt(dk, wk[...]) + dot_nt(dv, wv[...])
-    d_gain = jnp.sum(d_norm * normed, 0, keepdims=True)
+    d_norm = dot_nt(wq[...], dq) + dot_nt(wk[...], dk) + dot_nt(wv[...], dv)
+    d_gain = jnp.sum(d_norm * normed, 1, keepdims=True)
+    d_gain = jnp.broadcast_to(d_gain, (d_gain.shape[0], 128)).T[:1]
     for c in range(4):
         top = tail_of(g, c - 1, False) if c else head_of_rows([d_gain, dg[...]])
-        low = jnp.zeros((16, 128), F32) if c else tail_of(g, 3, False)
         g[c, ROWS : ROWS + 16, :] = top.astype(BF16)
-        g[c, ROWS + 16 :, :] = gain_rows(dg[...], low).astype(BF16)
-    stores = piece_copies(idx, [(keep, send)], g, False, out_sems, True)
+        g[c, ROWS + 16 :, :] = gain_rows(dg[...], jnp.zeros((16, 128), F32)).astype(BF16)
+    for _, copy in piece_copies(idx, 0, [[keep], [send]], g, out_sems.at[0], True):
+        copy.start()
+    scaled = d_norm * gain_column
+    dx_t[...] = d_mixed.T + inverse * (
+        scaled - normed * jnp.mean(scaled * normed, 0, keepdims=True)
+    )
+    y_t[...] = y_in[...].T.astype(BF16)
+    stores = [
+        pltpu.make_async_copy(src, dst, in_sem.at[i])
+        for i, (src, dst) in enumerate(((dx_t, dx_out), (y_t, y_out)))
+    ]
     for copy in stores:
         copy.start()
-    scaled = d_norm * gain[...]
-    dx_out[...] = d_mixed + inverse * (
-        scaled - normed * jnp.mean(scaled * normed, -1, keepdims=True)
-    )
     for copy in stores:
         copy.wait()
+    wait_plane(g, 0, out_sems.at[0])
 
 
 def halves_turned(low, high):
@@ -664,21 +736,27 @@
     return rows.reshape(-1)[: lay.shard]
 
 
-def run_layer(idx, own, twin, tokens, cotangent, positions):
-    length, width = tokens.shape
+def tables(positions):
+    cosine, sine = rope_tables(positions)
+    return jnp.concatenate([cosine, cosine], 1), jnp.concatenate([-sine, sine], 1)
+
+
+def layer_kernels(length, width):
     groups = length // SEQ_LEN * KV_HEADS
-    cosine, sine = rope_tables(positions)
-    cosine = jnp.concatenate([cosine, cosine], 1)
-    sine = jnp.concatenate([-sine, sine], 1)
     kv_width = KV_HEADS * HEAD
     smem = pl.BlockSpec(memory_space=pltpu.SMEM)
     vmem = pl.BlockSpec(memory_space=pltpu.VMEM)
+    hbm = pl.BlockSpec(memory_space=pltpu.HBM)
     anywhere = pl.BlockSpec(memory_space=pl.ANY)
+    params = pltpu.CompilerParams(vmem_limit_bytes=VMEM_LIMIT)
 
     def sds(shape, dtype):
         return jax.ShapeDtypeStruct(shape, dtype)
 
-    piece = sds((4, HALF, 128), BF16)
+    def cost(flops):
+        return pl.CostEstimate(flops=flops, bytes_accessed=8_000_000, transcendentals=600_000)
+
+    piece = [sds((4, HALF, 128), BF16)]
     weights = [sds((width, width), BF16), sds((width, kv_width), BF16)]
     weights = weights + [weights[1], weights[0]]
     saved = [
@@ -687,60 +765,65 @@
         sds((groups, SEQ_LEN, HEAD), BF16),
         sds((groups, SEQ_LEN, HEAD), BF16),
     ]
-    outs = [sds((length, width), BF16), sds((length, width), F32), sds((length, width), BF16)]
-    outs = outs + saved + weights + [sds((1, width), F32)] * 2
-    results = pl.pallas_call(
+    rows = sds((length, width), F32)
+    low_rows = sds((length, width), BF16)
+    gain = sds((1, width), F32)
+    outs = [rows, rows, gain, low_rows] + saved + weights + [gain]
+    forward = pl.pallas_call(
         first_kernel,
         name="forward_and_ff_backward",
-        in_specs=[smem] + [anywhere] * 12,
-        out_specs=[vmem] * len(outs) + [anywhere] * 6,
-        out_shape=outs + [piece] * 6,
-        scratch_shapes=[
+        in_specs=[smem] + [anywhere] * 14 + [hbm, vmem, vmem, hbm],
+        out_specs=[hbm] * len(outs) + [anywhere] * 6,
+        out_shape=outs + piece * 6,
+        scratch_shapes=[pltpu.VMEM(out.shape, out.dtype) for out in outs]
+        + [
             pltpu.VMEM((CANON, 2 * HALF, 128), BF16),
             pltpu.VMEM((12, 2 * HALF, 128), BF16),
+            pltpu.VMEM((width, length), BF16),
+            pltpu.VMEM((width, length), BF16),
             pltpu.VMEM((length, width), BF16),
-            pltpu.VMEM((length, width), BF16),
-            pltpu.VMEM((length, HEAD), F32),
-            pltpu.VMEM((length, HEAD), F32),
             pltpu.VMEM((length, width), F32),
             pltpu.VMEM((length, width), BF16),
             pltpu.VMEM((width, length), BF16),
             pltpu.VMEM((length, width), F32),
-            pltpu.VMEM((length, width), F32),
             pltpu.VMEM((width, 128), F32),
             pltpu.VMEM((width, 128), F32),
+            pltpu.SemaphoreType.DMA((2,)),
             pltpu.SemaphoreType.DMA((4,)),
-            pltpu.SemaphoreType.DMA((4, 8)),
-            pltpu.SemaphoreType.DMA((3, 8)),
+            pltpu.SemaphoreType.DMA((3,)),
+            pltpu.SemaphoreType.DMA((len(outs),)),
         ],
-        compiler_params=pltpu.CompilerParams(vmem_limit_bytes=VMEM_LIMIT),
-        cost_estimate=pl.CostEstimate(
-            flops=20 * length * width * FF, bytes_accessed=16_000_000, transcendentals=600_000
-        ),
-    )(idx, *own, *twin, tokens, cotangent, cosine, sine)
-    output, d_mixed, attended, probs, q3, k1, v1, wq, wk, wv, wo, gain, d_gain = results[:13]
-    keeps, sends = list(results[13:16]), list(results[16:19])
-    d_input, keep, send = pl.pallas_call(
+        compiler_params=params,
+        cost_estimate=cost(20 * length * width * FF),
+    )
+    attention_back = pl.pallas_call(
         second_kernel,
         name="attention_backward",
-        in_specs=[smem] + [vmem] * 15,
-        out_specs=[vmem] + [anywhere] * 2,
-        out_shape=[sds((length, width), F32), piece, piece],
+        in_specs=[smem] + [hbm] * 16,
+        out_specs=[hbm] * 2 + [anywhere] * 2,
+        out_shape=[sds((width, length), BF16), sds((width, length), F32)] + piece * 2,
         scratch_shapes=[
+            pltpu.VMEM((width, length), BF16),
+            pltpu.VMEM((length, HEAD), F32),
+            pltpu.VMEM((length, HEAD), F32),
+        ]
+        + [pltpu.VMEM(out.shape, out.dtype) for out in outs]
+        + [
             pltpu.VMEM((4, 2 * HALF, 128), BF16),
+            pltpu.VMEM((width, length), BF16),
+            pltpu.VMEM((width, length), F32),
             pltpu.VMEM((length, width), F32),
             pltpu.VMEM((length, kv_width), F32),
             pltpu.VMEM((length, kv_width), F32),
             pltpu.VMEM((width, 128), F32),
             pltpu.VMEM((width, 128), F32),
-            pltpu.SemaphoreType.DMA((1, 8)),
+            pltpu.SemaphoreType.DMA((16,)),
+            pltpu.SemaphoreType.DMA((1,)),
         ],
-        compiler_params=pltpu.CompilerParams(vmem_limit_bytes=VMEM_LIMIT),
-        cost_estimate=pl.CostEstimate(
-            flops=10 * length * width * width, bytes_accessed=10_000_000, transcendentals=0
-        ),
-    )(idx, tokens, cosine, sine, d_mixed, attended, probs, q3, k1, v1, wq, wk, wv, wo, gain, d_gain)
-    return output, d_input, d_gain[0], [keep] + keeps, [send] + sends
+        compiler_params=params,
+        cost_estimate=cost(10 * length * width * width),
+    )
+    return forward, attention_back
 
 
 def flat_of(payloads, lay):
@@ -765,9 +848,12 @@
     return jnp.stack([pack_payload(window, i, lay) for i, window in enumerate(windows)], 0)
 
 
-def canonical(own, twin, lay, canon, index, core):
-    own, twin = jnp.stack(own, 0), jnp.stack(twin, 0)
-    both = jnp.where(core == 0, jnp.stack([own, twin], 2), jnp.stack([twin, own], 2))
+def canonical(blocks, twins, lay, canon, index, core):
+    sides = []
+    for side in (blocks, twins):
+        side = jnp.stack([jnp.concatenate(value, 0) for value in side], 0)
+        sides.append(side.reshape(lay.count, lay.half, 128))
+    both = jnp.where(core == 0, jnp.stack(sides, 1), jnp.stack(sides[::-1], 1))
     both = both.reshape(lay.count, 2 * lay.half, 128)
     both = jnp.take(both, jnp.arange(lay.count, dtype=jnp.int32) ^ index, axis=0)
     flat = flat_of(both, lay)
@@ -779,12 +865,19 @@
             window = jnp.concatenate([zeros, window[canon.gains :]])
         rows.append(pack_payload(window, i, canon))
     rows = jnp.stack(rows, 0).reshape(PLANES, 4, 2, canon.half, 128)
-    return [list(rows[:, :, c]) for c in range(2)]
-
-
-def from_canonical(keeps, sends, lay, canon, place, core):
-    rows = jnp.stack([jnp.stack(keeps, 0), jnp.stack(sends, 0)], 2)
-    rows = rows.reshape(CANON, 2 * canon.half, 128)
+    pieces = []
+    for c in range(2):
+        side = rows[:, :, c]
+        pieces = pieces + [side[0]] + [side[p, :2] for p in range(1, PLANES)]
+        pieces = pieces + [side[p, 2:] for p in range(1, PLANES)]
+    return pieces
+
+
+def from_canonical(slots, lay, canon, place, core):
+    sides = []
+    for which in range(2):
+        sides.append(jnp.stack([slot[which] for slot in slots], 0))
+    rows = jnp.stack(sides, 2).reshape(CANON, 2 * canon.half, 128)
     flats = [unhead_narrow(rows[0, canon.rows : canon.rows + 10])]
     for i in range(CANON):
         body = rows[i, : canon.rows]
@@ -792,7 +885,13 @@
     rows = payloads_of(jnp.concatenate(flats), lay)
     rows = rows.reshape(PLANES, lay.in_plane, 2, lay.half, 128)
     rows = jnp.take(rows, jnp.arange(lay.in_plane, dtype=jnp.int32) ^ place, axis=1)
-    return list(jnp.take(rows, core, axis=2)), list(jnp.take(rows, 1 - core, axis=2))
+    rows = rows.reshape(PLANES, 1 << lay.y_bits, 1 << lay.x_bits, 2, lay.half, 128)
+    sides = [jnp.take(rows, side, axis=3) for side in (core, 1 - core)]
+    return [[list(side[p]) for p in range(PLANES)] for side in sides]
+
+
+def add(left, right):
+    return left.astype(F32) + right.astype(F32)
 
 
 def on_device(lay, canon, tokens_in, positions, params, cotangent):
@@ -801,38 +900,71 @@
     n, half, in_plane = lay.count, lay.half, lay.in_plane
     plane, place = index // in_plane, index % in_plane
     same = n == CANON
-    own, twin = gather(pack_own(params, index, core, lay), lay)
+    firsts, seconds = hops(lay)
+    forward, attention_back = layer_kernels(*tokens_in.shape)
+    mine = pack_own(params, index, core, lay)
+    angles = tables(positions)
     if same:
         idx = jnp.stack([plane, place, core, 1]).astype(jnp.int32)
+        pieces, angles = balanced_gather(mine, lay, angles)
     else:
-        own, twin = canonical(own, twin, lay, canon, index, core)
         idx = jnp.zeros((4,), jnp.int32)
-    output, d_input, d_gain, keeps, sends = run_layer(
-        idx, own, twin, tokens_in, cotangent, positions
-    )
-    if not same:
-        keeps, sends = from_canonical(keeps, sends, lay, canon, place, core)
-    planes = []
-    for keep, send in zip(keeps, sends):
-        pair = keep.astype(F32) + swap_rep(send).astype(F32)
-        planes.append(reduce_plane(pair.astype(BF16), lay))
+        blocks = gather(mine, lay)
+        twins = [[swap_rep(block) for block in value] for value in blocks]
+        pieces = canonical(blocks, twins, lay, canon, index, core)
+    results = forward(idx, *pieces, tokens_in.T, *angles, cotangent.T)
+    d_gain = results[2]
+    slots = [results[13 + 2 * p : 15 + 2 * p] for p in range(3)]
     if same:
-        at = ROWS - HALF
-        row = jnp.arange(16)[:, None]
-        late = jnp.where((core == 1) & (row < 10), planes[0][at + 16 : at + 32], jnp.zeros((16, 128), BF16))
-        planes[1] = jnp.concatenate([planes[1][:at], planes[1][at : at + 16] + late, planes[1][at + 16 :]])
-    planes = jnp.stack(planes, 0)
-    parts = [jnp.take(planes, plane, axis=0).astype(F32)]
-    for s in range(1, PLANES):
-        part = swap(jnp.take(planes, plane ^ s, axis=0), s << (lay.bits - 2), n)
-        parts.append(part.astype(F32))
-    total = (parts[0] + parts[1]) + (parts[2] + parts[3])
+        (first,), (second,) = firsts, seconds
+        keeps, twins = [slot[0] for slot in slots], [swap_rep(slot[1]) for slot in slots]
+        moved = [
+            hop(add(keep[2:], twin[2:]).astype(BF16), second, n)
+            for keep, twin in zip(keeps[:2], twins[:2])
+        ]
+    output, d_input, *slot = attention_back(idx, tokens_in.T, *angles, *results[:13])
+    output, d_input = output.T, d_input.T
+    if same:
+        moved, slot, twins[2] = lax.optimization_barrier((moved, slot, twins[2]))
+        early = [
+            (add(keeps[j][:2], twins[j][:2]) + moved[j].astype(F32)).astype(BF16) for j in range(2)
+        ]
+        early = [add(value[0], hop(value[1], first, n)).astype(BF16) for value in early]
+        ground = plane == 0
+        other = add(slot[0], swap_rep(slot[1])).astype(BF16)
+        third = add(keeps[2], twins[2]).astype(BF16)
+        third, mine = jnp.where(ground, third, other), jnp.where(ground, other, third)
+        third = add(third[:2], hop(third[2:], second, n)).astype(BF16)
+        crossed, moved = lax.optimization_barrier((hop(third[1], first, n), hop(mine[2:], second, n)))
+        third = add(third[0], crossed).astype(BF16)
+        mine = add(mine[:2], moved).astype(BF16)
+
+        def pick(values, s):
+            table = ((0, 1, 2), (2, 1, 0), (1, 2, 0), (1, 0, 2))
+            result = values[table[3][s - 1]]
+            for z in range(3):
+                result = jnp.where(plane == z, values[table[z][s - 1]], result)
+            return result
+
+        planes = early + [third]
+        parts = [swap(pick(planes, s), s << (lay.bits - 2), n) for s in range(1, PLANES)]
+        parts, crossed = lax.optimization_barrier((parts, hop(mine[1], first, n)))
+        total = add(mine[0], crossed) + parts[0].astype(F32) + add(parts[1], parts[2])
+    else:
+        keeps, sends = from_canonical([slot] + slots, lay, canon, place, core)
+        moved = []
+        for keep, send in zip(keeps, sends):
+            pair = pair_sum(keep, send)
+            moved.append(add_blocks(pair[0], send_blocks(pair, seconds, n)))
+        blocks = split_first(moved, lay)
+        planes = add_blocks(blocks[0], send_blocks(blocks, firsts, n))
+        total = reduce_planes(planes, plane, lay)
     other = swap_rep(total)
     if same:
         at = ROWS + 26 - HALF
         d_gain = jnp.where(core == 1, total[at : at + 5], other[at : at + 5]).reshape(-1)[: lay.width]
     else:
-        d_gain = sum_everywhere(d_gain, lay)
+        d_gain = sum_everywhere(d_gain[0], lay)
     return output, d_input, unpack_own(total, other, index, core, lay), d_gain
 
 

time: 150 us -> 147 us (0.980); the launches traced: 149 us -> 144 us
  waiting for transfers between devices: 57.5 us -> 64.5 us
  starting transfers between devices: 43.5 us -> 36.9 us
  Pallas kernels: 33.8 us -> 30.8 us
  local copies, waits for them, and re-layouts: 5.01 us -> 2.21 us
    ppermute x9 -> x12, waiting for transfers between devices: 0.02 us -> 8.11 us  [swap_rep(): return lax.ppermute(value, 'rep', [(0, 1), (1, 0)])]
    ppermute x16 -> x17, starting transfers between devices: 26.1 us -> 22.4 us  [hop(): return lax.ppermute(value, ('dp', 'rep'), pairs)]
    ppermute x9 -> x12, starting transfers between devices: 5.05 us -> 2.05 us  [swap_rep(): return lax.ppermute(value, 'rep', [(0, 1), (1, 0)])]
    pallas_call x2, Pallas kernels: 30.4 us -> 27.5 us  [the longest x1 17.1 us: on_device(): results = forward(idx, *pieces, tokens_in.T, *angles, cotangent.T)]
    unnamed x28 -> x34, local copies, waits for them, and re-layouts: 3.76 us -> 1.04 us
    select_n x1 -> x2, other arithmetic: 0.08 us -> 2.5 us  [the longest x1 2.2 us: on_device(): jnp.where(ground, other, third)]
    another operation x12 -> x4, other arithmetic: 1.83 us -> 0.24 us  [the longest x3 0.13 us: balanced_gather(): near = [jnp.stack([value, hop(value, first, n)], 0) for value in across]]
    ppermute x16 -> x17, waiting for transfers between devices: 32.1 us -> 31.2 us  [hop(): return lax.ppermute(value, ('dp', 'rep'), pairs)]
  transfers between devices with their start and end apart: 31 -> 35, of which waited for: 12 -> 21; matrix products, arithmetic and copies ran while one was open for 7% -> 4% of each run, Pallas kernels for 6% -> 7%
where the time goes in v3:
time: 147 us; the launch traced here: 144 us
  waiting for transfers between devices  64.5 us (44%)
  starting transfers between devices  36.9 us (25%)
  Pallas kernels  30.8 us (21%)
  other arithmetic  8.45 us (6%)
  local copies, waits for them, and re-layouts  2.21 us (2%)
    ppermute x17, waiting for transfers between devices, hop(): return lax.ppermute(value, ('dp', 'rep'), pairs)  31.2 us
    ppermute x6, waiting for transfers between devices, swap(): return lax.ppermute(value, 'dp', [(i, i ^ mask) for i in range(count)])  25.2 us
    ppermute x17, starting transfers between devices, hop(): return lax.ppermute(value, ('dp', 'rep'), pairs)  22.4 us
    pallas_call x1, Pallas kernels, on_device(): results = forward(idx, *pieces, tokens_in.T, *angles, cotangent.T)  17.1 us
    ppermute x6, starting transfers between devices, swap(): return lax.ppermute(value, 'dp', [(i, i ^ mask) for i in range(count)])  12.5 us
    pallas_call x1, Pallas kernels, on_device(): attention_back(idx, tokens_in.T, *angles, *results[:13])  10.4 us
    ppermute x12, waiting for transfers between devices, swap_rep(): return lax.ppermute(value, 'rep', [(0, 1), (1, 0)])  8.11 us
  transfers between devices with their start and end apart: 35, of which 21 were waited for; matrix products, arithmetic and copies ran while one was open for 4% of the time, Pallas kernels for 7%

profile of v3, /device:TPU:0, one launch (start us, length us, event | category | flops | bytes accessed | tf_op | source)
XLA Modules:
  0.0 143.9 jit_solution(9579871694152480376)
XLA Ops:
  3.0 2.9 %collective-permute-start = (bf16[880,128]{1,0:T(8,128)(2,1)S(1)}, bf16[880,128]{1,0:T(8,128)(2,1)S(1)}, u32[]{:S(2)}, u32[]{:S(2)}) collective-permute-start(bf16[880,128]{1,0:T(8,128)(2,1)S(1)} %pack_own_chunk.1), channel_id=1, source_target_pairs={{0,8},{2,10},{4,12},{6,14},{8,0},{10,2},{12,4},{14,6},{16,24},{18,... | collective-permute-start | bytes 675848 | tf_op jit(solution)/shard_map/ppermute | solution.py:110
  5.9 2.7 %collective-permute-start.1 = (bf16[880,128]{1,0:T(8,128)(2,1)S(1)}, bf16[880,128]{1,0:T(8,128)(2,1)S(1)}, u32[]{:S(2)}, u32[]{:S(2)}) collective-permute-start(bf16[880,128]{1,0:T(8,128)(2,1)S(1)} %pack_own_chunk.1), channel_id=1, source_target_pairs={{0,16},{2,18},{4,20},{6,22},{8,24},{10,26},{12,28},{14,30},{16,0},... | collective-permute-start | bytes 675848 | tf_op jit(solution)/shard_map/ppermute | solution.py:110
  8.6 1.8 %collective-permute-start.3 = (bf16[880,128]{1,0:T(8,128)(2,1)S(1)}, bf16[880,128]{1,0:T(8,128)(2,1)S(1)}, u32[]{:S(2)}, u32[]{:S(2)}) collective-permute-start(bf16[880,128]{1,0:T(8,128)(2,1)S(1)} %pack_own_chunk.1), channel_id=1, source_target_pairs={{0,2},{1,5},{2,0},{3,7},{4,6},{5,1},{6,4},{7,3},{8,10},{9,13},{10,... | collective-permute-start | bytes 675848 | tf_op jit(solution)/shard_map/ppermute | solution.py:119
  10.4 1.5 %collective-permute-start.4 = (bf16[880,128]{1,0:T(8,128)(2,1)S(1)}, bf16[880,128]{1,0:T(8,128)(2,1)S(1)}, u32[]{:S(2)}, u32[]{:S(2)}) collective-permute-start(bf16[880,128]{1,0:T(8,128)(2,1)S(1)} %pack_own_chunk.1), channel_id=1, source_target_pairs={{0,4},{1,3},{2,6},{3,1},{4,0},{5,7},{6,2},{7,5},{8,12},{9,11},{10,... | collective-permute-start | bytes 675848 | tf_op jit(solution)/shard_map/ppermute | solution.py:119
  11.9 3.5 %collective-permute-done = bf16[880,128]{1,0:T(8,128)(2,1)S(1)} collective-permute-done((bf16[880,128]{1,0:T(8,128)(2,1)S(1)}, bf16[880,128]{1,0:T(8,128)(2,1)S(1)}, u32[]{:S(2)}, u32[]{:S(2)}) %collective-permute-start) | collective-permute-done | bytes 225312 | tf_op jit(solution)/shard_map/ppermute | solution.py:110
  15.4 2.9 %collective-permute-start.5 = (bf16[880,128]{1,0:T(8,128)(2,1)S(1)}, bf16[880,128]{1,0:T(8,128)(2,1)S(1)}, u32[]{:S(2)}, u32[]{:S(2)}) collective-permute-start(bf16[880,128]{1,0:T(8,128)(2,1)S(1)} %pack_own_chunk.1), channel_id=1, source_target_pairs={{0,6},{1,7},{2,4},{3,5},{4,2},{5,3},{6,0},{7,1},{8,14},{9,15},{10,... | collective-permute-start | bytes 675848 | tf_op jit(solution)/shard_map/ppermute | solution.py:119
  19.0 5.9 %collective-permute-done.1 = bf16[880,128]{1,0:T(8,128)(2,1)S(1)} collective-permute-done((bf16[880,128]{1,0:T(8,128)(2,1)S(1)}, bf16[880,128]{1,0:T(8,128)(2,1)S(1)}, u32[]{:S(2)}, u32[]{:S(2)}) %collective-permute-start.1) | collective-permute-done | bytes 225312 | tf_op jit(solution)/shard_map/ppermute | solution.py:110
  24.9 1.5 %collective-permute-start.8 = (bf16[880,128]{1,0:T(8,128)(2,1)S(1)}, bf16[880,128]{1,0:T(8,128)(2,1)S(1)}, u32[]{:S(2)}, u32[]{:S(2)}) collective-permute-start(bf16[880,128]{1,0:T(8,128)(2,1)S(1)} %collective-permute-done.2), channel_id=1, source_target_pairs={{0,2},{1,5},{2,0},{3,7},{4,6},{5,1},{6,4},{7,3},{8,10},{9,13},{10,... | collective-permute-start | bytes 675848 | tf_op jit(solution)/shard_map/ppermute | solution.py:119
  27.0 5.0 %collective-permute-done.8 = bf16[880,128]{1,0:T(8,128)(2,1)S(1)} collective-permute-done((bf16[880,128]{1,0:T(8,128)(2,1)S(1)}, bf16[880,128]{1,0:T(8,128)(2,1)S(1)}, u32[]{:S(2)}, u32[]{:S(2)}) %collective-permute-start.8) | collective-permute-done | bytes 225312 | tf_op jit(solution)/shard_map/ppermute | solution.py:119
  34.0 1.5 %collective-permute-start.6 = (bf16[880,128]{1,0:T(8,128)(2,1)S(1)}, bf16[880,128]{1,0:T(8,128)(2,1)S(1)}, u32[]{:S(2)}, u32[]{:S(2)}) collective-permute-start(bf16[880,128]{1,0:T(8,128)(2,1)S(1)} %collective-permute-done), channel_id=1, source_target_pairs={{0,2},{1,5},{2,0},{3,7},{4,6},{5,1},{6,4},{7,3},{8,10},{9,13},{10,... | collective-permute-start | bytes 675848 | tf_op jit(solution)/shard_map/ppermute | solution.py:119
  35.5 1.3 collective-permute-done.7
  36.9 1.3 collective-permute-start.10
  38.1 4.3 %collective-permute-done.6 = bf16[880,128]{1,0:T(8,128)(2,1)S(1)} collective-permute-done((bf16[880,128]{1,0:T(8,128)(2,1)S(1)}, bf16[880,128]{1,0:T(8,128)(2,1)S(1)}, u32[]{:S(2)}, u32[]{:S(2)}) %collective-permute-start.6) | collective-permute-done | bytes 225312 | tf_op jit(solution)/shard_map/ppermute | solution.py:119
  44.3 3.6 %collective-permute-done.10.refs_5_ = bf16[2,880,128]{2,1,0:T(8,128)(2,1)} collective-permute-done((bf16[2,880,128]{2,1,0:T(8,128)(2,1)S(1)}, bf16[2,880,128]{2,1,0:T(8,128)(2,1)}, u32[]{:S(2)}, u32[]{:S(2)}) %collective-permute-start.10) | collective-permute-done | bytes 450592 | tf_op jit(solution)/shard_map/ppermute | solution.py:119
  47.8 4.7 %collective-permute-done.9.refs_4_ = bf16[2,880,128]{2,1,0:T(8,128)(2,1)S(1)} collective-permute-done((bf16[2,880,128]{2,1,0:T(8,128)(2,1)S(1)}, bf16[2,880,128]{2,1,0:T(8,128)(2,1)S(1)}, u32[]{:S(2)}, u32[]{:S(2)}) %collective-permute-start.9) | collective-permute-done | bytes 450592 | tf_op jit(solution)/shard_map/ppermute | solution.py:119
  54.2 1.8 %collective-permute-done.16.refs_11_ = bf16[2,880,128]{2,1,0:T(8,128)(2,1)} collective-permute-done((bf16[2,880,128]{2,1,0:T(8,128)(2,1)S(1)}, bf16[2,880,128]{2,1,0:T(8,128)(2,1)}, u32[]{:S(2)}, u32[]{:S(2)}) %collective-permute-start.16) | collective-permute-done | bytes 450592 | tf_op jit(solution)/shard_map/ppermute | solution.py:114
  57.0 17.1 %forward_and_ff_backward.1 = (f32[256,576]{1,0:T(8,128)}, f32[256,576]{1,0:T(8,128)}, f32[1,576]{1,0:T(1,128)S(1)}, bf16[256,576]{1,0:T(8,128)(2,1)}, f32[6,384,...) custom-call(s32[4]{0:T(128)S(1)} %pad_add_fusion.idx, ...), custom_call_target="tpu_custom_call" | custom-call | flops 4529848320 | bytes 8000000 | tf_op jit(solution)/shard_map/forward_and_ff_backward/pallas_call | solution.py:915
  74.8 2.0 %collective-permute-done.21 = bf16[4,880,128]{2,1,0:T(8,128)(2,1)S(1)} collective-permute-done((bf16[4,880,128]{2,1,0:T(8,128)(2,1)}, bf16[4,880,128]{2,1,0:T(8,128)(2,1)S(1)}, u32[]{:S(2)}, u32[]{:S(2)}) %collective-permute-start.21) | collective-permute-done | bytes 901152 | tf_op jit(solution)/shard_map/ppermute | solution.py:114
  80.8 10.4 %attention_backward.1 = (bf16[576,256]{1,0:T(8,128)(2,1)}, f32[576,256]{1,0:T(8,128)}, bf16[4,880,128]{2,1,0:T(8,128)(2,1)}, bf16[4,880,128]{2,1,0:T(8,128)(2,1)}) custom-call(s32[4]{0:T(128)S(1)} %pad_add_fusion.idx, bf16[576,256]{1,0:T(8,128)(2,1)S(1)} %bitcast.73, f32[256,64]{1,0:T(8,128)S(1)} %get-tuple-element.53.refs_15_.refs_1_, ...), custom_call_target="tpu_custom_call" | custom-call | flops 849346560 | bytes 8000000 | tf_op jit(solution)/shard_map/attention_backward/pallas_call | solution.py:925
  91.4 1.4 add_convert_fusion.2
  92.8 1.4 collective-permute-done.24
  94.2 2.2 %broadcast_select_fusion.1 = (bf16[4,880,128]{2,1,0:T(8,128)(2,1)S(1)}, bf16[4,880,128]{2,1,0:T(8,128)(2,1)S(1)}) fusion(pred[]{:T(512)S(6)} %eq.12, bf16[4,880,128]{2,1,0:T(8,128)(2,1)} %collective-permute-done.24, bf16[4,880,128]{2,1,0:T(8,128)(2,1)S(1)} %copy-done.7, bf16[4,880,128]{2,1,0:T(8,128)(2,1)} %collective-permute-done.23, ...), kind=kLoop, calls=%fused_computation.10 | loop fusion | flops 4505600 | bytes 5406721 | tf_op jit(solution)/shard_map/jit(_where)/select_n | solution.py:936
  97.7 1.6 %collective-permute-start.29 = (bf16[880,128]{1,0:T(8,128)(2,1)S(1)}, bf16[880,128]{1,0:T(8,128)(2,1)S(1)}, u32[]{:S(2)}, u32[]{:S(2)}) collective-permute-start(bf16[880,128]{1,0:T(8,128)(2,1)S(1)} %slice_bitcast_fusion.1), channel_id=1, source_target_pairs={{0,2},{1,5},{2,0},{3,7},{4,6},{5,1},{6,4},{7,3},{8,10},{9,13},{10,... | collective-permute-start | bytes 675848 | tf_op jit(solution)/shard_map/ppermute | solution.py:119
  101.3 6.0 %collective-permute-done.25 = bf16[2,880,128]{2,1,0:T(8,128)(2,1)S(1)} collective-permute-done((bf16[2,880,128]{2,1,0:T(8,128)(2,1)S(1)}, bf16[2,880,128]{2,1,0:T(8,128)(2,1)S(1)}, u32[]{:S(2)}, u32[]{:S(2)}) %collective-permute-start.25) | collective-permute-done | bytes 450592 | tf_op jit(solution)/shard_map/ppermute | solution.py:119
  109.7 5.2 %collective-permute-done.27 = bf16[2,880,128]{2,1,0:T(8,128)(2,1)S(1)} collective-permute-done((bf16[2,880,128]{2,1,0:T(8,128)(2,1)S(1)}, bf16[2,880,128]{2,1,0:T(8,128)(2,1)S(1)}, u32[]{:S(2)}, u32[]{:S(2)}) %collective-permute-start.27) | collective-permute-done | bytes 450592 | tf_op jit(solution)/shard_map/ppermute | solution.py:119
  116.4 3.4 %collective-permute-start.30 = (bf16[880,128]{1,0:T(8,128)(2,1)S(1)}, bf16[880,128]{1,0:T(8,128)(2,1)S(1)}, u32[]{:S(2)}, u32[]{:S(2)}) collective-permute-start(bf16[880,128]{1,0:T(8,128)(2,1)S(1)} %get-tuple-element.105), channel_id=1, source_target_pairs={{0,8},{2,10},{4,12},{6,14},{8,0},{10,2},{12,4},{14,6},{16,24},{18,... | collective-permute-start | bytes 675848 | tf_op jit(solution)/shard_map/ppermute | solution.py:110
  119.8 2.1 %collective-permute-start.31 = (bf16[880,128]{1,0:T(8,128)(2,1)S(1)}, bf16[880,128]{1,0:T(8,128)(2,1)S(1)}, u32[]{:S(2)}, u32[]{:S(2)}) collective-permute-start(bf16[880,128]{1,0:T(8,128)(2,1)S(1)} %get-tuple-element.104), channel_id=1, source_target_pairs={{0,16},{2,18},{4,20},{6,22},{8,24},{10,26},{12,28},{14,30},{16,0},... | collective-permute-start | bytes 675848 | tf_op jit(solution)/shard_map/ppermute | solution.py:110
  121.9 1.4 collective-permute-start.32
  123.3 7.7 %collective-permute-done.30 = bf16[880,128]{1,0:T(8,128)(2,1)S(1)} collective-permute-done((bf16[880,128]{1,0:T(8,128)(2,1)S(1)}, bf16[880,128]{1,0:T(8,128)(2,1)S(1)}, u32[]{:S(2)}, u32[]{:S(2)}) %collective-permute-start.30) | collective-permute-done | bytes 225312 | tf_op jit(solution)/shard_map/ppermute | solution.py:110
  131.0 8.1 %collective-permute-done.32 = bf16[880,128]{1,0:T(8,128)(2,1)S(1)} collective-permute-done((bf16[880,128]{1,0:T(8,128)(2,1)S(1)}, bf16[880,128]{1,0:T(8,128)(2,1)S(1)}, u32[]{:S(2)}, u32[]{:S(2)}) %collective-permute-start.32) | collective-permute-done | bytes 225312 | tf_op jit(solution)/shard_map/ppermute | solution.py:110
  139.3 1.8 %collective-permute-done.34.twin = f32[880,128]{1,0:T(8,128)S(1)} collective-permute-done((f32[880,128]{1,0:T(8,128)S(1)}, f32[880,128]{1,0:T(8,128)S(1)}, u32[]{:S(2)}, u32[]{:S(2)}) %collective-permute-start.34) | collective-permute-done | bytes 450592 | tf_op jit(solution)/shard_map/ppermute | solution.py:114
  141.1 2.2 %unpack_own_chunk.1 = f32[1736,128]{1,0:T(8,128)} custom-call(s32[4]{0:T(128)S(1)} %pad_add_fusion.1.idx, f32[880,128]{1,0:T(8,128)S(1)} %fusion.4.own, f32[880,128]{1,0:T(8,128)S(1)} %collective-permute-done.34.twin), custom_call_target="tpu_custom_call" | custom-call | tf_op jit(solution)/shard_map/unpack_own_chunk/pallas_call | solution.py:723
  (103 shorter events, 23.0 us)
Async XLA Ops:
  3.0 12.5 %collective-permute-start = (bf16[880,128]{1,0:T(8,128)(2,1)S(1)}, bf16[880,128]{1,0:T(8,128)(2,1)S(1)}, u32[]{:S(2)}, u32[]{:S(2)}) collective-permute-start(bf16[880,128]{1,0:T(8,128)(2,1)S(1)} %pack_own_chunk.1), channel_id=1, source_target_pairs={{0,8},{2,10},{4,12},{6,14},{8,0},{10,2},{12,4},{14,6},{16,24},{18,... | collective-permute-start | bytes 675848 | tf_op jit(solution)/shard_map/ppermute | solution.py:110
  5.9 19.0 %collective-permute-start.1 = (bf16[880,128]{1,0:T(8,128)(2,1)S(1)}, bf16[880,128]{1,0:T(8,128)(2,1)S(1)}, u32[]{:S(2)}, u32[]{:S(2)}) collective-permute-start(bf16[880,128]{1,0:T(8,128)(2,1)S(1)} %pack_own_chunk.1), channel_id=1, source_target_pairs={{0,16},{2,18},{4,20},{6,22},{8,24},{10,26},{12,28},{14,30},{16,0},... | collective-permute-start | bytes 675848 | tf_op jit(solution)/shard_map/ppermute | solution.py:110
  8.6 16.3 %collective-permute-start.2 = (bf16[880,128]{1,0:T(8,128)(2,1)S(1)}, bf16[880,128]{1,0:T(8,128)(2,1)S(1)}, u32[]{:S(2)}, u32[]{:S(2)}) collective-permute-start(bf16[880,128]{1,0:T(8,128)(2,1)S(1)} %pack_own_chunk.1), channel_id=1, source_target_pairs={{0,24},{2,26},{4,28},{6,30},{8,16},{10,18},{12,20},{14,22},{16,8},... | collective-permute-start | bytes 675848 | tf_op jit(solution)/shard_map/ppermute | solution.py:110
  8.6 16.3 %collective-permute-start.3 = (bf16[880,128]{1,0:T(8,128)(2,1)S(1)}, bf16[880,128]{1,0:T(8,128)(2,1)S(1)}, u32[]{:S(2)}, u32[]{:S(2)}) collective-permute-start(bf16[880,128]{1,0:T(8,128)(2,1)S(1)} %pack_own_chunk.1), channel_id=1, source_target_pairs={{0,2},{1,5},{2,0},{3,7},{4,6},{5,1},{6,4},{7,3},{8,10},{9,13},{10,... | collective-permute-start | bytes 675848 | tf_op jit(solution)/shard_map/ppermute | solution.py:119
  10.4 14.5 %collective-permute-start.4 = (bf16[880,128]{1,0:T(8,128)(2,1)S(1)}, bf16[880,128]{1,0:T(8,128)(2,1)S(1)}, u32[]{:S(2)}, u32[]{:S(2)}) collective-permute-start(bf16[880,128]{1,0:T(8,128)(2,1)S(1)} %pack_own_chunk.1), channel_id=1, source_target_pairs={{0,4},{1,3},{2,6},{3,1},{4,0},{5,7},{6,2},{7,5},{8,12},{9,11},{10,... | collective-permute-start | bytes 675848 | tf_op jit(solution)/shard_map/ppermute | solution.py:119
  15.4 9.4 %collective-permute-start.5 = (bf16[880,128]{1,0:T(8,128)(2,1)S(1)}, bf16[880,128]{1,0:T(8,128)(2,1)S(1)}, u32[]{:S(2)}, u32[]{:S(2)}) collective-permute-start(bf16[880,128]{1,0:T(8,128)(2,1)S(1)} %pack_own_chunk.1), channel_id=1, source_target_pairs={{0,6},{1,7},{2,4},{3,5},{4,2},{5,3},{6,0},{7,1},{8,14},{9,15},{10,... | collective-permute-start | bytes 675848 | tf_op jit(solution)/shard_map/ppermute | solution.py:119
  24.9 7.1 %collective-permute-start.8 = (bf16[880,128]{1,0:T(8,128)(2,1)S(1)}, bf16[880,128]{1,0:T(8,128)(2,1)S(1)}, u32[]{:S(2)}, u32[]{:S(2)}) collective-permute-start(bf16[880,128]{1,0:T(8,128)(2,1)S(1)} %collective-permute-done.2), channel_id=1, source_target_pairs={{0,2},{1,5},{2,0},{3,7},{4,6},{5,1},{6,4},{7,3},{8,10},{9,13},{10,... | collective-permute-start | bytes 675848 | tf_op jit(solution)/shard_map/ppermute | solution.py:119
  26.4 10.4 %collective-permute-start.7 = (bf16[880,128]{1,0:T(8,128)(2,1)S(1)}, bf16[880,128]{1,0:T(8,128)(2,1)S(1)}, u32[]{:S(2)}, u32[]{:S(2)}) collective-permute-start(bf16[880,128]{1,0:T(8,128)(2,1)S(1)} %collective-permute-done.1), channel_id=1, source_target_pairs={{0,2},{1,5},{2,0},{3,7},{4,6},{5,1},{6,4},{7,3},{8,10},{9,13},{10,... | collective-permute-start | bytes 675848 | tf_op jit(solution)/shard_map/ppermute | solution.py:119
  32.0 11.0 %collective-permute-start.11 = (bf16[2,880,128]{2,1,0:T(8,128)(2,1)S(1)}, bf16[2,880,128]{2,1,0:T(8,128)(2,1)}, u32[]{:S(2)}, u32[]{:S(2)}) collective-permute-start(bf16[2,880,128]{2,1,0:T(8,128)(2,1)S(1)} %pad_maximum_fusion.3.refs_3_), channel_id=1, source_target_pairs={{0,4},{1,3},{2,6},{3,1},{4,0},{5,7},{6,2},{7,5},{8,12},{9,11},{10,... | collective-permute-start | bytes 1351688 | tf_op jit(solution)/shard_map/ppermute | solution.py:119
  33.3 9.8 %collective-permute-start.15 = (bf16[2,880,128]{2,1,0:T(8,128)(2,1)S(1)}, bf16[2,880,128]{2,1,0:T(8,128)(2,1)S(1)}, u32[]{:S(2)}, u32[]{:S(2)}) collective-permute-start(bf16[2,880,128]{2,1,0:T(8,128)(2,1)S(1)} %pad_maximum_fusion.3.refs_3_), channel_id=1, source_target_pairs={{0,1},{1,0},{2,3},{3,2},{4,5},{5,4},{6,7},{7,6},{8,9},{9,8},{10,11... | collective-permute-start | bytes 1351688 | tf_op jit(solution)/shard_map/ppermute | solution.py:114
  33.4 19.1 %collective-permute-start.12 = (bf16[4,880,128]{2,1,0:T(8,128)(2,1)S(1)}, bf16[4,880,128]{2,1,0:T(8,128)(2,1)S(1)}, u32[]{:S(2)}, u32[]{:S(2)}) collective-permute-start(bf16[4,880,128]{2,1,0:T(8,128)(2,1)S(1)} %pad_maximum_fusion.refs_0_), channel_id=1, source_target_pairs={{0,1},{1,0},{2,3},{3,2},{4,5},{5,4},{6,7},{7,6},{8,9},{9,8},{10,11... | collective-permute-start | bytes 2703368 | tf_op jit(solution)/shard_map/ppermute | solution.py:114
  34.0 8.5 %collective-permute-start.6 = (bf16[880,128]{1,0:T(8,128)(2,1)S(1)}, bf16[880,128]{1,0:T(8,128)(2,1)S(1)}, u32[]{:S(2)}, u32[]{:S(2)}) collective-permute-start(bf16[880,128]{1,0:T(8,128)(2,1)S(1)} %collective-permute-done), channel_id=1, source_target_pairs={{0,2},{1,5},{2,0},{3,7},{4,6},{5,1},{6,4},{7,3},{8,10},{9,13},{10,... | collective-permute-start | bytes 675848 | tf_op jit(solution)/shard_map/ppermute | solution.py:119
  36.9 11.0 %collective-permute-start.10 = (bf16[2,880,128]{2,1,0:T(8,128)(2,1)S(1)}, bf16[2,880,128]{2,1,0:T(8,128)(2,1)}, u32[]{:S(2)}, u32[]{:S(2)}) collective-permute-start(bf16[2,880,128]{2,1,0:T(8,128)(2,1)S(1)} %pad_maximum_fusion.2.refs_2_), channel_id=1, source_target_pairs={{0,4},{1,3},{2,6},{3,1},{4,0},{5,7},{6,2},{7,5},{8,12},{9,11},{10,... | collective-permute-start | bytes 1351688 | tf_op jit(solution)/shard_map/ppermute | solution.py:119
  42.5 5.4 %collective-permute-start.14 = (bf16[2,880,128]{2,1,0:T(8,128)(2,1)S(1)}, bf16[2,880,128]{2,1,0:T(8,128)(2,1)S(1)}, u32[]{:S(2)}, u32[]{:S(2)}) collective-permute-start(bf16[2,880,128]{2,1,0:T(8,128)(2,1)S(1)} %pad_maximum_fusion.2.refs_2_), channel_id=1, source_target_pairs={{0,1},{1,0},{2,3},{3,2},{4,5},{5,4},{6,7},{7,6},{8,9},{9,8},{10,11... | collective-permute-start | bytes 1351688 | tf_op jit(solution)/shard_map/ppermute | solution.py:114
  43.0 4.8 %collective-permute-start.13 = (bf16[2,880,128]{2,1,0:T(8,128)(2,1)S(1)}, bf16[2,880,128]{2,1,0:T(8,128)(2,1)S(1)}, u32[]{:S(2)}, u32[]{:S(2)}) collective-permute-start(bf16[2,880,128]{2,1,0:T(8,128)(2,1)S(1)} %pad_maximum_fusion.1.refs_1_), channel_id=1, source_target_pairs={{0,1},{1,0},{2,3},{3,2},{4,5},{5,4},{6,7},{7,6},{8,9},{9,8},{10,11... | collective-permute-start | bytes 1351688 | tf_op jit(solution)/shard_map/ppermute | solution.py:114
  43.1 9.4 %collective-permute-start.9 = (bf16[2,880,128]{2,1,0:T(8,128)(2,1)S(1)}, bf16[2,880,128]{2,1,0:T(8,128)(2,1)S(1)}, u32[]{:S(2)}, u32[]{:S(2)}) collective-permute-start(bf16[2,880,128]{2,1,0:T(8,128)(2,1)S(1)} %pad_maximum_fusion.1.refs_1_), channel_id=1, source_target_pairs={{0,4},{1,3},{2,6},{3,1},{4,0},{5,7},{6,2},{7,5},{8,12},{9,11},{10,... | collective-permute-start | bytes 1351688 | tf_op jit(solution)/shard_map/ppermute | solution.py:119
  53.5 2.8 %collective-permute-start.17 = (bf16[2,880,128]{2,1,0:T(8,128)(2,1)}, bf16[2,880,128]{2,1,0:T(8,128)(2,1)}, u32[]{:S(2)}, u32[]{:S(2)}) collective-permute-start(bf16[2,880,128]{2,1,0:T(8,128)(2,1)} %collective-permute-done.10.refs_5_), channel_id=1, source_target_pairs={{0,1},{1,0},{2,3},{3,2},{4,5},{5,4},{6,7},{7,6},{8,9},{9,8},{10,11... | collective-permute-start | bytes 1351688 | tf_op jit(solution)/shard_map/ppermute | solution.py:114
  54.0 2.9 %collective-permute-start.18 = (bf16[2,880,128]{2,1,0:T(8,128)(2,1)}, bf16[2,880,128]{2,1,0:T(8,128)(2,1)}, u32[]{:S(2)}, u32[]{:S(2)}) collective-permute-start(bf16[2,880,128]{2,1,0:T(8,128)(2,1)} %collective-permute-done.11.refs_6_), channel_id=1, source_target_pairs={{0,1},{1,0},{2,3},{3,2},{4,5},{5,4},{6,7},{7,6},{8,9},{9,8},{10,11... | collective-permute-start | bytes 1351688 | tf_op jit(solution)/shard_map/ppermute | solution.py:114
  74.3 5.1 %collective-permute-start.19 = (bf16[4,880,128]{2,1,0:T(8,128)(2,1)}, bf16[4,880,128]{2,1,0:T(8,128)(2,1)S(1)}, u32[]{:S(2)}, u32[]{:S(2)}) collective-permute-start(bf16[4,880,128]{2,1,0:T(8,128)(2,1)} %get-tuple-element.84), channel_id=1, source_target_pairs={{0,1},{1,0},{2,3},{3,2},{4,5},{5,4},{6,7},{7,6},{8,9},{9,8},{10,11... | collective-permute-start | bytes 2703368 | tf_op jit(solution)/shard_map/ppermute | solution.py:114
  74.7 16.5 %collective-permute-start.23 = (bf16[4,880,128]{2,1,0:T(8,128)(2,1)}, bf16[4,880,128]{2,1,0:T(8,128)(2,1)}, u32[]{:S(2)}, u32[]{:S(2)}) collective-permute-start(bf16[4,880,128]{2,1,0:T(8,128)(2,1)} %get-tuple-element.89), channel_id=1, source_target_pairs={{0,1},{1,0},{2,3},{3,2},{4,5},{5,4},{6,7},{7,6},{8,9},{9,8},{10,11... | collective-permute-start | bytes 2703368 | tf_op jit(solution)/shard_map/ppermute | solution.py:114
  78.0 13.2 %collective-permute-start.22 = (bf16[2,880,128]{2,1,0:T(8,128)(2,1)S(1)}, bf16[2,880,128]{2,1,0:T(8,128)(2,1)}, u32[]{:S(2)}, u32[]{:S(2)}) collective-permute-start(bf16[2,880,128]{2,1,0:T(8,128)(2,1)S(1)} %add_convert_fusion.6), channel_id=1, source_target_pairs={{0,4},{1,3},{2,6},{3,1},{4,0},{5,7},{6,2},{7,5},{8,12},{9,11},{10,... | collective-permute-start | bytes 1351688 | tf_op jit(solution)/shard_map/ppermute | solution.py:119
  79.5 11.9 %collective-permute-start.20 = (bf16[2,880,128]{2,1,0:T(8,128)(2,1)S(1)}, bf16[2,880,128]{2,1,0:T(8,128)(2,1)}, u32[]{:S(2)}, u32[]{:S(2)}) collective-permute-start(bf16[2,880,128]{2,1,0:T(8,128)(2,1)S(1)} %add_convert_fusion.7), channel_id=1, source_target_pairs={{0,4},{1,3},{2,6},{3,1},{4,0},{5,7},{6,2},{7,5},{8,12},{9,11},{10,... | collective-permute-start | bytes 1351688 | tf_op jit(solution)/shard_map/ppermute | solution.py:119
  91.4 2.8 %collective-permute-start.24 = (bf16[4,880,128]{2,1,0:T(8,128)(2,1)}, bf16[4,880,128]{2,1,0:T(8,128)(2,1)}, u32[]{:S(2)}, u32[]{:S(2)}) collective-permute-start(bf16[4,880,128]{2,1,0:T(8,128)(2,1)} %get-tuple-element.91), channel_id=1, source_target_pairs={{0,1},{1,0},{2,3},{3,2},{4,5},{5,4},{6,7},{7,6},{8,9},{9,8},{10,11... | collective-permute-start | bytes 2703368 | tf_op jit(solution)/shard_map/ppermute | solution.py:114
  96.5 10.9 %collective-permute-start.25 = (bf16[2,880,128]{2,1,0:T(8,128)(2,1)S(1)}, bf16[2,880,128]{2,1,0:T(8,128)(2,1)S(1)}, u32[]{:S(2)}, u32[]{:S(2)}) collective-permute-start(bf16[2,880,128]{2,1,0:T(8,128)(2,1)S(1)} %slice.100), channel_id=1, source_target_pairs={{0,4},{1,3},{2,6},{3,1},{4,0},{5,7},{6,2},{7,5},{8,12},{9,11},{10,... | collective-permute-start | bytes 1351688 | tf_op jit(solution)/shard_map/ppermute | solution.py:119
  97.7 17.9 %collective-permute-start.29 = (bf16[880,128]{1,0:T(8,128)(2,1)S(1)}, bf16[880,128]{1,0:T(8,128)(2,1)S(1)}, u32[]{:S(2)}, u32[]{:S(2)}) collective-permute-start(bf16[880,128]{1,0:T(8,128)(2,1)S(1)} %slice_bitcast_fusion.1), channel_id=1, source_target_pairs={{0,2},{1,5},{2,0},{3,7},{4,6},{5,1},{6,4},{7,3},{8,10},{9,13},{10,... | collective-permute-start | bytes 675848 | tf_op jit(solution)/shard_map/ppermute | solution.py:119
  100.6 14.3 %collective-permute-start.27 = (bf16[2,880,128]{2,1,0:T(8,128)(2,1)S(1)}, bf16[2,880,128]{2,1,0:T(8,128)(2,1)S(1)}, u32[]{:S(2)}, u32[]{:S(2)}) collective-permute-start(bf16[2,880,128]{2,1,0:T(8,128)(2,1)S(1)} %slice.102), channel_id=1, source_target_pairs={{0,4},{1,3},{2,6},{3,1},{4,0},{5,7},{6,2},{7,5},{8,12},{9,11},{10,... | collective-permute-start | bytes 1351688 | tf_op jit(solution)/shard_map/ppermute | solution.py:119
  107.5 7.4 %collective-permute-start.26 = (bf16[880,128]{1,0:T(8,128)(2,1)S(1)}, bf16[880,128]{1,0:T(8,128)(2,1)S(1)}, u32[]{:S(2)}, u32[]{:S(2)}) collective-permute-start(bf16[880,128]{1,0:T(8,128)(2,1)S(1)} %slice_bitcast_fusion.7), channel_id=1, source_target_pairs={{0,2},{1,5},{2,0},{3,7},{4,6},{5,1},{6,4},{7,3},{8,10},{9,13},{10,... | collective-permute-start | bytes 675848 | tf_op jit(solution)/shard_map/ppermute | solution.py:119
  108.6 7.6 %collective-permute-start.28 = (bf16[880,128]{1,0:T(8,128)(2,1)S(1)}, bf16[880,128]{1,0:T(8,128)(2,1)S(1)}, u32[]{:S(2)}, u32[]{:S(2)}) collective-permute-start(bf16[880,128]{1,0:T(8,128)(2,1)S(1)} %slice_bitcast_fusion.4), channel_id=1, source_target_pairs={{0,2},{1,5},{2,0},{3,7},{4,6},{5,1},{6,4},{7,3},{8,10},{9,13},{10,... | collective-permute-start | bytes 675848 | tf_op jit(solution)/shard_map/ppermute | solution.py:119
  115.0 8.3 %collective-permute-start.33 = (bf16[880,128]{1,0:T(8,128)(2,1)S(1)}, bf16[880,128]{1,0:T(8,128)(2,1)S(1)}, u32[]{:S(2)}, u32[]{:S(2)}) collective-permute-start(bf16[880,128]{1,0:T(8,128)(2,1)S(1)} %slice_bitcast_fusion), channel_id=1, source_target_pairs={{0,2},{1,5},{2,0},{3,7},{4,6},{5,1},{6,4},{7,3},{8,10},{9,13},{10,... | collective-permute-start | bytes 675848 | tf_op jit(solution)/shard_map/ppermute | solution.py:119
  116.4 14.5 %collective-permute-start.30 = (bf16[880,128]{1,0:T(8,128)(2,1)S(1)}, bf16[880,128]{1,0:T(8,128)(2,1)S(1)}, u32[]{:S(2)}, u32[]{:S(2)}) collective-permute-start(bf16[880,128]{1,0:T(8,128)(2,1)S(1)} %get-tuple-element.105), channel_id=1, source_target_pairs={{0,8},{2,10},{4,12},{6,14},{8,0},{10,2},{12,4},{14,6},{16,24},{18,... | collective-permute-start | bytes 675848 | tf_op jit(solution)/shard_map/ppermute | solution.py:110
  119.8 11.2 %collective-permute-start.31 = (bf16[880,128]{1,0:T(8,128)(2,1)S(1)}, bf16[880,128]{1,0:T(8,128)(2,1)S(1)}, u32[]{:S(2)}, u32[]{:S(2)}) collective-permute-start(bf16[880,128]{1,0:T(8,128)(2,1)S(1)} %get-tuple-element.104), channel_id=1, source_target_pairs={{0,16},{2,18},{4,20},{6,22},{8,24},{10,26},{12,28},{14,30},{16,0},... | collective-permute-start | bytes 675848 | tf_op jit(solution)/shard_map/ppermute | solution.py:110
  121.9 17.2 %collective-permute-start.32 = (bf16[880,128]{1,0:T(8,128)(2,1)S(1)}, bf16[880,128]{1,0:T(8,128)(2,1)S(1)}, u32[]{:S(2)}, u32[]{:S(2)}) collective-permute-start(bf16[880,128]{1,0:T(8,128)(2,1)S(1)} %get-tuple-element.106), channel_id=1, source_target_pairs={{0,24},{2,26},{4,28},{6,30},{8,16},{10,18},{12,20},{14,22},{16,8},... | collective-permute-start | bytes 675848 | tf_op jit(solution)/shard_map/ppermute | solution.py:110
  (20 other events, 174.4 us)

commit v4 on v3

--- a/solution.py
+++ b/solution.py
@@ -153,8 +153,10 @@
     near = [jnp.stack([value, hop(value, first, n)], 0) for value in across]
     far = [hop(value, second, n) for value in near]
     early = [own] + near
-    far, twins = lax.optimization_barrier((far, [swap_rep(value) for value in early]))
-    return early + far + twins + [swap_rep(value) for value in far], beside
+    far[0], twins = lax.optimization_barrier(
+        (far[0], [swap_rep(value) for value in early + far[1:]])
+    )
+    return early + far + twins[:4] + [swap_rep(far[0])] + twins[4:], beside
 
 
 def pair_sum(keep, send):
@@ -313,11 +315,9 @@
         for d in range(4):
             turned = ((d & 1) << 1) | (d >> 1)
             chunk = 4 * at_plane + jnp.bitwise_xor(place, jnp.where(side * flip == 1, turned, d))
-            if len(refs) == 1:
-                parts = [(refs[0].at[d, pl.ds(at, size), :], at, size) for at, size in ((0, MAIN), (MAIN, REST))]
-            else:
-                parts = [(refs[d // 2].at[d % 2], 0, HALF)]
-            for outer, start, rows in parts:
+            ref = refs[0].at[d] if len(refs) == 1 else refs[d // 2].at[d % 2]
+            for start, rows in ((0, MAIN), (MAIN, REST)) if outward else ((0, HALF),):
+                outer = ref.at[pl.ds(start, rows), :]
                 at = pl.multiple_of(side * HALF + start, 16)
                 inner = dst.at[chunk, pl.ds(at, rows), :]
                 pair = (inner, outer) if outward else (outer, inner)
@@ -340,13 +340,14 @@
     pieces = list(zip(refs[:7], refs[7:14]))
     tok_hbm, cos, sin, cot_hbm = refs[14:18]
     refs = refs[18:]
-    results, outs = refs[:13], refs[13:19]
-    y_acc, dr_out, dg_out, att_out, p_out, q_out, k_out, v_out, wq, wk, wv, wo, gain_out = refs[19:32]
-    w, g, tok, cot_t, cot, att, n2_ref, n2t_ref, dn_acc, first, second = refs[32:43]
-    in_sem, sems, out_sems, result_sems = refs[43:]
+    results, outs = refs[:13], refs[13:23]
+    refs = refs[23:]
+    y_acc, dr_out, dg_out, att_out, p_out, q_out, k_out, v_out, wq, wk, wv, wo, gain_out = refs[:13]
+    w, g, tok, cot_t, cot, att, n2_ref, n2t_ref, dn_acc, first, second = refs[13:24]
+    in_sem, sems, out_sems, result_sems = refs[24:]
     saves = [
         pltpu.make_async_copy(src, dst, result_sems.at[i])
-        for i, (src, dst) in enumerate(zip(refs[19:32], results))
+        for i, (src, dst) in enumerate(zip(refs[:13], results))
     ]
     load = pltpu.make_async_copy(tok_hbm, tok, in_sem.at[0])
     load.start()
@@ -368,8 +369,6 @@
     wait_plane(w, 0, sems.at[0])
     for c in range(3):
         add_tail(w, c, False)
-    wait_plane(w, 4, sems.at[1])
-    add_tail(w, 3, False)
     gains = w[0, ROWS : ROWS + 16, :].astype(F32)
     gain_in, gain_mid = row_of_head(gains, 0), row_of_head(gains, 1)
     gain_out[...] = gain_in
@@ -381,7 +380,6 @@
     mixed_chunk = load_narrow(w, 2)
     spread(mixed_chunk[:192], first, second, wv)
     wo[:192, :] = mixed_chunk[192:]
-    wo[192:, :] = load_narrow(w, 3)
 
     query, keys, values = dot(n1, wq[...]), dot(n1, wk[...]), dot(n1, wv[...])
     row = lax.broadcasted_iota(jnp.int32, (3 * SEQ_LEN, SEQ_LEN), 0)
@@ -411,6 +409,9 @@
                 att[part, HEAD * h : HEAD * (h + 1)] = mix[SEQ_LEN * r : SEQ_LEN * (r + 1)]
     attended = att[...].astype(BF16)
     att_out[...] = attended
+    wait_plane(w, 4, sems.at[1])
+    add_tail(w, 3, False)
+    wo[192:, :] = load_narrow(w, 3)
     for copy in saves[3:]:
         copy.start()
     mixed = x + dot(attended, wo[...])
@@ -466,7 +467,9 @@
     lax.fori_loop(0, 2, block, 0)
     stores = []
     for slot in range(3):
-        sides = [[ref] for ref in outs[2 * slot : 2 * slot + 2]]
+        sides = [outs[4 * slot : 4 * slot + 2], outs[4 * slot + 2 : 4 * slot + 4]]
+        if slot == 2:
+            sides = [outs[8:9], outs[9:10]]
         at_plane = slot_plane(idx[0], slot) - 1
         stores = stores + piece_copies(idx, at_plane, sides, g, out_sems.at[slot], True)
     for last, copy in stores:
@@ -500,18 +503,16 @@
 
 
 def second_kernel(idx, *refs):
-    y_out, dx_out, keep, send = refs[16:20]
-    tok, cos, sin, y_in, dr, dg, att, p_in, q_in, k_in, v_in, wq, wk, wv, wo, gain = refs[20:36]
-    g, y_t, dx_t, dq_ref, dk_ref, dv_ref, first, second, in_sem, out_sems = refs[36:]
-    loads = [
-        pltpu.make_async_copy(src, dst, in_sem.at[i])
-        for i, (src, dst) in enumerate(zip(refs[:16], refs[20:36]))
+    tok, cos, sin, y_in, dr, dg, att, p_in, q_in, k_in, v_in, wq, wk, wv, wo, gain = refs[:16]
+    held, (y_out, dx_out), third, mine = refs[16:18], refs[18:20], refs[20:24], refs[24:26]
+    g, bounce, y_t, dx_t, dq_ref, dk_ref, dv_ref, first, second, in_sem, out_sems, held_sem = refs[26:]
+    tokens = tok.shape[1]
+    ground = idx[0] == 0
+    fetch = [
+        pltpu.make_async_copy(held[side], bounce.at[side], held_sem.at[side]) for side in range(2)
     ]
-    for copy in loads:
+    for copy in fetch:
         copy.start()
-    tokens = tok.shape[1]
-    for copy in loads:
-        copy.wait()
     d_mixed = dr[...]
     branch = d_mixed.astype(BF16)
     dw_out = dot_tn(att[...], branch)
@@ -538,6 +539,21 @@
                 dot_tn(d_score, q3) * HEAD**-0.5, cosine, sine
             )
     dq, dk, dv = dq_ref[...].astype(BF16), dk_ref[...].astype(BF16), dv_ref[...].astype(BF16)
+    for copy in fetch:
+        copy.wait()
+
+    @pl.when(ground)
+    def _():
+        for side in range(2):
+            for j in range(2):
+                source = bounce.at[side, pl.ds(2 * j, 2)]
+                pltpu.make_async_copy(source, third[2 * side + j], held_sem.at[2]).start()
+
+    @pl.when(jnp.logical_not(ground))
+    def _():
+        for side in range(2):
+            pltpu.make_async_copy(bounce.at[side], mine[side], held_sem.at[2]).start()
+
     x = tok[...].astype(F32)
     inverse = lax.rsqrt(jnp.mean(x * x, 0, keepdims=True) + EPS)
     normed = x * inverse
@@ -557,8 +573,17 @@
         top = tail_of(g, c - 1, False) if c else head_of_rows([d_gain, dg[...]])
         g[c, ROWS : ROWS + 16, :] = top.astype(BF16)
         g[c, ROWS + 16 :, :] = gain_rows(dg[...], jnp.zeros((16, 128), F32)).astype(BF16)
-    for _, copy in piece_copies(idx, 0, [[keep], [send]], g, out_sems.at[0], True):
-        copy.start()
+
+    @pl.when(ground)
+    def _():
+        for _, copy in piece_copies(idx, 0, [mine[:1], mine[1:]], g, out_sems.at[0], True):
+            copy.start()
+
+    @pl.when(jnp.logical_not(ground))
+    def _():
+        for _, copy in piece_copies(idx, 0, [third[:2], third[2:]], g, out_sems.at[0], True):
+            copy.start()
+
     scaled = d_norm * gain_column
     dx_t[...] = d_mixed.T + inverse * (
         scaled - normed * jnp.mean(scaled * normed, 0, keepdims=True)
@@ -573,6 +598,7 @@
     for copy in stores:
         copy.wait()
     wait_plane(g, 0, out_sems.at[0])
+    wait_plane(g, 0, held_sem.at[2])
 
 
 def halves_turned(low, high):
@@ -756,7 +782,7 @@
     def cost(flops):
         return pl.CostEstimate(flops=flops, bytes_accessed=8_000_000, transcendentals=600_000)
 
-    piece = [sds((4, HALF, 128), BF16)]
+    piece, block = sds((4, HALF, 128), BF16), sds((2, HALF, 128), BF16)
     weights = [sds((width, width), BF16), sds((width, kv_width), BF16)]
     weights = weights + [weights[1], weights[0]]
     saved = [
@@ -773,8 +799,8 @@
         first_kernel,
         name="forward_and_ff_backward",
         in_specs=[smem] + [anywhere] * 14 + [hbm, vmem, vmem, hbm],
-        out_specs=[hbm] * len(outs) + [anywhere] * 6,
-        out_shape=outs + piece * 6,
+        out_specs=[hbm] * len(outs) + [anywhere] * 10,
+        out_shape=outs + [block] * 8 + [piece] * 2,
         scratch_shapes=[pltpu.VMEM(out.shape, out.dtype) for out in outs]
         + [
             pltpu.VMEM((CANON, 2 * HALF, 128), BF16),
@@ -799,17 +825,12 @@
     attention_back = pl.pallas_call(
         second_kernel,
         name="attention_backward",
-        in_specs=[smem] + [hbm] * 16,
-        out_specs=[hbm] * 2 + [anywhere] * 2,
-        out_shape=[sds((width, length), BF16), sds((width, length), F32)] + piece * 2,
+        in_specs=[smem] + [vmem] * 16 + [anywhere] * 2,
+        out_specs=[hbm] * 2 + [anywhere] * 6,
+        out_shape=[sds((width, length), BF16), sds((width, length), F32)] + [block] * 4 + [piece] * 2,
         scratch_shapes=[
-            pltpu.VMEM((width, length), BF16),
-            pltpu.VMEM((length, HEAD), F32),
-            pltpu.VMEM((length, HEAD), F32),
-        ]
-        + [pltpu.VMEM(out.shape, out.dtype) for out in outs]
-        + [
             pltpu.VMEM((4, 2 * HALF, 128), BF16),
+            pltpu.VMEM((2, 4, HALF, 128), BF16),
             pltpu.VMEM((width, length), BF16),
             pltpu.VMEM((width, length), F32),
             pltpu.VMEM((length, width), F32),
@@ -817,8 +838,9 @@
             pltpu.VMEM((length, kv_width), F32),
             pltpu.VMEM((width, 128), F32),
             pltpu.VMEM((width, 128), F32),
-            pltpu.SemaphoreType.DMA((16,)),
+            pltpu.SemaphoreType.DMA((2,)),
             pltpu.SemaphoreType.DMA((1,)),
+            pltpu.SemaphoreType.DMA((3,)),
         ],
         compiler_params=params,
         cost_estimate=cost(10 * length * width * width),
@@ -914,30 +936,22 @@
         pieces = canonical(blocks, twins, lay, canon, index, core)
     results = forward(idx, *pieces, tokens_in.T, *angles, cotangent.T)
     d_gain = results[2]
-    slots = [results[13 + 2 * p : 15 + 2 * p] for p in range(3)]
+    saved, slots, held = results[:13], (results[13:17], results[17:21]), results[21:23]
     if same:
         (first,), (second,) = firsts, seconds
-        keeps, twins = [slot[0] for slot in slots], [swap_rep(slot[1]) for slot in slots]
-        moved = [
-            hop(add(keep[2:], twin[2:]).astype(BF16), second, n)
-            for keep, twin in zip(keeps[:2], twins[:2])
-        ]
-    output, d_input, *slot = attention_back(idx, tokens_in.T, *angles, *results[:13])
+        moved = [hop(add(far, swap_rep(send)).astype(BF16), second, n) for _, far, _, send in slots]
+        near = [add(keep, swap_rep(send)) for keep, _, send, _ in slots]
+    output, d_input, *results = attention_back(idx, tokens_in.T, *angles, *saved, *held)
     output, d_input = output.T, d_input.T
+    keep_near, keep_far, send_near, send_far, keep, send = results
     if same:
-        moved, slot, twins[2] = lax.optimization_barrier((moved, slot, twins[2]))
-        early = [
-            (add(keeps[j][:2], twins[j][:2]) + moved[j].astype(F32)).astype(BF16) for j in range(2)
-        ]
+        moved, send_far, send_near, send = lax.optimization_barrier((moved, send_far, send_near, send))
+        third = hop(add(keep_far, swap_rep(send_far)).astype(BF16), second, n)
+        early = [(near[j] + moved[j].astype(F32)).astype(BF16) for j in range(2)]
         early = [add(value[0], hop(value[1], first, n)).astype(BF16) for value in early]
-        ground = plane == 0
-        other = add(slot[0], swap_rep(slot[1])).astype(BF16)
-        third = add(keeps[2], twins[2]).astype(BF16)
-        third, mine = jnp.where(ground, third, other), jnp.where(ground, other, third)
-        third = add(third[:2], hop(third[2:], second, n)).astype(BF16)
-        crossed, moved = lax.optimization_barrier((hop(third[1], first, n), hop(mine[2:], second, n)))
-        third = add(third[0], crossed).astype(BF16)
-        mine = add(mine[:2], moved).astype(BF16)
+        third = (add(keep_near, swap_rep(send_near)) + third.astype(F32)).astype(BF16)
+        third = add(third[0], hop(third[1], first, n)).astype(BF16)
+        mine = add(keep, swap_rep(send)).astype(BF16)
 
         def pick(values, s):
             table = ((0, 1, 2), (2, 1, 0), (1, 2, 0), (1, 0, 2))
@@ -946,12 +960,22 @@
                 result = jnp.where(plane == z, values[table[z][s - 1]], result)
             return result
 
+        mine, third = lax.optimization_barrier((mine, third))
         planes = early + [third]
         parts = [swap(pick(planes, s), s << (lay.bits - 2), n) for s in range(1, PLANES)]
-        parts, crossed = lax.optimization_barrier((parts, hop(mine[1], first, n)))
-        total = add(mine[0], crossed) + parts[0].astype(F32) + add(parts[1], parts[2])
+        both = tuple(a ^ b for a, b in zip(first, second))
+        inner = [hop(mine[d], masks, n) for d, masks in ((1, first), (2, second), (3, both))]
+        parts, inner = lax.optimization_barrier((parts, inner))
+        total = (add(mine[0], inner[0]) + add(inner[1], inner[2])) + (
+            parts[0].astype(F32) + add(parts[1], parts[2])
+        )
     else:
-        keeps, sends = from_canonical([slot] + slots, lay, canon, place, core)
+        slots = [(near, far, other, last) for near, far, other, last in slots]
+        slots.append((keep_near, keep_far, send_near, send_far))
+        planes = [(keep, send)]
+        for near, far, other, last in slots:
+            planes.append((jnp.concatenate([near, far], 0), jnp.concatenate([other, last], 0)))
+        keeps, sends = from_canonical(planes, lay, canon, place, core)
         moved = []
         for keep, send in zip(keeps, sends):
             pair = pair_sum(keep, send)

time: 147 us -> 140 us (0.952); the launches traced: 144 us -> 139 us
  waiting for transfers between devices: 64.5 us -> 50.9 us
  starting transfers between devices: 36.9 us -> 45.8 us
  other arithmetic: 8.45 us -> 5.88 us
  local copies, waits for them, and re-layouts: 2.21 us -> 4.47 us
    ppermute x17 -> x18, waiting for transfers between devices: 31.2 us -> 25.9 us  [hop(): return lax.ppermute(value, ('dp', 'rep'), pairs)]
    ppermute x6, waiting for transfers between devices: 25.2 us -> 20 us  [swap(): return lax.ppermute(value, 'dp', [(i, i ^ mask) for i in range(count)])]
    ppermute x17 -> x18, starting transfers between devices: 22.4 us -> 27 us  [hop(): return lax.ppermute(value, ('dp', 'rep'), pairs)]
    ppermute x12 -> x15, waiting for transfers between devices: 8.11 us -> 4.9 us  [swap_rep(): return lax.ppermute(value, 'rep', [(0, 1), (1, 0)])]
    ppermute x12 -> x15, starting transfers between devices: 2.05 us -> 5.19 us  [swap_rep(): return lax.ppermute(value, 'rep', [(0, 1), (1, 0)])]
    unnamed x34 -> x50, local copies, waits for them, and re-layouts: 1.04 us -> 3.33 us
    select_n x1 -> x0, other arithmetic: 2.2 us -> none  [on_device(): jnp.where(ground, other, third)]
    convert_element_type x6 -> x8, other arithmetic: 4.15 us -> 3.84 us  [the longest x2 2.88 us: on_device(): add(far, swap_rep(send)).astype(BF16)]
  transfers between devices with their start and end apart: 35 -> 39, of which waited for: 21 -> 14; matrix products, arithmetic and copies ran while one was open for 4% -> 4% of each run, Pallas kernels for 7% -> 8%
where the time goes in v4:
time: 140 us; the launch traced here: 139 us
  waiting for transfers between devices  50.9 us (36%)
  starting transfers between devices  45.8 us (33%)
  Pallas kernels  31 us (22%)
  other arithmetic  5.88 us (4%)
  local copies, waits for them, and re-layouts  4.47 us (3%)
    ppermute x18, starting transfers between devices, hop(): return lax.ppermute(value, ('dp', 'rep'), pairs)  27 us
    ppermute x18, waiting for transfers between devices, hop(): return lax.ppermute(value, ('dp', 'rep'), pairs)  25.9 us
    ppermute x6, waiting for transfers between devices, swap(): return lax.ppermute(value, 'dp', [(i, i ^ mask) for i in range(count)])  20 us
    pallas_call x1, Pallas kernels, on_device(): results = forward(idx, *pieces, tokens_in.T, *angles, cotangent.T)  16.5 us
    ppermute x6, starting transfers between devices, swap(): return lax.ppermute(value, 'dp', [(i, i ^ mask) for i in range(count)])  13.5 us
    pallas_call x1, Pallas kernels, on_device(): attention_back(idx, tokens_in.T, *angles, *saved, *held)  11.1 us
    ppermute x15, starting transfers between devices, swap_rep(): return lax.ppermute(value, 'rep', [(0, 1), (1, 0)])  5.19 us
    ppermute x15, waiting for transfers between devices, swap_rep(): return lax.ppermute(value, 'rep', [(0, 1), (1, 0)])  4.9 us
  transfers between devices with their start and end apart: 39, of which 14 were waited for; matrix products, arithmetic and copies ran while one was open for 4% of the time, Pallas kernels for 8%

profile of v4, /device:TPU:0, one launch (start us, length us, event | category | flops | bytes accessed | tf_op | source)
XLA Modules:
  0.0 139.0 jit_solution(18242012259360720842)
XLA Ops:
  3.0 2.9 %collective-permute-start = (bf16[880,128]{1,0:T(8,128)(2,1)S(1)}, bf16[880,128]{1,0:T(8,128)(2,1)S(1)}, u32[]{:S(2)}, u32[]{:S(2)}) collective-permute-start(bf16[880,128]{1,0:T(8,128)(2,1)S(1)} %pack_own_chunk.1), channel_id=1, source_target_pairs={{0,8},{2,10},{4,12},{6,14},{8,0},{10,2},{12,4},{14,6},{16,24},{18,... | collective-permute-start | bytes 675848 | tf_op jit(solution)/shard_map/ppermute | solution.py:110
  5.9 2.7 %collective-permute-start.1 = (bf16[880,128]{1,0:T(8,128)(2,1)S(1)}, bf16[880,128]{1,0:T(8,128)(2,1)S(1)}, u32[]{:S(2)}, u32[]{:S(2)}) collective-permute-start(bf16[880,128]{1,0:T(8,128)(2,1)S(1)} %pack_own_chunk.1), channel_id=1, source_target_pairs={{0,16},{2,18},{4,20},{6,22},{8,24},{10,26},{12,28},{14,30},{16,0},... | collective-permute-start | bytes 675848 | tf_op jit(solution)/shard_map/ppermute | solution.py:110
  8.6 1.8 %collective-permute-start.3 = (bf16[880,128]{1,0:T(8,128)(2,1)S(1)}, bf16[880,128]{1,0:T(8,128)(2,1)S(1)}, u32[]{:S(2)}, u32[]{:S(2)}) collective-permute-start(bf16[880,128]{1,0:T(8,128)(2,1)S(1)} %pack_own_chunk.1), channel_id=1, source_target_pairs={{0,2},{1,5},{2,0},{3,7},{4,6},{5,1},{6,4},{7,3},{8,10},{9,13},{10,... | collective-permute-start | bytes 675848 | tf_op jit(solution)/shard_map/ppermute | solution.py:119
  10.4 1.5 %collective-permute-start.4 = (bf16[880,128]{1,0:T(8,128)(2,1)S(1)}, bf16[880,128]{1,0:T(8,128)(2,1)S(1)}, u32[]{:S(2)}, u32[]{:S(2)}) collective-permute-start(bf16[880,128]{1,0:T(8,128)(2,1)S(1)} %pack_own_chunk.1), channel_id=1, source_target_pairs={{0,4},{1,3},{2,6},{3,1},{4,0},{5,7},{6,2},{7,5},{8,12},{9,11},{10,... | collective-permute-start | bytes 675848 | tf_op jit(solution)/shard_map/ppermute | solution.py:119
  11.9 3.5 %collective-permute-done = bf16[880,128]{1,0:T(8,128)(2,1)S(1)} collective-permute-done((bf16[880,128]{1,0:T(8,128)(2,1)S(1)}, bf16[880,128]{1,0:T(8,128)(2,1)S(1)}, u32[]{:S(2)}, u32[]{:S(2)}) %collective-permute-start) | collective-permute-done | bytes 225312 | tf_op jit(solution)/shard_map/ppermute | solution.py:110
  15.4 2.9 %collective-permute-start.5 = (bf16[880,128]{1,0:T(8,128)(2,1)S(1)}, bf16[880,128]{1,0:T(8,128)(2,1)S(1)}, u32[]{:S(2)}, u32[]{:S(2)}) collective-permute-start(bf16[880,128]{1,0:T(8,128)(2,1)S(1)} %pack_own_chunk.1), channel_id=1, source_target_pairs={{0,6},{1,7},{2,4},{3,5},{4,2},{5,3},{6,0},{7,1},{8,14},{9,15},{10,... | collective-permute-start | bytes 675848 | tf_op jit(solution)/shard_map/ppermute | solution.py:119
  19.0 5.9 %collective-permute-done.1 = bf16[880,128]{1,0:T(8,128)(2,1)S(1)} collective-permute-done((bf16[880,128]{1,0:T(8,128)(2,1)S(1)}, bf16[880,128]{1,0:T(8,128)(2,1)S(1)}, u32[]{:S(2)}, u32[]{:S(2)}) %collective-permute-start.1) | collective-permute-done | bytes 225312 | tf_op jit(solution)/shard_map/ppermute | solution.py:110
  24.9 1.5 %collective-permute-start.8 = (bf16[880,128]{1,0:T(8,128)(2,1)S(1)}, bf16[880,128]{1,0:T(8,128)(2,1)S(1)}, u32[]{:S(2)}, u32[]{:S(2)}) collective-permute-start(bf16[880,128]{1,0:T(8,128)(2,1)S(1)} %collective-permute-done.2), channel_id=1, source_target_pairs={{0,2},{1,5},{2,0},{3,7},{4,6},{5,1},{6,4},{7,3},{8,10},{9,13},{10,... | collective-permute-start | bytes 675848 | tf_op jit(solution)/shard_map/ppermute | solution.py:119
  28.6 2.3 %collective-permute-done.8 = bf16[880,128]{1,0:T(8,128)(2,1)S(1)} collective-permute-done((bf16[880,128]{1,0:T(8,128)(2,1)S(1)}, bf16[880,128]{1,0:T(8,128)(2,1)S(1)}, u32[]{:S(2)}, u32[]{:S(2)}) %collective-permute-start.8) | collective-permute-done | bytes 225312 | tf_op jit(solution)/shard_map/ppermute | solution.py:119
  31.0 1.5 %collective-permute-start.16 = (bf16[2,880,128]{2,1,0:T(8,128)(2,1)S(1)}, bf16[2,880,128]{2,1,0:T(8,128)(2,1)S(1)}, u32[]{:S(2)}, u32[]{:S(2)}) collective-permute-start(bf16[2,880,128]{2,1,0:T(8,128)(2,1)S(1)} %pad_maximum_fusion.3.refs_3_), channel_id=1, source_target_pairs={{0,4},{1,3},{2,6},{3,1},{4,0},{5,7},{6,2},{7,5},{8,12},{9,11},{10,... | collective-permute-start | bytes 1351688 | tf_op jit(solution)/shard_map/ppermute | solution.py:119
  32.5 2.3 %collective-permute-done.7 = bf16[880,128]{1,0:T(8,128)(2,1)S(1)} collective-permute-done((bf16[880,128]{1,0:T(8,128)(2,1)S(1)}, bf16[880,128]{1,0:T(8,128)(2,1)S(1)}, u32[]{:S(2)}, u32[]{:S(2)}) %collective-permute-start.7) | collective-permute-done | bytes 225312 | tf_op jit(solution)/shard_map/ppermute | solution.py:119
  36.3 3.4 %collective-permute-done.6 = bf16[880,128]{1,0:T(8,128)(2,1)S(1)} collective-permute-done((bf16[880,128]{1,0:T(8,128)(2,1)S(1)}, bf16[880,128]{1,0:T(8,128)(2,1)S(1)}, u32[]{:S(2)}, u32[]{:S(2)}) %collective-permute-start.6) | collective-permute-done | bytes 225312 | tf_op jit(solution)/shard_map/ppermute | solution.py:119
  40.7 1.4 %collective-permute-start.9 = (bf16[2,880,128]{2,1,0:T(8,128)(2,1)S(1)}, bf16[2,880,128]{2,1,0:T(8,128)(2,1)}, u32[]{:S(2)}, u32[]{:S(2)}) collective-permute-start(bf16[2,880,128]{2,1,0:T(8,128)(2,1)S(1)} %pad_maximum_fusion.1.refs_1_), channel_id=1, source_target_pairs={{0,4},{1,3},{2,6},{3,1},{4,0},{5,7},{6,2},{7,5},{8,12},{9,11},{10,... | collective-permute-start | bytes 1351688 | tf_op jit(solution)/shard_map/ppermute | solution.py:119
  42.1 2.1 %collective-permute-done.14.refs_5_ = bf16[2,880,128]{2,1,0:T(8,128)(2,1)S(1)} collective-permute-done((bf16[2,880,128]{2,1,0:T(8,128)(2,1)S(1)}, bf16[2,880,128]{2,1,0:T(8,128)(2,1)S(1)}, u32[]{:S(2)}, u32[]{:S(2)}) %collective-permute-start.14) | collective-permute-done | bytes 450592 | tf_op jit(solution)/shard_map/ppermute | solution.py:119
  45.7 3.5 %collective-permute-done.9.refs_4_ = bf16[2,880,128]{2,1,0:T(8,128)(2,1)} collective-permute-done((bf16[2,880,128]{2,1,0:T(8,128)(2,1)S(1)}, bf16[2,880,128]{2,1,0:T(8,128)(2,1)}, u32[]{:S(2)}, u32[]{:S(2)}) %collective-permute-start.9) | collective-permute-done | bytes 450592 | tf_op jit(solution)/shard_map/ppermute | solution.py:119
  52.8 1.6 %collective-permute-done.18.refs_11_ = bf16[2,880,128]{2,1,0:T(8,128)(2,1)S(1)} collective-permute-done((bf16[2,880,128]{2,1,0:T(8,128)(2,1)}, bf16[2,880,128]{2,1,0:T(8,128)(2,1)S(1)}, u32[]{:S(2)}, u32[]{:S(2)}) %collective-permute-start.18) | collective-permute-done | bytes 450592 | tf_op jit(solution)/shard_map/ppermute | solution.py:114
  55.1 16.5 %forward_and_ff_backward.1 = (f32[256,576]{1,0:T(8,128)}, f32[256,576]{1,0:T(8,128)}, f32[1,576]{1,0:T(1,128)S(1)}, bf16[256,576]{1,0:T(8,128)(2,1)}, f32[6,384,...) custom-call(s32[4]{0:T(128)S(1)} %pad_add_fusion.idx, ...), custom_call_target="tpu_custom_call" | custom-call | flops 4529848320 | bytes 8000000 | tf_op jit(solution)/shard_map/forward_and_ff_backward/pallas_call | solution.py:937
  72.3 1.5 %collective-permute-done.21 = bf16[2,880,128]{2,1,0:T(8,128)(2,1)S(1)} collective-permute-done((bf16[2,880,128]{2,1,0:T(8,128)(2,1)}, bf16[2,880,128]{2,1,0:T(8,128)(2,1)S(1)}, u32[]{:S(2)}, u32[]{:S(2)}) %collective-permute-start.21) | collective-permute-done | bytes 450592 | tf_op jit(solution)/shard_map/ppermute | solution.py:114
  73.8 2.0 %add_convert_fusion.5 = bf16[2,880,128]{2,1,0:T(8,128)(2,1)} fusion(bf16[2,880,128]{2,1,0:T(8,128)(2,1)S(1)} %collective-permute-done.21, bf16[2,880,128]{2,1,0:T(8,128)(2,1)} %get-tuple-element.98), kind=kLoop, calls=%fused_computation.6 | loop fusion | flops 901120 | bytes 1351680 | tf_op jit(solution)/shard_map/convert_element_type | solution.py:942
  79.2 11.1 %attention_backward.1 = (bf16[576,256]{1,0:T(8,128)(2,1)}, f32[576,256]{1,0:T(8,128)}, bf16[2,880,128]{2,1,0:T(8,128)(2,1)}, bf16[2,880,128]{2,1,0:T(8,128)(2,1)...) custom-call(s32[4]{0:T(128)S(1)} %pad_add_fusion.idx, ...), custom_call_target="tpu_custom_call" | custom-call | flops 849346560 | bytes 8000000 | tf_op jit(solution)/shard_map/attention_backward/pallas_call | solution.py:944
  90.6 1.5 %collective-permute-start.31 = (bf16[880,128]{1,0:T(8,128)(2,1)S(1)}, bf16[880,128]{1,0:T(8,128)(2,1)S(1)}, u32[]{:S(2)}, u32[]{:S(2)}) collective-permute-start(bf16[880,128]{1,0:T(8,128)(2,1)S(1)} %slice_bitcast_fusion), channel_id=1, source_target_pairs={{0,2},{1,5},{2,0},{3,7},{4,6},{5,1},{6,4},{7,3},{8,10},{9,13},{10,... | collective-permute-start | bytes 675848 | tf_op jit(solution)/shard_map/ppermute | solution.py:119
  92.8 1.6 %collective-permute-start.26 = (bf16[2,880,128]{2,1,0:T(8,128)(2,1)S(1)}, bf16[2,880,128]{2,1,0:T(8,128)(2,1)S(1)}, u32[]{:S(2)}, u32[]{:S(2)}) collective-permute-start(bf16[2,880,128]{2,1,0:T(8,128)(2,1)S(1)} %add_convert_fusion.4), channel_id=1, source_target_pairs={{0,4},{1,3},{2,6},{3,1},{4,0},{5,7},{6,2},{7,5},{8,12},{9,11},{10,... | collective-permute-start | bytes 1351688 | tf_op jit(solution)/shard_map/ppermute | solution.py:119
  95.8 7.8 %collective-permute-done.26 = bf16[2,880,128]{2,1,0:T(8,128)(2,1)S(1)} collective-permute-done((bf16[2,880,128]{2,1,0:T(8,128)(2,1)S(1)}, bf16[2,880,128]{2,1,0:T(8,128)(2,1)S(1)}, u32[]{:S(2)}, u32[]{:S(2)}) %collective-permute-start.26) | collective-permute-done | bytes 450592 | tf_op jit(solution)/shard_map/ppermute | solution.py:119
  105.4 4.5 %collective-permute-done.27 = bf16[880,128]{1,0:T(8,128)(2,1)S(1)} collective-permute-done((bf16[880,128]{1,0:T(8,128)(2,1)S(1)}, bf16[880,128]{1,0:T(8,128)(2,1)S(1)}, u32[]{:S(2)}, u32[]{:S(2)}) %collective-permute-start.27) | collective-permute-done | bytes 225312 | tf_op jit(solution)/shard_map/ppermute | solution.py:119
  110.2 4.9 %collective-permute-start.32 = (bf16[880,128]{1,0:T(8,128)(2,1)S(1)}, bf16[880,128]{1,0:T(8,128)(2,1)S(1)}, u32[]{:S(2)}, u32[]{:S(2)}) collective-permute-start(bf16[880,128]{1,0:T(8,128)(2,1)S(1)} %get-tuple-element.123), channel_id=1, source_target_pairs={{0,8},{2,10},{4,12},{6,14},{8,0},{10,2},{12,4},{14,6},{16,24},{18,... | collective-permute-start | bytes 675848 | tf_op jit(solution)/shard_map/ppermute | solution.py:110
  115.1 1.6 %collective-permute-start.33 = (bf16[880,128]{1,0:T(8,128)(2,1)S(1)}, bf16[880,128]{1,0:T(8,128)(2,1)S(1)}, u32[]{:S(2)}, u32[]{:S(2)}) collective-permute-start(bf16[880,128]{1,0:T(8,128)(2,1)S(1)} %get-tuple-element.122), channel_id=1, source_target_pairs={{0,16},{2,18},{4,20},{6,22},{8,24},{10,26},{12,28},{14,30},{16,0},... | collective-permute-start | bytes 675848 | tf_op jit(solution)/shard_map/ppermute | solution.py:110
  119.5 1.4 %collective-permute-start.36 = (bf16[880,128]{1,0:T(8,128)(2,1)S(1)}, bf16[880,128]{1,0:T(8,128)(2,1)S(1)}, u32[]{:S(2)}, u32[]{:S(2)}) collective-permute-start(bf16[880,128]{1,0:T(8,128)(2,1)S(1)} %get-tuple-element.125), channel_id=1, source_target_pairs={{0,4},{1,3},{2,6},{3,1},{4,0},{5,7},{6,2},{7,5},{8,12},{9,11},{10,... | collective-permute-start | bytes 675848 | tf_op jit(solution)/shard_map/ppermute | solution.py:119
  120.9 2.9 %collective-permute-done.32 = bf16[880,128]{1,0:T(8,128)(2,1)S(1)} collective-permute-done((bf16[880,128]{1,0:T(8,128)(2,1)S(1)}, bf16[880,128]{1,0:T(8,128)(2,1)S(1)}, u32[]{:S(2)}, u32[]{:S(2)}) %collective-permute-start.32) | collective-permute-done | bytes 225312 | tf_op jit(solution)/shard_map/ppermute | solution.py:110
  123.9 2.6 %collective-permute-start.37 = (bf16[880,128]{1,0:T(8,128)(2,1)S(1)}, bf16[880,128]{1,0:T(8,128)(2,1)S(1)}, u32[]{:S(2)}, u32[]{:S(2)}) collective-permute-start(bf16[880,128]{1,0:T(8,128)(2,1)S(1)} %get-tuple-element.124), channel_id=1, source_target_pairs={{0,6},{1,7},{2,4},{3,5},{4,2},{5,3},{6,0},{7,1},{8,14},{9,15},{10,... | collective-permute-start | bytes 675848 | tf_op jit(solution)/shard_map/ppermute | solution.py:119
  126.4 7.7 %collective-permute-done.33 = bf16[880,128]{1,0:T(8,128)(2,1)S(1)} collective-permute-done((bf16[880,128]{1,0:T(8,128)(2,1)S(1)}, bf16[880,128]{1,0:T(8,128)(2,1)S(1)}, u32[]{:S(2)}, u32[]{:S(2)}) %collective-permute-start.33) | collective-permute-done | bytes 225312 | tf_op jit(solution)/shard_map/ppermute | solution.py:110
  134.4 1.8 %collective-permute-done.38.twin = f32[880,128]{1,0:T(8,128)S(1)} collective-permute-done((f32[880,128]{1,0:T(8,128)S(1)}, f32[880,128]{1,0:T(8,128)S(1)}, u32[]{:S(2)}, u32[]{:S(2)}) %collective-permute-start.38) | collective-permute-done | bytes 450592 | tf_op jit(solution)/shard_map/ppermute | solution.py:114
  136.2 2.2 %unpack_own_chunk.1 = f32[1736,128]{1,0:T(8,128)} custom-call(s32[4]{0:T(128)S(1)} %pad_add_fusion.1.idx, f32[880,128]{1,0:T(8,128)S(1)} %fusion.3.own, f32[880,128]{1,0:T(8,128)S(1)} %collective-permute-done.38.twin), custom_call_target="tpu_custom_call" | custom-call | tf_op jit(solution)/shard_map/unpack_own_chunk/pallas_call | solution.py:749
  (126 shorter events, 25.6 us)
Async XLA Ops:
  3.0 12.5 %collective-permute-start = (bf16[880,128]{1,0:T(8,128)(2,1)S(1)}, bf16[880,128]{1,0:T(8,128)(2,1)S(1)}, u32[]{:S(2)}, u32[]{:S(2)}) collective-permute-start(bf16[880,128]{1,0:T(8,128)(2,1)S(1)} %pack_own_chunk.1), channel_id=1, source_target_pairs={{0,8},{2,10},{4,12},{6,14},{8,0},{10,2},{12,4},{14,6},{16,24},{18,... | collective-permute-start | bytes 675848 | tf_op jit(solution)/shard_map/ppermute | solution.py:110
  5.9 19.0 %collective-permute-start.1 = (bf16[880,128]{1,0:T(8,128)(2,1)S(1)}, bf16[880,128]{1,0:T(8,128)(2,1)S(1)}, u32[]{:S(2)}, u32[]{:S(2)}) collective-permute-start(bf16[880,128]{1,0:T(8,128)(2,1)S(1)} %pack_own_chunk.1), channel_id=1, source_target_pairs={{0,16},{2,18},{4,20},{6,22},{8,24},{10,26},{12,28},{14,30},{16,0},... | collective-permute-start | bytes 675848 | tf_op jit(solution)/shard_map/ppermute | solution.py:110
  8.6 16.3 %collective-permute-start.2 = (bf16[880,128]{1,0:T(8,128)(2,1)S(1)}, bf16[880,128]{1,0:T(8,128)(2,1)S(1)}, u32[]{:S(2)}, u32[]{:S(2)}) collective-permute-start(bf16[880,128]{1,0:T(8,128)(2,1)S(1)} %pack_own_chunk.1), channel_id=1, source_target_pairs={{0,24},{2,26},{4,28},{6,30},{8,16},{10,18},{12,20},{14,22},{16,8},... | collective-permute-start | bytes 675848 | tf_op jit(solution)/shard_map/ppermute | solution.py:110
  8.6 16.3 %collective-permute-start.3 = (bf16[880,128]{1,0:T(8,128)(2,1)S(1)}, bf16[880,128]{1,0:T(8,128)(2,1)S(1)}, u32[]{:S(2)}, u32[]{:S(2)}) collective-permute-start(bf16[880,128]{1,0:T(8,128)(2,1)S(1)} %pack_own_chunk.1), channel_id=1, source_target_pairs={{0,2},{1,5},{2,0},{3,7},{4,6},{5,1},{6,4},{7,3},{8,10},{9,13},{10,... | collective-permute-start | bytes 675848 | tf_op jit(solution)/shard_map/ppermute | solution.py:119
  10.4 14.5 %collective-permute-start.4 = (bf16[880,128]{1,0:T(8,128)(2,1)S(1)}, bf16[880,128]{1,0:T(8,128)(2,1)S(1)}, u32[]{:S(2)}, u32[]{:S(2)}) collective-permute-start(bf16[880,128]{1,0:T(8,128)(2,1)S(1)} %pack_own_chunk.1), channel_id=1, source_target_pairs={{0,4},{1,3},{2,6},{3,1},{4,0},{5,7},{6,2},{7,5},{8,12},{9,11},{10,... | collective-permute-start | bytes 675848 | tf_op jit(solution)/shard_map/ppermute | solution.py:119
  15.4 9.4 %collective-permute-start.5 = (bf16[880,128]{1,0:T(8,128)(2,1)S(1)}, bf16[880,128]{1,0:T(8,128)(2,1)S(1)}, u32[]{:S(2)}, u32[]{:S(2)}) collective-permute-start(bf16[880,128]{1,0:T(8,128)(2,1)S(1)} %pack_own_chunk.1), channel_id=1, source_target_pairs={{0,6},{1,7},{2,4},{3,5},{4,2},{5,3},{6,0},{7,1},{8,14},{9,15},{10,... | collective-permute-start | bytes 675848 | tf_op jit(solution)/shard_map/ppermute | solution.py:119
  24.9 6.0 %collective-permute-start.8 = (bf16[880,128]{1,0:T(8,128)(2,1)S(1)}, bf16[880,128]{1,0:T(8,128)(2,1)S(1)}, u32[]{:S(2)}, u32[]{:S(2)}) collective-permute-start(bf16[880,128]{1,0:T(8,128)(2,1)S(1)} %collective-permute-done.2), channel_id=1, source_target_pairs={{0,2},{1,5},{2,0},{3,7},{4,6},{5,1},{6,4},{7,3},{8,10},{9,13},{10,... | collective-permute-start | bytes 675848 | tf_op jit(solution)/shard_map/ppermute | solution.py:119
  26.4 8.4 %collective-permute-start.7 = (bf16[880,128]{1,0:T(8,128)(2,1)S(1)}, bf16[880,128]{1,0:T(8,128)(2,1)S(1)}, u32[]{:S(2)}, u32[]{:S(2)}) collective-permute-start(bf16[880,128]{1,0:T(8,128)(2,1)S(1)} %collective-permute-done.1), channel_id=1, source_target_pairs={{0,2},{1,5},{2,0},{3,7},{4,6},{5,1},{6,4},{7,3},{8,10},{9,13},{10,... | collective-permute-start | bytes 675848 | tf_op jit(solution)/shard_map/ppermute | solution.py:119
  27.0 12.7 %collective-permute-start.6 = (bf16[880,128]{1,0:T(8,128)(2,1)S(1)}, bf16[880,128]{1,0:T(8,128)(2,1)S(1)}, u32[]{:S(2)}, u32[]{:S(2)}) collective-permute-start(bf16[880,128]{1,0:T(8,128)(2,1)S(1)} %collective-permute-done), channel_id=1, source_target_pairs={{0,2},{1,5},{2,0},{3,7},{4,6},{5,1},{6,4},{7,3},{8,10},{9,13},{10,... | collective-permute-start | bytes 675848 | tf_op jit(solution)/shard_map/ppermute | solution.py:119
  28.5 20.7 %collective-permute-start.10 = (bf16[4,880,128]{2,1,0:T(8,128)(2,1)S(1)}, bf16[4,880,128]{2,1,0:T(8,128)(2,1)S(1)}, u32[]{:S(2)}, u32[]{:S(2)}) collective-permute-start(bf16[4,880,128]{2,1,0:T(8,128)(2,1)S(1)} %pad_maximum_fusion.refs_0_), channel_id=1, source_target_pairs={{0,1},{1,0},{2,3},{3,2},{4,5},{5,4},{6,7},{7,6},{8,9},{9,8},{10,11... | collective-permute-start | bytes 2703368 | tf_op jit(solution)/shard_map/ppermute | solution.py:114
  31.0 8.7 %collective-permute-start.16 = (bf16[2,880,128]{2,1,0:T(8,128)(2,1)S(1)}, bf16[2,880,128]{2,1,0:T(8,128)(2,1)S(1)}, u32[]{:S(2)}, u32[]{:S(2)}) collective-permute-start(bf16[2,880,128]{2,1,0:T(8,128)(2,1)S(1)} %pad_maximum_fusion.3.refs_3_), channel_id=1, source_target_pairs={{0,4},{1,3},{2,6},{3,1},{4,0},{5,7},{6,2},{7,5},{8,12},{9,11},{10,... | collective-permute-start | bytes 1351688 | tf_op jit(solution)/shard_map/ppermute | solution.py:119
  32.5 8.2 %collective-permute-start.13 = (bf16[2,880,128]{2,1,0:T(8,128)(2,1)S(1)}, bf16[2,880,128]{2,1,0:T(8,128)(2,1)S(1)}, u32[]{:S(2)}, u32[]{:S(2)}) collective-permute-start(bf16[2,880,128]{2,1,0:T(8,128)(2,1)S(1)} %pad_maximum_fusion.3.refs_3_), channel_id=1, source_target_pairs={{0,1},{1,0},{2,3},{3,2},{4,5},{5,4},{6,7},{7,6},{8,9},{9,8},{10,11... | collective-permute-start | bytes 1351688 | tf_op jit(solution)/shard_map/ppermute | solution.py:114
  34.9 9.4 %collective-permute-start.14 = (bf16[2,880,128]{2,1,0:T(8,128)(2,1)S(1)}, bf16[2,880,128]{2,1,0:T(8,128)(2,1)S(1)}, u32[]{:S(2)}, u32[]{:S(2)}) collective-permute-start(bf16[2,880,128]{2,1,0:T(8,128)(2,1)S(1)} %pad_maximum_fusion.2.refs_2_), channel_id=1, source_target_pairs={{0,4},{1,3},{2,6},{3,1},{4,0},{5,7},{6,2},{7,5},{8,12},{9,11},{10,... | collective-permute-start | bytes 1351688 | tf_op jit(solution)/shard_map/ppermute | solution.py:119
  39.6 6.0 %collective-permute-start.12 = (bf16[2,880,128]{2,1,0:T(8,128)(2,1)S(1)}, bf16[2,880,128]{2,1,0:T(8,128)(2,1)S(1)}, u32[]{:S(2)}, u32[]{:S(2)}) collective-permute-start(bf16[2,880,128]{2,1,0:T(8,128)(2,1)S(1)} %pad_maximum_fusion.2.refs_2_), channel_id=1, source_target_pairs={{0,1},{1,0},{2,3},{3,2},{4,5},{5,4},{6,7},{7,6},{8,9},{9,8},{10,11... | collective-permute-start | bytes 1351688 | tf_op jit(solution)/shard_map/ppermute | solution.py:114
  39.7 6.0 %collective-permute-start.11 = (bf16[2,880,128]{2,1,0:T(8,128)(2,1)S(1)}, bf16[2,880,128]{2,1,0:T(8,128)(2,1)S(1)}, u32[]{:S(2)}, u32[]{:S(2)}) collective-permute-start(bf16[2,880,128]{2,1,0:T(8,128)(2,1)S(1)} %pad_maximum_fusion.1.refs_1_), channel_id=1, source_target_pairs={{0,1},{1,0},{2,3},{3,2},{4,5},{5,4},{6,7},{7,6},{8,9},{9,8},{10,11... | collective-permute-start | bytes 1351688 | tf_op jit(solution)/shard_map/ppermute | solution.py:114
  40.7 8.5 %collective-permute-start.9 = (bf16[2,880,128]{2,1,0:T(8,128)(2,1)S(1)}, bf16[2,880,128]{2,1,0:T(8,128)(2,1)}, u32[]{:S(2)}, u32[]{:S(2)}) collective-permute-start(bf16[2,880,128]{2,1,0:T(8,128)(2,1)S(1)} %pad_maximum_fusion.1.refs_1_), channel_id=1, source_target_pairs={{0,4},{1,3},{2,6},{3,1},{4,0},{5,7},{6,2},{7,5},{8,12},{9,11},{10,... | collective-permute-start | bytes 1351688 | tf_op jit(solution)/shard_map/ppermute | solution.py:119
  44.3 5.9 %collective-permute-start.17 = (bf16[2,880,128]{2,1,0:T(8,128)(2,1)S(1)}, bf16[2,880,128]{2,1,0:T(8,128)(2,1)S(1)}, u32[]{:S(2)}, u32[]{:S(2)}) collective-permute-start(bf16[2,880,128]{2,1,0:T(8,128)(2,1)S(1)} %collective-permute-done.16.refs_6_), channel_id=1, source_target_pairs={{0,1},{1,0},{2,3},{3,2},{4,5},{5,4},{6,7},{7,6},{8,9},{9,8},{10,11... | collective-permute-start | bytes 1351688 | tf_op jit(solution)/shard_map/ppermute | solution.py:114
  75.7 14.6 %collective-permute-start.22 = (bf16[2,880,128]{2,1,0:T(8,128)(2,1)}, bf16[2,880,128]{2,1,0:T(8,128)(2,1)S(1)}, u32[]{:S(2)}, u32[]{:S(2)}) collective-permute-start(bf16[2,880,128]{2,1,0:T(8,128)(2,1)} %add_convert_fusion.5), channel_id=1, source_target_pairs={{0,4},{1,3},{2,6},{3,1},{4,0},{5,7},{6,2},{7,5},{8,12},{9,11},{10,... | collective-permute-start | bytes 1351688 | tf_op jit(solution)/shard_map/ppermute | solution.py:119
  78.1 12.2 %collective-permute-start.20 = (bf16[2,880,128]{2,1,0:T(8,128)(2,1)}, bf16[2,880,128]{2,1,0:T(8,128)(2,1)S(1)}, u32[]{:S(2)}, u32[]{:S(2)}) collective-permute-start(bf16[2,880,128]{2,1,0:T(8,128)(2,1)} %add_convert_fusion.6), channel_id=1, source_target_pairs={{0,4},{1,3},{2,6},{3,1},{4,0},{5,7},{6,2},{7,5},{8,12},{9,11},{10,... | collective-permute-start | bytes 1351688 | tf_op jit(solution)/shard_map/ppermute | solution.py:119
  78.7 11.7 %collective-permute-start.30 = (bf16[2,880,128]{2,1,0:T(8,128)(2,1)}, bf16[2,880,128]{2,1,0:T(8,128)(2,1)S(1)}, u32[]{:S(2)}, u32[]{:S(2)}) collective-permute-start(bf16[2,880,128]{2,1,0:T(8,128)(2,1)} %get-tuple-element.114), channel_id=1, source_target_pairs={{0,1},{1,0},{2,3},{3,2},{4,5},{5,4},{6,7},{7,6},{8,9},{9,8},{10,11... | collective-permute-start | bytes 1351688 | tf_op jit(solution)/shard_map/ppermute | solution.py:114
  78.7 15.7 %collective-permute-start.28 = (bf16[2,880,128]{2,1,0:T(8,128)(2,1)}, bf16[2,880,128]{2,1,0:T(8,128)(2,1)S(1)}, u32[]{:S(2)}, u32[]{:S(2)}) collective-permute-start(bf16[2,880,128]{2,1,0:T(8,128)(2,1)} %get-tuple-element.110), channel_id=1, source_target_pairs={{0,1},{1,0},{2,3},{3,2},{4,5},{5,4},{6,7},{7,6},{8,9},{9,8},{10,11... | collective-permute-start | bytes 1351688 | tf_op jit(solution)/shard_map/ppermute | solution.py:114
  90.6 19.3 %collective-permute-start.31 = (bf16[880,128]{1,0:T(8,128)(2,1)S(1)}, bf16[880,128]{1,0:T(8,128)(2,1)S(1)}, u32[]{:S(2)}, u32[]{:S(2)}) collective-permute-start(bf16[880,128]{1,0:T(8,128)(2,1)S(1)} %slice_bitcast_fusion), channel_id=1, source_target_pairs={{0,2},{1,5},{2,0},{3,7},{4,6},{5,1},{6,4},{7,3},{8,10},{9,13},{10,... | collective-permute-start | bytes 675848 | tf_op jit(solution)/shard_map/ppermute | solution.py:119
  92.3 12.9 %collective-permute-start.23 = (bf16[4,880,128]{2,1,0:T(8,128)(2,1)S(1)}, bf16[4,880,128]{2,1,0:T(8,128)(2,1)S(1)}, u32[]{:S(2)}, u32[]{:S(2)}) collective-permute-start(bf16[4,880,128]{2,1,0:T(8,128)(2,1)S(1)} %copy-done.15), channel_id=1, source_target_pairs={{0,1},{1,0},{2,3},{3,2},{4,5},{5,4},{6,7},{7,6},{8,9},{9,8},{10,11... | collective-permute-start | bytes 2703368 | tf_op jit(solution)/shard_map/ppermute | solution.py:114
  92.8 10.9 %collective-permute-start.26 = (bf16[2,880,128]{2,1,0:T(8,128)(2,1)S(1)}, bf16[2,880,128]{2,1,0:T(8,128)(2,1)S(1)}, u32[]{:S(2)}, u32[]{:S(2)}) collective-permute-start(bf16[2,880,128]{2,1,0:T(8,128)(2,1)S(1)} %add_convert_fusion.4), channel_id=1, source_target_pairs={{0,4},{1,3},{2,6},{3,1},{4,0},{5,7},{6,2},{7,5},{8,12},{9,11},{10,... | collective-permute-start | bytes 1351688 | tf_op jit(solution)/shard_map/ppermute | solution.py:119
  94.6 15.4 %collective-permute-start.29 = (bf16[880,128]{1,0:T(8,128)(2,1)S(1)}, bf16[880,128]{1,0:T(8,128)(2,1)S(1)}, u32[]{:S(2)}, u32[]{:S(2)}) collective-permute-start(bf16[880,128]{1,0:T(8,128)(2,1)S(1)} %slice_bitcast_fusion.2), channel_id=1, source_target_pairs={{0,2},{1,5},{2,0},{3,7},{4,6},{5,1},{6,4},{7,3},{8,10},{9,13},{10,... | collective-permute-start | bytes 675848 | tf_op jit(solution)/shard_map/ppermute | solution.py:119
  103.9 6.0 %collective-permute-start.27 = (bf16[880,128]{1,0:T(8,128)(2,1)S(1)}, bf16[880,128]{1,0:T(8,128)(2,1)S(1)}, u32[]{:S(2)}, u32[]{:S(2)}) collective-permute-start(bf16[880,128]{1,0:T(8,128)(2,1)S(1)} %slice_bitcast_fusion.4), channel_id=1, source_target_pairs={{0,2},{1,5},{2,0},{3,7},{4,6},{5,1},{6,4},{7,3},{8,10},{9,13},{10,... | collective-permute-start | bytes 675848 | tf_op jit(solution)/shard_map/ppermute | solution.py:119
  110.2 13.7 %collective-permute-start.32 = (bf16[880,128]{1,0:T(8,128)(2,1)S(1)}, bf16[880,128]{1,0:T(8,128)(2,1)S(1)}, u32[]{:S(2)}, u32[]{:S(2)}) collective-permute-start(bf16[880,128]{1,0:T(8,128)(2,1)S(1)} %get-tuple-element.123), channel_id=1, source_target_pairs={{0,8},{2,10},{4,12},{6,14},{8,0},{10,2},{12,4},{14,6},{16,24},{18,... | collective-permute-start | bytes 675848 | tf_op jit(solution)/shard_map/ppermute | solution.py:110
  115.1 19.0 %collective-permute-start.33 = (bf16[880,128]{1,0:T(8,128)(2,1)S(1)}, bf16[880,128]{1,0:T(8,128)(2,1)S(1)}, u32[]{:S(2)}, u32[]{:S(2)}) collective-permute-start(bf16[880,128]{1,0:T(8,128)(2,1)S(1)} %get-tuple-element.122), channel_id=1, source_target_pairs={{0,16},{2,18},{4,20},{6,22},{8,24},{10,26},{12,28},{14,30},{16,0},... | collective-permute-start | bytes 675848 | tf_op jit(solution)/shard_map/ppermute | solution.py:110
  116.7 17.4 %collective-permute-start.34 = (bf16[880,128]{1,0:T(8,128)(2,1)S(1)}, bf16[880,128]{1,0:T(8,128)(2,1)S(1)}, u32[]{:S(2)}, u32[]{:S(2)}) collective-permute-start(bf16[880,128]{1,0:T(8,128)(2,1)S(1)} %get-tuple-element.127), channel_id=1, source_target_pairs={{0,24},{2,26},{4,28},{6,30},{8,16},{10,18},{12,20},{14,22},{16,8},... | collective-permute-start | bytes 675848 | tf_op jit(solution)/shard_map/ppermute | solution.py:110
  118.1 16.0 %collective-permute-start.35 = (bf16[880,128]{1,0:T(8,128)(2,1)S(1)}, bf16[880,128]{1,0:T(8,128)(2,1)S(1)}, u32[]{:S(2)}, u32[]{:S(2)}) collective-permute-start(bf16[880,128]{1,0:T(8,128)(2,1)S(1)} %get-tuple-element.126), channel_id=1, source_target_pairs={{0,2},{1,5},{2,0},{3,7},{4,6},{5,1},{6,4},{7,3},{8,10},{9,13},{10,... | collective-permute-start | bytes 675848 | tf_op jit(solution)/shard_map/ppermute | solution.py:119
  119.5 14.6 %collective-permute-start.36 = (bf16[880,128]{1,0:T(8,128)(2,1)S(1)}, bf16[880,128]{1,0:T(8,128)(2,1)S(1)}, u32[]{:S(2)}, u32[]{:S(2)}) collective-permute-start(bf16[880,128]{1,0:T(8,128)(2,1)S(1)} %get-tuple-element.125), channel_id=1, source_target_pairs={{0,4},{1,3},{2,6},{3,1},{4,0},{5,7},{6,2},{7,5},{8,12},{9,11},{10,... | collective-permute-start | bytes 675848 | tf_op jit(solution)/shard_map/ppermute | solution.py:119
  123.9 10.3 %collective-permute-start.37 = (bf16[880,128]{1,0:T(8,128)(2,1)S(1)}, bf16[880,128]{1,0:T(8,128)(2,1)S(1)}, u32[]{:S(2)}, u32[]{:S(2)}) collective-permute-start(bf16[880,128]{1,0:T(8,128)(2,1)S(1)} %get-tuple-element.124), channel_id=1, source_target_pairs={{0,6},{1,7},{2,4},{3,5},{4,2},{5,3},{6,0},{7,1},{8,14},{9,15},{10,... | collective-permute-start | bytes 675848 | tf_op jit(solution)/shard_map/ppermute | solution.py:119
  (32 other events, 242.3 us)

commit v5 on v4

--- a/solution.py
+++ b/solution.py
@@ -212,7 +212,7 @@
 
 
 def dot_tn(left, right):
-    return dot(left.astype(F32).T.astype(BF16), right)
+    return lax.dot_general(left, right, (((0,), (0,)), ((), ())), preferred_element_type=F32)
 
 
 def row_of_head(head, which):
@@ -353,13 +353,22 @@
     load.start()
     load_cot = pltpu.make_async_copy(cot_hbm, cot_t, in_sem.at[1])
     load_cot.start()
+    planes = []
     for s in range(PLANES):
         sides = [[ref] for ref in pieces[0]]
         if s:
             sides = list(zip(pieces[s], pieces[s + 3]))
         at_plane = jnp.bitwise_xor(idx[0], s)
-        for _, copy in piece_copies(idx, at_plane, sides, w, sems.at[at_plane], False):
-            copy.start()
+        copies = piece_copies(idx, at_plane, sides, w, sems.at[at_plane], False)
+        planes.append([copy for _, copy in copies])
+    for p in range(PLANES):
+        for s in range(PLANES):
+
+            @pl.when(jnp.bitwise_xor(idx[0], s) == p)
+            def _(copies=planes[s]):
+                for copy in copies:
+                    copy.start()
+
     tokens = tok.shape[1]
     load.wait()
     x = tok[...].astype(F32).T
@@ -511,12 +520,25 @@
     fetch = [
         pltpu.make_async_copy(held[side], bounce.at[side], held_sem.at[side]) for side in range(2)
     ]
-    for copy in fetch:
-        copy.start()
+
+    @pl.when(ground)
+    def _():
+        for copy in fetch:
+            copy.start()
+
     d_mixed = dr[...]
     branch = d_mixed.astype(BF16)
     dw_out = dot_tn(att[...], branch)
     d_att = dot_nt(branch, wo[...])
+    @pl.when(ground)
+    def _():
+        for copy in fetch:
+            copy.wait()
+        for side in range(2):
+            for j in range(2):
+                source = bounce.at[side, pl.ds(2 * j, 2)]
+                pltpu.make_async_copy(source, third[2 * side + j], held_sem.at[2]).start()
+
     for b in range(tokens // SEQ_LEN):
         part = slice(SEQ_LEN * b, SEQ_LEN * (b + 1))
         cosine, sine = cos[part, :], -sin[part, :]
@@ -539,21 +561,6 @@
                 dot_tn(d_score, q3) * HEAD**-0.5, cosine, sine
             )
     dq, dk, dv = dq_ref[...].astype(BF16), dk_ref[...].astype(BF16), dv_ref[...].astype(BF16)
-    for copy in fetch:
-        copy.wait()
-
-    @pl.when(ground)
-    def _():
-        for side in range(2):
-            for j in range(2):
-                source = bounce.at[side, pl.ds(2 * j, 2)]
-                pltpu.make_async_copy(source, third[2 * side + j], held_sem.at[2]).start()
-
-    @pl.when(jnp.logical_not(ground))
-    def _():
-        for side in range(2):
-            pltpu.make_async_copy(bounce.at[side], mine[side], held_sem.at[2]).start()
-
     x = tok[...].astype(F32)
     inverse = lax.rsqrt(jnp.mean(x * x, 0, keepdims=True) + EPS)
     normed = x * inverse
@@ -598,7 +605,10 @@
     for copy in stores:
         copy.wait()
     wait_plane(g, 0, out_sems.at[0])
-    wait_plane(g, 0, held_sem.at[2])
+
+    @pl.when(ground)
+    def _():
+        wait_plane(g, 0, held_sem.at[2])
 
 
 def halves_turned(low, high):
@@ -798,7 +808,7 @@
     forward = pl.pallas_call(
         first_kernel,
         name="forward_and_ff_backward",
-        in_specs=[smem] + [anywhere] * 14 + [hbm, vmem, vmem, hbm],
+        in_specs=[smem] + [hbm] * 14 + [hbm, vmem, vmem, hbm],
         out_specs=[hbm] * len(outs) + [anywhere] * 10,
         out_shape=outs + [block] * 8 + [piece] * 2,
         scratch_shapes=[pltpu.VMEM(out.shape, out.dtype) for out in outs]
@@ -951,6 +961,7 @@
         early = [add(value[0], hop(value[1], first, n)).astype(BF16) for value in early]
         third = (add(keep_near, swap_rep(send_near)) + third.astype(F32)).astype(BF16)
         third = add(third[0], hop(third[1], first, n)).astype(BF16)
+        keep, send = [jnp.where(plane == 0, a, b) for a, b in zip((keep, send), held)]
         mine = add(keep, swap_rep(send)).astype(BF16)
 
         def pick(values, s):

time: 140 us -> 138 us (0.986)
  starting transfers between devices: 45.8 us -> 44 us
    unnamed x50 -> x54, local copies, waits for them, and re-layouts: 3.33 us -> 3.31 us
  transfers between devices with their start and end apart: 39 -> 39, of which waited for: 14 -> 14; matrix products, arithmetic and copies ran while one was open for 4% -> 4% of each run, Pallas kernels for 8% -> 7%
where the time goes in v5:
time: 138 us; the launch traced here: 137 us
  waiting for transfers between devices  51.8 us (38%)
  starting transfers between devices  44 us (32%)
  Pallas kernels  29.9 us (22%)
  other arithmetic  6.08 us (4%)
  local copies, waits for them, and re-layouts  4.45 us (3%)
    ppermute x18, starting transfers between devices, hop(): return lax.ppermute(value, ('dp', 'rep'), pairs)  26.5 us
    ppermute x18, waiting for transfers between devices, hop(): return lax.ppermute(value, ('dp', 'rep'), pairs)  26 us
    ppermute x6, waiting for transfers between devices, swap(): return lax.ppermute(value, 'dp', [(i, i ^ mask) for i in range(count)])  20.9 us
    pallas_call x1, Pallas kernels, on_device(): results = forward(idx, *pieces, tokens_in.T, *angles, cotangent.T)  16.6 us
    ppermute x6, starting transfers between devices, swap(): return lax.ppermute(value, 'dp', [(i, i ^ mask) for i in range(count)])  12.3 us
    pallas_call x1, Pallas kernels, on_device(): attention_back(idx, tokens_in.T, *angles, *saved, *held)  9.92 us
    ppermute x15, starting transfers between devices, swap_rep(): return lax.ppermute(value, 'rep', [(0, 1), (1, 0)])  5.26 us
    ppermute x15, waiting for transfers between devices, swap_rep(): return lax.ppermute(value, 'rep', [(0, 1), (1, 0)])  4.89 us
  transfers between devices with their start and end apart: 39, of which 14 were waited for; matrix products, arithmetic and copies ran while one was open for 4% of the time, Pallas kernels for 7%

profile of v5, /device:TPU:0, one launch (start us, length us, event | category | flops | bytes accessed | tf_op | source)
XLA Modules:
  0.0 137.3 jit_solution(7873775146918525796)
XLA Ops:
  3.0 2.9 %collective-permute-start = (bf16[880,128]{1,0:T(8,128)(2,1)S(1)}, bf16[880,128]{1,0:T(8,128)(2,1)S(1)}, u32[]{:S(2)}, u32[]{:S(2)}) collective-permute-start(bf16[880,128]{1,0:T(8,128)(2,1)S(1)} %pack_own_chunk.1), channel_id=1, source_target_pairs={{0,8},{2,10},{4,12},{6,14},{8,0},{10,2},{12,4},{14,6},{16,24},{18,... | collective-permute-start | bytes 675848 | tf_op jit(solution)/shard_map/ppermute | solution.py:110
  5.9 2.7 %collective-permute-start.1 = (bf16[880,128]{1,0:T(8,128)(2,1)S(1)}, bf16[880,128]{1,0:T(8,128)(2,1)S(1)}, u32[]{:S(2)}, u32[]{:S(2)}) collective-permute-start(bf16[880,128]{1,0:T(8,128)(2,1)S(1)} %pack_own_chunk.1), channel_id=1, source_target_pairs={{0,16},{2,18},{4,20},{6,22},{8,24},{10,26},{12,28},{14,30},{16,0},... | collective-permute-start | bytes 675848 | tf_op jit(solution)/shard_map/ppermute | solution.py:110
  8.6 1.8 %collective-permute-start.3 = (bf16[880,128]{1,0:T(8,128)(2,1)S(1)}, bf16[880,128]{1,0:T(8,128)(2,1)S(1)}, u32[]{:S(2)}, u32[]{:S(2)}) collective-permute-start(bf16[880,128]{1,0:T(8,128)(2,1)S(1)} %pack_own_chunk.1), channel_id=1, source_target_pairs={{0,2},{1,5},{2,0},{3,7},{4,6},{5,1},{6,4},{7,3},{8,10},{9,13},{10,... | collective-permute-start | bytes 675848 | tf_op jit(solution)/shard_map/ppermute | solution.py:119
  10.4 1.5 %collective-permute-start.4 = (bf16[880,128]{1,0:T(8,128)(2,1)S(1)}, bf16[880,128]{1,0:T(8,128)(2,1)S(1)}, u32[]{:S(2)}, u32[]{:S(2)}) collective-permute-start(bf16[880,128]{1,0:T(8,128)(2,1)S(1)} %pack_own_chunk.1), channel_id=1, source_target_pairs={{0,4},{1,3},{2,6},{3,1},{4,0},{5,7},{6,2},{7,5},{8,12},{9,11},{10,... | collective-permute-start | bytes 675848 | tf_op jit(solution)/shard_map/ppermute | solution.py:119
  11.9 3.5 %collective-permute-done = bf16[880,128]{1,0:T(8,128)(2,1)S(1)} collective-permute-done((bf16[880,128]{1,0:T(8,128)(2,1)S(1)}, bf16[880,128]{1,0:T(8,128)(2,1)S(1)}, u32[]{:S(2)}, u32[]{:S(2)}) %collective-permute-start) | collective-permute-done | bytes 225312 | tf_op jit(solution)/shard_map/ppermute | solution.py:110
  15.4 2.9 %collective-permute-start.5 = (bf16[880,128]{1,0:T(8,128)(2,1)S(1)}, bf16[880,128]{1,0:T(8,128)(2,1)S(1)}, u32[]{:S(2)}, u32[]{:S(2)}) collective-permute-start(bf16[880,128]{1,0:T(8,128)(2,1)S(1)} %pack_own_chunk.1), channel_id=1, source_target_pairs={{0,6},{1,7},{2,4},{3,5},{4,2},{5,3},{6,0},{7,1},{8,14},{9,15},{10,... | collective-permute-start | bytes 675848 | tf_op jit(solution)/shard_map/ppermute | solution.py:119
  19.0 5.9 %collective-permute-done.1 = bf16[880,128]{1,0:T(8,128)(2,1)S(1)} collective-permute-done((bf16[880,128]{1,0:T(8,128)(2,1)S(1)}, bf16[880,128]{1,0:T(8,128)(2,1)S(1)}, u32[]{:S(2)}, u32[]{:S(2)}) %collective-permute-start.1) | collective-permute-done | bytes 225312 | tf_op jit(solution)/shard_map/ppermute | solution.py:110
  24.9 1.5 %collective-permute-start.8 = (bf16[880,128]{1,0:T(8,128)(2,1)S(1)}, bf16[880,128]{1,0:T(8,128)(2,1)S(1)}, u32[]{:S(2)}, u32[]{:S(2)}) collective-permute-start(bf16[880,128]{1,0:T(8,128)(2,1)S(1)} %collective-permute-done.2), channel_id=1, source_target_pairs={{0,2},{1,5},{2,0},{3,7},{4,6},{5,1},{6,4},{7,3},{8,10},{9,13},{10,... | collective-permute-start | bytes 675848 | tf_op jit(solution)/shard_map/ppermute | solution.py:119
  28.6 2.3 %collective-permute-done.8 = bf16[880,128]{1,0:T(8,128)(2,1)S(1)} collective-permute-done((bf16[880,128]{1,0:T(8,128)(2,1)S(1)}, bf16[880,128]{1,0:T(8,128)(2,1)S(1)}, u32[]{:S(2)}, u32[]{:S(2)}) %collective-permute-start.8) | collective-permute-done | bytes 225312 | tf_op jit(solution)/shard_map/ppermute | solution.py:119
  31.0 1.5 %collective-permute-start.16 = (bf16[2,880,128]{2,1,0:T(8,128)(2,1)S(1)}, bf16[2,880,128]{2,1,0:T(8,128)(2,1)S(1)}, u32[]{:S(2)}, u32[]{:S(2)}) collective-permute-start(bf16[2,880,128]{2,1,0:T(8,128)(2,1)S(1)} %pad_maximum_fusion.3.refs_3_), channel_id=1, source_target_pairs={{0,4},{1,3},{2,6},{3,1},{4,0},{5,7},{6,2},{7,5},{8,12},{9,11},{10,... | collective-permute-start | bytes 1351688 | tf_op jit(solution)/shard_map/ppermute | solution.py:119
  32.5 2.3 %collective-permute-done.7 = bf16[880,128]{1,0:T(8,128)(2,1)S(1)} collective-permute-done((bf16[880,128]{1,0:T(8,128)(2,1)S(1)}, bf16[880,128]{1,0:T(8,128)(2,1)S(1)}, u32[]{:S(2)}, u32[]{:S(2)}) %collective-permute-start.7) | collective-permute-done | bytes 225312 | tf_op jit(solution)/shard_map/ppermute | solution.py:119
  34.9 1.4 %collective-permute-start.14 = (bf16[2,880,128]{2,1,0:T(8,128)(2,1)S(1)}, bf16[2,880,128]{2,1,0:T(8,128)(2,1)S(1)}, u32[]{:S(2)}, u32[]{:S(2)}) collective-permute-start(bf16[2,880,128]{2,1,0:T(8,128)(2,1)S(1)} %pad_maximum_fusion.2.refs_2_), channel_id=1, source_target_pairs={{0,4},{1,3},{2,6},{3,1},{4,0},{5,7},{6,2},{7,5},{8,12},{9,11},{10,... | collective-permute-start | bytes 1351688 | tf_op jit(solution)/shard_map/ppermute | solution.py:119
  36.3 3.4 %collective-permute-done.6 = bf16[880,128]{1,0:T(8,128)(2,1)S(1)} collective-permute-done((bf16[880,128]{1,0:T(8,128)(2,1)S(1)}, bf16[880,128]{1,0:T(8,128)(2,1)S(1)}, u32[]{:S(2)}, u32[]{:S(2)}) %collective-permute-start.6) | collective-permute-done | bytes 225312 | tf_op jit(solution)/shard_map/ppermute | solution.py:119
  40.7 1.4 %collective-permute-start.9 = (bf16[2,880,128]{2,1,0:T(8,128)(2,1)S(1)}, bf16[2,880,128]{2,1,0:T(8,128)(2,1)}, u32[]{:S(2)}, u32[]{:S(2)}) collective-permute-start(bf16[2,880,128]{2,1,0:T(8,128)(2,1)S(1)} %pad_maximum_fusion.1.refs_1_), channel_id=1, source_target_pairs={{0,4},{1,3},{2,6},{3,1},{4,0},{5,7},{6,2},{7,5},{8,12},{9,11},{10,... | collective-permute-start | bytes 1351688 | tf_op jit(solution)/shard_map/ppermute | solution.py:119
  42.1 2.1 %collective-permute-done.14.refs_5_ = bf16[2,880,128]{2,1,0:T(8,128)(2,1)S(1)} collective-permute-done((bf16[2,880,128]{2,1,0:T(8,128)(2,1)S(1)}, bf16[2,880,128]{2,1,0:T(8,128)(2,1)S(1)}, u32[]{:S(2)}, u32[]{:S(2)}) %collective-permute-start.14) | collective-permute-done | bytes 450592 | tf_op jit(solution)/shard_map/ppermute | solution.py:119
  45.7 3.5 %collective-permute-done.9.refs_4_ = bf16[2,880,128]{2,1,0:T(8,128)(2,1)} collective-permute-done((bf16[2,880,128]{2,1,0:T(8,128)(2,1)S(1)}, bf16[2,880,128]{2,1,0:T(8,128)(2,1)}, u32[]{:S(2)}, u32[]{:S(2)}) %collective-permute-start.9) | collective-permute-done | bytes 450592 | tf_op jit(solution)/shard_map/ppermute | solution.py:119
  52.7 1.6 %collective-permute-done.18.refs_11_ = bf16[2,880,128]{2,1,0:T(8,128)(2,1)S(1)} collective-permute-done((bf16[2,880,128]{2,1,0:T(8,128)(2,1)}, bf16[2,880,128]{2,1,0:T(8,128)(2,1)S(1)}, u32[]{:S(2)}, u32[]{:S(2)}) %collective-permute-start.18) | collective-permute-done | bytes 450592 | tf_op jit(solution)/shard_map/ppermute | solution.py:114
  55.1 16.6 %forward_and_ff_backward.1 = (f32[256,576]{1,0:T(8,128)}, f32[256,576]{1,0:T(8,128)}, f32[1,576]{1,0:T(1,128)S(1)}, bf16[256,576]{1,0:T(8,128)(2,1)}, f32[6,384,...) custom-call(s32[4]{0:T(128)S(1)} %pad_add_fusion.idx, ...), custom_call_target="tpu_custom_call" | custom-call | flops 4529848320 | bytes 8000000 | tf_op jit(solution)/shard_map/forward_and_ff_backward/pallas_call | solution.py:947
  72.3 1.5 %collective-permute-done.21 = bf16[2,880,128]{2,1,0:T(8,128)(2,1)S(1)} collective-permute-done((bf16[2,880,128]{2,1,0:T(8,128)(2,1)}, bf16[2,880,128]{2,1,0:T(8,128)(2,1)S(1)}, u32[]{:S(2)}, u32[]{:S(2)}) %collective-permute-start.21) | collective-permute-done | bytes 450592 | tf_op jit(solution)/shard_map/ppermute | solution.py:114
  73.8 2.0 %add_convert_fusion.5 = bf16[2,880,128]{2,1,0:T(8,128)(2,1)} fusion(bf16[2,880,128]{2,1,0:T(8,128)(2,1)S(1)} %collective-permute-done.21, bf16[2,880,128]{2,1,0:T(8,128)(2,1)} %get-tuple-element.98), kind=kLoop, calls=%fused_computation.6 | loop fusion | flops 901120 | bytes 1351680 | tf_op jit(solution)/shard_map/convert_element_type | solution.py:952
  75.7 1.4 %collective-permute-start.22 = (bf16[2,880,128]{2,1,0:T(8,128)(2,1)}, bf16[2,880,128]{2,1,0:T(8,128)(2,1)S(1)}, u32[]{:S(2)}, u32[]{:S(2)}) collective-permute-start(bf16[2,880,128]{2,1,0:T(8,128)(2,1)} %add_convert_fusion.5), channel_id=1, source_target_pairs={{0,4},{1,3},{2,6},{3,1},{4,0},{5,7},{6,2},{7,5},{8,12},{9,11},{10,... | collective-permute-start | bytes 1351688 | tf_op jit(solution)/shard_map/ppermute | solution.py:119
  79.2 9.9 %attention_backward.1 = (bf16[576,256]{1,0:T(8,128)(2,1)}, f32[576,256]{1,0:T(8,128)}, bf16[2,880,128]{2,1,0:T(8,128)(2,1)}, bf16[2,880,128]{2,1,0:T(8,128)(2,1)...) custom-call(s32[4]{0:T(128)S(1)} %pad_add_fusion.idx, ...), custom_call_target="tpu_custom_call" | custom-call | flops 849346560 | bytes 8000000 | tf_op jit(solution)/shard_map/attention_backward/pallas_call | solution.py:954
  89.5 1.5 %collective-permute-start.31 = (bf16[880,128]{1,0:T(8,128)(2,1)S(1)}, bf16[880,128]{1,0:T(8,128)(2,1)S(1)}, u32[]{:S(2)}, u32[]{:S(2)}) collective-permute-start(bf16[880,128]{1,0:T(8,128)(2,1)S(1)} %slice_bitcast_fusion), channel_id=1, source_target_pairs={{0,2},{1,5},{2,0},{3,7},{4,6},{5,1},{6,4},{7,3},{8,10},{9,13},{10,... | collective-permute-start | bytes 675848 | tf_op jit(solution)/shard_map/ppermute | solution.py:119
  91.8 1.6 %collective-permute-start.26 = (bf16[2,880,128]{2,1,0:T(8,128)(2,1)S(1)}, bf16[2,880,128]{2,1,0:T(8,128)(2,1)S(1)}, u32[]{:S(2)}, u32[]{:S(2)}) collective-permute-start(bf16[2,880,128]{2,1,0:T(8,128)(2,1)S(1)} %add_convert_fusion.4), channel_id=1, source_target_pairs={{0,4},{1,3},{2,6},{3,1},{4,0},{5,7},{6,2},{7,5},{8,12},{9,11},{10,... | collective-permute-start | bytes 1351688 | tf_op jit(solution)/shard_map/ppermute | solution.py:119
  94.7 8.0 %collective-permute-done.26 = bf16[2,880,128]{2,1,0:T(8,128)(2,1)S(1)} collective-permute-done((bf16[2,880,128]{2,1,0:T(8,128)(2,1)S(1)}, bf16[2,880,128]{2,1,0:T(8,128)(2,1)S(1)}, u32[]{:S(2)}, u32[]{:S(2)}) %collective-permute-start.26) | collective-permute-done | bytes 450592 | tf_op jit(solution)/shard_map/ppermute | solution.py:119
  104.6 4.4 %collective-permute-done.27 = bf16[880,128]{1,0:T(8,128)(2,1)S(1)} collective-permute-done((bf16[880,128]{1,0:T(8,128)(2,1)S(1)}, bf16[880,128]{1,0:T(8,128)(2,1)S(1)}, u32[]{:S(2)}, u32[]{:S(2)}) %collective-permute-start.27) | collective-permute-done | bytes 225312 | tf_op jit(solution)/shard_map/ppermute | solution.py:119
  109.2 4.2 %collective-permute-start.32 = (bf16[880,128]{1,0:T(8,128)(2,1)S(1)}, bf16[880,128]{1,0:T(8,128)(2,1)S(1)}, u32[]{:S(2)}, u32[]{:S(2)}) collective-permute-start(bf16[880,128]{1,0:T(8,128)(2,1)S(1)} %get-tuple-element.123), channel_id=1, source_target_pairs={{0,8},{2,10},{4,12},{6,14},{8,0},{10,2},{12,4},{14,6},{16,24},{18,... | collective-permute-start | bytes 675848 | tf_op jit(solution)/shard_map/ppermute | solution.py:110
  118.5 3.4 %collective-permute-done.32 = bf16[880,128]{1,0:T(8,128)(2,1)S(1)} collective-permute-done((bf16[880,128]{1,0:T(8,128)(2,1)S(1)}, bf16[880,128]{1,0:T(8,128)(2,1)S(1)}, u32[]{:S(2)}, u32[]{:S(2)}) %collective-permute-start.32) | collective-permute-done | bytes 225312 | tf_op jit(solution)/shard_map/ppermute | solution.py:110
  121.9 2.4 %collective-permute-start.37 = (bf16[880,128]{1,0:T(8,128)(2,1)S(1)}, bf16[880,128]{1,0:T(8,128)(2,1)S(1)}, u32[]{:S(2)}, u32[]{:S(2)}) collective-permute-start(bf16[880,128]{1,0:T(8,128)(2,1)S(1)} %get-tuple-element.124), channel_id=1, source_target_pairs={{0,6},{1,7},{2,4},{3,5},{4,2},{5,3},{6,0},{7,1},{8,14},{9,15},{10,... | collective-permute-start | bytes 675848 | tf_op jit(solution)/shard_map/ppermute | solution.py:119
  124.3 8.1 %collective-permute-done.33 = bf16[880,128]{1,0:T(8,128)(2,1)S(1)} collective-permute-done((bf16[880,128]{1,0:T(8,128)(2,1)S(1)}, bf16[880,128]{1,0:T(8,128)(2,1)S(1)}, u32[]{:S(2)}, u32[]{:S(2)}) %collective-permute-start.33) | collective-permute-done | bytes 225312 | tf_op jit(solution)/shard_map/ppermute | solution.py:110
  132.7 1.8 %collective-permute-done.38.twin = f32[880,128]{1,0:T(8,128)S(1)} collective-permute-done((f32[880,128]{1,0:T(8,128)S(1)}, f32[880,128]{1,0:T(8,128)S(1)}, u32[]{:S(2)}, u32[]{:S(2)}) %collective-permute-start.38) | collective-permute-done | bytes 450592 | tf_op jit(solution)/shard_map/ppermute | solution.py:114
  134.5 2.2 %unpack_own_chunk.1 = f32[1736,128]{1,0:T(8,128)} custom-call(s32[4]{0:T(128)S(1)} %pad_add_fusion.1.idx, f32[880,128]{1,0:T(8,128)S(1)} %fusion.3.own, f32[880,128]{1,0:T(8,128)S(1)} %collective-permute-done.38.twin), custom_call_target="tpu_custom_call" | custom-call | tf_op jit(solution)/shard_map/unpack_own_chunk/pallas_call | solution.py:759
  (131 shorter events, 25.1 us)
Async XLA Ops:
  3.0 12.5 %collective-permute-start = (bf16[880,128]{1,0:T(8,128)(2,1)S(1)}, bf16[880,128]{1,0:T(8,128)(2,1)S(1)}, u32[]{:S(2)}, u32[]{:S(2)}) collective-permute-start(bf16[880,128]{1,0:T(8,128)(2,1)S(1)} %pack_own_chunk.1), channel_id=1, source_target_pairs={{0,8},{2,10},{4,12},{6,14},{8,0},{10,2},{12,4},{14,6},{16,24},{18,... | collective-permute-start | bytes 675848 | tf_op jit(solution)/shard_map/ppermute | solution.py:110
  5.9 19.0 %collective-permute-start.1 = (bf16[880,128]{1,0:T(8,128)(2,1)S(1)}, bf16[880,128]{1,0:T(8,128)(2,1)S(1)}, u32[]{:S(2)}, u32[]{:S(2)}) collective-permute-start(bf16[880,128]{1,0:T(8,128)(2,1)S(1)} %pack_own_chunk.1), channel_id=1, source_target_pairs={{0,16},{2,18},{4,20},{6,22},{8,24},{10,26},{12,28},{14,30},{16,0},... | collective-permute-start | bytes 675848 | tf_op jit(solution)/shard_map/ppermute | solution.py:110
  8.6 16.3 %collective-permute-start.2 = (bf16[880,128]{1,0:T(8,128)(2,1)S(1)}, bf16[880,128]{1,0:T(8,128)(2,1)S(1)}, u32[]{:S(2)}, u32[]{:S(2)}) collective-permute-start(bf16[880,128]{1,0:T(8,128)(2,1)S(1)} %pack_own_chunk.1), channel_id=1, source_target_pairs={{0,24},{2,26},{4,28},{6,30},{8,16},{10,18},{12,20},{14,22},{16,8},... | collective-permute-start | bytes 675848 | tf_op jit(solution)/shard_map/ppermute | solution.py:110
  8.6 16.3 %collective-permute-start.3 = (bf16[880,128]{1,0:T(8,128)(2,1)S(1)}, bf16[880,128]{1,0:T(8,128)(2,1)S(1)}, u32[]{:S(2)}, u32[]{:S(2)}) collective-permute-start(bf16[880,128]{1,0:T(8,128)(2,1)S(1)} %pack_own_chunk.1), channel_id=1, source_target_pairs={{0,2},{1,5},{2,0},{3,7},{4,6},{5,1},{6,4},{7,3},{8,10},{9,13},{10,... | collective-permute-start | bytes 675848 | tf_op jit(solution)/shard_map/ppermute | solution.py:119
  10.4 14.5 %collective-permute-start.4 = (bf16[880,128]{1,0:T(8,128)(2,1)S(1)}, bf16[880,128]{1,0:T(8,128)(2,1)S(1)}, u32[]{:S(2)}, u32[]{:S(2)}) collective-permute-start(bf16[880,128]{1,0:T(8,128)(2,1)S(1)} %pack_own_chunk.1), channel_id=1, source_target_pairs={{0,4},{1,3},{2,6},{3,1},{4,0},{5,7},{6,2},{7,5},{8,12},{9,11},{10,... | collective-permute-start | bytes 675848 | tf_op jit(solution)/shard_map/ppermute | solution.py:119
  15.4 9.4 %collective-permute-start.5 = (bf16[880,128]{1,0:T(8,128)(2,1)S(1)}, bf16[880,128]{1,0:T(8,128)(2,1)S(1)}, u32[]{:S(2)}, u32[]{:S(2)}) collective-permute-start(bf16[880,128]{1,0:T(8,128)(2,1)S(1)} %pack_own_chunk.1), channel_id=1, source_target_pairs={{0,6},{1,7},{2,4},{3,5},{4,2},{5,3},{6,0},{7,1},{8,14},{9,15},{10,... | collective-permute-start | bytes 675848 | tf_op jit(solution)/shard_map/ppermute | solution.py:119
  24.9 6.0 %collective-permute-start.8 = (bf16[880,128]{1,0:T(8,128)(2,1)S(1)}, bf16[880,128]{1,0:T(8,128)(2,1)S(1)}, u32[]{:S(2)}, u32[]{:S(2)}) collective-permute-start(bf16[880,128]{1,0:T(8,128)(2,1)S(1)} %collective-permute-done.2), channel_id=1, source_target_pairs={{0,2},{1,5},{2,0},{3,7},{4,6},{5,1},{6,4},{7,3},{8,10},{9,13},{10,... | collective-permute-start | bytes 675848 | tf_op jit(solution)/shard_map/ppermute | solution.py:119
  26.4 8.4 %collective-permute-start.7 = (bf16[880,128]{1,0:T(8,128)(2,1)S(1)}, bf16[880,128]{1,0:T(8,128)(2,1)S(1)}, u32[]{:S(2)}, u32[]{:S(2)}) collective-permute-start(bf16[880,128]{1,0:T(8,128)(2,1)S(1)} %collective-permute-done.1), channel_id=1, source_target_pairs={{0,2},{1,5},{2,0},{3,7},{4,6},{5,1},{6,4},{7,3},{8,10},{9,13},{10,... | collective-permute-start | bytes 675848 | tf_op jit(solution)/shard_map/ppermute | solution.py:119
  27.0 12.7 %collective-permute-start.6 = (bf16[880,128]{1,0:T(8,128)(2,1)S(1)}, bf16[880,128]{1,0:T(8,128)(2,1)S(1)}, u32[]{:S(2)}, u32[]{:S(2)}) collective-permute-start(bf16[880,128]{1,0:T(8,128)(2,1)S(1)} %collective-permute-done), channel_id=1, source_target_pairs={{0,2},{1,5},{2,0},{3,7},{4,6},{5,1},{6,4},{7,3},{8,10},{9,13},{10,... | collective-permute-start | bytes 675848 | tf_op jit(solution)/shard_map/ppermute | solution.py:119
  28.5 20.7 %collective-permute-start.10 = (bf16[4,880,128]{2,1,0:T(8,128)(2,1)S(1)}, bf16[4,880,128]{2,1,0:T(8,128)(2,1)S(1)}, u32[]{:S(2)}, u32[]{:S(2)}) collective-permute-start(bf16[4,880,128]{2,1,0:T(8,128)(2,1)S(1)} %pad_maximum_fusion.refs_0_), channel_id=1, source_target_pairs={{0,1},{1,0},{2,3},{3,2},{4,5},{5,4},{6,7},{7,6},{8,9},{9,8},{10,11... | collective-permute-start | bytes 2703368 | tf_op jit(solution)/shard_map/ppermute | solution.py:114
  31.0 8.7 %collective-permute-start.16 = (bf16[2,880,128]{2,1,0:T(8,128)(2,1)S(1)}, bf16[2,880,128]{2,1,0:T(8,128)(2,1)S(1)}, u32[]{:S(2)}, u32[]{:S(2)}) collective-permute-start(bf16[2,880,128]{2,1,0:T(8,128)(2,1)S(1)} %pad_maximum_fusion.3.refs_3_), channel_id=1, source_target_pairs={{0,4},{1,3},{2,6},{3,1},{4,0},{5,7},{6,2},{7,5},{8,12},{9,11},{10,... | collective-permute-start | bytes 1351688 | tf_op jit(solution)/shard_map/ppermute | solution.py:119
  32.5 8.2 %collective-permute-start.13 = (bf16[2,880,128]{2,1,0:T(8,128)(2,1)S(1)}, bf16[2,880,128]{2,1,0:T(8,128)(2,1)S(1)}, u32[]{:S(2)}, u32[]{:S(2)}) collective-permute-start(bf16[2,880,128]{2,1,0:T(8,128)(2,1)S(1)} %pad_maximum_fusion.3.refs_3_), channel_id=1, source_target_pairs={{0,1},{1,0},{2,3},{3,2},{4,5},{5,4},{6,7},{7,6},{8,9},{9,8},{10,11... | collective-permute-start | bytes 1351688 | tf_op jit(solution)/shard_map/ppermute | solution.py:114
  34.9 9.4 %collective-permute-start.14 = (bf16[2,880,128]{2,1,0:T(8,128)(2,1)S(1)}, bf16[2,880,128]{2,1,0:T(8,128)(2,1)S(1)}, u32[]{:S(2)}, u32[]{:S(2)}) collective-permute-start(bf16[2,880,128]{2,1,0:T(8,128)(2,1)S(1)} %pad_maximum_fusion.2.refs_2_), channel_id=1, source_target_pairs={{0,4},{1,3},{2,6},{3,1},{4,0},{5,7},{6,2},{7,5},{8,12},{9,11},{10,... | collective-permute-start | bytes 1351688 | tf_op jit(solution)/shard_map/ppermute | solution.py:119
  39.6 6.0 %collective-permute-start.12 = (bf16[2,880,128]{2,1,0:T(8,128)(2,1)S(1)}, bf16[2,880,128]{2,1,0:T(8,128)(2,1)S(1)}, u32[]{:S(2)}, u32[]{:S(2)}) collective-permute-start(bf16[2,880,128]{2,1,0:T(8,128)(2,1)S(1)} %pad_maximum_fusion.2.refs_2_), channel_id=1, source_target_pairs={{0,1},{1,0},{2,3},{3,2},{4,5},{5,4},{6,7},{7,6},{8,9},{9,8},{10,11... | collective-permute-start | bytes 1351688 | tf_op jit(solution)/shard_map/ppermute | solution.py:114
  39.7 6.0 %collective-permute-start.11 = (bf16[2,880,128]{2,1,0:T(8,128)(2,1)S(1)}, bf16[2,880,128]{2,1,0:T(8,128)(2,1)S(1)}, u32[]{:S(2)}, u32[]{:S(2)}) collective-permute-start(bf16[2,880,128]{2,1,0:T(8,128)(2,1)S(1)} %pad_maximum_fusion.1.refs_1_), channel_id=1, source_target_pairs={{0,1},{1,0},{2,3},{3,2},{4,5},{5,4},{6,7},{7,6},{8,9},{9,8},{10,11... | collective-permute-start | bytes 1351688 | tf_op jit(solution)/shard_map/ppermute | solution.py:114
  40.7 8.5 %collective-permute-start.9 = (bf16[2,880,128]{2,1,0:T(8,128)(2,1)S(1)}, bf16[2,880,128]{2,1,0:T(8,128)(2,1)}, u32[]{:S(2)}, u32[]{:S(2)}) collective-permute-start(bf16[2,880,128]{2,1,0:T(8,128)(2,1)S(1)} %pad_maximum_fusion.1.refs_1_), channel_id=1, source_target_pairs={{0,4},{1,3},{2,6},{3,1},{4,0},{5,7},{6,2},{7,5},{8,12},{9,11},{10,... | collective-permute-start | bytes 1351688 | tf_op jit(solution)/shard_map/ppermute | solution.py:119
  44.3 5.9 %collective-permute-start.17 = (bf16[2,880,128]{2,1,0:T(8,128)(2,1)S(1)}, bf16[2,880,128]{2,1,0:T(8,128)(2,1)S(1)}, u32[]{:S(2)}, u32[]{:S(2)}) collective-permute-start(bf16[2,880,128]{2,1,0:T(8,128)(2,1)S(1)} %collective-permute-done.16.refs_6_), channel_id=1, source_target_pairs={{0,1},{1,0},{2,3},{3,2},{4,5},{5,4},{6,7},{7,6},{8,9},{9,8},{10,11... | collective-permute-start | bytes 1351688 | tf_op jit(solution)/shard_map/ppermute | solution.py:114
  75.7 13.4 %collective-permute-start.22 = (bf16[2,880,128]{2,1,0:T(8,128)(2,1)}, bf16[2,880,128]{2,1,0:T(8,128)(2,1)S(1)}, u32[]{:S(2)}, u32[]{:S(2)}) collective-permute-start(bf16[2,880,128]{2,1,0:T(8,128)(2,1)} %add_convert_fusion.5), channel_id=1, source_target_pairs={{0,4},{1,3},{2,6},{3,1},{4,0},{5,7},{6,2},{7,5},{8,12},{9,11},{10,... | collective-permute-start | bytes 1351688 | tf_op jit(solution)/shard_map/ppermute | solution.py:119
  78.1 11.1 %collective-permute-start.20 = (bf16[2,880,128]{2,1,0:T(8,128)(2,1)}, bf16[2,880,128]{2,1,0:T(8,128)(2,1)S(1)}, u32[]{:S(2)}, u32[]{:S(2)}) collective-permute-start(bf16[2,880,128]{2,1,0:T(8,128)(2,1)} %add_convert_fusion.6), channel_id=1, source_target_pairs={{0,4},{1,3},{2,6},{3,1},{4,0},{5,7},{6,2},{7,5},{8,12},{9,11},{10,... | collective-permute-start | bytes 1351688 | tf_op jit(solution)/shard_map/ppermute | solution.py:119
  78.7 10.6 %collective-permute-start.30 = (bf16[2,880,128]{2,1,0:T(8,128)(2,1)}, bf16[2,880,128]{2,1,0:T(8,128)(2,1)S(1)}, u32[]{:S(2)}, u32[]{:S(2)}) collective-permute-start(bf16[2,880,128]{2,1,0:T(8,128)(2,1)} %get-tuple-element.114), channel_id=1, source_target_pairs={{0,1},{1,0},{2,3},{3,2},{4,5},{5,4},{6,7},{7,6},{8,9},{9,8},{10,11... | collective-permute-start | bytes 1351688 | tf_op jit(solution)/shard_map/ppermute | solution.py:114
  78.7 14.7 %collective-permute-start.28 = (bf16[2,880,128]{2,1,0:T(8,128)(2,1)}, bf16[2,880,128]{2,1,0:T(8,128)(2,1)S(1)}, u32[]{:S(2)}, u32[]{:S(2)}) collective-permute-start(bf16[2,880,128]{2,1,0:T(8,128)(2,1)} %get-tuple-element.110), channel_id=1, source_target_pairs={{0,1},{1,0},{2,3},{3,2},{4,5},{5,4},{6,7},{7,6},{8,9},{9,8},{10,11... | collective-permute-start | bytes 1351688 | tf_op jit(solution)/shard_map/ppermute | solution.py:114
  89.5 19.5 %collective-permute-start.31 = (bf16[880,128]{1,0:T(8,128)(2,1)S(1)}, bf16[880,128]{1,0:T(8,128)(2,1)S(1)}, u32[]{:S(2)}, u32[]{:S(2)}) collective-permute-start(bf16[880,128]{1,0:T(8,128)(2,1)S(1)} %slice_bitcast_fusion), channel_id=1, source_target_pairs={{0,2},{1,5},{2,0},{3,7},{4,6},{5,1},{6,4},{7,3},{8,10},{9,13},{10,... | collective-permute-start | bytes 675848 | tf_op jit(solution)/shard_map/ppermute | solution.py:119
  91.3 12.9 %collective-permute-start.23 = (bf16[4,880,128]{2,1,0:T(8,128)(2,1)S(1)}, bf16[4,880,128]{2,1,0:T(8,128)(2,1)S(1)}, u32[]{:S(2)}, u32[]{:S(2)}) collective-permute-start(bf16[4,880,128]{2,1,0:T(8,128)(2,1)S(1)} %broadcast_select_fusion), channel_id=1, source_target_pairs={{0,1},{1,0},{2,3},{3,2},{4,5},{5,4},{6,7},{7,6},{8,9},{9,8},{10,11... | collective-permute-start | bytes 2703368 | tf_op jit(solution)/shard_map/ppermute | solution.py:114
  91.8 10.9 %collective-permute-start.26 = (bf16[2,880,128]{2,1,0:T(8,128)(2,1)S(1)}, bf16[2,880,128]{2,1,0:T(8,128)(2,1)S(1)}, u32[]{:S(2)}, u32[]{:S(2)}) collective-permute-start(bf16[2,880,128]{2,1,0:T(8,128)(2,1)S(1)} %add_convert_fusion.4), channel_id=1, source_target_pairs={{0,4},{1,3},{2,6},{3,1},{4,0},{5,7},{6,2},{7,5},{8,12},{9,11},{10,... | collective-permute-start | bytes 1351688 | tf_op jit(solution)/shard_map/ppermute | solution.py:119
  93.6 15.4 %collective-permute-start.29 = (bf16[880,128]{1,0:T(8,128)(2,1)S(1)}, bf16[880,128]{1,0:T(8,128)(2,1)S(1)}, u32[]{:S(2)}, u32[]{:S(2)}) collective-permute-start(bf16[880,128]{1,0:T(8,128)(2,1)S(1)} %slice_bitcast_fusion.2), channel_id=1, source_target_pairs={{0,2},{1,5},{2,0},{3,7},{4,6},{5,1},{6,4},{7,3},{8,10},{9,13},{10,... | collective-permute-start | bytes 675848 | tf_op jit(solution)/shard_map/ppermute | solution.py:119
  102.9 6.0 %collective-permute-start.27 = (bf16[880,128]{1,0:T(8,128)(2,1)S(1)}, bf16[880,128]{1,0:T(8,128)(2,1)S(1)}, u32[]{:S(2)}, u32[]{:S(2)}) collective-permute-start(bf16[880,128]{1,0:T(8,128)(2,1)S(1)} %slice_bitcast_fusion.4), channel_id=1, source_target_pairs={{0,2},{1,5},{2,0},{3,7},{4,6},{5,1},{6,4},{7,3},{8,10},{9,13},{10,... | collective-permute-start | bytes 675848 | tf_op jit(solution)/shard_map/ppermute | solution.py:119
  109.2 12.7 %collective-permute-start.32 = (bf16[880,128]{1,0:T(8,128)(2,1)S(1)}, bf16[880,128]{1,0:T(8,128)(2,1)S(1)}, u32[]{:S(2)}, u32[]{:S(2)}) collective-permute-start(bf16[880,128]{1,0:T(8,128)(2,1)S(1)} %get-tuple-element.123), channel_id=1, source_target_pairs={{0,8},{2,10},{4,12},{6,14},{8,0},{10,2},{12,4},{14,6},{16,24},{18,... | collective-permute-start | bytes 675848 | tf_op jit(solution)/shard_map/ppermute | solution.py:110
  113.4 19.0 %collective-permute-start.33 = (bf16[880,128]{1,0:T(8,128)(2,1)S(1)}, bf16[880,128]{1,0:T(8,128)(2,1)S(1)}, u32[]{:S(2)}, u32[]{:S(2)}) collective-permute-start(bf16[880,128]{1,0:T(8,128)(2,1)S(1)} %get-tuple-element.122), channel_id=1, source_target_pairs={{0,16},{2,18},{4,20},{6,22},{8,24},{10,26},{12,28},{14,30},{16,0},... | collective-permute-start | bytes 675848 | tf_op jit(solution)/shard_map/ppermute | solution.py:110
  114.5 17.9 %collective-permute-start.34 = (bf16[880,128]{1,0:T(8,128)(2,1)S(1)}, bf16[880,128]{1,0:T(8,128)(2,1)S(1)}, u32[]{:S(2)}, u32[]{:S(2)}) collective-permute-start(bf16[880,128]{1,0:T(8,128)(2,1)S(1)} %get-tuple-element.127), channel_id=1, source_target_pairs={{0,24},{2,26},{4,28},{6,30},{8,16},{10,18},{12,20},{14,22},{16,8},... | collective-permute-start | bytes 675848 | tf_op jit(solution)/shard_map/ppermute | solution.py:110
  115.9 16.5 %collective-permute-start.35 = (bf16[880,128]{1,0:T(8,128)(2,1)S(1)}, bf16[880,128]{1,0:T(8,128)(2,1)S(1)}, u32[]{:S(2)}, u32[]{:S(2)}) collective-permute-start(bf16[880,128]{1,0:T(8,128)(2,1)S(1)} %get-tuple-element.126), channel_id=1, source_target_pairs={{0,2},{1,5},{2,0},{3,7},{4,6},{5,1},{6,4},{7,3},{8,10},{9,13},{10,... | collective-permute-start | bytes 675848 | tf_op jit(solution)/shard_map/ppermute | solution.py:119
  117.2 15.2 %collective-permute-start.36 = (bf16[880,128]{1,0:T(8,128)(2,1)S(1)}, bf16[880,128]{1,0:T(8,128)(2,1)S(1)}, u32[]{:S(2)}, u32[]{:S(2)}) collective-permute-start(bf16[880,128]{1,0:T(8,128)(2,1)S(1)} %get-tuple-element.125), channel_id=1, source_target_pairs={{0,4},{1,3},{2,6},{3,1},{4,0},{5,7},{6,2},{7,5},{8,12},{9,11},{10,... | collective-permute-start | bytes 675848 | tf_op jit(solution)/shard_map/ppermute | solution.py:119
  121.9 10.5 %collective-permute-start.37 = (bf16[880,128]{1,0:T(8,128)(2,1)S(1)}, bf16[880,128]{1,0:T(8,128)(2,1)S(1)}, u32[]{:S(2)}, u32[]{:S(2)}) collective-permute-start(bf16[880,128]{1,0:T(8,128)(2,1)S(1)} %get-tuple-element.124), channel_id=1, source_target_pairs={{0,6},{1,7},{2,4},{3,5},{4,2},{5,3},{6,0},{7,1},{8,14},{9,15},{10,... | collective-permute-start | bytes 675848 | tf_op jit(solution)/shard_map/ppermute | solution.py:119
  (34 other events, 251.9 us)

commit v6 on v5

--- a/solution.py
+++ b/solution.py
@@ -852,7 +852,7 @@
             pltpu.SemaphoreType.DMA((1,)),
             pltpu.SemaphoreType.DMA((3,)),
         ],
-        compiler_params=params,
+        compiler_params=pltpu.CompilerParams(vmem_limit_bytes=60 * 1024 * 1024),
         cost_estimate=cost(10 * length * width * width),
     )
     return forward, attention_back

time: 138 us -> 137 us (level)
  other arithmetic: 6.08 us -> 4.52 us
    convert_element_type x2, other arithmetic: 2.86 us -> 1.31 us  [on_device(): add(far, swap_rep(send)).astype(BF16)]
    unnamed x54 -> x72, local copies, waits for them, and re-layouts: 3.31 us -> 3.38 us
  transfers between devices with their start and end apart: 39 -> 39, of which waited for: 14 -> 14; matrix products, arithmetic and copies ran while one was open for 4% -> 3% of each run, Pallas kernels for 7% -> 8%
where the time goes in v6:
time: 137 us; the launch traced here: 136 us
  waiting for transfers between devices  51.7 us (38%)
  starting transfers between devices  44.1 us (32%)
  Pallas kernels  30.3 us (22%)
  local copies, waits for them, and re-layouts  4.52 us (3%)
  other arithmetic  4.52 us (3%)
    ppermute x18, starting transfers between devices, hop(): return lax.ppermute(value, ('dp', 'rep'), pairs)  26.7 us
    ppermute x18, waiting for transfers between devices, hop(): return lax.ppermute(value, ('dp', 'rep'), pairs)  26 us
    ppermute x6, waiting for transfers between devices, swap(): return lax.ppermute(value, 'dp', [(i, i ^ mask) for i in range(count)])  20.8 us
    pallas_call x1, Pallas kernels, on_device(): results = forward(idx, *pieces, tokens_in.T, *angles, cotangent.T)  16.5 us
    ppermute x6, starting transfers between devices, swap(): return lax.ppermute(value, 'dp', [(i, i ^ mask) for i in range(count)])  12.2 us
    pallas_call x1, Pallas kernels, on_device(): attention_back(idx, tokens_in.T, *angles, *saved, *held)  10.4 us
    ppermute x15, starting transfers between devices, swap_rep(): return lax.ppermute(value, 'rep', [(0, 1), (1, 0)])  5.26 us
    ppermute x15, waiting for transfers between devices, swap_rep(): return lax.ppermute(value, 'rep', [(0, 1), (1, 0)])  4.89 us
  transfers between devices with their start and end apart: 39, of which 14 were waited for; matrix products, arithmetic and copies ran while one was open for 3% of the time, Pallas kernels for 8%

profile of v6, /device:TPU:0, one launch (start us, length us, event | category | flops | bytes accessed | tf_op | source)
XLA Modules:
  0.0 136.4 jit_solution(652911227523140084)
XLA Ops:
  3.0 2.9 %collective-permute-start = (bf16[880,128]{1,0:T(8,128)(2,1)S(1)}, bf16[880,128]{1,0:T(8,128)(2,1)S(1)}, u32[]{:S(2)}, u32[]{:S(2)}) collective-permute-start(bf16[880,128]{1,0:T(8,128)(2,1)S(1)} %pack_own_chunk.1), channel_id=1, source_target_pairs={{0,8},{2,10},{4,12},{6,14},{8,0},{10,2},{12,4},{14,6},{16,24},{18,... | collective-permute-start | bytes 675848 | tf_op jit(solution)/shard_map/ppermute | solution.py:110
  5.9 2.7 %collective-permute-start.1 = (bf16[880,128]{1,0:T(8,128)(2,1)S(1)}, bf16[880,128]{1,0:T(8,128)(2,1)S(1)}, u32[]{:S(2)}, u32[]{:S(2)}) collective-permute-start(bf16[880,128]{1,0:T(8,128)(2,1)S(1)} %pack_own_chunk.1), channel_id=1, source_target_pairs={{0,16},{2,18},{4,20},{6,22},{8,24},{10,26},{12,28},{14,30},{16,0},... | collective-permute-start | bytes 675848 | tf_op jit(solution)/shard_map/ppermute | solution.py:110
  8.6 1.8 %collective-permute-start.3 = (bf16[880,128]{1,0:T(8,128)(2,1)S(1)}, bf16[880,128]{1,0:T(8,128)(2,1)S(1)}, u32[]{:S(2)}, u32[]{:S(2)}) collective-permute-start(bf16[880,128]{1,0:T(8,128)(2,1)S(1)} %pack_own_chunk.1), channel_id=1, source_target_pairs={{0,2},{1,5},{2,0},{3,7},{4,6},{5,1},{6,4},{7,3},{8,10},{9,13},{10,... | collective-permute-start | bytes 675848 | tf_op jit(solution)/shard_map/ppermute | solution.py:119
  10.4 1.5 %collective-permute-start.4 = (bf16[880,128]{1,0:T(8,128)(2,1)S(1)}, bf16[880,128]{1,0:T(8,128)(2,1)S(1)}, u32[]{:S(2)}, u32[]{:S(2)}) collective-permute-start(bf16[880,128]{1,0:T(8,128)(2,1)S(1)} %pack_own_chunk.1), channel_id=1, source_target_pairs={{0,4},{1,3},{2,6},{3,1},{4,0},{5,7},{6,2},{7,5},{8,12},{9,11},{10,... | collective-permute-start | bytes 675848 | tf_op jit(solution)/shard_map/ppermute | solution.py:119
  11.9 3.5 %collective-permute-done = bf16[880,128]{1,0:T(8,128)(2,1)S(1)} collective-permute-done((bf16[880,128]{1,0:T(8,128)(2,1)S(1)}, bf16[880,128]{1,0:T(8,128)(2,1)S(1)}, u32[]{:S(2)}, u32[]{:S(2)}) %collective-permute-start) | collective-permute-done | bytes 225312 | tf_op jit(solution)/shard_map/ppermute | solution.py:110
  15.4 2.9 %collective-permute-start.5 = (bf16[880,128]{1,0:T(8,128)(2,1)S(1)}, bf16[880,128]{1,0:T(8,128)(2,1)S(1)}, u32[]{:S(2)}, u32[]{:S(2)}) collective-permute-start(bf16[880,128]{1,0:T(8,128)(2,1)S(1)} %pack_own_chunk.1), channel_id=1, source_target_pairs={{0,6},{1,7},{2,4},{3,5},{4,2},{5,3},{6,0},{7,1},{8,14},{9,15},{10,... | collective-permute-start | bytes 675848 | tf_op jit(solution)/shard_map/ppermute | solution.py:119
  19.0 5.9 %collective-permute-done.1 = bf16[880,128]{1,0:T(8,128)(2,1)S(1)} collective-permute-done((bf16[880,128]{1,0:T(8,128)(2,1)S(1)}, bf16[880,128]{1,0:T(8,128)(2,1)S(1)}, u32[]{:S(2)}, u32[]{:S(2)}) %collective-permute-start.1) | collective-permute-done | bytes 225312 | tf_op jit(solution)/shard_map/ppermute | solution.py:110
  24.9 1.5 %collective-permute-start.8 = (bf16[880,128]{1,0:T(8,128)(2,1)S(1)}, bf16[880,128]{1,0:T(8,128)(2,1)S(1)}, u32[]{:S(2)}, u32[]{:S(2)}) collective-permute-start(bf16[880,128]{1,0:T(8,128)(2,1)S(1)} %collective-permute-done.2), channel_id=1, source_target_pairs={{0,2},{1,5},{2,0},{3,7},{4,6},{5,1},{6,4},{7,3},{8,10},{9,13},{10,... | collective-permute-start | bytes 675848 | tf_op jit(solution)/shard_map/ppermute | solution.py:119
  27.0 1.4 %collective-permute-start.6 = (bf16[880,128]{1,0:T(8,128)(2,1)S(1)}, bf16[880,128]{1,0:T(8,128)(2,1)S(1)}, u32[]{:S(2)}, u32[]{:S(2)}) collective-permute-start(bf16[880,128]{1,0:T(8,128)(2,1)S(1)} %collective-permute-done), channel_id=1, source_target_pairs={{0,2},{1,5},{2,0},{3,7},{4,6},{5,1},{6,4},{7,3},{8,10},{9,13},{10,... | collective-permute-start | bytes 675848 | tf_op jit(solution)/shard_map/ppermute | solution.py:119
  28.6 2.3 %collective-permute-done.8 = bf16[880,128]{1,0:T(8,128)(2,1)S(1)} collective-permute-done((bf16[880,128]{1,0:T(8,128)(2,1)S(1)}, bf16[880,128]{1,0:T(8,128)(2,1)S(1)}, u32[]{:S(2)}, u32[]{:S(2)}) %collective-permute-start.8) | collective-permute-done | bytes 225312 | tf_op jit(solution)/shard_map/ppermute | solution.py:119
  31.0 1.5 %collective-permute-start.16 = (bf16[2,880,128]{2,1,0:T(8,128)(2,1)S(1)}, bf16[2,880,128]{2,1,0:T(8,128)(2,1)S(1)}, u32[]{:S(2)}, u32[]{:S(2)}) collective-permute-start(bf16[2,880,128]{2,1,0:T(8,128)(2,1)S(1)} %pad_maximum_fusion.3.refs_3_), channel_id=1, source_target_pairs={{0,4},{1,3},{2,6},{3,1},{4,0},{5,7},{6,2},{7,5},{8,12},{9,11},{10,... | collective-permute-start | bytes 1351688 | tf_op jit(solution)/shard_map/ppermute | solution.py:119
  32.5 2.3 %collective-permute-done.7 = bf16[880,128]{1,0:T(8,128)(2,1)S(1)} collective-permute-done((bf16[880,128]{1,0:T(8,128)(2,1)S(1)}, bf16[880,128]{1,0:T(8,128)(2,1)S(1)}, u32[]{:S(2)}, u32[]{:S(2)}) %collective-permute-start.7) | collective-permute-done | bytes 225312 | tf_op jit(solution)/shard_map/ppermute | solution.py:119
  34.9 1.4 %collective-permute-start.14 = (bf16[2,880,128]{2,1,0:T(8,128)(2,1)S(1)}, bf16[2,880,128]{2,1,0:T(8,128)(2,1)S(1)}, u32[]{:S(2)}, u32[]{:S(2)}) collective-permute-start(bf16[2,880,128]{2,1,0:T(8,128)(2,1)S(1)} %pad_maximum_fusion.2.refs_2_), channel_id=1, source_target_pairs={{0,4},{1,3},{2,6},{3,1},{4,0},{5,7},{6,2},{7,5},{8,12},{9,11},{10,... | collective-permute-start | bytes 1351688 | tf_op jit(solution)/shard_map/ppermute | solution.py:119
  36.3 3.4 %collective-permute-done.6 = bf16[880,128]{1,0:T(8,128)(2,1)S(1)} collective-permute-done((bf16[880,128]{1,0:T(8,128)(2,1)S(1)}, bf16[880,128]{1,0:T(8,128)(2,1)S(1)}, u32[]{:S(2)}, u32[]{:S(2)}) %collective-permute-start.6) | collective-permute-done | bytes 225312 | tf_op jit(solution)/shard_map/ppermute | solution.py:119
  40.7 1.4 %collective-permute-start.9 = (bf16[2,880,128]{2,1,0:T(8,128)(2,1)S(1)}, bf16[2,880,128]{2,1,0:T(8,128)(2,1)}, u32[]{:S(2)}, u32[]{:S(2)}) collective-permute-start(bf16[2,880,128]{2,1,0:T(8,128)(2,1)S(1)} %pad_maximum_fusion.1.refs_1_), channel_id=1, source_target_pairs={{0,4},{1,3},{2,6},{3,1},{4,0},{5,7},{6,2},{7,5},{8,12},{9,11},{10,... | collective-permute-start | bytes 1351688 | tf_op jit(solution)/shard_map/ppermute | solution.py:119
  42.1 2.1 %collective-permute-done.14.refs_5_ = bf16[2,880,128]{2,1,0:T(8,128)(2,1)S(1)} collective-permute-done((bf16[2,880,128]{2,1,0:T(8,128)(2,1)S(1)}, bf16[2,880,128]{2,1,0:T(8,128)(2,1)S(1)}, u32[]{:S(2)}, u32[]{:S(2)}) %collective-permute-start.14) | collective-permute-done | bytes 450592 | tf_op jit(solution)/shard_map/ppermute | solution.py:119
  45.7 3.5 %collective-permute-done.9.refs_4_ = bf16[2,880,128]{2,1,0:T(8,128)(2,1)} collective-permute-done((bf16[2,880,128]{2,1,0:T(8,128)(2,1)S(1)}, bf16[2,880,128]{2,1,0:T(8,128)(2,1)}, u32[]{:S(2)}, u32[]{:S(2)}) %collective-permute-start.9) | collective-permute-done | bytes 450592 | tf_op jit(solution)/shard_map/ppermute | solution.py:119
  52.8 1.6 %collective-permute-done.18.refs_11_ = bf16[2,880,128]{2,1,0:T(8,128)(2,1)S(1)} collective-permute-done((bf16[2,880,128]{2,1,0:T(8,128)(2,1)}, bf16[2,880,128]{2,1,0:T(8,128)(2,1)S(1)}, u32[]{:S(2)}, u32[]{:S(2)}) %collective-permute-start.18) | collective-permute-done | bytes 450592 | tf_op jit(solution)/shard_map/ppermute | solution.py:114
  55.1 16.5 %forward_and_ff_backward.1 = (f32[256,576]{1,0:T(8,128)}, f32[256,576]{1,0:T(8,128)}, f32[1,576]{1,0:T(1,128)S(1)}, bf16[256,576]{1,0:T(8,128)(2,1)}, f32[6,384,...) custom-call(s32[4]{0:T(128)S(1)} %pad_add_fusion.idx, ...), custom_call_target="tpu_custom_call" | custom-call | flops 4529848320 | bytes 8000000 | tf_op jit(solution)/shard_map/forward_and_ff_backward/pallas_call | solution.py:947
  72.3 1.5 %collective-permute-done.21 = bf16[2,880,128]{2,1,0:T(8,128)(2,1)S(1)} collective-permute-done((bf16[2,880,128]{2,1,0:T(8,128)(2,1)}, bf16[2,880,128]{2,1,0:T(8,128)(2,1)S(1)}, u32[]{:S(2)}, u32[]{:S(2)}) %collective-permute-start.21) | collective-permute-done | bytes 450592 | tf_op jit(solution)/shard_map/ppermute | solution.py:114
  75.0 1.5 %collective-permute-start.22 = (bf16[2,880,128]{2,1,0:T(8,128)(2,1)S(1)}, bf16[2,880,128]{2,1,0:T(8,128)(2,1)S(1)}, u32[]{:S(2)}, u32[]{:S(2)}) collective-permute-start(bf16[2,880,128]{2,1,0:T(8,128)(2,1)S(1)} %add_convert_fusion.5), channel_id=1, source_target_pairs={{0,4},{1,3},{2,6},{3,1},{4,0},{5,7},{6,2},{7,5},{8,12},{9,11},{10,... | collective-permute-start | bytes 1351688 | tf_op jit(solution)/shard_map/ppermute | solution.py:119
  77.9 10.4 %attention_backward.1 = (bf16[576,256]{1,0:T(8,128)(2,1)}, f32[576,256]{1,0:T(8,128)}, bf16[2,880,128]{2,1,0:T(8,128)(2,1)}, bf16[2,880,128]{2,1,0:T(8,128)(2,1)...) custom-call(s32[4]{0:T(128)} %copy-done.9, ...), custom_call_target="tpu_custom_call" | custom-call | flops 849346560 | bytes 8000000 | tf_op jit(solution)/shard_map/attention_backward/pallas_call | solution.py:954
  88.7 1.5 %collective-permute-start.31 = (bf16[880,128]{1,0:T(8,128)(2,1)S(1)}, bf16[880,128]{1,0:T(8,128)(2,1)S(1)}, u32[]{:S(2)}, u32[]{:S(2)}) collective-permute-start(bf16[880,128]{1,0:T(8,128)(2,1)S(1)} %slice_bitcast_fusion), channel_id=1, source_target_pairs={{0,2},{1,5},{2,0},{3,7},{4,6},{5,1},{6,4},{7,3},{8,10},{9,13},{10,... | collective-permute-start | bytes 675848 | tf_op jit(solution)/shard_map/ppermute | solution.py:119
  91.0 1.6 %collective-permute-start.26 = (bf16[2,880,128]{2,1,0:T(8,128)(2,1)S(1)}, bf16[2,880,128]{2,1,0:T(8,128)(2,1)S(1)}, u32[]{:S(2)}, u32[]{:S(2)}) collective-permute-start(bf16[2,880,128]{2,1,0:T(8,128)(2,1)S(1)} %add_convert_fusion.4), channel_id=1, source_target_pairs={{0,4},{1,3},{2,6},{3,1},{4,0},{5,7},{6,2},{7,5},{8,12},{9,11},{10,... | collective-permute-start | bytes 1351688 | tf_op jit(solution)/shard_map/ppermute | solution.py:119
  93.9 8.0 %collective-permute-done.26 = bf16[2,880,128]{2,1,0:T(8,128)(2,1)S(1)} collective-permute-done((bf16[2,880,128]{2,1,0:T(8,128)(2,1)S(1)}, bf16[2,880,128]{2,1,0:T(8,128)(2,1)S(1)}, u32[]{:S(2)}, u32[]{:S(2)}) %collective-permute-start.26) | collective-permute-done | bytes 450592 | tf_op jit(solution)/shard_map/ppermute | solution.py:119
  103.7 4.4 %collective-permute-done.27 = bf16[880,128]{1,0:T(8,128)(2,1)S(1)} collective-permute-done((bf16[880,128]{1,0:T(8,128)(2,1)S(1)}, bf16[880,128]{1,0:T(8,128)(2,1)S(1)}, u32[]{:S(2)}, u32[]{:S(2)}) %collective-permute-start.27) | collective-permute-done | bytes 225312 | tf_op jit(solution)/shard_map/ppermute | solution.py:119
  108.4 4.1 %collective-permute-start.32 = (bf16[880,128]{1,0:T(8,128)(2,1)S(1)}, bf16[880,128]{1,0:T(8,128)(2,1)S(1)}, u32[]{:S(2)}, u32[]{:S(2)}) collective-permute-start(bf16[880,128]{1,0:T(8,128)(2,1)S(1)} %get-tuple-element.123), channel_id=1, source_target_pairs={{0,8},{2,10},{4,12},{6,14},{8,0},{10,2},{12,4},{14,6},{16,24},{18,... | collective-permute-start | bytes 675848 | tf_op jit(solution)/shard_map/ppermute | solution.py:110
  117.6 3.3 %collective-permute-done.32 = bf16[880,128]{1,0:T(8,128)(2,1)S(1)} collective-permute-done((bf16[880,128]{1,0:T(8,128)(2,1)S(1)}, bf16[880,128]{1,0:T(8,128)(2,1)S(1)}, u32[]{:S(2)}, u32[]{:S(2)}) %collective-permute-start.32) | collective-permute-done | bytes 225312 | tf_op jit(solution)/shard_map/ppermute | solution.py:110
  121.0 2.4 %collective-permute-start.37 = (bf16[880,128]{1,0:T(8,128)(2,1)S(1)}, bf16[880,128]{1,0:T(8,128)(2,1)S(1)}, u32[]{:S(2)}, u32[]{:S(2)}) collective-permute-start(bf16[880,128]{1,0:T(8,128)(2,1)S(1)} %get-tuple-element.124), channel_id=1, source_target_pairs={{0,6},{1,7},{2,4},{3,5},{4,2},{5,3},{6,0},{7,1},{8,14},{9,15},{10,... | collective-permute-start | bytes 675848 | tf_op jit(solution)/shard_map/ppermute | solution.py:119
  123.4 8.1 %collective-permute-done.33 = bf16[880,128]{1,0:T(8,128)(2,1)S(1)} collective-permute-done((bf16[880,128]{1,0:T(8,128)(2,1)S(1)}, bf16[880,128]{1,0:T(8,128)(2,1)S(1)}, u32[]{:S(2)}, u32[]{:S(2)}) %collective-permute-start.33) | collective-permute-done | bytes 225312 | tf_op jit(solution)/shard_map/ppermute | solution.py:110
  131.8 1.8 %collective-permute-done.38.twin = f32[880,128]{1,0:T(8,128)S(1)} collective-permute-done((f32[880,128]{1,0:T(8,128)S(1)}, f32[880,128]{1,0:T(8,128)S(1)}, u32[]{:S(2)}, u32[]{:S(2)}) %collective-permute-start.38) | collective-permute-done | bytes 450592 | tf_op jit(solution)/shard_map/ppermute | solution.py:114
  133.6 2.2 %unpack_own_chunk.1 = f32[1736,128]{1,0:T(8,128)} custom-call(s32[4]{0:T(128)S(1)} %pad_add_fusion.1.idx, f32[880,128]{1,0:T(8,128)S(1)} %fusion.3.own, f32[880,128]{1,0:T(8,128)S(1)} %collective-permute-done.38.twin), custom_call_target="tpu_custom_call" | custom-call | tf_op jit(solution)/shard_map/unpack_own_chunk/pallas_call | solution.py:759
  (149 shorter events, 24.3 us)
Async XLA Ops:
  3.0 12.5 %collective-permute-start = (bf16[880,128]{1,0:T(8,128)(2,1)S(1)}, bf16[880,128]{1,0:T(8,128)(2,1)S(1)}, u32[]{:S(2)}, u32[]{:S(2)}) collective-permute-start(bf16[880,128]{1,0:T(8,128)(2,1)S(1)} %pack_own_chunk.1), channel_id=1, source_target_pairs={{0,8},{2,10},{4,12},{6,14},{8,0},{10,2},{12,4},{14,6},{16,24},{18,... | collective-permute-start | bytes 675848 | tf_op jit(solution)/shard_map/ppermute | solution.py:110
  5.9 19.0 %collective-permute-start.1 = (bf16[880,128]{1,0:T(8,128)(2,1)S(1)}, bf16[880,128]{1,0:T(8,128)(2,1)S(1)}, u32[]{:S(2)}, u32[]{:S(2)}) collective-permute-start(bf16[880,128]{1,0:T(8,128)(2,1)S(1)} %pack_own_chunk.1), channel_id=1, source_target_pairs={{0,16},{2,18},{4,20},{6,22},{8,24},{10,26},{12,28},{14,30},{16,0},... | collective-permute-start | bytes 675848 | tf_op jit(solution)/shard_map/ppermute | solution.py:110
  8.6 16.3 %collective-permute-start.2 = (bf16[880,128]{1,0:T(8,128)(2,1)S(1)}, bf16[880,128]{1,0:T(8,128)(2,1)S(1)}, u32[]{:S(2)}, u32[]{:S(2)}) collective-permute-start(bf16[880,128]{1,0:T(8,128)(2,1)S(1)} %pack_own_chunk.1), channel_id=1, source_target_pairs={{0,24},{2,26},{4,28},{6,30},{8,16},{10,18},{12,20},{14,22},{16,8},... | collective-permute-start | bytes 675848 | tf_op jit(solution)/shard_map/ppermute | solution.py:110
  8.6 16.3 %collective-permute-start.3 = (bf16[880,128]{1,0:T(8,128)(2,1)S(1)}, bf16[880,128]{1,0:T(8,128)(2,1)S(1)}, u32[]{:S(2)}, u32[]{:S(2)}) collective-permute-start(bf16[880,128]{1,0:T(8,128)(2,1)S(1)} %pack_own_chunk.1), channel_id=1, source_target_pairs={{0,2},{1,5},{2,0},{3,7},{4,6},{5,1},{6,4},{7,3},{8,10},{9,13},{10,... | collective-permute-start | bytes 675848 | tf_op jit(solution)/shard_map/ppermute | solution.py:119
  10.4 14.5 %collective-permute-start.4 = (bf16[880,128]{1,0:T(8,128)(2,1)S(1)}, bf16[880,128]{1,0:T(8,128)(2,1)S(1)}, u32[]{:S(2)}, u32[]{:S(2)}) collective-permute-start(bf16[880,128]{1,0:T(8,128)(2,1)S(1)} %pack_own_chunk.1), channel_id=1, source_target_pairs={{0,4},{1,3},{2,6},{3,1},{4,0},{5,7},{6,2},{7,5},{8,12},{9,11},{10,... | collective-permute-start | bytes 675848 | tf_op jit(solution)/shard_map/ppermute | solution.py:119
  15.4 9.4 %collective-permute-start.5 = (bf16[880,128]{1,0:T(8,128)(2,1)S(1)}, bf16[880,128]{1,0:T(8,128)(2,1)S(1)}, u32[]{:S(2)}, u32[]{:S(2)}) collective-permute-start(bf16[880,128]{1,0:T(8,128)(2,1)S(1)} %pack_own_chunk.1), channel_id=1, source_target_pairs={{0,6},{1,7},{2,4},{3,5},{4,2},{5,3},{6,0},{7,1},{8,14},{9,15},{10,... | collective-permute-start | bytes 675848 | tf_op jit(solution)/shard_map/ppermute | solution.py:119
  24.9 6.0 %collective-permute-start.8 = (bf16[880,128]{1,0:T(8,128)(2,1)S(1)}, bf16[880,128]{1,0:T(8,128)(2,1)S(1)}, u32[]{:S(2)}, u32[]{:S(2)}) collective-permute-start(bf16[880,128]{1,0:T(8,128)(2,1)S(1)} %collective-permute-done.2), channel_id=1, source_target_pairs={{0,2},{1,5},{2,0},{3,7},{4,6},{5,1},{6,4},{7,3},{8,10},{9,13},{10,... | collective-permute-start | bytes 675848 | tf_op jit(solution)/shard_map/ppermute | solution.py:119
  26.4 8.4 %collective-permute-start.7 = (bf16[880,128]{1,0:T(8,128)(2,1)S(1)}, bf16[880,128]{1,0:T(8,128)(2,1)S(1)}, u32[]{:S(2)}, u32[]{:S(2)}) collective-permute-start(bf16[880,128]{1,0:T(8,128)(2,1)S(1)} %collective-permute-done.1), channel_id=1, source_target_pairs={{0,2},{1,5},{2,0},{3,7},{4,6},{5,1},{6,4},{7,3},{8,10},{9,13},{10,... | collective-permute-start | bytes 675848 | tf_op jit(solution)/shard_map/ppermute | solution.py:119
  27.0 12.7 %collective-permute-start.6 = (bf16[880,128]{1,0:T(8,128)(2,1)S(1)}, bf16[880,128]{1,0:T(8,128)(2,1)S(1)}, u32[]{:S(2)}, u32[]{:S(2)}) collective-permute-start(bf16[880,128]{1,0:T(8,128)(2,1)S(1)} %collective-permute-done), channel_id=1, source_target_pairs={{0,2},{1,5},{2,0},{3,7},{4,6},{5,1},{6,4},{7,3},{8,10},{9,13},{10,... | collective-permute-start | bytes 675848 | tf_op jit(solution)/shard_map/ppermute | solution.py:119
  28.5 20.7 %collective-permute-start.10 = (bf16[4,880,128]{2,1,0:T(8,128)(2,1)S(1)}, bf16[4,880,128]{2,1,0:T(8,128)(2,1)S(1)}, u32[]{:S(2)}, u32[]{:S(2)}) collective-permute-start(bf16[4,880,128]{2,1,0:T(8,128)(2,1)S(1)} %pad_maximum_fusion.refs_0_), channel_id=1, source_target_pairs={{0,1},{1,0},{2,3},{3,2},{4,5},{5,4},{6,7},{7,6},{8,9},{9,8},{10,11... | collective-permute-start | bytes 2703368 | tf_op jit(solution)/shard_map/ppermute | solution.py:114
  31.0 8.7 %collective-permute-start.16 = (bf16[2,880,128]{2,1,0:T(8,128)(2,1)S(1)}, bf16[2,880,128]{2,1,0:T(8,128)(2,1)S(1)}, u32[]{:S(2)}, u32[]{:S(2)}) collective-permute-start(bf16[2,880,128]{2,1,0:T(8,128)(2,1)S(1)} %pad_maximum_fusion.3.refs_3_), channel_id=1, source_target_pairs={{0,4},{1,3},{2,6},{3,1},{4,0},{5,7},{6,2},{7,5},{8,12},{9,11},{10,... | collective-permute-start | bytes 1351688 | tf_op jit(solution)/shard_map/ppermute | solution.py:119
  32.5 8.2 %collective-permute-start.13 = (bf16[2,880,128]{2,1,0:T(8,128)(2,1)S(1)}, bf16[2,880,128]{2,1,0:T(8,128)(2,1)S(1)}, u32[]{:S(2)}, u32[]{:S(2)}) collective-permute-start(bf16[2,880,128]{2,1,0:T(8,128)(2,1)S(1)} %pad_maximum_fusion.3.refs_3_), channel_id=1, source_target_pairs={{0,1},{1,0},{2,3},{3,2},{4,5},{5,4},{6,7},{7,6},{8,9},{9,8},{10,11... | collective-permute-start | bytes 1351688 | tf_op jit(solution)/shard_map/ppermute | solution.py:114
  34.9 9.4 %collective-permute-start.14 = (bf16[2,880,128]{2,1,0:T(8,128)(2,1)S(1)}, bf16[2,880,128]{2,1,0:T(8,128)(2,1)S(1)}, u32[]{:S(2)}, u32[]{:S(2)}) collective-permute-start(bf16[2,880,128]{2,1,0:T(8,128)(2,1)S(1)} %pad_maximum_fusion.2.refs_2_), channel_id=1, source_target_pairs={{0,4},{1,3},{2,6},{3,1},{4,0},{5,7},{6,2},{7,5},{8,12},{9,11},{10,... | collective-permute-start | bytes 1351688 | tf_op jit(solution)/shard_map/ppermute | solution.py:119
  39.6 6.0 %collective-permute-start.12 = (bf16[2,880,128]{2,1,0:T(8,128)(2,1)S(1)}, bf16[2,880,128]{2,1,0:T(8,128)(2,1)S(1)}, u32[]{:S(2)}, u32[]{:S(2)}) collective-permute-start(bf16[2,880,128]{2,1,0:T(8,128)(2,1)S(1)} %pad_maximum_fusion.2.refs_2_), channel_id=1, source_target_pairs={{0,1},{1,0},{2,3},{3,2},{4,5},{5,4},{6,7},{7,6},{8,9},{9,8},{10,11... | collective-permute-start | bytes 1351688 | tf_op jit(solution)/shard_map/ppermute | solution.py:114
  39.7 6.0 %collective-permute-start.11 = (bf16[2,880,128]{2,1,0:T(8,128)(2,1)S(1)}, bf16[2,880,128]{2,1,0:T(8,128)(2,1)S(1)}, u32[]{:S(2)}, u32[]{:S(2)}) collective-permute-start(bf16[2,880,128]{2,1,0:T(8,128)(2,1)S(1)} %pad_maximum_fusion.1.refs_1_), channel_id=1, source_target_pairs={{0,1},{1,0},{2,3},{3,2},{4,5},{5,4},{6,7},{7,6},{8,9},{9,8},{10,11... | collective-permute-start | bytes 1351688 | tf_op jit(solution)/shard_map/ppermute | solution.py:114
  40.7 8.5 %collective-permute-start.9 = (bf16[2,880,128]{2,1,0:T(8,128)(2,1)S(1)}, bf16[2,880,128]{2,1,0:T(8,128)(2,1)}, u32[]{:S(2)}, u32[]{:S(2)}) collective-permute-start(bf16[2,880,128]{2,1,0:T(8,128)(2,1)S(1)} %pad_maximum_fusion.1.refs_1_), channel_id=1, source_target_pairs={{0,4},{1,3},{2,6},{3,1},{4,0},{5,7},{6,2},{7,5},{8,12},{9,11},{10,... | collective-permute-start | bytes 1351688 | tf_op jit(solution)/shard_map/ppermute | solution.py:119
  44.3 5.9 %collective-permute-start.17 = (bf16[2,880,128]{2,1,0:T(8,128)(2,1)S(1)}, bf16[2,880,128]{2,1,0:T(8,128)(2,1)S(1)}, u32[]{:S(2)}, u32[]{:S(2)}) collective-permute-start(bf16[2,880,128]{2,1,0:T(8,128)(2,1)S(1)} %collective-permute-done.16.refs_6_), channel_id=1, source_target_pairs={{0,1},{1,0},{2,3},{3,2},{4,5},{5,4},{6,7},{7,6},{8,9},{9,8},{10,11... | collective-permute-start | bytes 1351688 | tf_op jit(solution)/shard_map/ppermute | solution.py:114
  75.0 13.3 %collective-permute-start.22 = (bf16[2,880,128]{2,1,0:T(8,128)(2,1)S(1)}, bf16[2,880,128]{2,1,0:T(8,128)(2,1)S(1)}, u32[]{:S(2)}, u32[]{:S(2)}) collective-permute-start(bf16[2,880,128]{2,1,0:T(8,128)(2,1)S(1)} %add_convert_fusion.5), channel_id=1, source_target_pairs={{0,4},{1,3},{2,6},{3,1},{4,0},{5,7},{6,2},{7,5},{8,12},{9,11},{10,... | collective-permute-start | bytes 1351688 | tf_op jit(solution)/shard_map/ppermute | solution.py:119
  76.7 11.6 %collective-permute-start.20 = (bf16[2,880,128]{2,1,0:T(8,128)(2,1)S(1)}, bf16[2,880,128]{2,1,0:T(8,128)(2,1)S(1)}, u32[]{:S(2)}, u32[]{:S(2)}) collective-permute-start(bf16[2,880,128]{2,1,0:T(8,128)(2,1)S(1)} %add_convert_fusion.6), channel_id=1, source_target_pairs={{0,4},{1,3},{2,6},{3,1},{4,0},{5,7},{6,2},{7,5},{8,12},{9,11},{10,... | collective-permute-start | bytes 1351688 | tf_op jit(solution)/shard_map/ppermute | solution.py:119
  77.3 11.1 %collective-permute-start.30 = (bf16[2,880,128]{2,1,0:T(8,128)(2,1)}, bf16[2,880,128]{2,1,0:T(8,128)(2,1)S(1)}, u32[]{:S(2)}, u32[]{:S(2)}) collective-permute-start(bf16[2,880,128]{2,1,0:T(8,128)(2,1)} %get-tuple-element.114), channel_id=1, source_target_pairs={{0,1},{1,0},{2,3},{3,2},{4,5},{5,4},{6,7},{7,6},{8,9},{9,8},{10,11... | collective-permute-start | bytes 1351688 | tf_op jit(solution)/shard_map/ppermute | solution.py:114
  77.4 15.2 %collective-permute-start.28 = (bf16[2,880,128]{2,1,0:T(8,128)(2,1)S(1)}, bf16[2,880,128]{2,1,0:T(8,128)(2,1)S(1)}, u32[]{:S(2)}, u32[]{:S(2)}) collective-permute-start(bf16[2,880,128]{2,1,0:T(8,128)(2,1)S(1)} %copy-done.29), channel_id=1, source_target_pairs={{0,1},{1,0},{2,3},{3,2},{4,5},{5,4},{6,7},{7,6},{8,9},{9,8},{10,11... | collective-permute-start | bytes 1351688 | tf_op jit(solution)/shard_map/ppermute | solution.py:114
  88.7 19.5 %collective-permute-start.31 = (bf16[880,128]{1,0:T(8,128)(2,1)S(1)}, bf16[880,128]{1,0:T(8,128)(2,1)S(1)}, u32[]{:S(2)}, u32[]{:S(2)}) collective-permute-start(bf16[880,128]{1,0:T(8,128)(2,1)S(1)} %slice_bitcast_fusion), channel_id=1, source_target_pairs={{0,2},{1,5},{2,0},{3,7},{4,6},{5,1},{6,4},{7,3},{8,10},{9,13},{10,... | collective-permute-start | bytes 675848 | tf_op jit(solution)/shard_map/ppermute | solution.py:119
  90.5 12.9 %collective-permute-start.23 = (bf16[4,880,128]{2,1,0:T(8,128)(2,1)S(1)}, bf16[4,880,128]{2,1,0:T(8,128)(2,1)S(1)}, u32[]{:S(2)}, u32[]{:S(2)}) collective-permute-start(bf16[4,880,128]{2,1,0:T(8,128)(2,1)S(1)} %broadcast_select_fusion), channel_id=1, source_target_pairs={{0,1},{1,0},{2,3},{3,2},{4,5},{5,4},{6,7},{7,6},{8,9},{9,8},{10,11... | collective-permute-start | bytes 2703368 | tf_op jit(solution)/shard_map/ppermute | solution.py:114
  91.0 10.9 %collective-permute-start.26 = (bf16[2,880,128]{2,1,0:T(8,128)(2,1)S(1)}, bf16[2,880,128]{2,1,0:T(8,128)(2,1)S(1)}, u32[]{:S(2)}, u32[]{:S(2)}) collective-permute-start(bf16[2,880,128]{2,1,0:T(8,128)(2,1)S(1)} %add_convert_fusion.4), channel_id=1, source_target_pairs={{0,4},{1,3},{2,6},{3,1},{4,0},{5,7},{6,2},{7,5},{8,12},{9,11},{10,... | collective-permute-start | bytes 1351688 | tf_op jit(solution)/shard_map/ppermute | solution.py:119
  92.8 15.4 %collective-permute-start.29 = (bf16[880,128]{1,0:T(8,128)(2,1)S(1)}, bf16[880,128]{1,0:T(8,128)(2,1)S(1)}, u32[]{:S(2)}, u32[]{:S(2)}) collective-permute-start(bf16[880,128]{1,0:T(8,128)(2,1)S(1)} %slice_bitcast_fusion.2), channel_id=1, source_target_pairs={{0,2},{1,5},{2,0},{3,7},{4,6},{5,1},{6,4},{7,3},{8,10},{9,13},{10,... | collective-permute-start | bytes 675848 | tf_op jit(solution)/shard_map/ppermute | solution.py:119
  102.1 6.0 %collective-permute-start.27 = (bf16[880,128]{1,0:T(8,128)(2,1)S(1)}, bf16[880,128]{1,0:T(8,128)(2,1)S(1)}, u32[]{:S(2)}, u32[]{:S(2)}) collective-permute-start(bf16[880,128]{1,0:T(8,128)(2,1)S(1)} %slice_bitcast_fusion.4), channel_id=1, source_target_pairs={{0,2},{1,5},{2,0},{3,7},{4,6},{5,1},{6,4},{7,3},{8,10},{9,13},{10,... | collective-permute-start | bytes 675848 | tf_op jit(solution)/shard_map/ppermute | solution.py:119
  108.4 12.6 %collective-permute-start.32 = (bf16[880,128]{1,0:T(8,128)(2,1)S(1)}, bf16[880,128]{1,0:T(8,128)(2,1)S(1)}, u32[]{:S(2)}, u32[]{:S(2)}) collective-permute-start(bf16[880,128]{1,0:T(8,128)(2,1)S(1)} %get-tuple-element.123), channel_id=1, source_target_pairs={{0,8},{2,10},{4,12},{6,14},{8,0},{10,2},{12,4},{14,6},{16,24},{18,... | collective-permute-start | bytes 675848 | tf_op jit(solution)/shard_map/ppermute | solution.py:110
  112.5 19.0 %collective-permute-start.33 = (bf16[880,128]{1,0:T(8,128)(2,1)S(1)}, bf16[880,128]{1,0:T(8,128)(2,1)S(1)}, u32[]{:S(2)}, u32[]{:S(2)}) collective-permute-start(bf16[880,128]{1,0:T(8,128)(2,1)S(1)} %get-tuple-element.122), channel_id=1, source_target_pairs={{0,16},{2,18},{4,20},{6,22},{8,24},{10,26},{12,28},{14,30},{16,0},... | collective-permute-start | bytes 675848 | tf_op jit(solution)/shard_map/ppermute | solution.py:110
  113.6 17.9 %collective-permute-start.34 = (bf16[880,128]{1,0:T(8,128)(2,1)S(1)}, bf16[880,128]{1,0:T(8,128)(2,1)S(1)}, u32[]{:S(2)}, u32[]{:S(2)}) collective-permute-start(bf16[880,128]{1,0:T(8,128)(2,1)S(1)} %get-tuple-element.127), channel_id=1, source_target_pairs={{0,24},{2,26},{4,28},{6,30},{8,16},{10,18},{12,20},{14,22},{16,8},... | collective-permute-start | bytes 675848 | tf_op jit(solution)/shard_map/ppermute | solution.py:110
  115.0 16.5 %collective-permute-start.35 = (bf16[880,128]{1,0:T(8,128)(2,1)S(1)}, bf16[880,128]{1,0:T(8,128)(2,1)S(1)}, u32[]{:S(2)}, u32[]{:S(2)}) collective-permute-start(bf16[880,128]{1,0:T(8,128)(2,1)S(1)} %get-tuple-element.126), channel_id=1, source_target_pairs={{0,2},{1,5},{2,0},{3,7},{4,6},{5,1},{6,4},{7,3},{8,10},{9,13},{10,... | collective-permute-start | bytes 675848 | tf_op jit(solution)/shard_map/ppermute | solution.py:119
  116.3 15.2 %collective-permute-start.36 = (bf16[880,128]{1,0:T(8,128)(2,1)S(1)}, bf16[880,128]{1,0:T(8,128)(2,1)S(1)}, u32[]{:S(2)}, u32[]{:S(2)}) collective-permute-start(bf16[880,128]{1,0:T(8,128)(2,1)S(1)} %get-tuple-element.125), channel_id=1, source_target_pairs={{0,4},{1,3},{2,6},{3,1},{4,0},{5,7},{6,2},{7,5},{8,12},{9,11},{10,... | collective-permute-start | bytes 675848 | tf_op jit(solution)/shard_map/ppermute | solution.py:119
  121.0 10.5 %collective-permute-start.37 = (bf16[880,128]{1,0:T(8,128)(2,1)S(1)}, bf16[880,128]{1,0:T(8,128)(2,1)S(1)}, u32[]{:S(2)}, u32[]{:S(2)}) collective-permute-start(bf16[880,128]{1,0:T(8,128)(2,1)S(1)} %get-tuple-element.124), channel_id=1, source_target_pairs={{0,6},{1,7},{2,4},{3,5},{4,2},{5,3},{6,0},{7,1},{8,14},{9,15},{10,... | collective-permute-start | bytes 675848 | tf_op jit(solution)/shard_map/ppermute | solution.py:119
  (43 other events, 369.1 us)

commit v7 on v6

--- a/solution.py
+++ b/solution.py
@@ -288,13 +288,13 @@
         part = value[:, 192 * m : 192 * (m + 1)].astype(F32)
         first[pl.ds(m, 192, stride=3), :] = part[:, :128]
         second[pl.ds(m, 192, stride=3), :] = jnp.concatenate([part[:, 128:], part[:, 128:]], 1)
-    out[:, :128] = first[...].astype(BF16)
-    out[:, 128:] = second[:, :64].astype(BF16)
+    out[:, :128] = first[:576, :].astype(BF16)
+    out[:, 128:] = second[:576, :64].astype(BF16)
 
 
 def unspread(value, first, second):
-    first[...] = value[:, :128]
-    second[...] = jnp.concatenate([value[:, 128:], value[:, 128:]], 1)
+    first[:576, :] = value[:, :128]
+    second[:576, :] = jnp.concatenate([value[:, 128:], value[:, 128:]], 1)
     parts = []
     for m in range(3):
         parts.append(first[pl.ds(m, 192, stride=3), :])
@@ -622,7 +622,7 @@
     rolled[0:16, :] = jnp.zeros((16, 128), F32)
     rolled[16:1752, :] = pltpu.roll(flat[...].astype(F32), right, 1)
     rolled[1752:1760, :] = jnp.zeros((8, 128), F32)
-    window[...] = jnp.where(
+    window[:1744, :] = jnp.where(
         lane >= right, rolled[pl.ds(16 - down, 1744), :], rolled[pl.ds(15 - down, 1744), :]
     )
     head = [window[k : k + 1, :] for k in range(9)]
@@ -644,7 +644,7 @@
         mixed[pl.ds(0, NARROW // 2, stride=2), :] = parts[4]
         mixed[pl.ds(1, NARROW // 2, stride=2), :] = pltpu.roll(parts[8], 64, 1)
         packed[4 * NARROW : ROWS, :] = jnp.where(
-            lane < 64, mixed[: NARROW // 2, :], pltpu.roll(mixed[NARROW // 2 :, :], 64, 1)
+            lane < 64, mixed[: NARROW // 2, :], pltpu.roll(mixed[NARROW // 2 : NARROW, :], 64, 1)
         )
 
     last = jnp.zeros((23, 128), F32)
@@ -682,7 +682,7 @@
     def _():
         half = packed[4 * NARROW : ROWS, :]
         mixed[: NARROW // 2, :] = half
-        mixed[NARROW // 2 :, :] = pltpu.roll(half, 64, 1)
+        mixed[NARROW // 2 : NARROW, :] = pltpu.roll(half, 64, 1)
         odd = []
         for j in range(4):
             window[pl.ds(9 + j, NARROW // 2, stride=9), :] = packed[
@@ -742,9 +742,9 @@
         out_shape=jax.ShapeDtypeStruct((HALF, 128), BF16),
         scratch_shapes=[
             pltpu.VMEM((1760, 128), F32),
-            pltpu.VMEM((1744, 128), F32),
+            pltpu.VMEM((1752, 128), F32),
             pltpu.VMEM((2 * HALF, 128), F32),
-            pltpu.VMEM((NARROW, 128), F32),
+            pltpu.VMEM((NARROW + 8, 128), F32),
         ],
         compiler_params=pltpu.CompilerParams(vmem_limit_bytes=VMEM_LIMIT),
     )(chunk_index(index, core, lay), flat)
@@ -765,7 +765,7 @@
         scratch_shapes=[
             pltpu.VMEM((2 * HALF, 128), F32),
             pltpu.VMEM((1752, 128), F32),
-            pltpu.VMEM((NARROW, 128), F32),
+            pltpu.VMEM((NARROW + 8, 128), F32),
         ],
         compiler_params=pltpu.CompilerParams(vmem_limit_bytes=VMEM_LIMIT),
     )(chunk_index(index, core, lay), own, twin)
@@ -822,8 +822,8 @@
             pltpu.VMEM((length, width), BF16),
             pltpu.VMEM((width, length), BF16),
             pltpu.VMEM((length, width), F32),
-            pltpu.VMEM((width, 128), F32),
-            pltpu.VMEM((width, 128), F32),
+            pltpu.VMEM((width + 8, 128), F32),
+            pltpu.VMEM((width + 8, 128), F32),
             pltpu.SemaphoreType.DMA((2,)),
             pltpu.SemaphoreType.DMA((4,)),
             pltpu.SemaphoreType.DMA((3,)),
@@ -846,8 +846,8 @@
             pltpu.VMEM((length, width), F32),
             pltpu.VMEM((length, kv_width), F32),
             pltpu.VMEM((length, kv_width), F32),
-            pltpu.VMEM((width, 128), F32),
-            pltpu.VMEM((width, 128), F32),
+            pltpu.VMEM((width + 8, 128), F32),
+            pltpu.VMEM((width + 8, 128), F32),
             pltpu.SemaphoreType.DMA((2,)),
             pltpu.SemaphoreType.DMA((1,)),
             pltpu.SemaphoreType.DMA((3,)),

time: 137 us -> 137 us (level)
  no operation moved by 1% of the time
where the time goes in v7:
time: 137 us; the launch traced here: 136 us
  waiting for transfers between devices  51.7 us (38%)
  starting transfers between devices  44.1 us (32%)
  Pallas kernels  30.3 us (22%)
  local copies, waits for them, and re-layouts  4.52 us (3%)
  other arithmetic  4.52 us (3%)
    ppermute x18, starting transfers between devices, hop(): return lax.ppermute(value, ('dp', 'rep'), pairs)  26.7 us
    ppermute x18, waiting for transfers between devices, hop(): return lax.ppermute(value, ('dp', 'rep'), pairs)  26 us
    ppermute x6, waiting for transfers between devices, swap(): return lax.ppermute(value, 'dp', [(i, i ^ mask) for i in range(count)])  20.8 us
    pallas_call x1, Pallas kernels, on_device(): results = forward(idx, *pieces, tokens_in.T, *angles, cotangent.T)  16.5 us
    ppermute x6, starting transfers between devices, swap(): return lax.ppermute(value, 'dp', [(i, i ^ mask) for i in range(count)])  12.2 us
    pallas_call x1, Pallas kernels, on_device(): attention_back(idx, tokens_in.T, *angles, *saved, *held)  10.4 us
    ppermute x15, starting transfers between devices, swap_rep(): return lax.ppermute(value, 'rep', [(0, 1), (1, 0)])  5.26 us
    ppermute x15, waiting for transfers between devices, swap_rep(): return lax.ppermute(value, 'rep', [(0, 1), (1, 0)])  4.89 us
  transfers between devices with their start and end apart: 39, of which 14 were waited for; matrix products, arithmetic and copies ran while one was open for 3% of the time, Pallas kernels for 8%

profile of v7, /device:TPU:0, one launch (start us, length us, event | category | flops | bytes accessed | tf_op | source)
XLA Modules:
  0.0 136.4 jit_solution(1203722196551659840)
XLA Ops:
  3.0 2.9 %collective-permute-start = (bf16[880,128]{1,0:T(8,128)(2,1)S(1)}, bf16[880,128]{1,0:T(8,128)(2,1)S(1)}, u32[]{:S(2)}, u32[]{:S(2)}) collective-permute-start(bf16[880,128]{1,0:T(8,128)(2,1)S(1)} %pack_own_chunk.1), channel_id=1, source_target_pairs={{0,8},{2,10},{4,12},{6,14},{8,0},{10,2},{12,4},{14,6},{16,24},{18,... | collective-permute-start | bytes 675848 | tf_op jit(solution)/shard_map/ppermute | solution.py:110
  5.9 2.7 %collective-permute-start.1 = (bf16[880,128]{1,0:T(8,128)(2,1)S(1)}, bf16[880,128]{1,0:T(8,128)(2,1)S(1)}, u32[]{:S(2)}, u32[]{:S(2)}) collective-permute-start(bf16[880,128]{1,0:T(8,128)(2,1)S(1)} %pack_own_chunk.1), channel_id=1, source_target_pairs={{0,16},{2,18},{4,20},{6,22},{8,24},{10,26},{12,28},{14,30},{16,0},... | collective-permute-start | bytes 675848 | tf_op jit(solution)/shard_map/ppermute | solution.py:110
  8.6 1.8 %collective-permute-start.3 = (bf16[880,128]{1,0:T(8,128)(2,1)S(1)}, bf16[880,128]{1,0:T(8,128)(2,1)S(1)}, u32[]{:S(2)}, u32[]{:S(2)}) collective-permute-start(bf16[880,128]{1,0:T(8,128)(2,1)S(1)} %pack_own_chunk.1), channel_id=1, source_target_pairs={{0,2},{1,5},{2,0},{3,7},{4,6},{5,1},{6,4},{7,3},{8,10},{9,13},{10,... | collective-permute-start | bytes 675848 | tf_op jit(solution)/shard_map/ppermute | solution.py:119
  10.4 1.5 %collective-permute-start.4 = (bf16[880,128]{1,0:T(8,128)(2,1)S(1)}, bf16[880,128]{1,0:T(8,128)(2,1)S(1)}, u32[]{:S(2)}, u32[]{:S(2)}) collective-permute-start(bf16[880,128]{1,0:T(8,128)(2,1)S(1)} %pack_own_chunk.1), channel_id=1, source_target_pairs={{0,4},{1,3},{2,6},{3,1},{4,0},{5,7},{6,2},{7,5},{8,12},{9,11},{10,... | collective-permute-start | bytes 675848 | tf_op jit(solution)/shard_map/ppermute | solution.py:119
  11.9 3.5 %collective-permute-done = bf16[880,128]{1,0:T(8,128)(2,1)S(1)} collective-permute-done((bf16[880,128]{1,0:T(8,128)(2,1)S(1)}, bf16[880,128]{1,0:T(8,128)(2,1)S(1)}, u32[]{:S(2)}, u32[]{:S(2)}) %collective-permute-start) | collective-permute-done | bytes 225312 | tf_op jit(solution)/shard_map/ppermute | solution.py:110
  15.4 2.9 %collective-permute-start.5 = (bf16[880,128]{1,0:T(8,128)(2,1)S(1)}, bf16[880,128]{1,0:T(8,128)(2,1)S(1)}, u32[]{:S(2)}, u32[]{:S(2)}) collective-permute-start(bf16[880,128]{1,0:T(8,128)(2,1)S(1)} %pack_own_chunk.1), channel_id=1, source_target_pairs={{0,6},{1,7},{2,4},{3,5},{4,2},{5,3},{6,0},{7,1},{8,14},{9,15},{10,... | collective-permute-start | bytes 675848 | tf_op jit(solution)/shard_map/ppermute | solution.py:119
  19.0 5.9 %collective-permute-done.1 = bf16[880,128]{1,0:T(8,128)(2,1)S(1)} collective-permute-done((bf16[880,128]{1,0:T(8,128)(2,1)S(1)}, bf16[880,128]{1,0:T(8,128)(2,1)S(1)}, u32[]{:S(2)}, u32[]{:S(2)}) %collective-permute-start.1) | collective-permute-done | bytes 225312 | tf_op jit(solution)/shard_map/ppermute | solution.py:110
  24.9 1.5 %collective-permute-start.8 = (bf16[880,128]{1,0:T(8,128)(2,1)S(1)}, bf16[880,128]{1,0:T(8,128)(2,1)S(1)}, u32[]{:S(2)}, u32[]{:S(2)}) collective-permute-start(bf16[880,128]{1,0:T(8,128)(2,1)S(1)} %collective-permute-done.2), channel_id=1, source_target_pairs={{0,2},{1,5},{2,0},{3,7},{4,6},{5,1},{6,4},{7,3},{8,10},{9,13},{10,... | collective-permute-start | bytes 675848 | tf_op jit(solution)/shard_map/ppermute | solution.py:119
  27.0 1.4 %collective-permute-start.6 = (bf16[880,128]{1,0:T(8,128)(2,1)S(1)}, bf16[880,128]{1,0:T(8,128)(2,1)S(1)}, u32[]{:S(2)}, u32[]{:S(2)}) collective-permute-start(bf16[880,128]{1,0:T(8,128)(2,1)S(1)} %collective-permute-done), channel_id=1, source_target_pairs={{0,2},{1,5},{2,0},{3,7},{4,6},{5,1},{6,4},{7,3},{8,10},{9,13},{10,... | collective-permute-start | bytes 675848 | tf_op jit(solution)/shard_map/ppermute | solution.py:119
  28.6 2.3 %collective-permute-done.8 = bf16[880,128]{1,0:T(8,128)(2,1)S(1)} collective-permute-done((bf16[880,128]{1,0:T(8,128)(2,1)S(1)}, bf16[880,128]{1,0:T(8,128)(2,1)S(1)}, u32[]{:S(2)}, u32[]{:S(2)}) %collective-permute-start.8) | collective-permute-done | bytes 225312 | tf_op jit(solution)/shard_map/ppermute | solution.py:119
  31.0 1.5 %collective-permute-start.16 = (bf16[2,880,128]{2,1,0:T(8,128)(2,1)S(1)}, bf16[2,880,128]{2,1,0:T(8,128)(2,1)S(1)}, u32[]{:S(2)}, u32[]{:S(2)}) collective-permute-start(bf16[2,880,128]{2,1,0:T(8,128)(2,1)S(1)} %pad_maximum_fusion.3.refs_3_), channel_id=1, source_target_pairs={{0,4},{1,3},{2,6},{3,1},{4,0},{5,7},{6,2},{7,5},{8,12},{9,11},{10,... | collective-permute-start | bytes 1351688 | tf_op jit(solution)/shard_map/ppermute | solution.py:119
  32.5 2.3 %collective-permute-done.7 = bf16[880,128]{1,0:T(8,128)(2,1)S(1)} collective-permute-done((bf16[880,128]{1,0:T(8,128)(2,1)S(1)}, bf16[880,128]{1,0:T(8,128)(2,1)S(1)}, u32[]{:S(2)}, u32[]{:S(2)}) %collective-permute-start.7) | collective-permute-done | bytes 225312 | tf_op jit(solution)/shard_map/ppermute | solution.py:119
  34.9 1.4 %collective-permute-start.14 = (bf16[2,880,128]{2,1,0:T(8,128)(2,1)S(1)}, bf16[2,880,128]{2,1,0:T(8,128)(2,1)S(1)}, u32[]{:S(2)}, u32[]{:S(2)}) collective-permute-start(bf16[2,880,128]{2,1,0:T(8,128)(2,1)S(1)} %pad_maximum_fusion.2.refs_2_), channel_id=1, source_target_pairs={{0,4},{1,3},{2,6},{3,1},{4,0},{5,7},{6,2},{7,5},{8,12},{9,11},{10,... | collective-permute-start | bytes 1351688 | tf_op jit(solution)/shard_map/ppermute | solution.py:119
  36.3 3.4 %collective-permute-done.6 = bf16[880,128]{1,0:T(8,128)(2,1)S(1)} collective-permute-done((bf16[880,128]{1,0:T(8,128)(2,1)S(1)}, bf16[880,128]{1,0:T(8,128)(2,1)S(1)}, u32[]{:S(2)}, u32[]{:S(2)}) %collective-permute-start.6) | collective-permute-done | bytes 225312 | tf_op jit(solution)/shard_map/ppermute | solution.py:119
  40.7 1.4 %collective-permute-start.9 = (bf16[2,880,128]{2,1,0:T(8,128)(2,1)S(1)}, bf16[2,880,128]{2,1,0:T(8,128)(2,1)}, u32[]{:S(2)}, u32[]{:S(2)}) collective-permute-start(bf16[2,880,128]{2,1,0:T(8,128)(2,1)S(1)} %pad_maximum_fusion.1.refs_1_), channel_id=1, source_target_pairs={{0,4},{1,3},{2,6},{3,1},{4,0},{5,7},{6,2},{7,5},{8,12},{9,11},{10,... | collective-permute-start | bytes 1351688 | tf_op jit(solution)/shard_map/ppermute | solution.py:119
  42.1 2.1 %collective-permute-done.14.refs_5_ = bf16[2,880,128]{2,1,0:T(8,128)(2,1)S(1)} collective-permute-done((bf16[2,880,128]{2,1,0:T(8,128)(2,1)S(1)}, bf16[2,880,128]{2,1,0:T(8,128)(2,1)S(1)}, u32[]{:S(2)}, u32[]{:S(2)}) %collective-permute-start.14) | collective-permute-done | bytes 450592 | tf_op jit(solution)/shard_map/ppermute | solution.py:119
  45.7 3.5 %collective-permute-done.9.refs_4_ = bf16[2,880,128]{2,1,0:T(8,128)(2,1)} collective-permute-done((bf16[2,880,128]{2,1,0:T(8,128)(2,1)S(1)}, bf16[2,880,128]{2,1,0:T(8,128)(2,1)}, u32[]{:S(2)}, u32[]{:S(2)}) %collective-permute-start.9) | collective-permute-done | bytes 450592 | tf_op jit(solution)/shard_map/ppermute | solution.py:119
  52.8 1.6 %collective-permute-done.18.refs_11_ = bf16[2,880,128]{2,1,0:T(8,128)(2,1)S(1)} collective-permute-done((bf16[2,880,128]{2,1,0:T(8,128)(2,1)}, bf16[2,880,128]{2,1,0:T(8,128)(2,1)S(1)}, u32[]{:S(2)}, u32[]{:S(2)}) %collective-permute-start.18) | collective-permute-done | bytes 450592 | tf_op jit(solution)/shard_map/ppermute | solution.py:114
  55.1 16.5 %forward_and_ff_backward.1 = (f32[256,576]{1,0:T(8,128)}, f32[256,576]{1,0:T(8,128)}, f32[1,576]{1,0:T(1,128)S(1)}, bf16[256,576]{1,0:T(8,128)(2,1)}, f32[6,384,...) custom-call(s32[4]{0:T(128)S(1)} %pad_add_fusion.idx, ...), custom_call_target="tpu_custom_call" | custom-call | flops 4529848320 | bytes 8000000 | tf_op jit(solution)/shard_map/forward_and_ff_backward/pallas_call | solution.py:947
  72.3 1.5 %collective-permute-done.21 = bf16[2,880,128]{2,1,0:T(8,128)(2,1)S(1)} collective-permute-done((bf16[2,880,128]{2,1,0:T(8,128)(2,1)}, bf16[2,880,128]{2,1,0:T(8,128)(2,1)S(1)}, u32[]{:S(2)}, u32[]{:S(2)}) %collective-permute-start.21) | collective-permute-done | bytes 450592 | tf_op jit(solution)/shard_map/ppermute | solution.py:114
  75.0 1.5 %collective-permute-start.22 = (bf16[2,880,128]{2,1,0:T(8,128)(2,1)S(1)}, bf16[2,880,128]{2,1,0:T(8,128)(2,1)S(1)}, u32[]{:S(2)}, u32[]{:S(2)}) collective-permute-start(bf16[2,880,128]{2,1,0:T(8,128)(2,1)S(1)} %add_convert_fusion.5), channel_id=1, source_target_pairs={{0,4},{1,3},{2,6},{3,1},{4,0},{5,7},{6,2},{7,5},{8,12},{9,11},{10,... | collective-permute-start | bytes 1351688 | tf_op jit(solution)/shard_map/ppermute | solution.py:119
  77.9 10.4 %attention_backward.1 = (bf16[576,256]{1,0:T(8,128)(2,1)}, f32[576,256]{1,0:T(8,128)}, bf16[2,880,128]{2,1,0:T(8,128)(2,1)}, bf16[2,880,128]{2,1,0:T(8,128)(2,1)...) custom-call(s32[4]{0:T(128)} %copy-done.9, ...), custom_call_target="tpu_custom_call" | custom-call | flops 849346560 | bytes 8000000 | tf_op jit(solution)/shard_map/attention_backward/pallas_call | solution.py:954
  88.7 1.5 %collective-permute-start.31 = (bf16[880,128]{1,0:T(8,128)(2,1)S(1)}, bf16[880,128]{1,0:T(8,128)(2,1)S(1)}, u32[]{:S(2)}, u32[]{:S(2)}) collective-permute-start(bf16[880,128]{1,0:T(8,128)(2,1)S(1)} %slice_bitcast_fusion), channel_id=1, source_target_pairs={{0,2},{1,5},{2,0},{3,7},{4,6},{5,1},{6,4},{7,3},{8,10},{9,13},{10,... | collective-permute-start | bytes 675848 | tf_op jit(solution)/shard_map/ppermute | solution.py:119
  91.0 1.6 %collective-permute-start.26 = (bf16[2,880,128]{2,1,0:T(8,128)(2,1)S(1)}, bf16[2,880,128]{2,1,0:T(8,128)(2,1)S(1)}, u32[]{:S(2)}, u32[]{:S(2)}) collective-permute-start(bf16[2,880,128]{2,1,0:T(8,128)(2,1)S(1)} %add_convert_fusion.4), channel_id=1, source_target_pairs={{0,4},{1,3},{2,6},{3,1},{4,0},{5,7},{6,2},{7,5},{8,12},{9,11},{10,... | collective-permute-start | bytes 1351688 | tf_op jit(solution)/shard_map/ppermute | solution.py:119
  93.9 8.0 %collective-permute-done.26 = bf16[2,880,128]{2,1,0:T(8,128)(2,1)S(1)} collective-permute-done((bf16[2,880,128]{2,1,0:T(8,128)(2,1)S(1)}, bf16[2,880,128]{2,1,0:T(8,128)(2,1)S(1)}, u32[]{:S(2)}, u32[]{:S(2)}) %collective-permute-start.26) | collective-permute-done | bytes 450592 | tf_op jit(solution)/shard_map/ppermute | solution.py:119
  103.7 4.4 %collective-permute-done.27 = bf16[880,128]{1,0:T(8,128)(2,1)S(1)} collective-permute-done((bf16[880,128]{1,0:T(8,128)(2,1)S(1)}, bf16[880,128]{1,0:T(8,128)(2,1)S(1)}, u32[]{:S(2)}, u32[]{:S(2)}) %collective-permute-start.27) | collective-permute-done | bytes 225312 | tf_op jit(solution)/shard_map/ppermute | solution.py:119
  108.4 4.1 %collective-permute-start.32 = (bf16[880,128]{1,0:T(8,128)(2,1)S(1)}, bf16[880,128]{1,0:T(8,128)(2,1)S(1)}, u32[]{:S(2)}, u32[]{:S(2)}) collective-permute-start(bf16[880,128]{1,0:T(8,128)(2,1)S(1)} %get-tuple-element.123), channel_id=1, source_target_pairs={{0,8},{2,10},{4,12},{6,14},{8,0},{10,2},{12,4},{14,6},{16,24},{18,... | collective-permute-start | bytes 675848 | tf_op jit(solution)/shard_map/ppermute | solution.py:110
  117.6 3.3 %collective-permute-done.32 = bf16[880,128]{1,0:T(8,128)(2,1)S(1)} collective-permute-done((bf16[880,128]{1,0:T(8,128)(2,1)S(1)}, bf16[880,128]{1,0:T(8,128)(2,1)S(1)}, u32[]{:S(2)}, u32[]{:S(2)}) %collective-permute-start.32) | collective-permute-done | bytes 225312 | tf_op jit(solution)/shard_map/ppermute | solution.py:110
  121.0 2.4 %collective-permute-start.37 = (bf16[880,128]{1,0:T(8,128)(2,1)S(1)}, bf16[880,128]{1,0:T(8,128)(2,1)S(1)}, u32[]{:S(2)}, u32[]{:S(2)}) collective-permute-start(bf16[880,128]{1,0:T(8,128)(2,1)S(1)} %get-tuple-element.124), channel_id=1, source_target_pairs={{0,6},{1,7},{2,4},{3,5},{4,2},{5,3},{6,0},{7,1},{8,14},{9,15},{10,... | collective-permute-start | bytes 675848 | tf_op jit(solution)/shard_map/ppermute | solution.py:119
  123.4 8.1 %collective-permute-done.33 = bf16[880,128]{1,0:T(8,128)(2,1)S(1)} collective-permute-done((bf16[880,128]{1,0:T(8,128)(2,1)S(1)}, bf16[880,128]{1,0:T(8,128)(2,1)S(1)}, u32[]{:S(2)}, u32[]{:S(2)}) %collective-permute-start.33) | collective-permute-done | bytes 225312 | tf_op jit(solution)/shard_map/ppermute | solution.py:110
  131.8 1.8 %collective-permute-done.38.twin = f32[880,128]{1,0:T(8,128)S(1)} collective-permute-done((f32[880,128]{1,0:T(8,128)S(1)}, f32[880,128]{1,0:T(8,128)S(1)}, u32[]{:S(2)}, u32[]{:S(2)}) %collective-permute-start.38) | collective-permute-done | bytes 450592 | tf_op jit(solution)/shard_map/ppermute | solution.py:114
  133.6 2.2 %unpack_own_chunk.1 = f32[1736,128]{1,0:T(8,128)} custom-call(s32[4]{0:T(128)S(1)} %pad_add_fusion.1.idx, f32[880,128]{1,0:T(8,128)S(1)} %fusion.3.own, f32[880,128]{1,0:T(8,128)S(1)} %collective-permute-done.38.twin), custom_call_target="tpu_custom_call" | custom-call | tf_op jit(solution)/shard_map/unpack_own_chunk/pallas_call | solution.py:759
  (149 shorter events, 24.3 us)
Async XLA Ops:
  3.0 12.5 %collective-permute-start = (bf16[880,128]{1,0:T(8,128)(2,1)S(1)}, bf16[880,128]{1,0:T(8,128)(2,1)S(1)}, u32[]{:S(2)}, u32[]{:S(2)}) collective-permute-start(bf16[880,128]{1,0:T(8,128)(2,1)S(1)} %pack_own_chunk.1), channel_id=1, source_target_pairs={{0,8},{2,10},{4,12},{6,14},{8,0},{10,2},{12,4},{14,6},{16,24},{18,... | collective-permute-start | bytes 675848 | tf_op jit(solution)/shard_map/ppermute | solution.py:110
  5.9 19.0 %collective-permute-start.1 = (bf16[880,128]{1,0:T(8,128)(2,1)S(1)}, bf16[880,128]{1,0:T(8,128)(2,1)S(1)}, u32[]{:S(2)}, u32[]{:S(2)}) collective-permute-start(bf16[880,128]{1,0:T(8,128)(2,1)S(1)} %pack_own_chunk.1), channel_id=1, source_target_pairs={{0,16},{2,18},{4,20},{6,22},{8,24},{10,26},{12,28},{14,30},{16,0},... | collective-permute-start | bytes 675848 | tf_op jit(solution)/shard_map/ppermute | solution.py:110
  8.6 16.3 %collective-permute-start.2 = (bf16[880,128]{1,0:T(8,128)(2,1)S(1)}, bf16[880,128]{1,0:T(8,128)(2,1)S(1)}, u32[]{:S(2)}, u32[]{:S(2)}) collective-permute-start(bf16[880,128]{1,0:T(8,128)(2,1)S(1)} %pack_own_chunk.1), channel_id=1, source_target_pairs={{0,24},{2,26},{4,28},{6,30},{8,16},{10,18},{12,20},{14,22},{16,8},... | collective-permute-start | bytes 675848 | tf_op jit(solution)/shard_map/ppermute | solution.py:110
  8.6 16.3 %collective-permute-start.3 = (bf16[880,128]{1,0:T(8,128)(2,1)S(1)}, bf16[880,128]{1,0:T(8,128)(2,1)S(1)}, u32[]{:S(2)}, u32[]{:S(2)}) collective-permute-start(bf16[880,128]{1,0:T(8,128)(2,1)S(1)} %pack_own_chunk.1), channel_id=1, source_target_pairs={{0,2},{1,5},{2,0},{3,7},{4,6},{5,1},{6,4},{7,3},{8,10},{9,13},{10,... | collective-permute-start | bytes 675848 | tf_op jit(solution)/shard_map/ppermute | solution.py:119
  10.4 14.5 %collective-permute-start.4 = (bf16[880,128]{1,0:T(8,128)(2,1)S(1)}, bf16[880,128]{1,0:T(8,128)(2,1)S(1)}, u32[]{:S(2)}, u32[]{:S(2)}) collective-permute-start(bf16[880,128]{1,0:T(8,128)(2,1)S(1)} %pack_own_chunk.1), channel_id=1, source_target_pairs={{0,4},{1,3},{2,6},{3,1},{4,0},{5,7},{6,2},{7,5},{8,12},{9,11},{10,... | collective-permute-start | bytes 675848 | tf_op jit(solution)/shard_map/ppermute | solution.py:119
  15.4 9.4 %collective-permute-start.5 = (bf16[880,128]{1,0:T(8,128)(2,1)S(1)}, bf16[880,128]{1,0:T(8,128)(2,1)S(1)}, u32[]{:S(2)}, u32[]{:S(2)}) collective-permute-start(bf16[880,128]{1,0:T(8,128)(2,1)S(1)} %pack_own_chunk.1), channel_id=1, source_target_pairs={{0,6},{1,7},{2,4},{3,5},{4,2},{5,3},{6,0},{7,1},{8,14},{9,15},{10,... | collective-permute-start | bytes 675848 | tf_op jit(solution)/shard_map/ppermute | solution.py:119
  24.9 6.0 %collective-permute-start.8 = (bf16[880,128]{1,0:T(8,128)(2,1)S(1)}, bf16[880,128]{1,0:T(8,128)(2,1)S(1)}, u32[]{:S(2)}, u32[]{:S(2)}) collective-permute-start(bf16[880,128]{1,0:T(8,128)(2,1)S(1)} %collective-permute-done.2), channel_id=1, source_target_pairs={{0,2},{1,5},{2,0},{3,7},{4,6},{5,1},{6,4},{7,3},{8,10},{9,13},{10,... | collective-permute-start | bytes 675848 | tf_op jit(solution)/shard_map/ppermute | solution.py:119
  26.4 8.4 %collective-permute-start.7 = (bf16[880,128]{1,0:T(8,128)(2,1)S(1)}, bf16[880,128]{1,0:T(8,128)(2,1)S(1)}, u32[]{:S(2)}, u32[]{:S(2)}) collective-permute-start(bf16[880,128]{1,0:T(8,128)(2,1)S(1)} %collective-permute-done.1), channel_id=1, source_target_pairs={{0,2},{1,5},{2,0},{3,7},{4,6},{5,1},{6,4},{7,3},{8,10},{9,13},{10,... | collective-permute-start | bytes 675848 | tf_op jit(solution)/shard_map/ppermute | solution.py:119
  27.0 12.7 %collective-permute-start.6 = (bf16[880,128]{1,0:T(8,128)(2,1)S(1)}, bf16[880,128]{1,0:T(8,128)(2,1)S(1)}, u32[]{:S(2)}, u32[]{:S(2)}) collective-permute-start(bf16[880,128]{1,0:T(8,128)(2,1)S(1)} %collective-permute-done), channel_id=1, source_target_pairs={{0,2},{1,5},{2,0},{3,7},{4,6},{5,1},{6,4},{7,3},{8,10},{9,13},{10,... | collective-permute-start | bytes 675848 | tf_op jit(solution)/shard_map/ppermute | solution.py:119
  28.5 20.7 %collective-permute-start.10 = (bf16[4,880,128]{2,1,0:T(8,128)(2,1)S(1)}, bf16[4,880,128]{2,1,0:T(8,128)(2,1)S(1)}, u32[]{:S(2)}, u32[]{:S(2)}) collective-permute-start(bf16[4,880,128]{2,1,0:T(8,128)(2,1)S(1)} %pad_maximum_fusion.refs_0_), channel_id=1, source_target_pairs={{0,1},{1,0},{2,3},{3,2},{4,5},{5,4},{6,7},{7,6},{8,9},{9,8},{10,11... | collective-permute-start | bytes 2703368 | tf_op jit(solution)/shard_map/ppermute | solution.py:114
  31.0 8.7 %collective-permute-start.16 = (bf16[2,880,128]{2,1,0:T(8,128)(2,1)S(1)}, bf16[2,880,128]{2,1,0:T(8,128)(2,1)S(1)}, u32[]{:S(2)}, u32[]{:S(2)}) collective-permute-start(bf16[2,880,128]{2,1,0:T(8,128)(2,1)S(1)} %pad_maximum_fusion.3.refs_3_), channel_id=1, source_target_pairs={{0,4},{1,3},{2,6},{3,1},{4,0},{5,7},{6,2},{7,5},{8,12},{9,11},{10,... | collective-permute-start | bytes 1351688 | tf_op jit(solution)/shard_map/ppermute | solution.py:119
  32.5 8.2 %collective-permute-start.13 = (bf16[2,880,128]{2,1,0:T(8,128)(2,1)S(1)}, bf16[2,880,128]{2,1,0:T(8,128)(2,1)S(1)}, u32[]{:S(2)}, u32[]{:S(2)}) collective-permute-start(bf16[2,880,128]{2,1,0:T(8,128)(2,1)S(1)} %pad_maximum_fusion.3.refs_3_), channel_id=1, source_target_pairs={{0,1},{1,0},{2,3},{3,2},{4,5},{5,4},{6,7},{7,6},{8,9},{9,8},{10,11... | collective-permute-start | bytes 1351688 | tf_op jit(solution)/shard_map/ppermute | solution.py:114
  34.9 9.4 %collective-permute-start.14 = (bf16[2,880,128]{2,1,0:T(8,128)(2,1)S(1)}, bf16[2,880,128]{2,1,0:T(8,128)(2,1)S(1)}, u32[]{:S(2)}, u32[]{:S(2)}) collective-permute-start(bf16[2,880,128]{2,1,0:T(8,128)(2,1)S(1)} %pad_maximum_fusion.2.refs_2_), channel_id=1, source_target_pairs={{0,4},{1,3},{2,6},{3,1},{4,0},{5,7},{6,2},{7,5},{8,12},{9,11},{10,... | collective-permute-start | bytes 1351688 | tf_op jit(solution)/shard_map/ppermute | solution.py:119
  39.6 6.0 %collective-permute-start.12 = (bf16[2,880,128]{2,1,0:T(8,128)(2,1)S(1)}, bf16[2,880,128]{2,1,0:T(8,128)(2,1)S(1)}, u32[]{:S(2)}, u32[]{:S(2)}) collective-permute-start(bf16[2,880,128]{2,1,0:T(8,128)(2,1)S(1)} %pad_maximum_fusion.2.refs_2_), channel_id=1, source_target_pairs={{0,1},{1,0},{2,3},{3,2},{4,5},{5,4},{6,7},{7,6},{8,9},{9,8},{10,11... | collective-permute-start | bytes 1351688 | tf_op jit(solution)/shard_map/ppermute | solution.py:114
  39.7 6.0 %collective-permute-start.11 = (bf16[2,880,128]{2,1,0:T(8,128)(2,1)S(1)}, bf16[2,880,128]{2,1,0:T(8,128)(2,1)S(1)}, u32[]{:S(2)}, u32[]{:S(2)}) collective-permute-start(bf16[2,880,128]{2,1,0:T(8,128)(2,1)S(1)} %pad_maximum_fusion.1.refs_1_), channel_id=1, source_target_pairs={{0,1},{1,0},{2,3},{3,2},{4,5},{5,4},{6,7},{7,6},{8,9},{9,8},{10,11... | collective-permute-start | bytes 1351688 | tf_op jit(solution)/shard_map/ppermute | solution.py:114
  40.7 8.5 %collective-permute-start.9 = (bf16[2,880,128]{2,1,0:T(8,128)(2,1)S(1)}, bf16[2,880,128]{2,1,0:T(8,128)(2,1)}, u32[]{:S(2)}, u32[]{:S(2)}) collective-permute-start(bf16[2,880,128]{2,1,0:T(8,128)(2,1)S(1)} %pad_maximum_fusion.1.refs_1_), channel_id=1, source_target_pairs={{0,4},{1,3},{2,6},{3,1},{4,0},{5,7},{6,2},{7,5},{8,12},{9,11},{10,... | collective-permute-start | bytes 1351688 | tf_op jit(solution)/shard_map/ppermute | solution.py:119
  44.3 5.9 %collective-permute-start.17 = (bf16[2,880,128]{2,1,0:T(8,128)(2,1)S(1)}, bf16[2,880,128]{2,1,0:T(8,128)(2,1)S(1)}, u32[]{:S(2)}, u32[]{:S(2)}) collective-permute-start(bf16[2,880,128]{2,1,0:T(8,128)(2,1)S(1)} %collective-permute-done.16.refs_6_), channel_id=1, source_target_pairs={{0,1},{1,0},{2,3},{3,2},{4,5},{5,4},{6,7},{7,6},{8,9},{9,8},{10,11... | collective-permute-start | bytes 1351688 | tf_op jit(solution)/shard_map/ppermute | solution.py:114
  75.0 13.3 %collective-permute-start.22 = (bf16[2,880,128]{2,1,0:T(8,128)(2,1)S(1)}, bf16[2,880,128]{2,1,0:T(8,128)(2,1)S(1)}, u32[]{:S(2)}, u32[]{:S(2)}) collective-permute-start(bf16[2,880,128]{2,1,0:T(8,128)(2,1)S(1)} %add_convert_fusion.5), channel_id=1, source_target_pairs={{0,4},{1,3},{2,6},{3,1},{4,0},{5,7},{6,2},{7,5},{8,12},{9,11},{10,... | collective-permute-start | bytes 1351688 | tf_op jit(solution)/shard_map/ppermute | solution.py:119
  76.7 11.6 %collective-permute-start.20 = (bf16[2,880,128]{2,1,0:T(8,128)(2,1)S(1)}, bf16[2,880,128]{2,1,0:T(8,128)(2,1)S(1)}, u32[]{:S(2)}, u32[]{:S(2)}) collective-permute-start(bf16[2,880,128]{2,1,0:T(8,128)(2,1)S(1)} %add_convert_fusion.6), channel_id=1, source_target_pairs={{0,4},{1,3},{2,6},{3,1},{4,0},{5,7},{6,2},{7,5},{8,12},{9,11},{10,... | collective-permute-start | bytes 1351688 | tf_op jit(solution)/shard_map/ppermute | solution.py:119
  77.3 11.1 %collective-permute-start.30 = (bf16[2,880,128]{2,1,0:T(8,128)(2,1)}, bf16[2,880,128]{2,1,0:T(8,128)(2,1)S(1)}, u32[]{:S(2)}, u32[]{:S(2)}) collective-permute-start(bf16[2,880,128]{2,1,0:T(8,128)(2,1)} %get-tuple-element.114), channel_id=1, source_target_pairs={{0,1},{1,0},{2,3},{3,2},{4,5},{5,4},{6,7},{7,6},{8,9},{9,8},{10,11... | collective-permute-start | bytes 1351688 | tf_op jit(solution)/shard_map/ppermute | solution.py:114
  77.4 15.2 %collective-permute-start.28 = (bf16[2,880,128]{2,1,0:T(8,128)(2,1)S(1)}, bf16[2,880,128]{2,1,0:T(8,128)(2,1)S(1)}, u32[]{:S(2)}, u32[]{:S(2)}) collective-permute-start(bf16[2,880,128]{2,1,0:T(8,128)(2,1)S(1)} %copy-done.29), channel_id=1, source_target_pairs={{0,1},{1,0},{2,3},{3,2},{4,5},{5,4},{6,7},{7,6},{8,9},{9,8},{10,11... | collective-permute-start | bytes 1351688 | tf_op jit(solution)/shard_map/ppermute | solution.py:114
  88.7 19.5 %collective-permute-start.31 = (bf16[880,128]{1,0:T(8,128)(2,1)S(1)}, bf16[880,128]{1,0:T(8,128)(2,1)S(1)}, u32[]{:S(2)}, u32[]{:S(2)}) collective-permute-start(bf16[880,128]{1,0:T(8,128)(2,1)S(1)} %slice_bitcast_fusion), channel_id=1, source_target_pairs={{0,2},{1,5},{2,0},{3,7},{4,6},{5,1},{6,4},{7,3},{8,10},{9,13},{10,... | collective-permute-start | bytes 675848 | tf_op jit(solution)/shard_map/ppermute | solution.py:119
  90.5 12.9 %collective-permute-start.23 = (bf16[4,880,128]{2,1,0:T(8,128)(2,1)S(1)}, bf16[4,880,128]{2,1,0:T(8,128)(2,1)S(1)}, u32[]{:S(2)}, u32[]{:S(2)}) collective-permute-start(bf16[4,880,128]{2,1,0:T(8,128)(2,1)S(1)} %broadcast_select_fusion), channel_id=1, source_target_pairs={{0,1},{1,0},{2,3},{3,2},{4,5},{5,4},{6,7},{7,6},{8,9},{9,8},{10,11... | collective-permute-start | bytes 2703368 | tf_op jit(solution)/shard_map/ppermute | solution.py:114
  91.0 10.9 %collective-permute-start.26 = (bf16[2,880,128]{2,1,0:T(8,128)(2,1)S(1)}, bf16[2,880,128]{2,1,0:T(8,128)(2,1)S(1)}, u32[]{:S(2)}, u32[]{:S(2)}) collective-permute-start(bf16[2,880,128]{2,1,0:T(8,128)(2,1)S(1)} %add_convert_fusion.4), channel_id=1, source_target_pairs={{0,4},{1,3},{2,6},{3,1},{4,0},{5,7},{6,2},{7,5},{8,12},{9,11},{10,... | collective-permute-start | bytes 1351688 | tf_op jit(solution)/shard_map/ppermute | solution.py:119
  92.8 15.4 %collective-permute-start.29 = (bf16[880,128]{1,0:T(8,128)(2,1)S(1)}, bf16[880,128]{1,0:T(8,128)(2,1)S(1)}, u32[]{:S(2)}, u32[]{:S(2)}) collective-permute-start(bf16[880,128]{1,0:T(8,128)(2,1)S(1)} %slice_bitcast_fusion.2), channel_id=1, source_target_pairs={{0,2},{1,5},{2,0},{3,7},{4,6},{5,1},{6,4},{7,3},{8,10},{9,13},{10,... | collective-permute-start | bytes 675848 | tf_op jit(solution)/shard_map/ppermute | solution.py:119
  102.1 6.0 %collective-permute-start.27 = (bf16[880,128]{1,0:T(8,128)(2,1)S(1)}, bf16[880,128]{1,0:T(8,128)(2,1)S(1)}, u32[]{:S(2)}, u32[]{:S(2)}) collective-permute-start(bf16[880,128]{1,0:T(8,128)(2,1)S(1)} %slice_bitcast_fusion.4), channel_id=1, source_target_pairs={{0,2},{1,5},{2,0},{3,7},{4,6},{5,1},{6,4},{7,3},{8,10},{9,13},{10,... | collective-permute-start | bytes 675848 | tf_op jit(solution)/shard_map/ppermute | solution.py:119
  108.4 12.6 %collective-permute-start.32 = (bf16[880,128]{1,0:T(8,128)(2,1)S(1)}, bf16[880,128]{1,0:T(8,128)(2,1)S(1)}, u32[]{:S(2)}, u32[]{:S(2)}) collective-permute-start(bf16[880,128]{1,0:T(8,128)(2,1)S(1)} %get-tuple-element.123), channel_id=1, source_target_pairs={{0,8},{2,10},{4,12},{6,14},{8,0},{10,2},{12,4},{14,6},{16,24},{18,... | collective-permute-start | bytes 675848 | tf_op jit(solution)/shard_map/ppermute | solution.py:110
  112.5 19.0 %collective-permute-start.33 = (bf16[880,128]{1,0:T(8,128)(2,1)S(1)}, bf16[880,128]{1,0:T(8,128)(2,1)S(1)}, u32[]{:S(2)}, u32[]{:S(2)}) collective-permute-start(bf16[880,128]{1,0:T(8,128)(2,1)S(1)} %get-tuple-element.122), channel_id=1, source_target_pairs={{0,16},{2,18},{4,20},{6,22},{8,24},{10,26},{12,28},{14,30},{16,0},... | collective-permute-start | bytes 675848 | tf_op jit(solution)/shard_map/ppermute | solution.py:110
  113.6 17.9 %collective-permute-start.34 = (bf16[880,128]{1,0:T(8,128)(2,1)S(1)}, bf16[880,128]{1,0:T(8,128)(2,1)S(1)}, u32[]{:S(2)}, u32[]{:S(2)}) collective-permute-start(bf16[880,128]{1,0:T(8,128)(2,1)S(1)} %get-tuple-element.127), channel_id=1, source_target_pairs={{0,24},{2,26},{4,28},{6,30},{8,16},{10,18},{12,20},{14,22},{16,8},... | collective-permute-start | bytes 675848 | tf_op jit(solution)/shard_map/ppermute | solution.py:110
  115.0 16.5 %collective-permute-start.35 = (bf16[880,128]{1,0:T(8,128)(2,1)S(1)}, bf16[880,128]{1,0:T(8,128)(2,1)S(1)}, u32[]{:S(2)}, u32[]{:S(2)}) collective-permute-start(bf16[880,128]{1,0:T(8,128)(2,1)S(1)} %get-tuple-element.126), channel_id=1, source_target_pairs={{0,2},{1,5},{2,0},{3,7},{4,6},{5,1},{6,4},{7,3},{8,10},{9,13},{10,... | collective-permute-start | bytes 675848 | tf_op jit(solution)/shard_map/ppermute | solution.py:119
  116.3 15.2 %collective-permute-start.36 = (bf16[880,128]{1,0:T(8,128)(2,1)S(1)}, bf16[880,128]{1,0:T(8,128)(2,1)S(1)}, u32[]{:S(2)}, u32[]{:S(2)}) collective-permute-start(bf16[880,128]{1,0:T(8,128)(2,1)S(1)} %get-tuple-element.125), channel_id=1, source_target_pairs={{0,4},{1,3},{2,6},{3,1},{4,0},{5,7},{6,2},{7,5},{8,12},{9,11},{10,... | collective-permute-start | bytes 675848 | tf_op jit(solution)/shard_map/ppermute | solution.py:119
  121.0 10.5 %collective-permute-start.37 = (bf16[880,128]{1,0:T(8,128)(2,1)S(1)}, bf16[880,128]{1,0:T(8,128)(2,1)S(1)}, u32[]{:S(2)}, u32[]{:S(2)}) collective-permute-start(bf16[880,128]{1,0:T(8,128)(2,1)S(1)} %get-tuple-element.124), channel_id=1, source_target_pairs={{0,6},{1,7},{2,4},{3,5},{4,2},{5,3},{6,0},{7,1},{8,14},{9,15},{10,... | collective-permute-start | bytes 675848 | tf_op jit(solution)/shard_map/ppermute | solution.py:119
  (43 other events, 369.1 us)
